TPU v7x, 512 devices: a whole 4x8x8 slice. The times are simulated.
512 devices in a mesh: ctx: 64 (over z, y_hi, core), head: 8 (over y_lo, x).
Axes of the slice: x: 4, y: 8 (y_hi: 4, y_lo: 2; y = y_hi * 2 + y_lo), z: 8, core: 2. Of those that a mesh axis runs over, the one named last changes fastest.
Arguments:
- queries: bfloat16 [8192, 2048], P('ctx', 'head'), may hold values from -100 to 100
- keys: bfloat16 [8192, 2048], P('ctx', 'head'), may hold values from -50 to 50
- values: bfloat16 [8192, 2048], P('ctx', 'head'), may hold values from -6 to 6
- out_weight: bfloat16 [2048, 4096], P('head'), may hold values from -0.125 to 0.125
- mixed_grad: bfloat16 [8192, 4096], P('ctx', 'head'), may hold values from -6 to 6
- lengths: int32 [64], replicated, may hold values from 1 to 384, 8192 in all
- dilation: int32 [16], P('head'), may hold values from 1 to 8
Outputs:
- mixed: bfloat16 [8192, 4096], P('ctx', 'head')
- grad_queries: bfloat16 [8192, 2048], P('ctx', 'head')
- grad_keys: bfloat16 [8192, 2048], P('ctx', 'head')
- grad_values: bfloat16 [8192, 2048], P('ctx', 'head')
Inputs may be any that keep to these rules, and one draw needn't show every extreme that they name: The lengths sum to 8192, and the longest document has exactly 384 tokens.
All inputs are finite; a program needn't handle non-finite values.
Results may differ from a plain program's by a relative error of at most 0.029.
Values may be sent and summed in bfloat16 or wider, within the bound.
No kernel may reach another device: no remote copies, remote signals or barrier semaphores. Data moves between devices by JAX's collectives and lax.ppermute only.
A program may use at most 64 MiB of HBM per device.

v0:
```python
import jax
import jax.numpy as jnp
from jax import lax
from jax.sharding import PartitionSpec as P

HALF = 32
MAXD = 8


def passed_along(value, axis, steps):
    count = lax.axis_size(axis)
    initial, last = (max(0, -steps), min(count, count - steps))
    return lax.ppermute(value, axis, [(source, source + steps) for source in range(initial, last)])


def in_blocks(x, dim, length):
    before, after = (x.shape[:dim], x.shape[dim + 1 :])
    return jnp.moveaxis(x.reshape(*before, length, -1, *after), dim, 0)


def sent_and_summed(x, axis, dim):
    length = lax.axis_size(axis)
    blocks = lax.all_to_all(in_blocks(x, dim, length), axis, 0, 0, tiled=True)
    return jnp.sum(blocks.astype(jnp.float32), axis=0)


def from_everyone(x, axis):
    length = lax.axis_size(axis)
    return lax.all_to_all(jnp.broadcast_to(x[None], (length, *x.shape)), axis, 0, 0, tiled=True)


def laid_out(blocks, dim):
    blocks = jnp.moveaxis(blocks, 0, dim)
    dims = blocks.shape
    return blocks.reshape(*dims[:dim], dims[dim] * dims[dim + 1], *dims[dim + 2 :])


def collect(x, axis, dim):
    blocks = from_everyone(x, axis)
    return laid_out(blocks, dim)


def segment_of(positions, lengths):
    boundary = jnp.cumsum(lengths)
    return jnp.sum((positions[:, None] >= boundary[None, :]).astype(jnp.int32), axis=1)


def allowed(query_pos, key_pos, query_seg, key_seg, dilation, reach, total):
    offset_grid = query_pos[:, None] - key_pos[None, :]
    common = (
        (query_seg[:, None] == key_seg[None, :])
        & (key_pos[None, :] >= 0)
        & (key_pos[None, :] < total)
    )
    common = common & (query_pos[:, None] >= 0) & (query_pos[:, None] < total)
    stride = dilation[:, None, None]
    within = (jnp.abs(offset_grid)[None] <= reach * stride) & (
        jnp.remainder(offset_grid[None], stride) == 0
    )
    return within & common[None]


def scores_of(query_heads, key_heads, factor):
    return (
        jnp.einsum("thd,shd->hts", query_heads, key_heads, preferred_element_type=jnp.float32)
        * factor
    )


def weights_and_slopes(
    query_heads, key_heads, value_heads, grad_heads, log_total, row_delta, mask, factor
):
    scores = scores_of(query_heads, key_heads, factor)
    weights = jnp.where(mask, jnp.exp(scores - log_total[:, :, None]), 0.0)
    grad_prob = jnp.einsum(
        "thd,shd->hts", grad_heads, value_heads, preferred_element_type=jnp.float32
    )
    slopes = (weights * (grad_prob - row_delta[:, :, None])).astype(jnp.bfloat16)
    return (weights.astype(jnp.bfloat16), slopes)


def per_device(queries, keys, values, out_weight, mixed_grad, lengths, dilation):
    row_count = queries.shape[0]
    local_heads = dilation.shape[0]
    head_width = queries.shape[1] // local_heads
    factor = head_width ** (-0.5)
    total = row_count * lax.axis_size("ctx")
    hop_count = (HALF * MAXD + row_count - 1) // row_count
    device_index = lax.axis_index("ctx")
    flat_width = local_heads * head_width

    def locate(offset):
        positions = (device_index + offset) * row_count + jnp.arange(row_count, dtype=jnp.int32)
        return (positions, segment_of(positions, lengths))

    def split(array):
        return array.reshape(row_count, local_heads, head_width)

    offset_list = [0]
    for distance in range(1, hop_count + 1):
        offset_list = offset_list + [distance, -distance]
    own_pos, own_seg = locate(0)
    slab_store = {0: (keys, values)}
    for offset in offset_list[1:]:
        slab_store[offset] = passed_along((keys, values), "ctx", -offset)
    query_heads = split(queries)
    masks = {}
    running_top = jnp.full((local_heads, row_count), -jnp.inf, jnp.float32)
    running_sum = jnp.zeros((local_heads, row_count), jnp.float32)
    for offset in offset_list:
        key_pos, key_seg = locate(offset)
        mask = allowed(own_pos, key_pos, own_seg, key_seg, dilation, HALF, total)
        masks[offset] = mask

        def update(top_now=running_top, sum_now=running_sum, offset=offset, mask=mask):
            scores = scores_of(query_heads, split(slab_store[offset][0]), factor)
            top_new = jnp.maximum(top_now, jnp.max(jnp.where(mask, scores, -jnp.inf), axis=2))
            fresh = jnp.sum(jnp.where(mask, jnp.exp(scores - top_new[:, :, None]), 0.0), axis=2)
            return (top_new, sum_now * jnp.exp(top_now - top_new) + fresh)

        running_top, running_sum = update()
    log_total = running_top + jnp.log(running_sum)
    context = jnp.zeros((row_count, local_heads, head_width), jnp.float32)
    for offset in offset_list:

        def accumulate(context_now=context, offset=offset):
            mask = masks[offset]
            scores = scores_of(query_heads, split(slab_store[offset][0]), factor)
            probs = jnp.where(mask, jnp.exp(scores - log_total[:, :, None]), 0.0).astype(
                jnp.bfloat16
            )
            return context_now + jnp.einsum(
                "hts,shd->thd",
                probs,
                split(slab_store[offset][1]),
                preferred_element_type=jnp.float32,
            )

        context = accumulate()
    attention = context.astype(jnp.bfloat16).reshape(row_count, flat_width)
    partial_value = jnp.dot(attention, out_weight, preferred_element_type=jnp.float32)
    mixed = sent_and_summed(partial_value.astype(jnp.bfloat16), "head", 1).astype(jnp.bfloat16)
    grad_attention = lax.dot_general(
        collect(mixed_grad, "head", 1),
        out_weight,
        (((1,), (1,)), ((), ())),
        preferred_element_type=jnp.float32,
    ).astype(jnp.bfloat16)
    grad_heads = split(grad_attention)
    row_delta = jnp.sum(
        grad_heads.astype(jnp.float32) * context.astype(jnp.bfloat16).astype(jnp.float32), axis=2
    ).T
    zero_flat = jnp.zeros((row_count, flat_width), jnp.float32)
    grad_query = zero_flat
    grad_key = zero_flat
    grad_value = zero_flat
    for offset in offset_list:

        def all_terms(offset=offset):
            key_heads = split(slab_store[offset][0])
            value_heads = split(slab_store[offset][1])
            probs, slopes = weights_and_slopes(
                query_heads,
                key_heads,
                value_heads,
                grad_heads,
                log_total,
                row_delta,
                masks[offset],
                factor,
            )
            query_term = (
                jnp.einsum("hts,shd->thd", slopes, key_heads, preferred_element_type=jnp.float32)
                * factor
            )
            key_term = (
                jnp.einsum("hts,thd->shd", slopes, query_heads, preferred_element_type=jnp.float32)
                * factor
            )
            value_term = jnp.einsum(
                "hts,thd->shd", probs, grad_heads, preferred_element_type=jnp.float32
            )
            return (
                query_term.reshape(row_count, flat_width),
                key_term.reshape(row_count, flat_width),
                value_term.reshape(row_count, flat_width),
            )

        query_term, key_term, value_term = all_terms()
        grad_query = grad_query + query_term
        if offset == 0:
            grad_key = key_term
            grad_value = value_term
        else:
            key_back, value_back = (
                passed_along(key_term.astype(jnp.bfloat16), "ctx", offset).astype(key_term.dtype),
                passed_along(value_term.astype(jnp.bfloat16), "ctx", offset).astype(
                    value_term.dtype
                ),
            )
            grad_key = grad_key + key_back
            grad_value = grad_value + value_back
    return (
        mixed,
        grad_query.astype(jnp.bfloat16),
        grad_key.astype(jnp.bfloat16),
        grad_value.astype(jnp.bfloat16),
    )


def solution(mesh):
    placed = (
        P("ctx", "head"),
        P("ctx", "head"),
        P("ctx", "head"),
        P("head", None),
        P("ctx", "head"),
        P(),
        P("head"),
    )
    return jax.shard_map(
        per_device,
        mesh=mesh,
        in_specs=placed,
        out_specs=(P("ctx", "head"), P("ctx", "head"), P("ctx", "head"), P("ctx", "head")),
        check_vma=False,
    )
```

profile of v0, /device:TPU:244, one launch (start us, length us, event | category | flops | bytes accessed | tf_op | source)
XLA Modules:
  0.0 156.4 jit_solution(6528619388484020936)
XLA Ops:
  0.6 1.7 %copy.343 = bf16[128,256]{0,1:T(8,128)(2,1)} copy(bf16[128,256]{1,0:T(8,128)(2,1)} %param.10) | data formatting | bytes 131072 | tf_op jit(solution)/shard_map/reshape | solution.py:97
  2.4 4.8 %collective-permute-start.3 = (bf16[128,256]{0,1:T(8,128)(2,1)}, bf16[128,256]{0,1:T(8,128)(2,1)S(1)}, u32[]{:S(2)}, u32[]{:S(2)}) collective-permute-start(bf16[128,256]{0,1:T(8,128)(2,1)} %copy.343), channel_id=1, source_target_pairs={{0,16},{8,24},{16,32},{24,40},{32,48},{40,56},{48,64},{56,72},{64,... | collective-permute-start | bytes 196616 | tf_op jit(solution)/shard_map/ppermute | solution.py:13
  7.2 1.9 %collective-permute-start.2 = (bf16[128,256]{0,1:T(8,128)(2,1)}, bf16[128,256]{0,1:T(8,128)(2,1)S(1)}, u32[]{:S(2)}, u32[]{:S(2)}) collective-permute-start(bf16[128,256]{0,1:T(8,128)(2,1)} %copy.343), channel_id=1, source_target_pairs={{16,0},{24,8},{32,16},{40,24},{48,32},{56,40},{64,48},{72,56},{80,... | collective-permute-start | bytes 196616 | tf_op jit(solution)/shard_map/ppermute | solution.py:13
  9.1 1.9 %collective-permute-start.1 = (bf16[128,256]{0,1:T(8,128)(2,1)}, bf16[128,256]{0,1:T(8,128)(2,1)S(1)}, u32[]{:S(2)}, u32[]{:S(2)}) collective-permute-start(bf16[128,256]{0,1:T(8,128)(2,1)} %copy.343), channel_id=1, source_target_pairs={{0,8},{8,16},{16,24},{24,32},{32,40},{40,48},{48,56},{56,64},{64,7... | collective-permute-start | bytes 196616 | tf_op jit(solution)/shard_map/ppermute | solution.py:13
  11.0 4.5 %collective-permute-start = (bf16[128,256]{0,1:T(8,128)(2,1)}, bf16[128,256]{0,1:T(8,128)(2,1)}, u32[]{:S(2)}, u32[]{:S(2)}) collective-permute-start(bf16[128,256]{0,1:T(8,128)(2,1)} %copy.343), channel_id=1, source_target_pairs={{8,0},{16,8},{24,16},{32,24},{40,32},{48,40},{56,48},{64,56},{72,6... | collective-permute-start | bytes 196616 | tf_op jit(solution)/shard_map/ppermute | solution.py:13
  15.6 1.0 copy.255
  16.6 1.1 broadcast_in_dim.38
  17.7 5.8 %all-to-all-start.1 = ((bf16[8,128,512]{1,2,0:T(8,128)(2,1)}), bf16[8,128,512]{1,2,0:T(8,128)(2,1)S(1)}, u32[]{:S(2)}, u32[]{:S(2)}) async-start(bf16[8,128,512]{1,2,0:T(8,128)(2,1)} %broadcast_in_dim.38), calls=%async_computation.1 | async-start | bytes 2097152 | tf_op jit(solution)/shard_map/all_to_all | solution.py:29
  23.5 1.9 %collective-permute-start.4 = (bf16[128,256]{1,0:T(8,128)(2,1)}, bf16[128,256]{1,0:T(8,128)(2,1)}, u32[]{:S(2)}, u32[]{:S(2)}) collective-permute-start(bf16[128,256]{1,0:T(8,128)(2,1)} %param.11), channel_id=1, source_target_pairs={{8,0},{16,8},{24,16},{32,24},{40,32},{48,40},{56,48},{64,56},{72,6... | collective-permute-start | bytes 196616 | tf_op jit(solution)/shard_map/ppermute | solution.py:13
  28.4 0.8 subtract_abs_fusion.3
  29.3 0.8 subtract_bitcast_fusion.3
  30.1 1.2 broadcast_multiply_fusion
  31.3 1.2 compare_bitcast_fusion
  32.5 1.2 fusion.56
  34.7 1.4 convert_reduce_fusion.1
  36.0 0.9 copy.342
  37.0 1.1 and_and_fusion.3
  38.1 2.3 %select_reduce_fusion.9 = (f32[2,128]{1,0:T(2,128)S(1)}, pred[2,128,128]{1,2,0:T(32,128)(4,1)S(1)}, f32[2,128,128]{1,2,0:T(8,128)S(1)}) fusion(pred[128,128]{0,1:T(8,128)(4,1)S(1)} %get-tuple-element.50, pred[2]{0:T(512)(128)(4,1)} %compare_bitcast_fusion, s32[2]{0:T(128)} %fusion.56, s32[128,128]{0,1:T(8,128)S(1)} %get-tuple-element.60, ...), kind=kOutput, calls=%fused_computation.89 | convolution fusion | flops 8847104 | bytes 443410 | tf_op jit(solution)/shard_map/thd,shd->hts/dot_general | solution.py:65
  40.5 5.6 %collective-permute-start.6 = (bf16[128,256]{1,0:T(8,128)(2,1)}, bf16[128,256]{1,0:T(8,128)(2,1)}, u32[]{:S(2)}, u32[]{:S(2)}) collective-permute-start(bf16[128,256]{1,0:T(8,128)(2,1)} %param.11), channel_id=1, source_target_pairs={{16,0},{24,8},{32,16},{40,24},{48,32},{56,40},{64,48},{72,56},{80,... | collective-permute-start | bytes 196616 | tf_op jit(solution)/shard_map/ppermute | solution.py:13
  46.3 7.8 %collective-permute-start.7 = (bf16[128,256]{1,0:T(8,128)(2,1)}, bf16[128,256]{1,0:T(8,128)(2,1)}, u32[]{:S(2)}, u32[]{:S(2)}) collective-permute-start(bf16[128,256]{1,0:T(8,128)(2,1)} %param.11), channel_id=1, source_target_pairs={{0,16},{8,24},{16,32},{24,40},{32,48},{40,56},{48,64},{56,72},{64,... | collective-permute-start | bytes 196616 | tf_op jit(solution)/shard_map/ppermute | solution.py:13
  54.1 1.1 convolution_multiply_fusion.6
  55.2 2.1 %collective-permute-start.5 = (bf16[128,256]{1,0:T(8,128)(2,1)}, bf16[128,256]{1,0:T(8,128)(2,1)}, u32[]{:S(2)}, u32[]{:S(2)}) collective-permute-start(bf16[128,256]{1,0:T(8,128)(2,1)} %param.11), channel_id=1, source_target_pairs={{0,8},{8,16},{16,24},{24,32},{32,40},{40,48},{48,56},{56,64},{64,7... | collective-permute-start | bytes 196616 | tf_op jit(solution)/shard_map/ppermute | solution.py:13
  58.2 7.6 %select_reduce_fusion.8 = (f32[2,128]{1,0:T(2,128)S(1)}, pred[2,128,128]{1,2,0:T(32,128)(4,1)}, f32[2,128]{1,0:T(2,128)S(1)}, pred[2,128,128]{1,2,0:T(32,128)(4,...) fusion(pred[128,128]{0,1:T(8,128)(4,1)S(1)} %get-tuple-element., ...), kind=kOutput, calls=%fused_computation.88 | convolution fusion | flops 10124288 | bytes 1380370 | tf_op jit(solution)/shard_map/thd,shd->hts/dot_general | solution.py:65
  65.9 0.9 copy.246
  66.8 1.6 %copy.250 = bf16[128,256]{0,1:T(8,128)(2,1)} copy(bf16[128,256]{1,0:T(8,128)(2,1)} %collective-permute-done.6) | data formatting | bytes 131072 | tf_op jit(solution)/shard_map/ppermute | solution.py:13
  68.4 1.6 %copy.252 = bf16[128,256]{0,1:T(8,128)(2,1)} copy(bf16[128,256]{1,0:T(8,128)(2,1)} %collective-permute-done.7) | data formatting | bytes 131072 | tf_op jit(solution)/shard_map/ppermute | solution.py:13
  70.0 1.6 copy.248
  72.2 1.0 select_reduce_fusion.2
  73.2 0.8 select_reduce_fusion.1
  74.0 0.8 select_reduce_fusion
  74.8 1.0 select_reduce_fusion.3
  75.8 1.1 fusion.51
  77.0 1.7 %fusion.61 = f32[2,128,128]{1,2,0:T(8,128)} fusion(bf16[128,2,128]{0,2,1:T(8,128)(2,1)} %bitcast.180, pred[2,128,128]{1,2,0:T(32,128)(4,1)} %get-tuple-element.43, f32[2,128,128]{1,2,0:T(8,128)S(1)} %convolution_multiply_fusion.6, f32[2,128]{1,0:T(2,128)S(1)} %log_add_fusion), kind=kOutput, calls=%fused_computation.161 | convolution fusion | flops 8486912 | bytes 361472 | tf_op jit(solution)/shard_map/hts,shd->thd/dot_general | solution.py:132
  78.6 1.6 %fusion.58 = f32[2,128,128]{1,2,0:T(8,128)} fusion(bf16[128,2,128]{0,2,1:T(8,128)(2,1)} %bitcast.182, pred[2,128,128]{1,2,0:T(32,128)(4,1)} %get-tuple-element.45, f32[2,128,128]{1,2,0:T(8,128)S(1)} %convolution_multiply_fusion.5, f32[2,128]{1,0:T(2,128)S(1)} %log_add_fusion), kind=kOutput, calls=%fused_computation.160 | convolution fusion | flops 8486912 | bytes 361472 | tf_op jit(solution)/shard_map/hts,shd->thd/dot_general | solution.py:132
  80.3 1.7 %convolution_add_fusion.3 = f32[2,128,128]{1,2,0:T(8,128)} fusion(f32[2,128,128]{1,2,0:T(8,128)S(1)} %fusion.51, bf16[128,2,128]{0,2,1:T(8,128)(2,1)S(1)} %bitcast.176, pred[2,128,128]{1,2,0:T(32,128)(4,1)} %get-tuple-element.37, f32[2,128,128]{1,2,0:T(8,128)} %get-tuple-element.61, f32[2,128]{1,0:T(2,128)S(1)} %log_add_fusion), kind=kOutput, calls=%fused_computation.5 | convolution fusion | flops 8519680 | bytes 492544 | tf_op jit(solution)/shard_map/hts,shd->thd/dot_general | solution.py:132
  82.0 1.5 convolution_convert_fusion.1
  83.6 1.0 copy.256
  84.6 1.8 %convolution_convert_fusion.5 = bf16[2,128,128]{2,1,0:T(8,128)(2,1)} fusion(bf16[128,2,128]{0,2,1:T(8,128)(2,1)S(1)} %bitcast.153, pred[2,128,128]{1,2,0:T(32,128)(4,1)} %get-tuple-element.37, f32[2,128,128]{1,2,0:T(8,128)} %get-tuple-element.61, f32[2,128]{1,0:T(2,128)S(1)} %log_add_fusion), kind=kOutput, calls=%fused_computation.45 | convolution fusion | flops 8519680 | bytes 295936 | tf_op jit(solution)/shard_map/hts,thd->shd/dot_general | solution.py:180
  86.4 1.7 %convolution_convert_fusion.4 = bf16[2,128,128]{2,1,0:T(8,128)(2,1)} fusion(bf16[128,2,128]{0,2,1:T(8,128)(2,1)S(1)} %bitcast.154, pred[2,128,128]{1,2,0:T(32,128)(4,1)} %get-tuple-element.41, f32[2,128,128]{1,2,0:T(8,128)} %copy-done.1, f32[2,128]{1,0:T(2,128)S(1)} %log_add_fusion), kind=kOutput, calls=%fused_computation.44 | convolution fusion | flops 8519680 | bytes 295936 | tf_op jit(solution)/shard_map/hts,thd->shd/dot_general | solution.py:180
  88.1 0.9 convolution_convert_fusion.3
  89.1 0.9 convolution_convert_fusion.2
  90.0 1.3 multiply_reduce_fusion
  91.6 1.0 fusion.11
  93.3 1.0 fusion.76
  94.6 1.6 %copy.295 = bf16[128,256]{1,0:T(8,128)(2,1)} copy(bf16[128,256]{0,1:T(8,128)(2,1)} %bitcast.197) | data formatting | bytes 131072 | tf_op jit(solution)/shard_map/convert_element_type | solution.py:197
  96.2 4.7 %collective-permute-start.12 = (bf16[128,256]{1,0:T(8,128)(2,1)}, bf16[128,256]{1,0:T(8,128)(2,1)}, u32[]{:S(2)}, u32[]{:S(2)}) collective-permute-start(bf16[128,256]{1,0:T(8,128)(2,1)} %copy.295), channel_id=1, source_target_pairs={{0,8},{8,16},{16,24},{24,32},{32,40},{40,48},{48,56},{56,64},{64,7... | collective-permute-start | bytes 196616 | tf_op jit(solution)/shard_map/ppermute | solution.py:13
  100.9 1.6 copy.298
  102.5 1.9 %collective-permute-start.13 = (bf16[128,256]{1,0:T(8,128)(2,1)}, bf16[128,256]{1,0:T(8,128)(2,1)}, u32[]{:S(2)}, u32[]{:S(2)}) collective-permute-start(bf16[128,256]{1,0:T(8,128)(2,1)} %copy.298), channel_id=1, source_target_pairs={{8,0},{16,8},{24,16},{32,24},{40,32},{48,40},{56,48},{64,56},{72,6... | collective-permute-start | bytes 196616 | tf_op jit(solution)/shard_map/ppermute | solution.py:13
  105.1 7.9 %collective-permute-start.14 = (bf16[128,256]{1,0:T(8,128)(2,1)}, bf16[128,256]{1,0:T(8,128)(2,1)}, u32[]{:S(2)}, u32[]{:S(2)}) collective-permute-start(bf16[128,256]{1,0:T(8,128)(2,1)} %copy.300), channel_id=1, source_target_pairs={{0,16},{8,24},{16,32},{24,40},{32,48},{40,56},{48,64},{56,72},{64,... | collective-permute-start | bytes 196616 | tf_op jit(solution)/shard_map/ppermute | solution.py:13
  113.8 1.9 %collective-permute-start.15 = (bf16[128,256]{1,0:T(8,128)(2,1)}, bf16[128,256]{1,0:T(8,128)(2,1)}, u32[]{:S(2)}, u32[]{:S(2)}) collective-permute-start(bf16[128,256]{1,0:T(8,128)(2,1)} %copy.302), channel_id=1, source_target_pairs={{16,0},{24,8},{32,16},{40,24},{48,32},{56,40},{64,48},{72,56},{80,... | collective-permute-start | bytes 196616 | tf_op jit(solution)/shard_map/ppermute | solution.py:13
  115.9 0.7 copy.286
  116.6 1.9 %collective-permute-start.9 = (bf16[128,256]{1,0:T(8,128)(2,1)}, bf16[128,256]{1,0:T(8,128)(2,1)}, u32[]{:S(2)}, u32[]{:S(2)}) collective-permute-start(bf16[128,256]{1,0:T(8,128)(2,1)} %copy.286), channel_id=1, source_target_pairs={{8,0},{16,8},{24,16},{32,24},{40,32},{48,40},{56,48},{64,56},{72,6... | collective-permute-start | bytes 196616 | tf_op jit(solution)/shard_map/ppermute | solution.py:13
  118.6 1.0 fusion.78
  120.1 1.1 copy.355
  121.2 5.7 %all-to-all-start = ((bf16[8,128,512]{2,1,0:T(8,128)(2,1)}), bf16[8,128,512]{2,1,0:T(8,128)(2,1)}, u32[]{:S(2)}, u32[]{:S(2)}) async-start(bf16[8,128,512]{2,1,0:T(8,128)(2,1)} %bitcast.175), calls=%async_computation | async-start | bytes 2097152 | tf_op jit(solution)/shard_map/all_to_all | solution.py:23
  127.5 1.0 convolution_add_fusion.1
  128.5 1.0 fusion.10
  131.0 1.9 %collective-permute-start.8 = (bf16[128,256]{1,0:T(8,128)(2,1)S(1)}, bf16[128,256]{1,0:T(8,128)(2,1)S(1)}, u32[]{:S(2)}, u32[]{:S(2)}) collective-permute-start(bf16[128,256]{1,0:T(8,128)(2,1)S(1)} %copy.282), channel_id=1, source_target_pairs={{0,8},{8,16},{16,24},{24,32},{32,40},{40,48},{48,56},{56,64},{64,7... | collective-permute-start | bytes 196616 | tf_op jit(solution)/shard_map/ppermute | solution.py:13
  132.9 8.1 %collective-permute-start.10 = (bf16[128,256]{1,0:T(8,128)(2,1)S(1)}, bf16[128,256]{1,0:T(8,128)(2,1)S(1)}, u32[]{:S(2)}, u32[]{:S(2)}) collective-permute-start(bf16[128,256]{1,0:T(8,128)(2,1)S(1)} %copy.289), channel_id=1, source_target_pairs={{0,16},{8,24},{16,32},{24,40},{32,48},{40,56},{48,64},{56,72},{64,... | collective-permute-start | bytes 196616 | tf_op jit(solution)/shard_map/ppermute | solution.py:13
  141.1 1.9 %collective-permute-start.11 = (bf16[128,256]{1,0:T(8,128)(2,1)S(1)}, bf16[128,256]{1,0:T(8,128)(2,1)S(1)}, u32[]{:S(2)}, u32[]{:S(2)}) collective-permute-start(bf16[128,256]{1,0:T(8,128)(2,1)S(1)} %copy.292), channel_id=1, source_target_pairs={{16,0},{24,8},{32,16},{40,24},{48,32},{56,40},{64,48},{72,56},{80,... | collective-permute-start | bytes 196616 | tf_op jit(solution)/shard_map/ppermute | solution.py:13
  143.0 1.6 %add_convert_fusion = bf16[128,256]{1,0:T(8,128)(2,1)} fusion(bf16[128,256]{1,0:T(8,128)(2,1)} %collective-permute-done.15, bf16[128,256]{1,0:T(8,128)(2,1)} %collective-permute-done.14, bf16[128,256]{1,0:T(8,128)(2,1)} %collective-permute-done.13, f32[128,256]{1,0:T(8,128)S(1)} %copy.296, bf16[128,256]{1,0:T(8,128)(2,1)} %collective-permute-done.12), kind=kLoop, calls=%fused_computation.72 | loop fusion | flops 294912 | bytes 458752 | tf_op jit(solution)/shard_map/convert_element_type | solution.py:207
  144.6 8.2 %collective-permute-done.11 = bf16[128,256]{1,0:T(8,128)(2,1)S(1)} collective-permute-done((bf16[128,256]{1,0:T(8,128)(2,1)S(1)}, bf16[128,256]{1,0:T(8,128)(2,1)S(1)}, u32[]{:S(2)}, u32[]{:S(2)}) %collective-permute-start.11) | collective-permute-done | bytes 65568 | tf_op jit(solution)/shard_map/ppermute | solution.py:13
  152.8 1.5 add_convert_fusion.1
  154.4 2.1 %reduce_sum.125 = bf16[128,512]{1,0:T(8,128)(2,1)} reduce(bf16[8,128,512]{2,1,0:T(8,128)(2,1)} %all-to-all-done, bf16[]{:T(256)} %constant.49.clone.1), dimensions={0}, to_apply=%region_16.18 | reduce | flops 458752 | bytes 1179650 | tf_op jit(solution)/shard_map/reduce_sum | solution.py:24
  (93 shorter events, 11.2 us)
Async XLA Ops:
  0.6 81.4 %copy-start = (bf16[256,4096]{1,0:T(8,128)(2,1)S(1)}, bf16[256,4096]{1,0:T(8,128)(2,1)}, u32[]{:S(2)}) copy-start(bf16[256,4096]{1,0:T(8,128)(2,1)} %param.12) | copy-start | bytes 6291460
  2.4 38.1 %collective-permute-start.3 = (bf16[128,256]{0,1:T(8,128)(2,1)}, bf16[128,256]{0,1:T(8,128)(2,1)S(1)}, u32[]{:S(2)}, u32[]{:S(2)}) collective-permute-start(bf16[128,256]{0,1:T(8,128)(2,1)} %copy.343), channel_id=1, source_target_pairs={{0,16},{8,24},{16,32},{24,40},{32,48},{40,56},{48,64},{56,72},{64,... | collective-permute-start | bytes 196616 | tf_op jit(solution)/shard_map/ppermute | solution.py:13
  7.2 39.1 %collective-permute-start.2 = (bf16[128,256]{0,1:T(8,128)(2,1)}, bf16[128,256]{0,1:T(8,128)(2,1)S(1)}, u32[]{:S(2)}, u32[]{:S(2)}) collective-permute-start(bf16[128,256]{0,1:T(8,128)(2,1)} %copy.343), channel_id=1, source_target_pairs={{16,0},{24,8},{32,16},{40,24},{48,32},{56,40},{64,48},{72,56},{80,... | collective-permute-start | bytes 196616 | tf_op jit(solution)/shard_map/ppermute | solution.py:13
  9.1 46.1 %collective-permute-start.1 = (bf16[128,256]{0,1:T(8,128)(2,1)}, bf16[128,256]{0,1:T(8,128)(2,1)S(1)}, u32[]{:S(2)}, u32[]{:S(2)}) collective-permute-start(bf16[128,256]{0,1:T(8,128)(2,1)} %copy.343), channel_id=1, source_target_pairs={{0,8},{8,16},{16,24},{24,32},{32,40},{40,48},{48,56},{56,64},{64,7... | collective-permute-start | bytes 196616 | tf_op jit(solution)/shard_map/ppermute | solution.py:13
  11.0 46.6 %collective-permute-start = (bf16[128,256]{0,1:T(8,128)(2,1)}, bf16[128,256]{0,1:T(8,128)(2,1)}, u32[]{:S(2)}, u32[]{:S(2)}) collective-permute-start(bf16[128,256]{0,1:T(8,128)(2,1)} %copy.343), channel_id=1, source_target_pairs={{8,0},{16,8},{24,16},{32,24},{40,32},{48,40},{56,48},{64,56},{72,6... | collective-permute-start | bytes 196616 | tf_op jit(solution)/shard_map/ppermute | solution.py:13
  17.7 64.3 %all-to-all-start.1 = ((bf16[8,128,512]{1,2,0:T(8,128)(2,1)}), bf16[8,128,512]{1,2,0:T(8,128)(2,1)S(1)}, u32[]{:S(2)}, u32[]{:S(2)}) async-start(bf16[8,128,512]{1,2,0:T(8,128)(2,1)} %broadcast_in_dim.38), calls=%async_computation.1 | async-start | bytes 2097152 | tf_op jit(solution)/shard_map/all_to_all | solution.py:29
  23.5 42.3 %collective-permute-start.4 = (bf16[128,256]{1,0:T(8,128)(2,1)}, bf16[128,256]{1,0:T(8,128)(2,1)}, u32[]{:S(2)}, u32[]{:S(2)}) collective-permute-start(bf16[128,256]{1,0:T(8,128)(2,1)} %param.11), channel_id=1, source_target_pairs={{8,0},{16,8},{24,16},{32,24},{40,32},{48,40},{56,48},{64,56},{72,6... | collective-permute-start | bytes 196616 | tf_op jit(solution)/shard_map/ppermute | solution.py:13
  27.2 6.5 %copy-start.19 = (s32[128]{0:T(128)}, s32[128]{0:T(128)S(1)}, u32[]{:S(2)}) copy-start(s32[128]{0:T(128)S(1)} %get-tuple-element.76) | copy-start | bytes 1540
  40.4 17.0 %copy-start.4 = (f32[2,128,128]{1,2,0:T(8,128)}, f32[2,128,128]{1,2,0:T(8,128)S(1)}, u32[]{:S(2)}) copy-start(f32[2,128,128]{1,2,0:T(8,128)S(1)} %get-tuple-element.62) | copy-start | bytes 393220
  40.4 17.0 %copy-start.12 = (pred[2,128,128]{1,2,0:T(32,128)(4,1)}, pred[2,128,128]{1,2,0:T(32,128)(4,1)S(1)}, u32[]{:S(2)}) copy-start(pred[2,128,128]{1,2,0:T(32,128)(4,1)S(1)} %get-tuple-element.39) | copy-start | bytes 98308
  40.5 13.7 %copy-start.16 = (bf16[128,256]{0,1:T(8,128)(2,1)}, bf16[128,256]{0,1:T(8,128)(2,1)S(1)}, u32[]{:S(2)}) copy-start(bf16[128,256]{0,1:T(8,128)(2,1)S(1)} %collective-permute-done.3) | copy-start | bytes 196612
  40.5 26.3 %collective-permute-start.6 = (bf16[128,256]{1,0:T(8,128)(2,1)}, bf16[128,256]{1,0:T(8,128)(2,1)}, u32[]{:S(2)}, u32[]{:S(2)}) collective-permute-start(bf16[128,256]{1,0:T(8,128)(2,1)} %param.11), channel_id=1, source_target_pairs={{16,0},{24,8},{32,16},{40,24},{48,32},{56,40},{64,48},{72,56},{80,... | collective-permute-start | bytes 196616 | tf_op jit(solution)/shard_map/ppermute | solution.py:13
  46.3 7.8 %copy-start.17 = (bf16[128,256]{0,1:T(8,128)(2,1)}, bf16[128,256]{0,1:T(8,128)(2,1)S(1)}, u32[]{:S(2)}) copy-start(bf16[128,256]{0,1:T(8,128)(2,1)S(1)} %collective-permute-done.2) | copy-start | bytes 196612
  46.3 22.1 %collective-permute-start.7 = (bf16[128,256]{1,0:T(8,128)(2,1)}, bf16[128,256]{1,0:T(8,128)(2,1)}, u32[]{:S(2)}, u32[]{:S(2)}) collective-permute-start(bf16[128,256]{1,0:T(8,128)(2,1)} %param.11), channel_id=1, source_target_pairs={{0,16},{8,24},{16,32},{24,40},{32,48},{40,56},{48,64},{56,72},{64,... | collective-permute-start | bytes 196616 | tf_op jit(solution)/shard_map/ppermute | solution.py:13
  55.2 10.7 %copy-start.15 = (bf16[128,256]{0,1:T(8,128)(2,1)}, bf16[128,256]{0,1:T(8,128)(2,1)S(1)}, u32[]{:S(2)}) copy-start(bf16[128,256]{0,1:T(8,128)(2,1)S(1)} %collective-permute-done.1) | copy-start | bytes 196612
  55.2 14.8 %collective-permute-start.5 = (bf16[128,256]{1,0:T(8,128)(2,1)}, bf16[128,256]{1,0:T(8,128)(2,1)}, u32[]{:S(2)}, u32[]{:S(2)}) collective-permute-start(bf16[128,256]{1,0:T(8,128)(2,1)} %param.11), channel_id=1, source_target_pairs={{0,8},{8,16},{16,24},{24,32},{32,40},{40,48},{48,56},{56,64},{64,7... | collective-permute-start | bytes 196616 | tf_op jit(solution)/shard_map/ppermute | solution.py:13
  57.6 0.7 copy-start.1
  83.5 7.8 %copy-start.2 = (f32[2,128,128]{1,2,0:T(8,128)S(1)}, f32[2,128,128]{1,2,0:T(8,128)}, u32[]{:S(2)}) copy-start(f32[2,128,128]{1,2,0:T(8,128)} %copy-done.1) | copy-start | bytes 393220
  83.5 7.9 %copy-start.6 = (bf16[128,256]{0,1:T(8,128)(2,1)S(1)}, bf16[128,256]{0,1:T(8,128)(2,1)}, u32[]{:S(2)}) copy-start(bf16[128,256]{0,1:T(8,128)(2,1)} %copy.248) | copy-start | bytes 196612
  83.5 7.9 %copy-start.9 = (pred[2,128,128]{1,2,0:T(32,128)(4,1)S(1)}, pred[2,128,128]{1,2,0:T(32,128)(4,1)}, u32[]{:S(2)}) copy-start(pred[2,128,128]{1,2,0:T(32,128)(4,1)} %get-tuple-element.41) | copy-start | bytes 98308
  83.5 8.1 %copy-start.5 = (f32[2,128,128]{1,2,0:T(8,128)S(1)}, f32[2,128,128]{1,2,0:T(8,128)}, u32[]{:S(2)}) copy-start(f32[2,128,128]{1,2,0:T(8,128)} %copy-done.4) | copy-start | bytes 393220
  83.5 8.1 %copy-start.13 = (pred[2,128,128]{1,2,0:T(32,128)(4,1)S(1)}, pred[2,128,128]{1,2,0:T(32,128)(4,1)}, u32[]{:S(2)}) copy-start(pred[2,128,128]{1,2,0:T(32,128)(4,1)} %copy-done.12) | copy-start | bytes 98308
  83.5 9.1 %copy-start.7 = (bf16[128,256]{0,1:T(8,128)(2,1)S(1)}, bf16[128,256]{0,1:T(8,128)(2,1)}, u32[]{:S(2)}) copy-start(bf16[128,256]{0,1:T(8,128)(2,1)} %copy.250) | copy-start | bytes 196612
  83.5 9.1 %copy-start.11 = (pred[2,128,128]{1,2,0:T(32,128)(4,1)S(1)}, pred[2,128,128]{1,2,0:T(32,128)(4,1)}, u32[]{:S(2)}) copy-start(pred[2,128,128]{1,2,0:T(32,128)(4,1)} %get-tuple-element.43) | copy-start | bytes 98308
  83.5 9.3 %copy-start.8 = (bf16[128,256]{0,1:T(8,128)(2,1)S(1)}, bf16[128,256]{0,1:T(8,128)(2,1)}, u32[]{:S(2)}) copy-start(bf16[128,256]{0,1:T(8,128)(2,1)} %copy.252) | copy-start | bytes 196612
  83.6 9.3 %copy-start.10 = (pred[2,128,128]{1,2,0:T(32,128)(4,1)S(1)}, pred[2,128,128]{1,2,0:T(32,128)(4,1)}, u32[]{:S(2)}) copy-start(pred[2,128,128]{1,2,0:T(32,128)(4,1)} %get-tuple-element.45) | copy-start | bytes 98308
  84.6 9.9 %copy-start.18 = (bf16[128,256]{0,1:T(8,128)(2,1)S(1)}, bf16[128,256]{0,1:T(8,128)(2,1)}, u32[]{:S(2)}) copy-start(bf16[128,256]{0,1:T(8,128)(2,1)} %copy-done.17) | copy-start | bytes 196612
  96.2 34.8 %collective-permute-start.12 = (bf16[128,256]{1,0:T(8,128)(2,1)}, bf16[128,256]{1,0:T(8,128)(2,1)}, u32[]{:S(2)}, u32[]{:S(2)}) collective-permute-start(bf16[128,256]{1,0:T(8,128)(2,1)} %copy.295), channel_id=1, source_target_pairs={{0,8},{8,16},{16,24},{24,32},{32,40},{40,48},{48,56},{56,64},{64,7... | collective-permute-start | bytes 196616 | tf_op jit(solution)/shard_map/ppermute | solution.py:13
  102.5 30.4 %collective-permute-start.13 = (bf16[128,256]{1,0:T(8,128)(2,1)}, bf16[128,256]{1,0:T(8,128)(2,1)}, u32[]{:S(2)}, u32[]{:S(2)}) collective-permute-start(bf16[128,256]{1,0:T(8,128)(2,1)} %copy.298), channel_id=1, source_target_pairs={{8,0},{16,8},{24,16},{32,24},{40,32},{48,40},{56,48},{64,56},{72,6... | collective-permute-start | bytes 196616 | tf_op jit(solution)/shard_map/ppermute | solution.py:13
  105.1 35.9 %collective-permute-start.14 = (bf16[128,256]{1,0:T(8,128)(2,1)}, bf16[128,256]{1,0:T(8,128)(2,1)}, u32[]{:S(2)}, u32[]{:S(2)}) collective-permute-start(bf16[128,256]{1,0:T(8,128)(2,1)} %copy.300), channel_id=1, source_target_pairs={{0,16},{8,24},{16,32},{24,40},{32,48},{40,56},{48,64},{56,72},{64,... | collective-permute-start | bytes 196616 | tf_op jit(solution)/shard_map/ppermute | solution.py:13
  113.8 29.2 %collective-permute-start.15 = (bf16[128,256]{1,0:T(8,128)(2,1)}, bf16[128,256]{1,0:T(8,128)(2,1)}, u32[]{:S(2)}, u32[]{:S(2)}) collective-permute-start(bf16[128,256]{1,0:T(8,128)(2,1)} %copy.302), channel_id=1, source_target_pairs={{16,0},{24,8},{32,16},{40,24},{48,32},{56,40},{64,48},{72,56},{80,... | collective-permute-start | bytes 196616 | tf_op jit(solution)/shard_map/ppermute | solution.py:13
  116.6 28.0 %collective-permute-start.9 = (bf16[128,256]{1,0:T(8,128)(2,1)}, bf16[128,256]{1,0:T(8,128)(2,1)}, u32[]{:S(2)}, u32[]{:S(2)}) collective-permute-start(bf16[128,256]{1,0:T(8,128)(2,1)} %copy.286), channel_id=1, source_target_pairs={{8,0},{16,8},{24,16},{32,24},{40,32},{48,40},{56,48},{64,56},{72,6... | collective-permute-start | bytes 196616 | tf_op jit(solution)/shard_map/ppermute | solution.py:13
  120.0 7.2 %copy-start.3 = (f32[2,128,128]{1,2,0:T(8,128)S(1)}, f32[2,128,128]{1,2,0:T(8,128)}, u32[]{:S(2)}) copy-start(f32[2,128,128]{1,2,0:T(8,128)} %get-tuple-element.61) | copy-start | bytes 393220
  120.0 7.2 %copy-start.14 = (pred[2,128,128]{1,2,0:T(32,128)(4,1)S(1)}, pred[2,128,128]{1,2,0:T(32,128)(4,1)}, u32[]{:S(2)}) copy-start(pred[2,128,128]{1,2,0:T(32,128)(4,1)} %get-tuple-element.37) | copy-start | bytes 98308
  121.2 33.2 %all-to-all-start = ((bf16[8,128,512]{2,1,0:T(8,128)(2,1)}), bf16[8,128,512]{2,1,0:T(8,128)(2,1)}, u32[]{:S(2)}, u32[]{:S(2)}) async-start(bf16[8,128,512]{2,1,0:T(8,128)(2,1)} %bitcast.175), calls=%async_computation | async-start | bytes 2097152 | tf_op jit(solution)/shard_map/all_to_all | solution.py:23
  131.0 13.6 %collective-permute-start.8 = (bf16[128,256]{1,0:T(8,128)(2,1)S(1)}, bf16[128,256]{1,0:T(8,128)(2,1)S(1)}, u32[]{:S(2)}, u32[]{:S(2)}) collective-permute-start(bf16[128,256]{1,0:T(8,128)(2,1)S(1)} %copy.282), channel_id=1, source_target_pairs={{0,8},{8,16},{16,24},{24,32},{32,40},{40,48},{48,56},{56,64},{64,7... | collective-permute-start | bytes 196616 | tf_op jit(solution)/shard_map/ppermute | solution.py:13
  132.9 11.7 %collective-permute-start.10 = (bf16[128,256]{1,0:T(8,128)(2,1)S(1)}, bf16[128,256]{1,0:T(8,128)(2,1)S(1)}, u32[]{:S(2)}, u32[]{:S(2)}) collective-permute-start(bf16[128,256]{1,0:T(8,128)(2,1)S(1)} %copy.289), channel_id=1, source_target_pairs={{0,16},{8,24},{16,32},{24,40},{32,48},{40,56},{48,64},{56,72},{64,... | collective-permute-start | bytes 196616 | tf_op jit(solution)/shard_map/ppermute | solution.py:13
  141.1 11.8 %collective-permute-start.11 = (bf16[128,256]{1,0:T(8,128)(2,1)S(1)}, bf16[128,256]{1,0:T(8,128)(2,1)S(1)}, u32[]{:S(2)}, u32[]{:S(2)}) collective-permute-start(bf16[128,256]{1,0:T(8,128)(2,1)S(1)} %copy.292), channel_id=1, source_target_pairs={{16,0},{24,8},{32,16},{40,24},{48,32},{56,40},{64,48},{72,56},{80,... | collective-permute-start | bytes 196616 | tf_op jit(solution)/shard_map/ppermute | solution.py:13
where the time goes:
time: 159 us; the launch traced here: 156 us
  starting transfers between devices  72.5 us (46%)
  matrix products  33.3 us (21%)
  local copies, waits for them, and re-layouts  20.7 us (13%)
  other arithmetic  20.4 us (13%)
  waiting for transfers between devices  8.27 us (5%)
    ppermute x16, starting transfers between devices, passed_along(): lax.ppermute(value, axis, [(source, source + steps) for source in range(i...  61 us
    dot_general x5, matrix products, scores_of(): jnp.einsum('thd,shd->hts', query_heads, key_heads, preferred_element_type...  11.4 us
    ppermute x16, waiting for transfers between devices, passed_along(): lax.ppermute(value, axis, [(source, source + steps) for source in range(i...  8.26 us
    dot_general x5, matrix products, accumulate(): jnp.einsum('hts,shd->thd', probs, split(slab_store[offset][1]), preferred...  7.54 us
    all_to_all x1, starting transfers between devices, from_everyone(): lax.all_to_all(jnp.broadcast_to(x[None], (length, *x.shape)), axis, 0, 0,...  5.8 us
    all_to_all x1, starting transfers between devices, sent_and_summed(): blocks = lax.all_to_all(in_blocks(x, dim, length), axis, 0, 0, tiled=True)  5.7 us
    ppermute x4, local copies, waits for them, and re-layouts, passed_along(): lax.ppermute(value, axis, [(source, source + steps) for source in range(i...  5.66 us
    dot_general x5, matrix products, all_terms(): jnp.einsum('hts,thd->shd', probs, grad_heads, preferred_element_type=jnp....  5.55 us
  transfers between devices with their start and end apart: 18, of which 1 were waited for; matrix products, arithmetic and copies ran while one was open for 36% of the time, Pallas kernels for 0%

commit v1 on v0

v1 whole, which is shorter than its diff:
```python
import functools

import jax
import jax.numpy as jnp
from jax import lax
from jax.experimental import pallas as pl
from jax.experimental.pallas import tpu as pltpu
from jax.sharding import PartitionSpec as P

HALF = 32
BF = jnp.bfloat16
F32 = jnp.float32
VMEM = pl.BlockSpec(memory_space=pltpu.VMEM)
SMEM = pl.BlockSpec(memory_space=pltpu.SMEM)


def dot(a, b, dims):
    return lax.dot_general(a, b, (dims, ((), ())), preferred_element_type=F32)


def call(body, outs, ins, name, flops=0, scratch=()):
    moved = sum(x.size * x.dtype.itemsize for x in (*ins, *outs))
    return pl.pallas_call(
        body,
        out_shape=outs,
        in_specs=[SMEM if x.ndim == 1 else VMEM for x in ins],
        out_specs=[VMEM] * len(outs),
        scratch_shapes=scratch,
        compiler_params=pltpu.CompilerParams(vmem_limit_bytes=24 << 20),
        cost_estimate=pl.CostEstimate(flops=flops, bytes_accessed=moved, transcendentals=0),
        name=name,
    )(*ins)


def shape(dims, dtype):
    return jax.ShapeDtypeStruct(dims, dtype)


def pack_kernel(k_ref, v_ref, mg_ref, kv_ref, all_ref):
    w = k_ref.shape[1]
    kv_ref[:, :w] = k_ref[...]
    kv_ref[:, w:] = v_ref[...]
    for b in range(all_ref.shape[0]):
        all_ref[b] = mg_ref[...]


def document_codes(lens, row_pos, col_pos):
    n = lens.shape[1]
    down = lax.broadcasted_iota(jnp.int32, (n, n), 0)
    across = lax.broadcasted_iota(jnp.int32, (n, n), 1)
    wide = jnp.broadcast_to(lens, (n, n))
    ends_col = jnp.sum(jnp.where(across <= down, wide, 0.0), axis=1, keepdims=True)
    lens_col = jnp.sum(jnp.where(across == down, wide, 0.0), axis=1, keepdims=True)
    ends_row = jnp.sum(jnp.where(down <= across, lens_col, 0.0), axis=0, keepdims=True)
    row_doc = jnp.sum(jnp.where(row_pos >= ends_col, 1.0, 0.0), axis=0, keepdims=True)
    col_doc = jnp.sum(jnp.where(col_pos >= ends_row, 1.0, 0.0), axis=1, keepdims=True)
    return row_doc, col_doc


def forward_kernel(
    heads, total, where_ref, dil_ref, lens_ref, q_ref, prev_ref, own_ref, next_ref, w_ref,
    part_ref, weight_ref, attn_ref, win_ref,
):
    rows = q_ref.shape[0]
    width = q_ref.shape[1]
    hd = width // heads
    keys = win_ref.shape[0]
    slab = where_ref[0]
    core = lax.rem(slab, 2)
    six = [prev_ref, prev_ref, own_ref, own_ref, next_ref, next_ref]

    @pl.when(core == 0)
    def _():
        for i in range(5):
            win_ref[i * rows : (i + 1) * rows, :] = six[i][i % 2]

    @pl.when(core == 1)
    def _():
        for i in range(5):
            win_ref[i * rows : (i + 1) * rows, :] = six[i + 1][(i + 1) % 2]

    first = slab * rows
    row_idx = lax.broadcasted_iota(jnp.int32, (1, keys), 1) + (first - 2 * rows)
    col_idx = lax.broadcasted_iota(jnp.int32, (rows, 1), 0) + first
    row_pos, col_pos = row_idx.astype(F32), col_idx.astype(F32)
    row_doc, col_doc = document_codes(lens_ref[...].astype(F32), row_pos, col_pos)
    inside = (row_pos >= 0.0) & (row_pos < float(total))
    distance = jnp.abs(col_pos - row_pos)
    for h in range(heads):
        stride = dil_ref[h].astype(F32)

        def residue(pos, doc):
            steps = jnp.floor((pos + 0.5) / jnp.full(pos.shape, stride))
            return doc * 8.0 + (pos - steps * stride)

        row_code = jnp.where(inside, residue(row_pos, row_doc), -1.0)
        col_code = residue(col_pos, col_doc)
        mask = (row_code == col_code) & (distance <= stride * float(HALF))
        q = q_ref[:, h * hd : (h + 1) * hd]
        k = win_ref[:, h * hd : (h + 1) * hd]
        v = win_ref[:, width + h * hd : width + (h + 1) * hd]
        s = dot(q, k, ((1,), (1,))) * (hd**-0.5)
        s = jnp.where(mask, s, -jnp.inf)
        top = jnp.max(s, axis=1, keepdims=True)
        e = jnp.exp(s - top)
        weight = e / jnp.sum(e, axis=1, keepdims=True)
        weight_ref[h] = weight
        attn_ref[:, h * hd : (h + 1) * hd] = dot(weight.astype(BF), v, ((1,), (0,))).astype(BF)
    attn = attn_ref[...]
    span = part_ref.shape[2]
    for b in range(part_ref.shape[0]):
        part_ref[b] = dot(attn, w_ref[:, b * span : (b + 1) * span], ((1,), (0,))).astype(BF)


def backward_kernel(
    heads, q_ref, win_ref, weight_ref, attn_ref, mg_ref, w_ref, dq_ref, keep_ref, give_ref, ga_ref
):
    rows = q_ref.shape[0]
    width = q_ref.shape[1]
    hd = width // heads
    factor = hd**-0.5
    span = mg_ref.shape[2]
    total = jnp.zeros((rows, width), F32)
    for b in range(mg_ref.shape[0]):
        total = total + dot(mg_ref[b], w_ref[:, b * span : (b + 1) * span], ((1,), (1,)))
    ga_ref[...] = total.astype(BF)
    for h in range(heads):
        cols = slice(h * hd, (h + 1) * hd)
        vcols = slice(width + h * hd, width + (h + 1) * hd)
        ga = ga_ref[:, cols]
        q = q_ref[:, cols]
        delta = jnp.sum(ga.astype(F32) * attn_ref[:, cols].astype(F32), axis=1, keepdims=True)
        grad_prob = dot(ga, win_ref[:, vcols], ((1,), (1,)))
        weight = weight_ref[h]
        slopes = (weight * (grad_prob - delta)).astype(BF)
        probs = weight.astype(BF)
        dq_ref[:, cols] = (dot(slopes, win_ref[:, cols], ((1,), (0,))) * factor).astype(BF)
        dk = dot(slopes, q, ((0,), (0,))) * factor
        dv = dot(probs, ga, ((0,), (0,)))
        for i in range(5):
            part = slice(i * rows, (i + 1) * rows)
            if i % 2 == 0:
                keep_ref[i // 2, :, cols] = dk[part]
                keep_ref[i // 2, :, vcols] = dv[part]
            else:
                give_ref[i // 2, :, cols] = dk[part].astype(BF)
                give_ref[i // 2, :, vcols] = dv[part].astype(BF)


def share_kernel(where_ref, keep_ref, got_ref, down_ref, up_ref, own_ref):
    core = lax.rem(where_ref[0], 2)

    @pl.when(core == 0)
    def _():
        down_ref[...] = keep_ref[0].astype(BF)
        own_ref[...] = keep_ref[1] + got_ref[1, 0].astype(F32)
        up_ref[...] = (keep_ref[2] + got_ref[1, 1].astype(F32)).astype(BF)

    @pl.when(core == 1)
    def _():
        down_ref[...] = (keep_ref[0] + got_ref[0, 0].astype(F32)).astype(BF)
        own_ref[...] = keep_ref[1] + got_ref[0, 1].astype(F32)
        up_ref[...] = keep_ref[2].astype(BF)


def finish_kernel(own_ref, a_ref, b_ref, dk_ref, dv_ref):
    w = dk_ref.shape[1]
    total = own_ref[...] + a_ref[...].astype(F32) + b_ref[...].astype(F32)
    dk_ref[...] = total[:, :w].astype(BF)
    dv_ref[...] = total[:, w:].astype(BF)


def mixed_kernel(x_ref, o_ref):
    total = x_ref[0].astype(F32)
    for b in range(1, x_ref.shape[0]):
        total = total + x_ref[b].astype(F32)
    o_ref[...] = total.astype(BF)


def shifted(x, steps):
    count = lax.axis_size("ctx")
    first, last = max(0, -steps), min(count, count - steps)
    return lax.ppermute(x, "ctx", [(i, i + steps) for i in range(first, last)])


def in_chip(x):
    pairs = [[i, i + 1] for i in range(0, lax.axis_size("ctx"), 2)]
    return lax.all_gather(x, "ctx", axis=0, axis_index_groups=pairs)


def per_device(queries, keys, values, out_weight, mixed_grad, lengths, dilation):
    rows, width = queries.shape
    heads = dilation.shape[0]
    groups = lax.axis_size("head")
    span = mixed_grad.shape[1]
    total = rows * lax.axis_size("ctx")
    where = lax.axis_index("ctx").astype(jnp.int32).reshape(1)
    lens = lengths.reshape(1, -1)

    kv, spread = call(
        pack_kernel,
        [shape((rows, 2 * width), BF), shape((groups, rows, span), BF)],
        [keys, values, mixed_grad],
        "pack",
    )
    prev = shifted(kv, 2)
    follow = shifted(kv, -2)
    gathered = lax.all_to_all(spread, "head", 0, 0, tiled=True)
    own2, prev2, next2 = in_chip(kv), in_chip(prev), in_chip(follow)
    part, weight, attn, window = call(
        functools.partial(forward_kernel, heads, total),
        [
            shape((groups, rows, span), BF),
            shape((heads, rows, 5 * rows), F32),
            shape((rows, width), BF),
            shape((5 * rows, 2 * width), BF),
        ],
        [where, dilation, lens, queries, prev2, own2, next2, out_weight],
        "forward",
        flops=2 * rows * width * (groups * span + 10 * rows),
    )
    summed = lax.all_to_all(part, "head", 0, 0, tiled=True)
    dq, keep, give = call(
        functools.partial(backward_kernel, heads),
        [
            shape((rows, width), BF),
            shape((3, rows, 2 * width), F32),
            shape((2, rows, 2 * width), BF),
        ],
        [queries, window, weight, attn, gathered, out_weight],
        "backward",
        flops=2 * rows * width * (groups * span + 20 * rows),
        scratch=[pltpu.VMEM((rows, width), BF)],
    )
    got = in_chip(give)
    down, up, own = call(
        share_kernel,
        [shape((rows, 2 * width), BF), shape((rows, 2 * width), BF), shape((rows, 2 * width), F32)],
        [where, keep, got],
        "share",
    )
    from_next = shifted(down, -2)
    from_prev = shifted(up, 2)
    dk, dv = call(
        finish_kernel,
        [shape((rows, width), BF), shape((rows, width), BF)],
        [own, from_prev, from_next],
        "finish",
    )
    (mixed,) = call(mixed_kernel, [shape((rows, span), BF)], [summed], "mixed")
    return mixed, dq, dk, dv


def solution(mesh):
    placed = (
        P("ctx", "head"),
        P("ctx", "head"),
        P("ctx", "head"),
        P("head", None),
        P("ctx", "head"),
        P(),
        P("head"),
    )
    return jax.shard_map(
        per_device,
        mesh=mesh,
        in_specs=placed,
        out_specs=(P("ctx", "head"), P("ctx", "head"), P("ctx", "head"), P("ctx", "head")),
        check_vma=False,
    )
```

time: 159 us -> 74 us (0.47)
  the two profiles are of different devices: /device:TPU:244 before, /device:TPU:242 now
where the time goes in v1:
time: 74 us; the launch traced here: 73.4 us
  starting transfers between devices  31.4 us (42%)
  waiting for transfers between devices  16.2 us (22%)
  local copies, waits for them, and re-layouts  10.7 us (14%)
  blocking collectives  8.34 us (11%)
  Pallas kernels  5.95 us (8%)
  between operations  0.77 us (1%)
    ppermute x4, starting transfers between devices, shifted(): return lax.ppermute(x, 'ctx', [(i, i + steps) for i in range(first, last)])  16.8 us
    ppermute x4, waiting for transfers between devices, shifted(): return lax.ppermute(x, 'ctx', [(i, i + steps) for i in range(first, last)])  16.2 us
    unnamed x30, local copies, waits for them, and re-layouts  10.7 us
    all_to_all x1, starting transfers between devices, per_device(): summed = lax.all_to_all(part, 'head', 0, 0, tiled=True)  9.68 us
    all_gather x4, blocking collectives, in_chip(): return lax.all_gather(x, 'ctx', axis=0, axis_index_groups=pairs)  8.34 us
    pallas_call x6, Pallas kernels, call(): pl.pallas_call(body, out_shape=outs, in_specs=[SMEM if x.ndim == 1 else V...  5.95 us
    all_to_all x1, starting transfers between devices, per_device(): gathered = lax.all_to_all(spread, 'head', 0, 0, tiled=True)  4.94 us
  transfers between devices with their start and end apart: 6, of which 3 were waited for; matrix products, arithmetic and copies ran while one was open for 0% of the time, Pallas kernels for 7%

profile of v1, /device:TPU:242, one launch (start us, length us, event | category | flops | bytes accessed | tf_op | source)
XLA Modules:
  0.0 73.4 jit_solution(18010874365972479541)
XLA Ops:
  0.6 0.0 copy-start
  0.6 0.0 copy-start.9
  0.7 0.0 copy-start.10
  0.7 1.0 %copy-done.10 = bf16[128,512]{1,0:T(8,128)(2,1)S(1)} copy-done((bf16[128,512]{1,0:T(8,128)(2,1)S(1)}, bf16[128,512]{1,0:T(8,128)(2,1)}, u32[]{:S(2)}) %copy-start.10) | copy-done | bytes 131096
  1.7 0.0 copy-start.11
  1.7 0.8 %copy-done.11 = bf16[128,256]{1,0:T(8,128)(2,1)S(1)} copy-done((bf16[128,256]{1,0:T(8,128)(2,1)S(1)}, bf16[128,256]{1,0:T(8,128)(2,1)}, u32[]{:S(2)}) %copy-start.11) | copy-done | bytes 65560
  2.5 0.0 copy-start.12
  2.6 0.8 %copy-done.12 = bf16[128,256]{1,0:T(8,128)(2,1)S(1)} copy-done((bf16[128,256]{1,0:T(8,128)(2,1)S(1)}, bf16[128,256]{1,0:T(8,128)(2,1)}, u32[]{:S(2)}) %copy-start.12) | copy-done | bytes 65560
  3.4 0.0 copy-start.13
  3.4 0.0 copy-start.14
  3.4 0.1 pack.1
  3.5 0.0 copy-start.3
  3.5 0.9 %copy-done.3 = bf16[8,128,512]{2,1,0:T(8,128)(2,1)} copy-done((bf16[8,128,512]{2,1,0:T(8,128)(2,1)}, bf16[8,128,512]{2,1,0:T(8,128)(2,1)S(1)}, u32[]{:S(2)}) %copy-start.3) | copy-done | bytes 1048600
  4.4 4.9 %all-to-all-start.1 = ((bf16[8,128,512]{2,1,0:T(8,128)(2,1)}), bf16[8,128,512]{2,1,0:T(8,128)(2,1)S(1)}, u32[]{:S(2)}, u32[]{:S(2)}) async-start(bf16[8,128,512]{2,1,0:T(8,128)(2,1)} %copy-done.3), calls=%async_computation.1 | async-start | bytes 2097152 | tf_op jit(solution)/shard_map/all_to_all | solution.py:208
  9.4 4.0 %collective-permute-start.1 = (bf16[128,512]{1,0:T(8,128)(2,1)S(1)}, bf16[128,512]{1,0:T(8,128)(2,1)}, u32[]{:S(2)}, u32[]{:S(2)}) collective-permute-start(bf16[128,512]{1,0:T(8,128)(2,1)S(1)} %get-tuple-element.18), channel_id=1, source_target_pairs={{16,0},{24,8},{32,16},{40,24},{48,32},{56,40},{64,48},{72,56},{80,... | collective-permute-start | bytes 393224 | tf_op jit(solution)/shard_map/ppermute | solution.py:183
  13.4 6.0 %collective-permute-start = (bf16[128,512]{1,0:T(8,128)(2,1)S(1)}, bf16[128,512]{1,0:T(8,128)(2,1)S(1)}, u32[]{:S(2)}, u32[]{:S(2)}) collective-permute-start(bf16[128,512]{1,0:T(8,128)(2,1)S(1)} %get-tuple-element.18), channel_id=1, source_target_pairs={{0,16},{8,24},{16,32},{24,40},{32,48},{40,56},{48,64},{56,72},{64,... | collective-permute-start | bytes 393224 | tf_op jit(solution)/shard_map/ppermute | solution.py:183
  19.4 2.0 %all-gather.1 = bf16[256,512]{1,0:T(8,128)(2,1)S(1)} all-gather(bf16[128,512]{1,0:T(8,128)(2,1)S(1)} %get-tuple-element.18), channel_id=3, replica_groups={{0,8},{16,24},{32,40},{48,56},{64,72},{80,88},{96,104},{112,120},{128,1..., dimensions={0}, use_global_device_ids=true | all-gather | bytes 393216 | tf_op jit(solution)/shard_map/all_gather | solution.py:188
  21.4 0.0 collective-permute-done.1
  21.4 2.2 %all-gather.2 = bf16[256,512]{1,0:T(8,128)(2,1)S(1)} all-gather(bf16[128,512]{1,0:T(8,128)(2,1)} %collective-permute-done.1), channel_id=4, replica_groups={{0,8},{16,24},{32,40},{48,56},{64,72},{80,88},{96,104},{112,120},{128,1..., dimensions={0}, use_global_device_ids=true | all-gather | bytes 393216 | tf_op jit(solution)/shard_map/all_gather | solution.py:188
  23.6 5.1 %collective-permute-done = bf16[128,512]{1,0:T(8,128)(2,1)S(1)} collective-permute-done((bf16[128,512]{1,0:T(8,128)(2,1)S(1)}, bf16[128,512]{1,0:T(8,128)(2,1)S(1)}, u32[]{:S(2)}, u32[]{:S(2)}) %collective-permute-start) | collective-permute-done | bytes 131104 | tf_op jit(solution)/shard_map/ppermute | solution.py:183
  28.7 2.0 %all-gather = bf16[256,512]{1,0:T(8,128)(2,1)S(1)} all-gather(bf16[128,512]{1,0:T(8,128)(2,1)S(1)} %collective-permute-done), channel_id=2, replica_groups={{0,8},{16,24},{32,40},{48,56},{64,72},{80,88},{96,104},{112,120},{128,1..., dimensions={0}, use_global_device_ids=true | all-gather | bytes 393216 | tf_op jit(solution)/shard_map/all_gather | solution.py:188
  30.7 0.0 copy-done
  30.7 0.0 copy-done.9
  30.7 0.0 copy-done.13
  30.7 0.0 copy-done.14
  30.7 2.0 %forward.1 = (bf16[8,128,512]{2,1,0:T(8,128)(2,1)S(1)}, f32[2,128,640]{2,1,0:T(8,128)S(1)}, bf16[128,256]{1,0:T(8,128)(2,1)S(1)}, bf16[640,512]{1,0:T(8,128)(2,1)S(1)}) custom-call(s32[1]{0:T(128)} %bitcast.where_ref, s32[2]{0:T(128)S(1)} %copy-done.13, s32[1,64]{1,0:T(1,128)S(1)} %bitcast.10, bf16[128,256]{1,0:T(8,128)(2,1)S(1)} %copy-done.9, ...), custom_call_target="tpu_custom_call" | custom-call | flops 352321536 | bytes 5374220 | tf_op jit(solution)/shard_map/forward/pallas_call | solution.py:23
  32.7 0.0 copy-start.4
  32.7 1.0 %copy-done.4 = bf16[8,128,512]{2,1,0:T(8,128)(2,1)} copy-done((bf16[8,128,512]{2,1,0:T(8,128)(2,1)}, bf16[8,128,512]{2,1,0:T(8,128)(2,1)S(1)}, u32[]{:S(2)}) %copy-start.4) | copy-done | bytes 1048600
  33.7 0.0 copy-start.5
  33.7 0.9 %copy-done.5 = f32[2,128,640]{2,1,0:T(8,128)} copy-done((f32[2,128,640]{2,1,0:T(8,128)}, f32[2,128,640]{2,1,0:T(8,128)S(1)}, u32[]{:S(2)}) %copy-start.5) | copy-done | bytes 655384
  34.6 0.0 copy-start.7
  34.6 0.8 %copy-done.7 = bf16[640,512]{1,0:T(8,128)(2,1)} copy-done((bf16[640,512]{1,0:T(8,128)(2,1)}, bf16[640,512]{1,0:T(8,128)(2,1)S(1)}, u32[]{:S(2)}) %copy-start.7) | copy-done | bytes 655384
  35.4 0.0 all-to-all-done.1.mg_ref
  35.4 0.0 copy-start.1
  35.4 0.9 %copy-done.1 = bf16[8,128,512]{2,1,0:T(8,128)(2,1)} copy-done((bf16[8,128,512]{2,1,0:T(8,128)(2,1)}, bf16[8,128,512]{2,1,0:T(8,128)(2,1)S(1)}, u32[]{:S(2)}) %copy-start.1) | copy-done | bytes 1048600
  36.4 9.7 %all-to-all-start = ((bf16[8,128,512]{2,1,0:T(8,128)(2,1)}), bf16[8,128,512]{2,1,0:T(8,128)(2,1)S(1)}, u32[]{:S(2)}, u32[]{:S(2)}) async-start(bf16[8,128,512]{2,1,0:T(8,128)(2,1)} %copy-done.4), calls=%async_computation | async-start | bytes 2097152 | tf_op jit(solution)/shard_map/all_to_all | solution.py:222
  46.1 0.0 copy-start.2
  46.1 1.2 %copy-done.2 = bf16[8,128,512]{2,1,0:T(8,128)(2,1)S(1)} copy-done((bf16[8,128,512]{2,1,0:T(8,128)(2,1)S(1)}, bf16[8,128,512]{2,1,0:T(8,128)(2,1)}, u32[]{:S(2)}) %copy-start.2) | copy-done | bytes 1048600
  47.3 0.0 copy-start.6
  47.3 1.1 %copy-done.6 = f32[2,128,640]{2,1,0:T(8,128)S(1)} copy-done((f32[2,128,640]{2,1,0:T(8,128)S(1)}, f32[2,128,640]{2,1,0:T(8,128)}, u32[]{:S(2)}) %copy-start.6) | copy-done | bytes 655384
  48.4 0.0 copy-start.8
  48.4 1.1 %copy-done.8 = bf16[640,512]{1,0:T(8,128)(2,1)S(1)} copy-done((bf16[640,512]{1,0:T(8,128)(2,1)S(1)}, bf16[640,512]{1,0:T(8,128)(2,1)}, u32[]{:S(2)}) %copy-start.8) | copy-done | bytes 655384
  49.5 2.4 %backward.1 = (bf16[128,256]{1,0:T(8,128)(2,1)}, f32[3,128,512]{2,1,0:T(8,128)S(1)}, bf16[2,128,512]{2,1,0:T(8,128)(2,1)S(1)}) custom-call(bf16[128,256]{1,0:T(8,128)(2,1)S(1)} %copy-done.9, bf16[640,512]{1,0:T(8,128)(2,1)S(1)} %copy-done.8, f32[2,128,640]{2,1,0:T(8,128)S(1)} %copy-done.6, bf16[128,256]{1,0:T(8,128)(2,1)S(1)} %get-tuple-element.22.attn_ref, ...), custom_call_target="tpu_custom_call" | custom-call | flops 436207616 | bytes 5701632 | tf_op jit(solution)/shard_map/backward/pallas_call | solution.py:23
  51.8 2.2 %all-gather.3 = bf16[4,128,512]{2,1,0:T(8,128)(2,1)S(1)} all-gather(bf16[2,128,512]{2,1,0:T(8,128)(2,1)S(1)} %get-tuple-element.26), channel_id=5, replica_groups={{0,8},{16,24},{32,40},{48,56},{64,72},{80,88},{96,104},{112,120},{128,1..., dimensions={0}, use_global_device_ids=true | all-gather | bytes 786432 | tf_op jit(solution)/shard_map/all_gather | solution.py:188
  54.0 0.1 share.1
  54.1 4.5 %collective-permute-start.2 = (bf16[128,512]{1,0:T(8,128)(2,1)S(1)}, bf16[128,512]{1,0:T(8,128)(2,1)S(1)}, u32[]{:S(2)}, u32[]{:S(2)}) collective-permute-start(bf16[128,512]{1,0:T(8,128)(2,1)S(1)} %get-tuple-element.28), channel_id=1, source_target_pairs={{0,16},{8,24},{16,32},{24,40},{32,48},{40,56},{48,64},{56,72},{64,... | collective-permute-start | bytes 393224 | tf_op jit(solution)/shard_map/ppermute | solution.py:183
  58.6 2.3 %collective-permute-start.3 = (bf16[128,512]{1,0:T(8,128)(2,1)S(1)}, bf16[128,512]{1,0:T(8,128)(2,1)S(1)}, u32[]{:S(2)}, u32[]{:S(2)}) collective-permute-start(bf16[128,512]{1,0:T(8,128)(2,1)S(1)} %get-tuple-element.29), channel_id=1, source_target_pairs={{16,0},{24,8},{32,16},{40,24},{48,32},{56,40},{64,48},{72,56},{80,... | collective-permute-start | bytes 393224 | tf_op jit(solution)/shard_map/ppermute | solution.py:183
  60.8 0.0 all-to-all-done.x_ref
  60.8 0.8 %mixed.1 = bf16[128,512]{1,0:T(8,128)(2,1)} custom-call(bf16[8,128,512]{2,1,0:T(8,128)(2,1)S(1)} %all-to-all-done.x_ref), custom_call_target="tpu_custom_call" | custom-call | bytes 1179648 | tf_op jit(solution)/shard_map/mixed/pallas_call | solution.py:23
  61.6 1.3 %collective-permute-done.2.a_ref = bf16[128,512]{1,0:T(8,128)(2,1)S(1)} collective-permute-done((bf16[128,512]{1,0:T(8,128)(2,1)S(1)}, bf16[128,512]{1,0:T(8,128)(2,1)S(1)}, u32[]{:S(2)}, u32[]{:S(2)}) %collective-permute-start.2) | collective-permute-done | bytes 131104 | tf_op jit(solution)/shard_map/ppermute | solution.py:183
  62.9 9.9 %collective-permute-done.3.b_ref = bf16[128,512]{1,0:T(8,128)(2,1)S(1)} collective-permute-done((bf16[128,512]{1,0:T(8,128)(2,1)S(1)}, bf16[128,512]{1,0:T(8,128)(2,1)S(1)}, u32[]{:S(2)}, u32[]{:S(2)}) %collective-permute-start.3) | collective-permute-done | bytes 131104 | tf_op jit(solution)/shard_map/ppermute | solution.py:183
  72.8 0.7 finish.1
Async XLA Ops:
  0.6 30.1 %copy-start = (bf16[256,4096]{1,0:T(8,128)(2,1)S(1)}, bf16[256,4096]{1,0:T(8,128)(2,1)}, u32[]{:S(2)}) copy-start(bf16[256,4096]{1,0:T(8,128)(2,1)} %w_ref.3) | copy-start | bytes 6291460
  0.6 30.1 %copy-start.9 = (bf16[128,256]{1,0:T(8,128)(2,1)S(1)}, bf16[128,256]{1,0:T(8,128)(2,1)}, u32[]{:S(2)}) copy-start(bf16[128,256]{1,0:T(8,128)(2,1)} %q_ref.3) | copy-start | bytes 196612
  0.7 1.1 %copy-start.10 = (bf16[128,512]{1,0:T(8,128)(2,1)S(1)}, bf16[128,512]{1,0:T(8,128)(2,1)}, u32[]{:S(2)}) copy-start(bf16[128,512]{1,0:T(8,128)(2,1)} %mg_ref.1) | copy-start | bytes 393220
  1.7 0.8 %copy-start.11 = (bf16[128,256]{1,0:T(8,128)(2,1)S(1)}, bf16[128,256]{1,0:T(8,128)(2,1)}, u32[]{:S(2)}) copy-start(bf16[128,256]{1,0:T(8,128)(2,1)} %k_ref.1) | copy-start | bytes 196612
  2.5 0.8 %copy-start.12 = (bf16[128,256]{1,0:T(8,128)(2,1)S(1)}, bf16[128,256]{1,0:T(8,128)(2,1)}, u32[]{:S(2)}) copy-start(bf16[128,256]{1,0:T(8,128)(2,1)} %v_ref.1) | copy-start | bytes 196612
  3.4 27.3 %copy-start.13 = (s32[2]{0:T(128)S(1)}, s32[2]{0:T(128)}, u32[]{:S(2)}) copy-start(s32[2]{0:T(128)} %dil_ref.1) | copy-start | bytes 28
  3.4 27.3 %copy-start.14 = (s32[64]{0:T(128)S(1)}, s32[64]{0:T(128)}, u32[]{:S(2)}) copy-start(s32[64]{0:T(128)} %param.12) | copy-start | bytes 772
  3.5 0.9 %copy-start.3 = (bf16[8,128,512]{2,1,0:T(8,128)(2,1)}, bf16[8,128,512]{2,1,0:T(8,128)(2,1)S(1)}, u32[]{:S(2)}) copy-start(bf16[8,128,512]{2,1,0:T(8,128)(2,1)S(1)} %get-tuple-element.23) | copy-start | bytes 3145732
  4.4 31.0 %all-to-all-start.1 = ((bf16[8,128,512]{2,1,0:T(8,128)(2,1)}), bf16[8,128,512]{2,1,0:T(8,128)(2,1)S(1)}, u32[]{:S(2)}, u32[]{:S(2)}) async-start(bf16[8,128,512]{2,1,0:T(8,128)(2,1)} %copy-done.3), calls=%async_computation.1 | async-start | bytes 2097152 | tf_op jit(solution)/shard_map/all_to_all | solution.py:208
  9.4 12.1 %collective-permute-start.1 = (bf16[128,512]{1,0:T(8,128)(2,1)S(1)}, bf16[128,512]{1,0:T(8,128)(2,1)}, u32[]{:S(2)}, u32[]{:S(2)}) collective-permute-start(bf16[128,512]{1,0:T(8,128)(2,1)S(1)} %get-tuple-element.18), channel_id=1, source_target_pairs={{16,0},{24,8},{32,16},{40,24},{48,32},{56,40},{64,48},{72,56},{80,... | collective-permute-start | bytes 393224 | tf_op jit(solution)/shard_map/ppermute | solution.py:183
  13.4 15.3 %collective-permute-start = (bf16[128,512]{1,0:T(8,128)(2,1)S(1)}, bf16[128,512]{1,0:T(8,128)(2,1)S(1)}, u32[]{:S(2)}, u32[]{:S(2)}) collective-permute-start(bf16[128,512]{1,0:T(8,128)(2,1)S(1)} %get-tuple-element.18), channel_id=1, source_target_pairs={{0,16},{8,24},{16,32},{24,40},{32,48},{40,56},{48,64},{56,72},{64,... | collective-permute-start | bytes 393224 | tf_op jit(solution)/shard_map/ppermute | solution.py:183
  32.7 1.0 %copy-start.4 = (bf16[8,128,512]{2,1,0:T(8,128)(2,1)}, bf16[8,128,512]{2,1,0:T(8,128)(2,1)S(1)}, u32[]{:S(2)}) copy-start(bf16[8,128,512]{2,1,0:T(8,128)(2,1)S(1)} %get-tuple-element.19) | copy-start | bytes 3145732
  33.7 0.9 %copy-start.5 = (f32[2,128,640]{2,1,0:T(8,128)}, f32[2,128,640]{2,1,0:T(8,128)S(1)}, u32[]{:S(2)}) copy-start(f32[2,128,640]{2,1,0:T(8,128)S(1)} %get-tuple-element.21.weight_ref) | copy-start | bytes 1966084
  34.6 0.8 %copy-start.7 = (bf16[640,512]{1,0:T(8,128)(2,1)}, bf16[640,512]{1,0:T(8,128)(2,1)S(1)}, u32[]{:S(2)}) copy-start(bf16[640,512]{1,0:T(8,128)(2,1)S(1)} %get-tuple-element.20.win_ref) | copy-start | bytes 1966084
  35.4 0.9 %copy-start.1 = (bf16[8,128,512]{2,1,0:T(8,128)(2,1)}, bf16[8,128,512]{2,1,0:T(8,128)(2,1)S(1)}, u32[]{:S(2)}) copy-start(bf16[8,128,512]{2,1,0:T(8,128)(2,1)S(1)} %all-to-all-done.1.mg_ref) | copy-start | bytes 3145732
  36.4 24.5 %all-to-all-start = ((bf16[8,128,512]{2,1,0:T(8,128)(2,1)}), bf16[8,128,512]{2,1,0:T(8,128)(2,1)S(1)}, u32[]{:S(2)}, u32[]{:S(2)}) async-start(bf16[8,128,512]{2,1,0:T(8,128)(2,1)} %copy-done.4), calls=%async_computation | async-start | bytes 2097152 | tf_op jit(solution)/shard_map/all_to_all | solution.py:222
  46.1 1.2 %copy-start.2 = (bf16[8,128,512]{2,1,0:T(8,128)(2,1)S(1)}, bf16[8,128,512]{2,1,0:T(8,128)(2,1)}, u32[]{:S(2)}) copy-start(bf16[8,128,512]{2,1,0:T(8,128)(2,1)} %copy-done.1) | copy-start | bytes 3145732
  47.3 1.1 %copy-start.6 = (f32[2,128,640]{2,1,0:T(8,128)S(1)}, f32[2,128,640]{2,1,0:T(8,128)}, u32[]{:S(2)}) copy-start(f32[2,128,640]{2,1,0:T(8,128)} %copy-done.5) | copy-start | bytes 1966084
  48.4 1.1 %copy-start.8 = (bf16[640,512]{1,0:T(8,128)(2,1)S(1)}, bf16[640,512]{1,0:T(8,128)(2,1)}, u32[]{:S(2)}) copy-start(bf16[640,512]{1,0:T(8,128)(2,1)} %copy-done.7) | copy-start | bytes 1966084
  54.1 8.8 %collective-permute-start.2 = (bf16[128,512]{1,0:T(8,128)(2,1)S(1)}, bf16[128,512]{1,0:T(8,128)(2,1)S(1)}, u32[]{:S(2)}, u32[]{:S(2)}) collective-permute-start(bf16[128,512]{1,0:T(8,128)(2,1)S(1)} %get-tuple-element.28), channel_id=1, source_target_pairs={{0,16},{8,24},{16,32},{24,40},{32,48},{40,56},{48,64},{56,72},{64,... | collective-permute-start | bytes 393224 | tf_op jit(solution)/shard_map/ppermute | solution.py:183
  58.6 14.2 %collective-permute-start.3 = (bf16[128,512]{1,0:T(8,128)(2,1)S(1)}, bf16[128,512]{1,0:T(8,128)(2,1)S(1)}, u32[]{:S(2)}, u32[]{:S(2)}) collective-permute-start(bf16[128,512]{1,0:T(8,128)(2,1)S(1)} %get-tuple-element.29), channel_id=1, source_target_pairs={{16,0},{24,8},{32,16},{40,24},{48,32},{56,40},{64,48},{72,56},{80,... | collective-permute-start | bytes 393224 | tf_op jit(solution)/shard_map/ppermute | solution.py:183

commit v2 on v1

v2 whole, which is shorter than its diff:
```python
import functools

import jax
import jax.numpy as jnp
from jax import lax
from jax.experimental import pallas as pl
from jax.experimental.pallas import tpu as pltpu
from jax.sharding import PartitionSpec as P

HALF = 32
BF = jnp.bfloat16
F32 = jnp.float32
VMEM = pl.BlockSpec(memory_space=pltpu.VMEM)
SMEM = pl.BlockSpec(memory_space=pltpu.SMEM)
HBM = pl.BlockSpec(memory_space=pltpu.HBM)


def dot(a, b, dims):
    return lax.dot_general(a, b, (dims, ((), ())), preferred_element_type=F32)


def call(body, outs, ins, name, flops=0, scratch=(), hbm_in=(), hbm_out=()):
    moved = sum(x.size * x.dtype.itemsize for x in (*ins, *outs))
    held = [
        pltpu.with_memory_space_constraint(x, pltpu.HBM) if i in hbm_in else x
        for i, x in enumerate(ins)
    ]
    return pl.pallas_call(
        body,
        out_shape=[pltpu.HBM(x.shape, x.dtype) if i in hbm_out else x for i, x in enumerate(outs)],
        in_specs=[SMEM if x.ndim == 1 else HBM if i in hbm_in else VMEM for i, x in enumerate(ins)],
        out_specs=[HBM if i in hbm_out else VMEM for i in range(len(outs))],
        scratch_shapes=scratch,
        compiler_params=pltpu.CompilerParams(vmem_limit_bytes=24 << 20),
        cost_estimate=pl.CostEstimate(flops=flops, bytes_accessed=moved, transcendentals=0),
        name=name,
    )(*held)


def shape(dims, dtype):
    return jax.ShapeDtypeStruct(dims, dtype)


def pack_kernel(k_ref, v_ref, mg_ref, kv_ref, all_ref, sems):
    w = k_ref.shape[1]
    copies = [
        pltpu.make_async_copy(k_ref, kv_ref.at[:, :w], sems.at[0]),
        pltpu.make_async_copy(v_ref, kv_ref.at[:, w:], sems.at[1]),
    ]
    for b in range(all_ref.shape[0]):
        copies.append(pltpu.make_async_copy(mg_ref, all_ref.at[b], sems.at[2 + b]))
    for c in copies:
        c.start()
    for c in copies:
        c.wait()


def document_codes(lens, row_pos, col_pos):
    n = lens.shape[1]
    down = lax.broadcasted_iota(jnp.int32, (n, n), 0)
    across = lax.broadcasted_iota(jnp.int32, (n, n), 1)
    wide = jnp.broadcast_to(lens, (n, n))
    ends_col = jnp.sum(jnp.where(across <= down, wide, 0.0), axis=1, keepdims=True)
    lens_col = jnp.sum(jnp.where(across == down, wide, 0.0), axis=1, keepdims=True)
    ends_row = jnp.sum(jnp.where(down <= across, lens_col, 0.0), axis=0, keepdims=True)
    row_doc = jnp.sum(jnp.where(row_pos >= ends_col, 1.0, 0.0), axis=0, keepdims=True)
    col_doc = jnp.sum(jnp.where(col_pos >= ends_row, 1.0, 0.0), axis=1, keepdims=True)
    return row_doc, col_doc


def forward_kernel(
    heads, total, where_ref, dil_ref, lens_ref, q_ref, own_ref, far_ref, w_ref,
    part_ref, out_probs_ref, out_attn_ref, out_win_ref,
    hold_ref, win_ref, probs_ref, attn_ref, sems,
):
    rows = q_ref.shape[0]
    width = q_ref.shape[1]
    hd = width // heads
    keys = win_ref.shape[0]
    slab = where_ref[0]
    core = lax.rem(slab, 2)
    prev, follow = far_ref.at[0], far_ref.at[1]
    six = [prev.at[0], prev.at[1], own_ref.at[0], own_ref.at[1], follow.at[0], follow.at[1]]

    @pl.when(core == 0)
    def _():
        for i in range(5):
            win_ref[i * rows : (i + 1) * rows, :] = six[i][...]

    @pl.when(core == 1)
    def _():
        for i in range(5):
            win_ref[i * rows : (i + 1) * rows, :] = six[i + 1][...]

    copies = [pltpu.make_async_copy(win_ref, out_win_ref, sems.at[part_ref.shape[0]])]
    copies[0].start()

    first = slab * rows
    row_idx = lax.broadcasted_iota(jnp.int32, (1, keys), 1) + (first - 2 * rows)
    col_idx = lax.broadcasted_iota(jnp.int32, (rows, 1), 0) + first
    row_pos, col_pos = row_idx.astype(F32), col_idx.astype(F32)
    row_doc, col_doc = document_codes(lens_ref[...].astype(F32), row_pos, col_pos)
    inside = (row_pos >= 0.0) & (row_pos < float(total))
    distance = jnp.abs(col_pos - row_pos)
    for h in range(heads):
        stride = dil_ref[h].astype(F32)

        def residue(pos, doc):
            steps = jnp.floor((pos + 0.5) / jnp.full(pos.shape, stride))
            return doc * 8.0 + (pos - steps * stride)

        row_code = jnp.where(inside, residue(row_pos, row_doc), -1.0)
        col_code = residue(col_pos, col_doc)
        mask = (row_code == col_code) & (distance <= stride * float(HALF))
        q = q_ref[:, h * hd : (h + 1) * hd]
        k = win_ref[:, h * hd : (h + 1) * hd]
        v = win_ref[:, width + h * hd : width + (h + 1) * hd]
        s = dot(q, k, ((1,), (1,))) * (hd**-0.5)
        s = jnp.where(mask, s, -jnp.inf)
        top = jnp.max(s, axis=1, keepdims=True)
        e = jnp.exp(s - top)
        probs = (e * (1.0 / jnp.sum(e, axis=1, keepdims=True))).astype(BF)
        probs_ref[h] = probs
        attn_ref[:, h * hd : (h + 1) * hd] = dot(probs, v, ((1,), (0,))).astype(BF)
    for i, (a, b) in enumerate(((probs_ref, out_probs_ref), (attn_ref, out_attn_ref))):
        copies.append(pltpu.make_async_copy(a, b, sems.at[part_ref.shape[0] + 1 + i]))
        copies[-1].start()
    attn = attn_ref[...]
    span = part_ref.shape[2]
    for b in range(part_ref.shape[0]):
        hold_ref[b] = dot(attn, w_ref[:, b * span : (b + 1) * span], ((1,), (0,))).astype(BF)
        copies.append(pltpu.make_async_copy(hold_ref.at[b], part_ref.at[b], sems.at[b]))
        copies[-1].start()
    for c in copies:
        c.wait()


def backward_kernel(
    heads, where_ref, q_hbm, win_hbm, probs_hbm, attn_hbm, mg_ref, w_ref,
    dq_ref, own_ref, pass_ref, give_ref,
    mgv_ref, ga_ref, terms_ref, q_ref, win_ref, probs_ref, attn_ref, sems,
):
    rows = q_ref.shape[0]
    width = q_ref.shape[1]
    hd = width // heads
    factor = hd**-0.5
    span = mg_ref.shape[2]
    groups = mg_ref.shape[0]
    copies = [pltpu.make_async_copy(mg_ref.at[b], mgv_ref.at[b], sems.at[b]) for b in range(groups)]
    held = ((q_hbm, q_ref), (attn_hbm, attn_ref), (win_hbm, win_ref), (probs_hbm, probs_ref))
    for i, (a, b) in enumerate(held):
        copies.append(pltpu.make_async_copy(a, b, sems.at[groups + i]))
    for c in copies:
        c.start()
    total = jnp.zeros((rows, width), F32)
    for b in range(groups):
        copies[b].wait()
        total = total + dot(mgv_ref[b], w_ref[:, b * span : (b + 1) * span], ((1,), (1,)))
    ga_ref[...] = total.astype(BF)
    for c in copies[groups:]:
        c.wait()
    for h in range(heads):
        cols = slice(h * hd, (h + 1) * hd)
        vcols = slice(width + h * hd, width + (h + 1) * hd)
        ga = ga_ref[:, cols]
        q = q_ref[:, cols]
        delta = jnp.sum(ga.astype(F32) * attn_ref[:, cols].astype(F32), axis=1, keepdims=True)
        grad_prob = dot(ga, win_ref[:, vcols], ((1,), (1,)))
        probs = probs_ref[h]
        slopes = (probs.astype(F32) * (grad_prob - delta)).astype(BF)
        dq_ref[:, cols] = (dot(slopes, win_ref[:, cols], ((1,), (0,))) * factor).astype(BF)
        dk = dot(slopes, q, ((0,), (0,))) * factor
        dv = dot(probs, ga, ((0,), (0,)))
        for i in range(5):
            part = slice(i * rows, (i + 1) * rows)
            if i == 2:
                own_ref[:, cols] = dk[part]
                own_ref[:, vcols] = dv[part]
            else:
                terms_ref[i, :, cols] = dk[part].astype(BF)
                terms_ref[i, :, vcols] = dv[part].astype(BF)
    core = lax.rem(where_ref[0], 2)
    for value, given, kept in ((0, (0, 1, 3), 4), (1, (1, 3, 4), 0)):

        @pl.when(core == value)
        def _(given=given, kept=kept):
            pass_ref[...] = terms_ref[kept]
            for i, slab in enumerate(given):
                give_ref[i] = terms_ref[slab]


def share_kernel(where_ref, own_ref, pass_ref, got_ref, send_ref, sum_ref):
    core = lax.rem(where_ref[0], 2)
    mine = pass_ref[...].astype(F32)

    @pl.when(core == 0)
    def _():
        sum_ref[...] = own_ref[...] + got_ref[1, 0].astype(F32)
        send_ref[0] = (mine + got_ref[1, 1].astype(F32)).astype(BF)
        send_ref[1] = got_ref[1, 2]

    @pl.when(core == 1)
    def _():
        sum_ref[...] = own_ref[...] + got_ref[0, 2].astype(F32)
        send_ref[0] = got_ref[0, 0]
        send_ref[1] = (mine + got_ref[0, 1].astype(F32)).astype(BF)


def finish_kernel(where_ref, own_ref, far_ref, dk_ref, dv_ref):
    w = dk_ref.shape[1]
    core = lax.rem(where_ref[0], 2)
    total = own_ref[...] + far_ref[0, core].astype(F32) + far_ref[1, core].astype(F32)
    dk_ref[...] = total[:, :w].astype(BF)
    dv_ref[...] = total[:, w:].astype(BF)


def mixed_kernel(x_ref, o_ref):
    total = x_ref[0].astype(F32)
    for b in range(1, x_ref.shape[0]):
        total = total + x_ref[b].astype(F32)
    o_ref[...] = total.astype(BF)


def to_neighbours(x):
    count = lax.axis_size("ctx")
    ahead = [(i, i + 2) for i in range(0, count - 2, 2)]
    back = [(i, i - 2) for i in range(3, count, 2)]
    return lax.ppermute(x, "ctx", ahead + back)


def in_chip(x):
    pairs = [[i, i + 1] for i in range(0, lax.axis_size("ctx"), 2)]
    return lax.all_gather(x, "ctx", axis=0, axis_index_groups=pairs)


def per_device(queries, keys, values, out_weight, mixed_grad, lengths, dilation):
    rows, width = queries.shape
    heads = dilation.shape[0]
    groups = lax.axis_size("head")
    span = mixed_grad.shape[1]
    total = rows * lax.axis_size("ctx")
    where = lax.axis_index("ctx").astype(jnp.int32).reshape(1)
    lens = lengths.reshape(1, -1)

    kv, spread = call(
        pack_kernel,
        [shape((rows, 2 * width), BF), shape((groups, rows, span), BF)],
        [keys, values, mixed_grad],
        "pack",
        scratch=[pltpu.SemaphoreType.DMA((2 + groups,))],
        hbm_in=(0, 1, 2),
        hbm_out=(1,),
    )
    own2, spread = lax.optimization_barrier((in_chip(kv), spread))
    far = in_chip(to_neighbours(own2))
    gathered = lax.all_to_all(spread, "head", 0, 0, tiled=True)
    part, probs, attn, window = call(
        functools.partial(forward_kernel, heads, total),
        [
            shape((groups, rows, span), BF),
            shape((heads, rows, 5 * rows), BF),
            shape((rows, width), BF),
            shape((5 * rows, 2 * width), BF),
        ],
        [where, dilation, lens, queries, own2, far, out_weight],
        "forward",
        flops=2 * rows * width * (groups * span + 10 * rows),
        scratch=[
            pltpu.VMEM((groups, rows, span), BF),
            pltpu.VMEM((5 * rows, 2 * width), BF),
            pltpu.VMEM((heads, rows, 5 * rows), BF),
            pltpu.VMEM((rows, width), BF),
            pltpu.SemaphoreType.DMA((groups + 3,)),
        ],
        hbm_out=(0, 1, 2, 3),
    )
    summed = lax.all_to_all(part, "head", 0, 0, tiled=True)
    dq, own, passed, give = call(
        functools.partial(backward_kernel, heads),
        [
            shape((rows, width), BF),
            shape((rows, 2 * width), F32),
            shape((rows, 2 * width), BF),
            shape((3, rows, 2 * width), BF),
        ],
        [where, queries, window, probs, attn, gathered, out_weight],
        "backward",
        flops=2 * rows * width * (groups * span + 20 * rows),
        scratch=[
            pltpu.VMEM((groups, rows, span), BF),
            pltpu.VMEM((rows, width), BF),
            pltpu.VMEM((5, rows, 2 * width), BF),
            pltpu.VMEM((rows, width), BF),
            pltpu.VMEM((5 * rows, 2 * width), BF),
            pltpu.VMEM((heads, rows, 5 * rows), BF),
            pltpu.VMEM((rows, width), BF),
            pltpu.SemaphoreType.DMA((groups + 4,)),
        ],
        hbm_in=(1, 2, 3, 4, 5),
    )
    send, own = call(
        share_kernel,
        [shape((2, rows, 2 * width), BF), shape((rows, 2 * width), F32)],
        [where, own, passed, in_chip(give)],
        "share",
    )
    dk, dv = call(
        finish_kernel,
        [shape((rows, width), BF), shape((rows, width), BF)],
        [where, own, in_chip(to_neighbours(send))],
        "finish",
    )
    (mixed,) = call(mixed_kernel, [shape((rows, span), BF)], [summed], "mixed")
    return mixed, dq, dk, dv


def solution(mesh):
    placed = (
        P("ctx", "head"),
        P("ctx", "head"),
        P("ctx", "head"),
        P("head", None),
        P("ctx", "head"),
        P(),
        P("head"),
    )
    return jax.shard_map(
        per_device,
        mesh=mesh,
        in_specs=placed,
        out_specs=(P("ctx", "head"), P("ctx", "head"), P("ctx", "head"), P("ctx", "head")),
        check_vma=False,
    )
```

time: 74 us -> 97.8 us (1.32)
  the two profiles are of different devices: /device:TPU:242 before, /device:TPU:267 now
where the time goes in v2:
time: 97.8 us; the launch traced here: 97.5 us
  Pallas kernels  41.4 us (42%)
  waiting for transfers between devices  25.1 us (26%)
  starting transfers between devices  19.7 us (20%)
  blocking collectives  10.5 us (11%)
    pallas_call x6, Pallas kernels, call(): pl.pallas_call(body, out_shape=[pltpu.HBM(x.shape, x.dtype) if i in hbm_o...  41.4 us
    ppermute x2, waiting for transfers between devices, to_neighbours(): return lax.ppermute(x, 'ctx', ahead + back)  25.1 us
    all_gather x4, blocking collectives, in_chip(): return lax.all_gather(x, 'ctx', axis=0, axis_index_groups=pairs)  10.5 us
    ppermute x2, starting transfers between devices, to_neighbours(): return lax.ppermute(x, 'ctx', ahead + back)  9.35 us
    all_to_all x1, starting transfers between devices, per_device(): gathered = lax.all_to_all(spread, 'head', 0, 0, tiled=True)  5.17 us
    all_to_all x1, starting transfers between devices, per_device(): summed = lax.all_to_all(part, 'head', 0, 0, tiled=True)  5.16 us
  transfers between devices with their start and end apart: 4, of which 2 were waited for; matrix products, arithmetic and copies ran while one was open for 0% of the time, Pallas kernels for 8%

profile of v2, /device:TPU:267, one launch (start us, length us, event | category | flops | bytes accessed | tf_op | source)
XLA Modules:
  0.0 97.5 jit_solution(4402725774962585168)
XLA Ops:
  0.6 0.0 copy-start
  0.6 0.0 copy-start.1
  0.7 0.0 copy-start.2
  0.7 0.0 copy-start.3
  0.7 33.0 %pack.1 = (bf16[128,512]{1,0:T(8,128)(2,1)S(1)}, bf16[8,128,512]{2,1,0:T(8,128)(2,1)}) custom-call(bf16[128,256]{1,0:T(8,128)(2,1)} %k_ref.1, bf16[128,256]{1,0:T(8,128)(2,1)} %v_ref.1, bf16[128,512]{1,0:T(8,128)(2,1)} %mg_ref.1), custom_call_target="tpu_custom_call" | custom-call | bytes 1441792 | tf_op jit(solution)/shard_map/pack/pallas_call | solution.py:28
  33.6 2.3 %all-gather = bf16[256,512]{1,0:T(8,128)(2,1)S(1)} all-gather(bf16[128,512]{1,0:T(8,128)(2,1)S(1)} %get-tuple-element.20), channel_id=2, replica_groups={{0,8},{16,24},{32,40},{48,56},{64,72},{80,88},{96,104},{112,120},{128,1..., dimensions={0}, use_global_device_ids=true | all-gather | bytes 393216 | tf_op jit(solution)/shard_map/all_gather | solution.py:233
  35.9 5.2 %all-to-all-start.1 = ((bf16[8,128,512]{2,1,0:T(8,128)(2,1)}), bf16[8,128,512]{2,1,0:T(8,128)(2,1)}, u32[]{:S(2)}, u32[]{:S(2)}) async-start(bf16[8,128,512]{2,1,0:T(8,128)(2,1)} %get-tuple-element.27), calls=%async_computation.1 | async-start | bytes 2097152 | tf_op jit(solution)/shard_map/all_to_all | solution.py:256
  41.1 4.1 %collective-permute-start = (bf16[2,128,512]{2,1,0:T(8,128)(2,1)S(1)}, bf16[2,128,512]{2,1,0:T(8,128)(2,1)S(1)}, u32[]{:S(2)}, u32[]{:S(2)}) collective-permute-start(bf16[2,128,512]{2,1,0:T(8,128)(2,1)S(1)} %bitcast.9), channel_id=1, source_target_pairs={{0,16},{16,32},{32,48},{48,64},{64,80},{80,96},{96,112},{112,128},... | collective-permute-start | bytes 786440 | tf_op jit(solution)/shard_map/ppermute | solution.py:228
  45.2 16.3 %collective-permute-done = bf16[2,128,512]{2,1,0:T(8,128)(2,1)S(1)} collective-permute-done((bf16[2,128,512]{2,1,0:T(8,128)(2,1)S(1)}, bf16[2,128,512]{2,1,0:T(8,128)(2,1)S(1)}, u32[]{:S(2)}, u32[]{:S(2)}) %collective-permute-start) | collective-permute-done | bytes 262176 | tf_op jit(solution)/shard_map/ppermute | solution.py:228
  61.5 2.2 %all-gather.1 = bf16[4,128,512]{2,1,0:T(8,128)(2,1)S(1)} all-gather(bf16[2,128,512]{2,1,0:T(8,128)(2,1)S(1)} %collective-permute-done), channel_id=3, replica_groups={{0,8},{16,24},{32,40},{48,56},{64,72},{80,88},{96,104},{112,120},{128,1..., dimensions={0}, use_global_device_ids=true | all-gather | bytes 786432 | tf_op jit(solution)/shard_map/all_gather | solution.py:233
  63.7 0.0 copy-done
  63.7 0.0 copy-done.1
  63.7 0.0 copy-done.2
  63.7 0.0 copy-done.3
  63.7 2.8 %forward.1 = (bf16[8,128,512]{2,1,0:T(8,128)(2,1)}, bf16[2,128,640]{2,1,0:T(8,128)(2,1)}, bf16[128,256]{1,0:T(8,128)(2,1)}, bf16[640,512]{1,0:T(8,128)(2,1)}) custom-call(s32[1]{0:T(128)} %bitcast.where_ref, s32[2]{0:T(128)S(1)} %copy-done.2, s32[1,64]{1,0:T(1,128)S(1)} %bitcast.11, bf16[128,256]{1,0:T(8,128)(2,1)S(1)} %copy-done.1, ...), custom_call_target="tpu_custom_call" | custom-call | flops 352321536 | bytes 5046540 | tf_op jit(solution)/shard_map/forward/pallas_call | solution.py:28
  66.5 0.0 all-to-all-done.1.mg_ref
  66.5 5.2 %all-to-all-start = ((bf16[8,128,512]{2,1,0:T(8,128)(2,1)}), bf16[8,128,512]{2,1,0:T(8,128)(2,1)S(1)}, u32[]{:S(2)}, u32[]{:S(2)}) async-start(bf16[8,128,512]{2,1,0:T(8,128)(2,1)} %get-tuple-element.23), calls=%async_computation | async-start | bytes 2097152 | tf_op jit(solution)/shard_map/all_to_all | solution.py:277
  71.6 4.2 %backward.1 = (bf16[128,256]{1,0:T(8,128)(2,1)}, f32[128,512]{1,0:T(8,128)S(1)}, bf16[128,512]{1,0:T(8,128)(2,1)S(1)}, bf16[3,128,512]{2,1,0:T(8,128)(2,1)S(1)}) custom-call(s32[1]{0:T(128)} %bitcast.where_ref, bf16[128,256]{1,0:T(8,128)(2,1)} %q_hbm.1, bf16[640,512]{1,0:T(8,128)(2,1)} %get-tuple-element.24.win_hbm, ...), custom_call_target="tpu_custom_call" | custom-call | flops 436207616 | bytes 5111812 | tf_op jit(solution)/shard_map/backward/pallas_call | solution.py:28
  75.8 2.7 %all-gather.2 = bf16[6,128,512]{2,1,0:T(8,128)(2,1)S(1)} all-gather(bf16[3,128,512]{2,1,0:T(8,128)(2,1)S(1)} %get-tuple-element.31), channel_id=4, replica_groups={{0,8},{16,24},{32,40},{48,56},{64,72},{80,88},{96,104},{112,120},{128,1..., dimensions={0}, use_global_device_ids=true | all-gather | bytes 1179648 | tf_op jit(solution)/shard_map/all_gather | solution.py:233
  78.5 0.1 share.1
  78.6 5.3 %collective-permute-start.1 = (bf16[2,128,512]{2,1,0:T(8,128)(2,1)S(1)}, bf16[2,128,512]{2,1,0:T(8,128)(2,1)S(1)}, u32[]{:S(2)}, u32[]{:S(2)}) collective-permute-start(bf16[2,128,512]{2,1,0:T(8,128)(2,1)S(1)} %get-tuple-element.33), channel_id=1, source_target_pairs={{0,16},{16,32},{32,48},{48,64},{64,80},{80,96},{96,112},{112,128},... | collective-permute-start | bytes 786440 | tf_op jit(solution)/shard_map/ppermute | solution.py:228
  83.9 8.9 %collective-permute-done.1 = bf16[2,128,512]{2,1,0:T(8,128)(2,1)S(1)} collective-permute-done((bf16[2,128,512]{2,1,0:T(8,128)(2,1)S(1)}, bf16[2,128,512]{2,1,0:T(8,128)(2,1)S(1)}, u32[]{:S(2)}, u32[]{:S(2)}) %collective-permute-start.1) | collective-permute-done | bytes 262176 | tf_op jit(solution)/shard_map/ppermute | solution.py:228
  92.7 3.3 %all-gather.3 = bf16[4,128,512]{2,1,0:T(8,128)(2,1)S(1)} all-gather(bf16[2,128,512]{2,1,0:T(8,128)(2,1)S(1)} %collective-permute-done.1), channel_id=5, replica_groups={{0,8},{16,24},{32,40},{48,56},{64,72},{80,88},{96,104},{112,120},{128,1..., dimensions={0}, use_global_device_ids=true | all-gather | bytes 786432 | tf_op jit(solution)/shard_map/all_gather | solution.py:233
  96.0 0.7 finish.1
  96.7 0.0 all-to-all-done.x_ref
  96.7 0.8 mixed.1
Async XLA Ops:
  0.6 63.0 %copy-start = (bf16[256,4096]{1,0:T(8,128)(2,1)S(1)}, bf16[256,4096]{1,0:T(8,128)(2,1)}, u32[]{:S(2)}) copy-start(bf16[256,4096]{1,0:T(8,128)(2,1)} %w_ref.3) | copy-start | bytes 6291460
  0.6 63.0 %copy-start.1 = (bf16[128,256]{1,0:T(8,128)(2,1)S(1)}, bf16[128,256]{1,0:T(8,128)(2,1)}, u32[]{:S(2)}) copy-start(bf16[128,256]{1,0:T(8,128)(2,1)} %q_hbm.1) | copy-start | bytes 196612
  0.7 63.0 %copy-start.2 = (s32[2]{0:T(128)S(1)}, s32[2]{0:T(128)}, u32[]{:S(2)}) copy-start(s32[2]{0:T(128)} %dil_ref.1) | copy-start | bytes 28
  0.7 63.0 %copy-start.3 = (s32[64]{0:T(128)S(1)}, s32[64]{0:T(128)}, u32[]{:S(2)}) copy-start(s32[64]{0:T(128)} %param.12) | copy-start | bytes 772
  35.9 30.5 %all-to-all-start.1 = ((bf16[8,128,512]{2,1,0:T(8,128)(2,1)}), bf16[8,128,512]{2,1,0:T(8,128)(2,1)}, u32[]{:S(2)}, u32[]{:S(2)}) async-start(bf16[8,128,512]{2,1,0:T(8,128)(2,1)} %get-tuple-element.27), calls=%async_computation.1 | async-start | bytes 2097152 | tf_op jit(solution)/shard_map/all_to_all | solution.py:256
  41.1 20.4 %collective-permute-start = (bf16[2,128,512]{2,1,0:T(8,128)(2,1)S(1)}, bf16[2,128,512]{2,1,0:T(8,128)(2,1)S(1)}, u32[]{:S(2)}, u32[]{:S(2)}) collective-permute-start(bf16[2,128,512]{2,1,0:T(8,128)(2,1)S(1)} %bitcast.9), channel_id=1, source_target_pairs={{0,16},{16,32},{32,48},{48,64},{64,80},{80,96},{96,112},{112,128},... | collective-permute-start | bytes 786440 | tf_op jit(solution)/shard_map/ppermute | solution.py:228
  66.5 30.2 %all-to-all-start = ((bf16[8,128,512]{2,1,0:T(8,128)(2,1)}), bf16[8,128,512]{2,1,0:T(8,128)(2,1)S(1)}, u32[]{:S(2)}, u32[]{:S(2)}) async-start(bf16[8,128,512]{2,1,0:T(8,128)(2,1)} %get-tuple-element.23), calls=%async_computation | async-start | bytes 2097152 | tf_op jit(solution)/shard_map/all_to_all | solution.py:277
  78.6 14.1 %collective-permute-start.1 = (bf16[2,128,512]{2,1,0:T(8,128)(2,1)S(1)}, bf16[2,128,512]{2,1,0:T(8,128)(2,1)S(1)}, u32[]{:S(2)}, u32[]{:S(2)}) collective-permute-start(bf16[2,128,512]{2,1,0:T(8,128)(2,1)S(1)} %get-tuple-element.33), channel_id=1, source_target_pairs={{0,16},{16,32},{32,48},{48,64},{64,80},{80,96},{96,112},{112,128},... | collective-permute-start | bytes 786440 | tf_op jit(solution)/shard_map/ppermute | solution.py:228

commit v3 on v2

--- a/solution.py
+++ b/solution.py
@@ -41,14 +41,22 @@
     return jax.ShapeDtypeStruct(dims, dtype)
 
 
-def pack_kernel(k_ref, v_ref, mg_ref, kv_ref, all_ref, sems):
+def pack_kernel(k_ref, v_ref, kv_ref, sems):
     w = k_ref.shape[1]
     copies = [
         pltpu.make_async_copy(k_ref, kv_ref.at[:, :w], sems.at[0]),
         pltpu.make_async_copy(v_ref, kv_ref.at[:, w:], sems.at[1]),
     ]
-    for b in range(all_ref.shape[0]):
-        copies.append(pltpu.make_async_copy(mg_ref, all_ref.at[b], sems.at[2 + b]))
+    for c in copies:
+        c.start()
+    for c in copies:
+        c.wait()
+
+
+def spread_kernel(mg_ref, after_ref, all_ref, sems):
+    copies = [
+        pltpu.make_async_copy(mg_ref, all_ref.at[b], sems.at[b]) for b in range(all_ref.shape[0])
+    ]
     for c in copies:
         c.start()
     for c in copies:
@@ -242,18 +250,26 @@
     where = lax.axis_index("ctx").astype(jnp.int32).reshape(1)
     lens = lengths.reshape(1, -1)
 
-    kv, spread = call(
+    (kv,) = call(
         pack_kernel,
-        [shape((rows, 2 * width), BF), shape((groups, rows, span), BF)],
-        [keys, values, mixed_grad],
+        [shape((rows, 2 * width), BF)],
+        [keys, values],
         "pack",
-        scratch=[pltpu.SemaphoreType.DMA((2 + groups,))],
-        hbm_in=(0, 1, 2),
-        hbm_out=(1,),
-    )
-    own2, spread = lax.optimization_barrier((in_chip(kv), spread))
-    far = in_chip(to_neighbours(own2))
+        scratch=[pltpu.SemaphoreType.DMA((2,))],
+        hbm_in=(0, 1),
+    )
+    own2 = in_chip(kv)
+    near = to_neighbours(own2)
+    (spread,) = call(
+        spread_kernel,
+        [shape((groups, rows, span), BF)],
+        [mixed_grad, own2],
+        "spread",
+        scratch=[pltpu.SemaphoreType.DMA((groups,))],
+        hbm_out=(0,),
+    )
     gathered = lax.all_to_all(spread, "head", 0, 0, tiled=True)
+    far = in_chip(near)
     part, probs, attn, window = call(
         functools.partial(forward_kernel, heads, total),
         [
@@ -264,7 +280,7 @@
         ],
         [where, dilation, lens, queries, own2, far, out_weight],
         "forward",
-        flops=2 * rows * width * (groups * span + 10 * rows),
+        flops=80 * 2 * rows * width * (groups * span + 10 * rows),
         scratch=[
             pltpu.VMEM((groups, rows, span), BF),
             pltpu.VMEM((5 * rows, 2 * width), BF),

time: 97.8 us -> 61.2 us (0.63)
  the two profiles are of different devices: /device:TPU:267 before, /device:TPU:259 now
where the time goes in v3:
time: 61.2 us; the launch traced here: 60.8 us
  blocking collectives  18.6 us (30%)
  starting transfers between devices  18 us (29%)
  waiting for transfers between devices  12.1 us (20%)
  Pallas kernels  10.4 us (17%)
  local copies, waits for them, and re-layouts  0.91 us (1%)
  between operations  0.7 us (1%)
    all_gather x4, blocking collectives, in_chip(): return lax.all_gather(x, 'ctx', axis=0, axis_index_groups=pairs)  18.6 us
    pallas_call x7, Pallas kernels, call(): pl.pallas_call(body, out_shape=[pltpu.HBM(x.shape, x.dtype) if i in hbm_o...  10.4 us
    ppermute x2, starting transfers between devices, to_neighbours(): return lax.ppermute(x, 'ctx', ahead + back)  8.29 us
    ppermute x2, waiting for transfers between devices, to_neighbours(): return lax.ppermute(x, 'ctx', ahead + back)  6.67 us
    all_to_all x1, waiting for transfers between devices, per_device(): gathered = lax.all_to_all(spread, 'head', 0, 0, tiled=True)  5.46 us
    all_to_all x1, starting transfers between devices, per_device(): summed = lax.all_to_all(part, 'head', 0, 0, tiled=True)  5.34 us
    all_to_all x1, starting transfers between devices, per_device(): gathered = lax.all_to_all(spread, 'head', 0, 0, tiled=True)  4.4 us
  transfers between devices with their start and end apart: 4, of which 2 were waited for; matrix products, arithmetic and copies ran while one was open for 0% of the time, Pallas kernels for 14%

profile of v3, /device:TPU:259, one launch (start us, length us, event | category | flops | bytes accessed | tf_op | source)
XLA Modules:
  0.0 60.8 jit_solution(15869285567762889552)
XLA Ops:
  0.6 0.9 %pack.1 = bf16[128,512]{1,0:T(8,128)(2,1)S(1)} custom-call(bf16[128,256]{1,0:T(8,128)(2,1)} %k_ref.1, bf16[128,256]{1,0:T(8,128)(2,1)} %v_ref.1), custom_call_target="tpu_custom_call" | custom-call | bytes 262144 | tf_op jit(solution)/shard_map/pack/pallas_call | solution.py:28
  1.5 2.3 %all-gather = bf16[256,512]{1,0:T(8,128)(2,1)S(1)} all-gather(bf16[128,512]{1,0:T(8,128)(2,1)S(1)} %pack.1), channel_id=2, replica_groups={{0,8},{16,24},{32,40},{48,56},{64,72},{80,88},{96,104},{112,120},{128,1..., dimensions={0}, use_global_device_ids=true | all-gather | bytes 393216 | tf_op jit(solution)/shard_map/all_gather | solution.py:241
  3.8 0.0 copy-start
  3.8 5.1 %collective-permute-start = (bf16[2,128,512]{2,1,0:T(8,128)(2,1)S(1)}, bf16[2,128,512]{2,1,0:T(8,128)(2,1)S(1)}, u32[]{:S(2)}, u32[]{:S(2)}) collective-permute-start(bf16[2,128,512]{2,1,0:T(8,128)(2,1)S(1)} %bitcast.8), channel_id=1, source_target_pairs={{0,16},{16,32},{32,48},{48,64},{64,80},{80,96},{96,112},{112,128},... | collective-permute-start | bytes 786440 | tf_op jit(solution)/shard_map/ppermute | solution.py:236
  8.9 0.0 copy-start.1
  9.0 0.9 %copy-done.1 = bf16[128,512]{1,0:T(8,128)(2,1)S(1)} copy-done((bf16[128,512]{1,0:T(8,128)(2,1)S(1)}, bf16[128,512]{1,0:T(8,128)(2,1)}, u32[]{:S(2)}) %copy-start.1) | copy-done | bytes 131096
  9.8 0.0 copy-start.2
  9.8 0.0 copy-start.3
  9.9 0.0 copy-start.4
  9.9 1.0 %spread.1 = bf16[8,128,512]{2,1,0:T(8,128)(2,1)} custom-call(bf16[128,512]{1,0:T(8,128)(2,1)S(1)} %copy-done.1, bf16[2,128,512]{2,1,0:T(8,128)(2,1)S(1)} %bitcast.9), custom_call_target="tpu_custom_call" | custom-call | bytes 1441792 | tf_op jit(solution)/shard_map/spread/pallas_call | solution.py:28
  10.9 4.4 %all-to-all-start.1 = ((bf16[8,128,512]{2,1,0:T(8,128)(2,1)}), bf16[8,128,512]{2,1,0:T(8,128)(2,1)}, u32[]{:S(2)}, u32[]{:S(2)}) async-start(bf16[8,128,512]{2,1,0:T(8,128)(2,1)} %spread.1), calls=%async_computation.1 | async-start | bytes 2097152 | tf_op jit(solution)/shard_map/all_to_all | solution.py:271
  15.3 0.0 collective-permute-done
  15.3 5.2 %all-gather.1 = bf16[4,128,512]{2,1,0:T(8,128)(2,1)S(1)} all-gather(bf16[2,128,512]{2,1,0:T(8,128)(2,1)S(1)} %collective-permute-done), channel_id=3, replica_groups={{0,8},{16,24},{32,40},{48,56},{64,72},{80,88},{96,104},{112,120},{128,1..., dimensions={0}, use_global_device_ids=true | all-gather | bytes 786432 | tf_op jit(solution)/shard_map/all_gather | solution.py:241
  20.5 0.0 copy-done
  20.5 0.0 copy-done.2
  20.5 0.0 copy-done.3
  20.5 0.0 copy-done.4
  20.5 2.8 %forward.1 = (bf16[8,128,512]{2,1,0:T(8,128)(2,1)}, bf16[2,128,640]{2,1,0:T(8,128)(2,1)}, bf16[128,256]{1,0:T(8,128)(2,1)}, bf16[640,512]{1,0:T(8,128)(2,1)}) custom-call(s32[1]{0:T(128)} %bitcast.where_ref, s32[2]{0:T(128)S(1)} %copy-done.3, s32[1,64]{1,0:T(1,128)S(1)} %bitcast.12, bf16[128,256]{1,0:T(8,128)(2,1)S(1)} %copy-done.2, ...), custom_call_target="tpu_custom_call" | custom-call | flops 28185722880 | bytes 5046540 | tf_op jit(solution)/shard_map/forward/pallas_call | solution.py:28
  23.3 5.5 %all-to-all-done.1.mg_ref = bf16[8,128,512]{2,1,0:T(8,128)(2,1)} async-done(((bf16[8,128,512]{2,1,0:T(8,128)(2,1)}), bf16[8,128,512]{2,1,0:T(8,128)(2,1)}, u32[]{:S(2)}, u32[]{:S(2)}) %all-to-all-start.1) | async-done | bytes 1048608 | tf_op jit(solution)/shard_map/all_to_all | solution.py:271
  28.8 5.3 %all-to-all-start = ((bf16[8,128,512]{2,1,0:T(8,128)(2,1)}), bf16[8,128,512]{2,1,0:T(8,128)(2,1)S(1)}, u32[]{:S(2)}, u32[]{:S(2)}) async-start(bf16[8,128,512]{2,1,0:T(8,128)(2,1)} %get-tuple-element.16), calls=%async_computation | async-start | bytes 2097152 | tf_op jit(solution)/shard_map/all_to_all | solution.py:293
  34.1 4.2 %backward.1 = (bf16[128,256]{1,0:T(8,128)(2,1)}, f32[128,512]{1,0:T(8,128)S(1)}, bf16[128,512]{1,0:T(8,128)(2,1)S(1)}, bf16[3,128,512]{2,1,0:T(8,128)(2,1)S(1)}) custom-call(s32[1]{0:T(128)} %bitcast.where_ref, bf16[128,256]{1,0:T(8,128)(2,1)} %q_hbm.1, bf16[640,512]{1,0:T(8,128)(2,1)} %get-tuple-element.17.win_hbm, ...), custom_call_target="tpu_custom_call" | custom-call | flops 436207616 | bytes 5111812 | tf_op jit(solution)/shard_map/backward/pallas_call | solution.py:28
  38.3 3.5 %all-gather.2 = bf16[6,128,512]{2,1,0:T(8,128)(2,1)S(1)} all-gather(bf16[3,128,512]{2,1,0:T(8,128)(2,1)S(1)} %get-tuple-element.23), channel_id=4, replica_groups={{0,8},{16,24},{32,40},{48,56},{64,72},{80,88},{96,104},{112,120},{128,1..., dimensions={0}, use_global_device_ids=true | all-gather | bytes 1179648 | tf_op jit(solution)/shard_map/all_gather | solution.py:241
  41.8 0.1 share.1
  41.9 3.2 %collective-permute-start.1 = (bf16[2,128,512]{2,1,0:T(8,128)(2,1)S(1)}, bf16[2,128,512]{2,1,0:T(8,128)(2,1)S(1)}, u32[]{:S(2)}, u32[]{:S(2)}) collective-permute-start(bf16[2,128,512]{2,1,0:T(8,128)(2,1)S(1)} %get-tuple-element.25), channel_id=1, source_target_pairs={{0,16},{16,32},{32,48},{48,64},{64,80},{80,96},{96,112},{112,128},... | collective-permute-start | bytes 786440 | tf_op jit(solution)/shard_map/ppermute | solution.py:236
  45.1 6.7 %collective-permute-done.1 = bf16[2,128,512]{2,1,0:T(8,128)(2,1)S(1)} collective-permute-done((bf16[2,128,512]{2,1,0:T(8,128)(2,1)S(1)}, bf16[2,128,512]{2,1,0:T(8,128)(2,1)S(1)}, u32[]{:S(2)}, u32[]{:S(2)}) %collective-permute-start.1) | collective-permute-done | bytes 262176 | tf_op jit(solution)/shard_map/ppermute | solution.py:236
  51.7 7.6 %all-gather.3 = bf16[4,128,512]{2,1,0:T(8,128)(2,1)S(1)} all-gather(bf16[2,128,512]{2,1,0:T(8,128)(2,1)S(1)} %collective-permute-done.1), channel_id=5, replica_groups={{0,8},{16,24},{32,40},{48,56},{64,72},{80,88},{96,104},{112,120},{128,1..., dimensions={0}, use_global_device_ids=true | all-gather | bytes 786432 | tf_op jit(solution)/shard_map/all_gather | solution.py:241
  59.3 0.7 %finish.1 = (bf16[128,256]{1,0:T(8,128)(2,1)}, bf16[128,256]{1,0:T(8,128)(2,1)}) custom-call(s32[1]{0:T(128)} %bitcast.where_ref, f32[128,512]{1,0:T(8,128)S(1)} %get-tuple-element.24.own_ref, bf16[2,2,128,512]{3,2,1,0:T(8,128)(2,1)S(1)} %bitcast.7), custom_call_target="tpu_custom_call" | custom-call | bytes 917508 | tf_op jit(solution)/shard_map/finish/pallas_call | solution.py:28
  60.0 0.0 all-to-all-done.x_ref
  60.0 0.8 %mixed.1 = bf16[128,512]{1,0:T(8,128)(2,1)} custom-call(bf16[8,128,512]{2,1,0:T(8,128)(2,1)S(1)} %all-to-all-done.x_ref), custom_call_target="tpu_custom_call" | custom-call | bytes 1179648 | tf_op jit(solution)/shard_map/mixed/pallas_call | solution.py:28
Async XLA Ops:
  3.8 16.7 %copy-start = (bf16[256,4096]{1,0:T(8,128)(2,1)S(1)}, bf16[256,4096]{1,0:T(8,128)(2,1)}, u32[]{:S(2)}) copy-start(bf16[256,4096]{1,0:T(8,128)(2,1)} %w_ref.3) | copy-start | bytes 6291460
  3.8 11.5 %collective-permute-start = (bf16[2,128,512]{2,1,0:T(8,128)(2,1)S(1)}, bf16[2,128,512]{2,1,0:T(8,128)(2,1)S(1)}, u32[]{:S(2)}, u32[]{:S(2)}) collective-permute-start(bf16[2,128,512]{2,1,0:T(8,128)(2,1)S(1)} %bitcast.8), channel_id=1, source_target_pairs={{0,16},{16,32},{32,48},{48,64},{64,80},{80,96},{96,112},{112,128},... | collective-permute-start | bytes 786440 | tf_op jit(solution)/shard_map/ppermute | solution.py:236
  8.9 0.9 %copy-start.1 = (bf16[128,512]{1,0:T(8,128)(2,1)S(1)}, bf16[128,512]{1,0:T(8,128)(2,1)}, u32[]{:S(2)}) copy-start(bf16[128,512]{1,0:T(8,128)(2,1)} %mg_ref.1) | copy-start | bytes 393220
  9.8 10.7 %copy-start.2 = (bf16[128,256]{1,0:T(8,128)(2,1)S(1)}, bf16[128,256]{1,0:T(8,128)(2,1)}, u32[]{:S(2)}) copy-start(bf16[128,256]{1,0:T(8,128)(2,1)} %q_hbm.1) | copy-start | bytes 196612
  9.8 10.7 %copy-start.3 = (s32[2]{0:T(128)S(1)}, s32[2]{0:T(128)}, u32[]{:S(2)}) copy-start(s32[2]{0:T(128)} %dil_ref.1) | copy-start | bytes 28
  9.9 10.7 %copy-start.4 = (s32[64]{0:T(128)S(1)}, s32[64]{0:T(128)}, u32[]{:S(2)}) copy-start(s32[64]{0:T(128)} %param.12) | copy-start | bytes 772
  10.9 17.9 %all-to-all-start.1 = ((bf16[8,128,512]{2,1,0:T(8,128)(2,1)}), bf16[8,128,512]{2,1,0:T(8,128)(2,1)}, u32[]{:S(2)}, u32[]{:S(2)}) async-start(bf16[8,128,512]{2,1,0:T(8,128)(2,1)} %spread.1), calls=%async_computation.1 | async-start | bytes 2097152 | tf_op jit(solution)/shard_map/all_to_all | solution.py:271
  28.8 31.2 %all-to-all-start = ((bf16[8,128,512]{2,1,0:T(8,128)(2,1)}), bf16[8,128,512]{2,1,0:T(8,128)(2,1)S(1)}, u32[]{:S(2)}, u32[]{:S(2)}) async-start(bf16[8,128,512]{2,1,0:T(8,128)(2,1)} %get-tuple-element.16), calls=%async_computation | async-start | bytes 2097152 | tf_op jit(solution)/shard_map/all_to_all | solution.py:293
  41.9 9.9 %collective-permute-start.1 = (bf16[2,128,512]{2,1,0:T(8,128)(2,1)S(1)}, bf16[2,128,512]{2,1,0:T(8,128)(2,1)S(1)}, u32[]{:S(2)}, u32[]{:S(2)}) collective-permute-start(bf16[2,128,512]{2,1,0:T(8,128)(2,1)S(1)} %get-tuple-element.25), channel_id=1, source_target_pairs={{0,16},{16,32},{32,48},{48,64},{64,80},{80,96},{96,112},{112,128},... | collective-permute-start | bytes 786440 | tf_op jit(solution)/shard_map/ppermute | solution.py:236

commit v4 on v3

--- a/solution.py
+++ b/solution.py
@@ -41,9 +41,10 @@
     return jax.ShapeDtypeStruct(dims, dtype)
 
 
-def pack_kernel(k_ref, v_ref, kv_ref, sems):
+def pack_kernel(k_ref, v_ref, mg_ref, kv_ref, mgv_ref, sems):
     w = k_ref.shape[1]
     copies = [
+        pltpu.make_async_copy(mg_ref, mgv_ref, sems.at[2]),
         pltpu.make_async_copy(k_ref, kv_ref.at[:, :w], sems.at[0]),
         pltpu.make_async_copy(v_ref, kv_ref.at[:, w:], sems.at[1]),
     ]
@@ -53,7 +54,7 @@
         c.wait()
 
 
-def spread_kernel(mg_ref, after_ref, all_ref, sems):
+def spread_kernel(mg_ref, all_ref, sems):
     copies = [
         pltpu.make_async_copy(mg_ref, all_ref.at[b], sems.at[b]) for b in range(all_ref.shape[0])
     ]
@@ -77,9 +78,8 @@
 
 
 def forward_kernel(
-    heads, total, where_ref, dil_ref, lens_ref, q_ref, own_ref, far_ref, w_ref,
-    part_ref, out_probs_ref, out_attn_ref, out_win_ref,
-    hold_ref, win_ref, probs_ref, attn_ref, sems,
+    heads, total, where_ref, dil_ref, lens_ref, q_ref, prev_ref, own_ref, next_ref, w_ref,
+    part_ref, probs_ref, attn_ref, win_ref, hold_ref, sems,
 ):
     rows = q_ref.shape[0]
     width = q_ref.shape[1]
@@ -87,8 +87,7 @@
     keys = win_ref.shape[0]
     slab = where_ref[0]
     core = lax.rem(slab, 2)
-    prev, follow = far_ref.at[0], far_ref.at[1]
-    six = [prev.at[0], prev.at[1], own_ref.at[0], own_ref.at[1], follow.at[0], follow.at[1]]
+    six = [x.at[i] for x in (prev_ref, own_ref, next_ref) for i in range(2)]
 
     @pl.when(core == 0)
     def _():
@@ -99,9 +98,6 @@
     def _():
         for i in range(5):
             win_ref[i * rows : (i + 1) * rows, :] = six[i + 1][...]
-
-    copies = [pltpu.make_async_copy(win_ref, out_win_ref, sems.at[part_ref.shape[0]])]
-    copies[0].start()
 
     first = slab * rows
     row_idx = lax.broadcasted_iota(jnp.int32, (1, keys), 1) + (first - 2 * rows)
@@ -130,11 +126,9 @@
         probs = (e * (1.0 / jnp.sum(e, axis=1, keepdims=True))).astype(BF)
         probs_ref[h] = probs
         attn_ref[:, h * hd : (h + 1) * hd] = dot(probs, v, ((1,), (0,))).astype(BF)
-    for i, (a, b) in enumerate(((probs_ref, out_probs_ref), (attn_ref, out_attn_ref))):
-        copies.append(pltpu.make_async_copy(a, b, sems.at[part_ref.shape[0] + 1 + i]))
-        copies[-1].start()
     attn = attn_ref[...]
     span = part_ref.shape[2]
+    copies = []
     for b in range(part_ref.shape[0]):
         hold_ref[b] = dot(attn, w_ref[:, b * span : (b + 1) * span], ((1,), (0,))).astype(BF)
         copies.append(pltpu.make_async_copy(hold_ref.at[b], part_ref.at[b], sems.at[b]))
@@ -144,9 +138,9 @@
 
 
 def backward_kernel(
-    heads, where_ref, q_hbm, win_hbm, probs_hbm, attn_hbm, mg_ref, w_ref,
+    heads, where_ref, q_ref, win_ref, probs_ref, attn_ref, mg_ref, w_ref,
     dq_ref, own_ref, pass_ref, give_ref,
-    mgv_ref, ga_ref, terms_ref, q_ref, win_ref, probs_ref, attn_ref, sems,
+    mgv_ref, ga_ref, terms_ref, sems,
 ):
     rows = q_ref.shape[0]
     width = q_ref.shape[1]
@@ -155,9 +149,6 @@
     span = mg_ref.shape[2]
     groups = mg_ref.shape[0]
     copies = [pltpu.make_async_copy(mg_ref.at[b], mgv_ref.at[b], sems.at[b]) for b in range(groups)]
-    held = ((q_hbm, q_ref), (attn_hbm, attn_ref), (win_hbm, win_ref), (probs_hbm, probs_ref))
-    for i, (a, b) in enumerate(held):
-        copies.append(pltpu.make_async_copy(a, b, sems.at[groups + i]))
     for c in copies:
         c.start()
     total = jnp.zeros((rows, width), F32)
@@ -165,8 +156,6 @@
         copies[b].wait()
         total = total + dot(mgv_ref[b], w_ref[:, b * span : (b + 1) * span], ((1,), (1,)))
     ga_ref[...] = total.astype(BF)
-    for c in copies[groups:]:
-        c.wait()
     for h in range(heads):
         cols = slice(h * hd, (h + 1) * hd)
         vcols = slice(width + h * hd, width + (h + 1) * hd)
@@ -222,11 +211,24 @@
     dv_ref[...] = total[:, w:].astype(BF)
 
 
-def mixed_kernel(x_ref, o_ref):
-    total = x_ref[0].astype(F32)
-    for b in range(1, x_ref.shape[0]):
-        total = total + x_ref[b].astype(F32)
+def mixed_kernel(x_ref, o_ref, hold_ref, sems):
+    copies = [
+        pltpu.make_async_copy(x_ref.at[b], hold_ref.at[b], sems.at[b])
+        for b in range(x_ref.shape[0])
+    ]
+    for c in copies:
+        c.start()
+    total = jnp.zeros(o_ref.shape, F32)
+    for b, c in enumerate(copies):
+        c.wait()
+        total = total + hold_ref[b].astype(F32)
     o_ref[...] = total.astype(BF)
+
+
+def shifted(x, steps):
+    count = lax.axis_size("ctx")
+    first, last = max(0, -steps), min(count, count - steps)
+    return lax.ppermute(x, "ctx", [(i, i + steps) for i in range(first, last)])
 
 
 def to_neighbours(x):
@@ -250,26 +252,26 @@
     where = lax.axis_index("ctx").astype(jnp.int32).reshape(1)
     lens = lengths.reshape(1, -1)
 
-    (kv,) = call(
+    kv, mgv = call(
         pack_kernel,
-        [shape((rows, 2 * width), BF)],
-        [keys, values],
+        [shape((rows, 2 * width), BF), shape((rows, span), BF)],
+        [keys, values, mixed_grad],
         "pack",
-        scratch=[pltpu.SemaphoreType.DMA((2,))],
-        hbm_in=(0, 1),
-    )
-    own2 = in_chip(kv)
-    near = to_neighbours(own2)
+        scratch=[pltpu.SemaphoreType.DMA((3,))],
+        hbm_in=(0, 1, 2),
+    )
+    prev = shifted(kv, 2)
+    follow = shifted(kv, -2)
     (spread,) = call(
         spread_kernel,
         [shape((groups, rows, span), BF)],
-        [mixed_grad, own2],
+        [mgv],
         "spread",
         scratch=[pltpu.SemaphoreType.DMA((groups,))],
         hbm_out=(0,),
     )
     gathered = lax.all_to_all(spread, "head", 0, 0, tiled=True)
-    far = in_chip(near)
+    own2, prev2, next2 = in_chip(kv), in_chip(prev), in_chip(follow)
     part, probs, attn, window = call(
         functools.partial(forward_kernel, heads, total),
         [
@@ -278,17 +280,14 @@
             shape((rows, width), BF),
             shape((5 * rows, 2 * width), BF),
         ],
-        [where, dilation, lens, queries, own2, far, out_weight],
+        [where, dilation, lens, queries, prev2, own2, next2, out_weight],
         "forward",
         flops=80 * 2 * rows * width * (groups * span + 10 * rows),
         scratch=[
             pltpu.VMEM((groups, rows, span), BF),
-            pltpu.VMEM((5 * rows, 2 * width), BF),
-            pltpu.VMEM((heads, rows, 5 * rows), BF),
-            pltpu.VMEM((rows, width), BF),
-            pltpu.SemaphoreType.DMA((groups + 3,)),
+            pltpu.SemaphoreType.DMA((groups,)),
         ],
-        hbm_out=(0, 1, 2, 3),
+        hbm_out=(0,),
     )
     summed = lax.all_to_all(part, "head", 0, 0, tiled=True)
     dq, own, passed, give = call(
@@ -306,13 +305,9 @@
             pltpu.VMEM((groups, rows, span), BF),
             pltpu.VMEM((rows, width), BF),
             pltpu.VMEM((5, rows, 2 * width), BF),
-            pltpu.VMEM((rows, width), BF),
-            pltpu.VMEM((5 * rows, 2 * width), BF),
-            pltpu.VMEM((heads, rows, 5 * rows), BF),
-            pltpu.VMEM((rows, width), BF),
-            pltpu.SemaphoreType.DMA((groups + 4,)),
+            pltpu.SemaphoreType.DMA((groups,)),
         ],
-        hbm_in=(1, 2, 3, 4, 5),
+        hbm_in=(5,),
     )
     send, own = call(
         share_kernel,
@@ -320,13 +315,20 @@
         [where, own, passed, in_chip(give)],
         "share",
     )
+    (mixed,) = call(
+        mixed_kernel,
+        [shape((rows, span), BF)],
+        [summed],
+        "mixed",
+        scratch=[pltpu.VMEM((groups, rows, span), BF), pltpu.SemaphoreType.DMA((groups,))],
+        hbm_in=(0,),
+    )
     dk, dv = call(
         finish_kernel,
         [shape((rows, width), BF), shape((rows, width), BF)],
         [where, own, in_chip(to_neighbours(send))],
         "finish",
     )
-    (mixed,) = call(mixed_kernel, [shape((rows, span), BF)], [summed], "mixed")
     return mixed, dq, dk, dv
 
 

time: 61.2 us -> 62.3 us (1.018)
  the two profiles are of different devices: /device:TPU:259 before, /device:TPU:267 now
where the time goes in v4:
time: 62.3 us; the launch traced here: 61.9 us
  starting transfers between devices  20.8 us (33%)
  blocking collectives  17.2 us (28%)
  Pallas kernels  11.6 us (19%)
  waiting for transfers between devices  11.5 us (18%)
  between operations  0.75 us (1%)
    all_gather x5, blocking collectives, in_chip(): return lax.all_gather(x, 'ctx', axis=0, axis_index_groups=pairs)  17.2 us
    pallas_call x7, Pallas kernels, call(): pl.pallas_call(body, out_shape=[pltpu.HBM(x.shape, x.dtype) if i in hbm_o...  11.6 us
    ppermute x2, starting transfers between devices, shifted(): return lax.ppermute(x, 'ctx', [(i, i + steps) for i in range(first, last)])  9.5 us
    all_to_all x1, starting transfers between devices, per_device(): gathered = lax.all_to_all(spread, 'head', 0, 0, tiled=True)  5.18 us
    all_to_all x1, waiting for transfers between devices, per_device(): summed = lax.all_to_all(part, 'head', 0, 0, tiled=True)  4.86 us
    all_to_all x1, waiting for transfers between devices, per_device(): gathered = lax.all_to_all(spread, 'head', 0, 0, tiled=True)  4.26 us
    all_to_all x1, starting transfers between devices, per_device(): summed = lax.all_to_all(part, 'head', 0, 0, tiled=True)  4.24 us
    ppermute x1, waiting for transfers between devices, to_neighbours(): return lax.ppermute(x, 'ctx', ahead + back)  2.38 us
  transfers between devices with their start and end apart: 5, of which 3 were waited for; matrix products, arithmetic and copies ran while one was open for 0% of the time, Pallas kernels for 16%

profile of v4, /device:TPU:267, one launch (start us, length us, event | category | flops | bytes accessed | tf_op | source)
XLA Modules:
  0.0 61.9 jit_solution(17286433024812728731)
XLA Ops:
  0.6 1.0 %pack.1 = (bf16[128,512]{1,0:T(8,128)(2,1)S(1)}, bf16[128,512]{1,0:T(8,128)(2,1)S(1)}) custom-call(bf16[128,256]{1,0:T(8,128)(2,1)} %k_ref.1, bf16[128,256]{1,0:T(8,128)(2,1)} %v_ref.1, bf16[128,512]{1,0:T(8,128)(2,1)} %mg_ref.1), custom_call_target="tpu_custom_call" | custom-call | bytes 524288 | tf_op jit(solution)/shard_map/pack/pallas_call | solution.py:28
  1.6 4.2 %collective-permute-start = (bf16[128,512]{1,0:T(8,128)(2,1)S(1)}, bf16[128,512]{1,0:T(8,128)(2,1)S(1)}, u32[]{:S(2)}, u32[]{:S(2)}) collective-permute-start(bf16[128,512]{1,0:T(8,128)(2,1)S(1)} %get-tuple-element.18), channel_id=1, source_target_pairs={{0,16},{8,24},{16,32},{24,40},{32,48},{40,56},{48,64},{56,72},{64,... | collective-permute-start | bytes 393224 | tf_op jit(solution)/shard_map/ppermute | solution.py:231
  5.8 5.3 %collective-permute-start.1 = (bf16[128,512]{1,0:T(8,128)(2,1)S(1)}, bf16[128,512]{1,0:T(8,128)(2,1)S(1)}, u32[]{:S(2)}, u32[]{:S(2)}) collective-permute-start(bf16[128,512]{1,0:T(8,128)(2,1)S(1)} %get-tuple-element.18), channel_id=1, source_target_pairs={{16,0},{24,8},{32,16},{40,24},{48,32},{56,40},{64,48},{72,56},{80,... | collective-permute-start | bytes 393224 | tf_op jit(solution)/shard_map/ppermute | solution.py:231
  11.1 0.0 copy-start
  11.1 0.0 copy-start.1
  11.1 0.0 copy-start.2
  11.2 0.0 copy-start.3
  11.2 1.0 %spread.1 = bf16[8,128,512]{2,1,0:T(8,128)(2,1)} custom-call(bf16[128,512]{1,0:T(8,128)(2,1)S(1)} %get-tuple-element.23.mg_ref), custom_call_target="tpu_custom_call" | custom-call | bytes 1179648 | tf_op jit(solution)/shard_map/spread/pallas_call | solution.py:28
  12.2 5.2 %all-to-all-start.1 = ((bf16[8,128,512]{2,1,0:T(8,128)(2,1)}), bf16[8,128,512]{2,1,0:T(8,128)(2,1)}, u32[]{:S(2)}, u32[]{:S(2)}) async-start(bf16[8,128,512]{2,1,0:T(8,128)(2,1)} %spread.1), calls=%async_computation.1 | async-start | bytes 2097152 | tf_op jit(solution)/shard_map/all_to_all | solution.py:273
  17.4 3.4 %all-gather.1 = bf16[256,512]{1,0:T(8,128)(2,1)S(1)} all-gather(bf16[128,512]{1,0:T(8,128)(2,1)S(1)} %get-tuple-element.18), channel_id=3, replica_groups={{0,8},{16,24},{32,40},{48,56},{64,72},{80,88},{96,104},{112,120},{128,1..., dimensions={0}, use_global_device_ids=true | all-gather | bytes 393216 | tf_op jit(solution)/shard_map/all_gather | solution.py:243
  20.8 0.0 collective-permute-done
  20.8 2.0 %all-gather = bf16[256,512]{1,0:T(8,128)(2,1)S(1)} all-gather(bf16[128,512]{1,0:T(8,128)(2,1)S(1)} %collective-permute-done), channel_id=2, replica_groups={{0,8},{16,24},{32,40},{48,56},{64,72},{80,88},{96,104},{112,120},{128,1..., dimensions={0}, use_global_device_ids=true | all-gather | bytes 393216 | tf_op jit(solution)/shard_map/all_gather | solution.py:243
  22.8 0.0 collective-permute-done.1
  22.8 2.0 %all-gather.2 = bf16[256,512]{1,0:T(8,128)(2,1)S(1)} all-gather(bf16[128,512]{1,0:T(8,128)(2,1)S(1)} %collective-permute-done.1), channel_id=4, replica_groups={{0,8},{16,24},{32,40},{48,56},{64,72},{80,88},{96,104},{112,120},{128,1..., dimensions={0}, use_global_device_ids=true | all-gather | bytes 393216 | tf_op jit(solution)/shard_map/all_gather | solution.py:243
  24.8 0.0 copy-done
  24.8 0.0 copy-done.1
  24.8 0.0 copy-done.2
  24.8 0.0 copy-done.3
  24.8 2.8 %forward.1 = (bf16[8,128,512]{2,1,0:T(8,128)(2,1)}, bf16[2,128,640]{2,1,0:T(8,128)(2,1)S(1)}, bf16[128,256]{1,0:T(8,128)(2,1)S(1)}, bf16[640,512]{1,0:T(8,128)(2,1)S(1)}) custom-call(s32[1]{0:T(128)} %bitcast.where_ref, s32[2]{0:T(128)S(1)} %copy-done.2, s32[1,64]{1,0:T(1,128)S(1)} %bitcast.12, bf16[128,256]{1,0:T(8,128)(2,1)S(1)} %copy-done.1, ...), custom_call_target="tpu_custom_call" | custom-call | flops 28185722880 | bytes 5046540 | tf_op jit(solution)/shard_map/forward/pallas_call | solution.py:28
  27.6 4.3 %all-to-all-done.1.mg_ref = bf16[8,128,512]{2,1,0:T(8,128)(2,1)} async-done(((bf16[8,128,512]{2,1,0:T(8,128)(2,1)}), bf16[8,128,512]{2,1,0:T(8,128)(2,1)}, u32[]{:S(2)}, u32[]{:S(2)}) %all-to-all-start.1) | async-done | bytes 1048608 | tf_op jit(solution)/shard_map/all_to_all | solution.py:273
  31.9 4.2 %all-to-all-start = ((bf16[8,128,512]{2,1,0:T(8,128)(2,1)}), bf16[8,128,512]{2,1,0:T(8,128)(2,1)}, u32[]{:S(2)}, u32[]{:S(2)}) async-start(bf16[8,128,512]{2,1,0:T(8,128)(2,1)} %get-tuple-element.19), calls=%async_computation | async-start | bytes 2097152 | tf_op jit(solution)/shard_map/all_to_all | solution.py:292
  36.1 4.1 %backward.1 = (bf16[128,256]{1,0:T(8,128)(2,1)}, f32[128,512]{1,0:T(8,128)S(1)}, bf16[128,512]{1,0:T(8,128)(2,1)S(1)}, bf16[3,128,512]{2,1,0:T(8,128)(2,1)S(1)}) custom-call(s32[1]{0:T(128)} %bitcast.where_ref, bf16[128,256]{1,0:T(8,128)(2,1)S(1)} %copy-done.1, bf16[640,512]{1,0:T(8,128)(2,1)S(1)} %get-tuple-element.20.win_ref, ...), custom_call_target="tpu_custom_call" | custom-call | flops 436207616 | bytes 5111812 | tf_op jit(solution)/shard_map/backward/pallas_call | solution.py:28
  40.2 3.5 %all-gather.3 = bf16[6,128,512]{2,1,0:T(8,128)(2,1)S(1)} all-gather(bf16[3,128,512]{2,1,0:T(8,128)(2,1)S(1)} %get-tuple-element.27), channel_id=5, replica_groups={{0,8},{16,24},{32,40},{48,56},{64,72},{80,88},{96,104},{112,120},{128,1..., dimensions={0}, use_global_device_ids=true | all-gather | bytes 1179648 | tf_op jit(solution)/shard_map/all_gather | solution.py:243
  43.7 0.1 share.1
  43.8 1.9 %collective-permute-start.2 = (bf16[2,128,512]{2,1,0:T(8,128)(2,1)S(1)}, bf16[2,128,512]{2,1,0:T(8,128)(2,1)S(1)}, u32[]{:S(2)}, u32[]{:S(2)}) collective-permute-start(bf16[2,128,512]{2,1,0:T(8,128)(2,1)S(1)} %get-tuple-element.29), channel_id=1, source_target_pairs={{0,16},{16,32},{32,48},{48,64},{64,80},{80,96},{96,112},{112,128},... | collective-permute-start | bytes 786440 | tf_op jit(solution)/shard_map/ppermute | solution.py:238
  45.7 4.9 %all-to-all-done.x_ref = bf16[8,128,512]{2,1,0:T(8,128)(2,1)} async-done(((bf16[8,128,512]{2,1,0:T(8,128)(2,1)}), bf16[8,128,512]{2,1,0:T(8,128)(2,1)}, u32[]{:S(2)}, u32[]{:S(2)}) %all-to-all-start) | async-done | bytes 1048608 | tf_op jit(solution)/shard_map/all_to_all | solution.py:292
  50.6 2.0 %mixed.1 = bf16[128,512]{1,0:T(8,128)(2,1)} custom-call(bf16[8,128,512]{2,1,0:T(8,128)(2,1)} %all-to-all-done.x_ref), custom_call_target="tpu_custom_call" | custom-call | bytes 1179648 | tf_op jit(solution)/shard_map/mixed/pallas_call | solution.py:28
  52.6 2.4 %collective-permute-done.2 = bf16[2,128,512]{2,1,0:T(8,128)(2,1)S(1)} collective-permute-done((bf16[2,128,512]{2,1,0:T(8,128)(2,1)S(1)}, bf16[2,128,512]{2,1,0:T(8,128)(2,1)S(1)}, u32[]{:S(2)}, u32[]{:S(2)}) %collective-permute-start.2) | collective-permute-done | bytes 262176 | tf_op jit(solution)/shard_map/ppermute | solution.py:238
  55.0 6.2 %all-gather.4 = bf16[4,128,512]{2,1,0:T(8,128)(2,1)S(1)} all-gather(bf16[2,128,512]{2,1,0:T(8,128)(2,1)S(1)} %collective-permute-done.2), channel_id=6, replica_groups={{0,8},{16,24},{32,40},{48,56},{64,72},{80,88},{96,104},{112,120},{128,1..., dimensions={0}, use_global_device_ids=true | all-gather | bytes 786432 | tf_op jit(solution)/shard_map/all_gather | solution.py:243
  61.3 0.7 %finish.1 = (bf16[128,256]{1,0:T(8,128)(2,1)}, bf16[128,256]{1,0:T(8,128)(2,1)}) custom-call(s32[1]{0:T(128)} %bitcast.where_ref, f32[128,512]{1,0:T(8,128)S(1)} %get-tuple-element.28.own_ref, bf16[2,2,128,512]{3,2,1,0:T(8,128)(2,1)S(1)} %bitcast.8), custom_call_target="tpu_custom_call" | custom-call | bytes 917508 | tf_op jit(solution)/shard_map/finish/pallas_call | solution.py:28
Async XLA Ops:
  1.6 19.2 %collective-permute-start = (bf16[128,512]{1,0:T(8,128)(2,1)S(1)}, bf16[128,512]{1,0:T(8,128)(2,1)S(1)}, u32[]{:S(2)}, u32[]{:S(2)}) collective-permute-start(bf16[128,512]{1,0:T(8,128)(2,1)S(1)} %get-tuple-element.18), channel_id=1, source_target_pairs={{0,16},{8,24},{16,32},{24,40},{32,48},{40,56},{48,64},{56,72},{64,... | collective-permute-start | bytes 393224 | tf_op jit(solution)/shard_map/ppermute | solution.py:231
  5.8 17.0 %collective-permute-start.1 = (bf16[128,512]{1,0:T(8,128)(2,1)S(1)}, bf16[128,512]{1,0:T(8,128)(2,1)S(1)}, u32[]{:S(2)}, u32[]{:S(2)}) collective-permute-start(bf16[128,512]{1,0:T(8,128)(2,1)S(1)} %get-tuple-element.18), channel_id=1, source_target_pairs={{16,0},{24,8},{32,16},{40,24},{48,32},{56,40},{64,48},{72,56},{80,... | collective-permute-start | bytes 393224 | tf_op jit(solution)/shard_map/ppermute | solution.py:231
  11.1 13.7 %copy-start = (bf16[256,4096]{1,0:T(8,128)(2,1)S(1)}, bf16[256,4096]{1,0:T(8,128)(2,1)}, u32[]{:S(2)}) copy-start(bf16[256,4096]{1,0:T(8,128)(2,1)} %w_ref.3) | copy-start | bytes 6291460
  11.1 13.7 %copy-start.1 = (bf16[128,256]{1,0:T(8,128)(2,1)S(1)}, bf16[128,256]{1,0:T(8,128)(2,1)}, u32[]{:S(2)}) copy-start(bf16[128,256]{1,0:T(8,128)(2,1)} %q_ref.3) | copy-start | bytes 196612
  11.1 13.7 %copy-start.2 = (s32[2]{0:T(128)S(1)}, s32[2]{0:T(128)}, u32[]{:S(2)}) copy-start(s32[2]{0:T(128)} %dil_ref.1) | copy-start | bytes 28
  11.2 13.6 %copy-start.3 = (s32[64]{0:T(128)S(1)}, s32[64]{0:T(128)}, u32[]{:S(2)}) copy-start(s32[64]{0:T(128)} %param.12) | copy-start | bytes 772
  12.2 19.7 %all-to-all-start.1 = ((bf16[8,128,512]{2,1,0:T(8,128)(2,1)}), bf16[8,128,512]{2,1,0:T(8,128)(2,1)}, u32[]{:S(2)}, u32[]{:S(2)}) async-start(bf16[8,128,512]{2,1,0:T(8,128)(2,1)} %spread.1), calls=%async_computation.1 | async-start | bytes 2097152 | tf_op jit(solution)/shard_map/all_to_all | solution.py:273
  31.9 18.7 %all-to-all-start = ((bf16[8,128,512]{2,1,0:T(8,128)(2,1)}), bf16[8,128,512]{2,1,0:T(8,128)(2,1)}, u32[]{:S(2)}, u32[]{:S(2)}) async-start(bf16[8,128,512]{2,1,0:T(8,128)(2,1)} %get-tuple-element.19), calls=%async_computation | async-start | bytes 2097152 | tf_op jit(solution)/shard_map/all_to_all | solution.py:292
  43.8 11.2 %collective-permute-start.2 = (bf16[2,128,512]{2,1,0:T(8,128)(2,1)S(1)}, bf16[2,128,512]{2,1,0:T(8,128)(2,1)S(1)}, u32[]{:S(2)}, u32[]{:S(2)}) collective-permute-start(bf16[2,128,512]{2,1,0:T(8,128)(2,1)S(1)} %get-tuple-element.29), channel_id=1, source_target_pairs={{0,16},{16,32},{32,48},{48,64},{64,80},{80,96},{96,112},{112,128},... | collective-permute-start | bytes 786440 | tf_op jit(solution)/shard_map/ppermute | solution.py:238

commit v5 on v4

--- a/solution.py
+++ b/solution.py
@@ -137,37 +137,37 @@
         c.wait()
 
 
+def cotangent_kernel(mg_ref, w_ref, ga_ref):
+    span = mg_ref.shape[2]
+    total = jnp.zeros(ga_ref.shape, F32)
+    for b in range(mg_ref.shape[0]):
+        total = total + dot(mg_ref[b], w_ref[:, b * span : (b + 1) * span], ((1,), (1,)))
+    ga_ref[...] = total.astype(BF)
+
+
 def backward_kernel(
-    heads, where_ref, q_ref, win_ref, probs_ref, attn_ref, mg_ref, w_ref,
-    dq_ref, own_ref, pass_ref, give_ref,
-    mgv_ref, ga_ref, terms_ref, sems,
+    heads, where_ref, q_hbm, win_ref, probs_ref, attn_ref, ga_ref,
+    dq_ref, own_ref, pass_ref, give_ref, terms_ref, q_ref, sem,
 ):
     rows = q_ref.shape[0]
     width = q_ref.shape[1]
+    fetch = pltpu.make_async_copy(q_hbm, q_ref, sem)
+    fetch.start()
     hd = width // heads
     factor = hd**-0.5
-    span = mg_ref.shape[2]
-    groups = mg_ref.shape[0]
-    copies = [pltpu.make_async_copy(mg_ref.at[b], mgv_ref.at[b], sems.at[b]) for b in range(groups)]
-    for c in copies:
-        c.start()
-    total = jnp.zeros((rows, width), F32)
-    for b in range(groups):
-        copies[b].wait()
-        total = total + dot(mgv_ref[b], w_ref[:, b * span : (b + 1) * span], ((1,), (1,)))
-    ga_ref[...] = total.astype(BF)
     for h in range(heads):
         cols = slice(h * hd, (h + 1) * hd)
         vcols = slice(width + h * hd, width + (h + 1) * hd)
         ga = ga_ref[:, cols]
-        q = q_ref[:, cols]
         delta = jnp.sum(ga.astype(F32) * attn_ref[:, cols].astype(F32), axis=1, keepdims=True)
         grad_prob = dot(ga, win_ref[:, vcols], ((1,), (1,)))
         probs = probs_ref[h]
         slopes = (probs.astype(F32) * (grad_prob - delta)).astype(BF)
         dq_ref[:, cols] = (dot(slopes, win_ref[:, cols], ((1,), (0,))) * factor).astype(BF)
-        dk = dot(slopes, q, ((0,), (0,))) * factor
         dv = dot(probs, ga, ((0,), (0,)))
+        if h == 0:
+            fetch.wait()
+        dk = dot(slopes, q_ref[:, cols], ((0,), (0,))) * factor
         for i in range(5):
             part = slice(i * rows, (i + 1) * rows)
             if i == 2:
@@ -211,17 +211,10 @@
     dv_ref[...] = total[:, w:].astype(BF)
 
 
-def mixed_kernel(x_ref, o_ref, hold_ref, sems):
-    copies = [
-        pltpu.make_async_copy(x_ref.at[b], hold_ref.at[b], sems.at[b])
-        for b in range(x_ref.shape[0])
-    ]
-    for c in copies:
-        c.start()
-    total = jnp.zeros(o_ref.shape, F32)
-    for b, c in enumerate(copies):
-        c.wait()
-        total = total + hold_ref[b].astype(F32)
+def mixed_kernel(x_ref, o_ref):
+    total = x_ref[0].astype(F32)
+    for b in range(1, x_ref.shape[0]):
+        total = total + x_ref[b].astype(F32)
     o_ref[...] = total.astype(BF)
 
 
@@ -289,6 +282,14 @@
         ],
         hbm_out=(0,),
     )
+    (ga,) = call(
+        cotangent_kernel,
+        [shape((rows, width), BF)],
+        [gathered, out_weight],
+        "cotangent",
+        flops=2 * rows * width * groups * span,
+    )
+    ga, part = lax.optimization_barrier((ga, part))
     summed = lax.all_to_all(part, "head", 0, 0, tiled=True)
     dq, own, passed, give = call(
         functools.partial(backward_kernel, heads),
@@ -298,16 +299,15 @@
             shape((rows, 2 * width), BF),
             shape((3, rows, 2 * width), BF),
         ],
-        [where, queries, window, probs, attn, gathered, out_weight],
+        [where, queries, window, probs, attn, ga],
         "backward",
-        flops=2 * rows * width * (groups * span + 20 * rows),
+        flops=2 * rows * width * 20 * rows,
         scratch=[
-            pltpu.VMEM((groups, rows, span), BF),
+            pltpu.VMEM((5, rows, 2 * width), BF),
             pltpu.VMEM((rows, width), BF),
-            pltpu.VMEM((5, rows, 2 * width), BF),
-            pltpu.SemaphoreType.DMA((groups,)),
+            pltpu.SemaphoreType.DMA,
         ],
-        hbm_in=(5,),
+        hbm_in=(1,),
     )
     send, own = call(
         share_kernel,
@@ -315,18 +315,12 @@
         [where, own, passed, in_chip(give)],
         "share",
     )
-    (mixed,) = call(
-        mixed_kernel,
-        [shape((rows, span), BF)],
-        [summed],
-        "mixed",
-        scratch=[pltpu.VMEM((groups, rows, span), BF), pltpu.SemaphoreType.DMA((groups,))],
-        hbm_in=(0,),
-    )
+    (mixed,) = call(mixed_kernel, [shape((rows, span), BF)], [summed], "mixed")
+    arrived, mixed = lax.optimization_barrier((to_neighbours(send), mixed))
     dk, dv = call(
         finish_kernel,
         [shape((rows, width), BF), shape((rows, width), BF)],
-        [where, own, in_chip(to_neighbours(send))],
+        [where, own, in_chip(arrived)],
         "finish",
     )
     return mixed, dq, dk, dv

time: 62.3 us -> 60.9 us (0.978)
  the two profiles are of different devices: /device:TPU:267 before, /device:TPU:259 now
where the time goes in v5:
time: 60.9 us; the launch traced here: 60.5 us
  starting transfers between devices  22.8 us (37%)
  blocking collectives  19.8 us (33%)
  Pallas kernels  9.26 us (15%)
  waiting for transfers between devices  6.38 us (10%)
  local copies, waits for them, and re-layouts  1.5 us (2%)
  between operations  0.77 us (1%)
    all_gather x5, blocking collectives, in_chip(): return lax.all_gather(x, 'ctx', axis=0, axis_index_groups=pairs)  19.8 us
    pallas_call x8, Pallas kernels, call(): pl.pallas_call(body, out_shape=[pltpu.HBM(x.shape, x.dtype) if i in hbm_o...  9.26 us
    ppermute x2, starting transfers between devices, shifted(): return lax.ppermute(x, 'ctx', [(i, i + steps) for i in range(first, last)])  6.89 us
    ppermute x1, starting transfers between devices, to_neighbours(): return lax.ppermute(x, 'ctx', ahead + back)  6.07 us
    all_to_all x1, starting transfers between devices, per_device(): summed = lax.all_to_all(part, 'head', 0, 0, tiled=True)  5.25 us
    ppermute x1, waiting for transfers between devices, to_neighbours(): return lax.ppermute(x, 'ctx', ahead + back)  4.65 us
    all_to_all x1, starting transfers between devices, per_device(): gathered = lax.all_to_all(spread, 'head', 0, 0, tiled=True)  4.58 us
    unnamed x16, local copies, waits for them, and re-layouts  1.5 us
  transfers between devices with their start and end apart: 5, of which 3 were waited for; matrix products, arithmetic and copies ran while one was open for 0% of the time, Pallas kernels for 11%

profile of v5, /device:TPU:259, one launch (start us, length us, event | category | flops | bytes accessed | tf_op | source)
XLA Modules:
  0.0 60.5 jit_solution(10415318874200544131)
XLA Ops:
  0.6 1.0 %pack.1 = (bf16[128,512]{1,0:T(8,128)(2,1)S(1)}, bf16[128,512]{1,0:T(8,128)(2,1)S(1)}) custom-call(bf16[128,256]{1,0:T(8,128)(2,1)} %k_ref.1, bf16[128,256]{1,0:T(8,128)(2,1)} %v_ref.1, bf16[128,512]{1,0:T(8,128)(2,1)} %mg_ref.1), custom_call_target="tpu_custom_call" | custom-call | bytes 524288 | tf_op jit(solution)/shard_map/pack/pallas_call | solution.py:28
  1.6 5.0 %collective-permute-start.1 = (bf16[128,512]{1,0:T(8,128)(2,1)S(1)}, bf16[128,512]{1,0:T(8,128)(2,1)}, u32[]{:S(2)}, u32[]{:S(2)}) collective-permute-start(bf16[128,512]{1,0:T(8,128)(2,1)S(1)} %get-tuple-element.22), channel_id=1, source_target_pairs={{16,0},{24,8},{32,16},{40,24},{48,32},{56,40},{64,48},{72,56},{80,... | collective-permute-start | bytes 393224 | tf_op jit(solution)/shard_map/ppermute | solution.py:224
  6.6 1.9 %collective-permute-start = (bf16[128,512]{1,0:T(8,128)(2,1)S(1)}, bf16[128,512]{1,0:T(8,128)(2,1)S(1)}, u32[]{:S(2)}, u32[]{:S(2)}) collective-permute-start(bf16[128,512]{1,0:T(8,128)(2,1)S(1)} %get-tuple-element.22), channel_id=1, source_target_pairs={{0,16},{8,24},{16,32},{24,40},{32,48},{40,56},{48,64},{56,72},{64,... | collective-permute-start | bytes 393224 | tf_op jit(solution)/shard_map/ppermute | solution.py:224
  8.5 0.0 copy-start
  8.5 0.0 copy-start.3
  8.5 0.0 copy-start.6
  8.5 0.0 copy-start.7
  8.6 1.1 %spread.1 = bf16[8,128,512]{2,1,0:T(8,128)(2,1)} custom-call(bf16[128,512]{1,0:T(8,128)(2,1)S(1)} %get-tuple-element.26.mg_ref), custom_call_target="tpu_custom_call" | custom-call | bytes 1179648 | tf_op jit(solution)/shard_map/spread/pallas_call | solution.py:28
  9.6 4.6 %all-to-all-start = ((bf16[8,128,512]{2,1,0:T(8,128)(2,1)}), bf16[8,128,512]{2,1,0:T(8,128)(2,1)S(1)}, u32[]{:S(2)}, u32[]{:S(2)}) async-start(bf16[8,128,512]{2,1,0:T(8,128)(2,1)} %spread.1), calls=%async_computation | async-start | bytes 2097152 | tf_op jit(solution)/shard_map/all_to_all | solution.py:266
  14.2 3.4 %all-gather.1 = bf16[256,512]{1,0:T(8,128)(2,1)S(1)} all-gather(bf16[128,512]{1,0:T(8,128)(2,1)S(1)} %get-tuple-element.22), channel_id=3, replica_groups={{0,8},{16,24},{32,40},{48,56},{64,72},{80,88},{96,104},{112,120},{128,1..., dimensions={0}, use_global_device_ids=true | all-gather | bytes 393216 | tf_op jit(solution)/shard_map/all_gather | solution.py:236
  17.6 0.0 collective-permute-done.1
  17.6 2.2 %all-gather.2 = bf16[256,512]{1,0:T(8,128)(2,1)S(1)} all-gather(bf16[128,512]{1,0:T(8,128)(2,1)} %collective-permute-done.1), channel_id=4, replica_groups={{0,8},{16,24},{32,40},{48,56},{64,72},{80,88},{96,104},{112,120},{128,1..., dimensions={0}, use_global_device_ids=true | all-gather | bytes 393216 | tf_op jit(solution)/shard_map/all_gather | solution.py:236
  19.8 0.0 collective-permute-done
  19.8 2.4 %all-gather = bf16[256,512]{1,0:T(8,128)(2,1)S(1)} all-gather(bf16[128,512]{1,0:T(8,128)(2,1)S(1)} %collective-permute-done), channel_id=2, replica_groups={{0,8},{16,24},{32,40},{48,56},{64,72},{80,88},{96,104},{112,120},{128,1..., dimensions={0}, use_global_device_ids=true | all-gather | bytes 393216 | tf_op jit(solution)/shard_map/all_gather | solution.py:236
  22.3 0.0 copy-done
  22.3 0.0 copy-done.3
  22.3 0.0 copy-done.6
  22.3 0.0 copy-done.7
  22.3 2.8 %forward.1 = (bf16[8,128,512]{2,1,0:T(8,128)(2,1)}, bf16[2,128,640]{2,1,0:T(8,128)(2,1)S(1)}, bf16[128,256]{1,0:T(8,128)(2,1)S(1)}, bf16[640,512]{1,0:T(8,128)(2,1)S(1)}) custom-call(s32[1]{0:T(128)} %bitcast.where_ref, s32[2]{0:T(128)S(1)} %copy-done.6, s32[1,64]{1,0:T(1,128)S(1)} %bitcast.12, bf16[128,256]{1,0:T(8,128)(2,1)S(1)} %copy-done.3, ...), custom_call_target="tpu_custom_call" | custom-call | flops 28185722880 | bytes 5046540 | tf_op jit(solution)/shard_map/forward/pallas_call | solution.py:28
  25.1 0.0 copy-start.1
  25.1 0.8 %copy-done.1 = bf16[640,512]{1,0:T(8,128)(2,1)} copy-done((bf16[640,512]{1,0:T(8,128)(2,1)}, bf16[640,512]{1,0:T(8,128)(2,1)S(1)}, u32[]{:S(2)}) %copy-start.1) | copy-done | bytes 655384
  25.9 0.0 copy-start.4
  25.9 0.6 %copy-done.4 = bf16[128,256]{1,0:T(8,128)(2,1)} copy-done((bf16[128,256]{1,0:T(8,128)(2,1)}, bf16[128,256]{1,0:T(8,128)(2,1)S(1)}, u32[]{:S(2)}) %copy-start.4) | copy-done | bytes 65560
  26.5 1.1 %all-to-all-done.mg_ref = bf16[8,128,512]{2,1,0:T(8,128)(2,1)S(1)} async-done(((bf16[8,128,512]{2,1,0:T(8,128)(2,1)}), bf16[8,128,512]{2,1,0:T(8,128)(2,1)S(1)}, u32[]{:S(2)}, u32[]{:S(2)}) %all-to-all-start) | async-done | bytes 1048608 | tf_op jit(solution)/shard_map/all_to_all | solution.py:266
  27.6 0.8 %cotangent.1.ga_ref = bf16[128,256]{1,0:T(8,128)(2,1)S(1)} custom-call(bf16[8,128,512]{2,1,0:T(8,128)(2,1)S(1)} %all-to-all-done.mg_ref, bf16[256,4096]{1,0:T(8,128)(2,1)S(1)} %copy-done), custom_call_target="tpu_custom_call" | custom-call | flops 268435456 | bytes 3211264 | tf_op jit(solution)/shard_map/cotangent/pallas_call | solution.py:28
  28.4 0.0 copy-start.2
  28.4 0.0 copy-start.5
  28.5 5.2 %all-to-all-start.1 = ((bf16[8,128,512]{2,1,0:T(8,128)(2,1)}), bf16[8,128,512]{2,1,0:T(8,128)(2,1)S(1)}, u32[]{:S(2)}, u32[]{:S(2)}) async-start(bf16[8,128,512]{2,1,0:T(8,128)(2,1)} %get-tuple-element.33), calls=%async_computation.1 | async-start | bytes 2097152 | tf_op jit(solution)/shard_map/all_to_all | solution.py:293
  33.7 0.0 copy-done.2
  33.7 0.0 copy-done.5
  33.7 2.1 %backward.1 = (bf16[128,256]{1,0:T(8,128)(2,1)}, f32[128,512]{1,0:T(8,128)S(1)}, bf16[128,512]{1,0:T(8,128)(2,1)S(1)}, bf16[3,128,512]{2,1,0:T(8,128)(2,1)S(1)}) custom-call(s32[1]{0:T(128)} %bitcast.where_ref, bf16[128,256]{1,0:T(8,128)(2,1)} %q_hbm.1, bf16[640,512]{1,0:T(8,128)(2,1)S(1)} %copy-done.2, ...), custom_call_target="tpu_custom_call" | custom-call | flops 167772160 | bytes 2031620 | tf_op jit(solution)/shard_map/backward/pallas_call | solution.py:28
  35.8 4.5 %all-gather.3 = bf16[6,128,512]{2,1,0:T(8,128)(2,1)S(1)} all-gather(bf16[3,128,512]{2,1,0:T(8,128)(2,1)S(1)} %get-tuple-element.31), channel_id=5, replica_groups={{0,8},{16,24},{32,40},{48,56},{64,72},{80,88},{96,104},{112,120},{128,1..., dimensions={0}, use_global_device_ids=true | all-gather | bytes 1179648 | tf_op jit(solution)/shard_map/all_gather | solution.py:236
  40.3 0.1 share.1
  40.4 6.1 %collective-permute-start.2 = (bf16[2,128,512]{2,1,0:T(8,128)(2,1)S(1)}, bf16[2,128,512]{2,1,0:T(8,128)(2,1)S(1)}, u32[]{:S(2)}, u32[]{:S(2)}) collective-permute-start(bf16[2,128,512]{2,1,0:T(8,128)(2,1)S(1)} %get-tuple-element.32), channel_id=1, source_target_pairs={{0,16},{16,32},{32,48},{48,64},{64,80},{80,96},{96,112},{112,128},... | collective-permute-start | bytes 786440 | tf_op jit(solution)/shard_map/ppermute | solution.py:231
  46.4 0.7 %all-to-all-done.1.x_ref = bf16[8,128,512]{2,1,0:T(8,128)(2,1)S(1)} async-done(((bf16[8,128,512]{2,1,0:T(8,128)(2,1)}), bf16[8,128,512]{2,1,0:T(8,128)(2,1)S(1)}, u32[]{:S(2)}, u32[]{:S(2)}) %all-to-all-start.1) | async-done | bytes 1048608 | tf_op jit(solution)/shard_map/all_to_all | solution.py:293
  47.1 0.8 %mixed.1 = bf16[128,512]{1,0:T(8,128)(2,1)} custom-call(bf16[8,128,512]{2,1,0:T(8,128)(2,1)S(1)} %all-to-all-done.1.x_ref), custom_call_target="tpu_custom_call" | custom-call | bytes 1179648 | tf_op jit(solution)/shard_map/mixed/pallas_call | solution.py:28
  47.9 4.6 %collective-permute-done.2 = bf16[2,128,512]{2,1,0:T(8,128)(2,1)S(1)} collective-permute-done((bf16[2,128,512]{2,1,0:T(8,128)(2,1)S(1)}, bf16[2,128,512]{2,1,0:T(8,128)(2,1)S(1)}, u32[]{:S(2)}, u32[]{:S(2)}) %collective-permute-start.2) | collective-permute-done | bytes 262176 | tf_op jit(solution)/shard_map/ppermute | solution.py:231
  52.5 7.3 %all-gather.4 = bf16[4,128,512]{2,1,0:T(8,128)(2,1)S(1)} all-gather(bf16[2,128,512]{2,1,0:T(8,128)(2,1)S(1)} %collective-permute-done.2), channel_id=6, replica_groups={{0,8},{16,24},{32,40},{48,56},{64,72},{80,88},{96,104},{112,120},{128,1..., dimensions={0}, use_global_device_ids=true | all-gather | bytes 786432 | tf_op jit(solution)/shard_map/all_gather | solution.py:236
  59.8 0.7 %finish.1 = (bf16[128,256]{1,0:T(8,128)(2,1)}, bf16[128,256]{1,0:T(8,128)(2,1)}) custom-call(s32[1]{0:T(128)} %bitcast.where_ref, f32[128,512]{1,0:T(8,128)S(1)} %get-tuple-element.36.own_ref, bf16[2,2,128,512]{3,2,1,0:T(8,128)(2,1)S(1)} %bitcast.8), custom_call_target="tpu_custom_call" | custom-call | bytes 917508 | tf_op jit(solution)/shard_map/finish/pallas_call | solution.py:28
Async XLA Ops:
  1.6 16.0 %collective-permute-start.1 = (bf16[128,512]{1,0:T(8,128)(2,1)S(1)}, bf16[128,512]{1,0:T(8,128)(2,1)}, u32[]{:S(2)}, u32[]{:S(2)}) collective-permute-start(bf16[128,512]{1,0:T(8,128)(2,1)S(1)} %get-tuple-element.22), channel_id=1, source_target_pairs={{16,0},{24,8},{32,16},{40,24},{48,32},{56,40},{64,48},{72,56},{80,... | collective-permute-start | bytes 393224 | tf_op jit(solution)/shard_map/ppermute | solution.py:224
  6.6 13.2 %collective-permute-start = (bf16[128,512]{1,0:T(8,128)(2,1)S(1)}, bf16[128,512]{1,0:T(8,128)(2,1)S(1)}, u32[]{:S(2)}, u32[]{:S(2)}) collective-permute-start(bf16[128,512]{1,0:T(8,128)(2,1)S(1)} %get-tuple-element.22), channel_id=1, source_target_pairs={{0,16},{8,24},{16,32},{24,40},{32,48},{40,56},{48,64},{56,72},{64,... | collective-permute-start | bytes 393224 | tf_op jit(solution)/shard_map/ppermute | solution.py:224
  8.5 13.7 %copy-start = (bf16[256,4096]{1,0:T(8,128)(2,1)S(1)}, bf16[256,4096]{1,0:T(8,128)(2,1)}, u32[]{:S(2)}) copy-start(bf16[256,4096]{1,0:T(8,128)(2,1)} %w_ref.3) | copy-start | bytes 6291460
  8.5 13.7 %copy-start.3 = (bf16[128,256]{1,0:T(8,128)(2,1)S(1)}, bf16[128,256]{1,0:T(8,128)(2,1)}, u32[]{:S(2)}) copy-start(bf16[128,256]{1,0:T(8,128)(2,1)} %q_hbm.1) | copy-start | bytes 196612
  8.5 13.7 %copy-start.6 = (s32[2]{0:T(128)S(1)}, s32[2]{0:T(128)}, u32[]{:S(2)}) copy-start(s32[2]{0:T(128)} %dil_ref.1) | copy-start | bytes 28
  8.5 13.7 %copy-start.7 = (s32[64]{0:T(128)S(1)}, s32[64]{0:T(128)}, u32[]{:S(2)}) copy-start(s32[64]{0:T(128)} %param.12) | copy-start | bytes 772
  9.6 18.0 %all-to-all-start = ((bf16[8,128,512]{2,1,0:T(8,128)(2,1)}), bf16[8,128,512]{2,1,0:T(8,128)(2,1)S(1)}, u32[]{:S(2)}, u32[]{:S(2)}) async-start(bf16[8,128,512]{2,1,0:T(8,128)(2,1)} %spread.1), calls=%async_computation | async-start | bytes 2097152 | tf_op jit(solution)/shard_map/all_to_all | solution.py:266
  25.1 0.8 %copy-start.1 = (bf16[640,512]{1,0:T(8,128)(2,1)}, bf16[640,512]{1,0:T(8,128)(2,1)S(1)}, u32[]{:S(2)}) copy-start(bf16[640,512]{1,0:T(8,128)(2,1)S(1)} %get-tuple-element.23.win_ref) | copy-start | bytes 1966084
  25.9 0.6 %copy-start.4 = (bf16[128,256]{1,0:T(8,128)(2,1)}, bf16[128,256]{1,0:T(8,128)(2,1)S(1)}, u32[]{:S(2)}) copy-start(bf16[128,256]{1,0:T(8,128)(2,1)S(1)} %get-tuple-element.25.attn_ref) | copy-start | bytes 196612
  28.4 5.3 %copy-start.2 = (bf16[640,512]{1,0:T(8,128)(2,1)S(1)}, bf16[640,512]{1,0:T(8,128)(2,1)}, u32[]{:S(2)}) copy-start(bf16[640,512]{1,0:T(8,128)(2,1)} %copy-done.1) | copy-start | bytes 1966084
  28.4 5.3 %copy-start.5 = (bf16[128,256]{1,0:T(8,128)(2,1)S(1)}, bf16[128,256]{1,0:T(8,128)(2,1)}, u32[]{:S(2)}) copy-start(bf16[128,256]{1,0:T(8,128)(2,1)} %copy-done.4) | copy-start | bytes 196612
  28.5 18.7 %all-to-all-start.1 = ((bf16[8,128,512]{2,1,0:T(8,128)(2,1)}), bf16[8,128,512]{2,1,0:T(8,128)(2,1)S(1)}, u32[]{:S(2)}, u32[]{:S(2)}) async-start(bf16[8,128,512]{2,1,0:T(8,128)(2,1)} %get-tuple-element.33), calls=%async_computation.1 | async-start | bytes 2097152 | tf_op jit(solution)/shard_map/all_to_all | solution.py:293
  40.4 12.2 %collective-permute-start.2 = (bf16[2,128,512]{2,1,0:T(8,128)(2,1)S(1)}, bf16[2,128,512]{2,1,0:T(8,128)(2,1)S(1)}, u32[]{:S(2)}, u32[]{:S(2)}) collective-permute-start(bf16[2,128,512]{2,1,0:T(8,128)(2,1)S(1)} %get-tuple-element.32), channel_id=1, source_target_pairs={{0,16},{16,32},{32,48},{48,64},{64,80},{80,96},{96,112},{112,128},... | collective-permute-start | bytes 786440 | tf_op jit(solution)/shard_map/ppermute | solution.py:231

commit v6 on v5

--- a/solution.py
+++ b/solution.py
@@ -54,7 +54,7 @@
         c.wait()
 
 
-def spread_kernel(mg_ref, all_ref, sems):
+def spread_kernel(mg_ref, after_ref, all_ref, sems):
     copies = [
         pltpu.make_async_copy(mg_ref, all_ref.at[b], sems.at[b]) for b in range(all_ref.shape[0])
     ]
@@ -78,7 +78,7 @@
 
 
 def forward_kernel(
-    heads, total, where_ref, dil_ref, lens_ref, q_ref, prev_ref, own_ref, next_ref, w_ref,
+    heads, total, where_ref, dil_ref, lens_ref, q_ref, own_ref, far_ref, w_ref,
     part_ref, probs_ref, attn_ref, win_ref, hold_ref, sems,
 ):
     rows = q_ref.shape[0]
@@ -87,7 +87,7 @@
     keys = win_ref.shape[0]
     slab = where_ref[0]
     core = lax.rem(slab, 2)
-    six = [x.at[i] for x in (prev_ref, own_ref, next_ref) for i in range(2)]
+    six = [x.at[i] for x in (far_ref.at[0], own_ref, far_ref.at[1]) for i in range(2)]
 
     @pl.when(core == 0)
     def _():
@@ -127,11 +127,13 @@
         probs_ref[h] = probs
         attn_ref[:, h * hd : (h + 1) * hd] = dot(probs, v, ((1,), (0,))).astype(BF)
     attn = attn_ref[...]
-    span = part_ref.shape[2]
+    span = part_ref.shape[3]
     copies = []
-    for b in range(part_ref.shape[0]):
+    cols = part_ref.shape[0]
+    for b in range(2 * cols):
+        row, col = b // cols, b % cols
         hold_ref[b] = dot(attn, w_ref[:, b * span : (b + 1) * span], ((1,), (0,))).astype(BF)
-        copies.append(pltpu.make_async_copy(hold_ref.at[b], part_ref.at[b], sems.at[b]))
+        copies.append(pltpu.make_async_copy(hold_ref.at[b], part_ref.at[col, row], sems.at[b]))
         copies[-1].start()
     for c in copies:
         c.wait()
@@ -211,17 +213,22 @@
     dv_ref[...] = total[:, w:].astype(BF)
 
 
-def mixed_kernel(x_ref, o_ref):
-    total = x_ref[0].astype(F32)
-    for b in range(1, x_ref.shape[0]):
-        total = total + x_ref[b].astype(F32)
-    o_ref[...] = total.astype(BF)
-
-
-def shifted(x, steps):
-    count = lax.axis_size("ctx")
-    first, last = max(0, -steps), min(count, count - steps)
-    return lax.ppermute(x, "ctx", [(i, i + steps) for i in range(first, last)])
+def row_sum_kernel(where_ref, x_ref, keep_ref, give_ref):
+    row = where_ref[1]
+    cols = x_ref.shape[0]
+
+    def total(r):
+        acc = x_ref[0, r].astype(F32)
+        for b in range(1, cols):
+            acc = acc + x_ref[b, r].astype(F32)
+        return acc
+
+    keep_ref[...] = total(row)
+    give_ref[...] = total(1 - row).astype(BF)
+
+
+def mixed_kernel(where_ref, keep_ref, got_ref, o_ref):
+    o_ref[...] = (keep_ref[...] + got_ref[1 - where_ref[1]].astype(F32)).astype(BF)
 
 
 def to_neighbours(x):
@@ -242,7 +249,10 @@
     groups = lax.axis_size("head")
     span = mixed_grad.shape[1]
     total = rows * lax.axis_size("ctx")
-    where = lax.axis_index("ctx").astype(jnp.int32).reshape(1)
+    cols = groups // 2
+    along_row = [[r * cols + c for c in range(cols)] for r in range(2)]
+    across_rows = [[c, cols + c] for c in range(cols)]
+    where = jnp.stack([lax.axis_index("ctx"), lax.axis_index("head") // cols]).astype(jnp.int32)
     lens = lengths.reshape(1, -1)
 
     kv, mgv = call(
@@ -253,27 +263,27 @@
         scratch=[pltpu.SemaphoreType.DMA((3,))],
         hbm_in=(0, 1, 2),
     )
-    prev = shifted(kv, 2)
-    follow = shifted(kv, -2)
+    own2 = in_chip(kv)
+    near = to_neighbours(own2)
     (spread,) = call(
         spread_kernel,
         [shape((groups, rows, span), BF)],
-        [mgv],
+        [mgv, own2],
         "spread",
         scratch=[pltpu.SemaphoreType.DMA((groups,))],
         hbm_out=(0,),
     )
     gathered = lax.all_to_all(spread, "head", 0, 0, tiled=True)
-    own2, prev2, next2 = in_chip(kv), in_chip(prev), in_chip(follow)
+    far = in_chip(near)
     part, probs, attn, window = call(
         functools.partial(forward_kernel, heads, total),
         [
-            shape((groups, rows, span), BF),
+            shape((groups // 2, 2, rows, span), BF),
             shape((heads, rows, 5 * rows), BF),
             shape((rows, width), BF),
             shape((5 * rows, 2 * width), BF),
         ],
-        [where, dilation, lens, queries, prev2, own2, next2, out_weight],
+        [where, dilation, lens, queries, own2, far, out_weight],
         "forward",
         flops=80 * 2 * rows * width * (groups * span + 10 * rows),
         scratch=[
@@ -290,7 +300,7 @@
         flops=2 * rows * width * groups * span,
     )
     ga, part = lax.optimization_barrier((ga, part))
-    summed = lax.all_to_all(part, "head", 0, 0, tiled=True)
+    summed = lax.all_to_all(part, "head", 0, 0, tiled=True, axis_index_groups=along_row)
     dq, own, passed, give = call(
         functools.partial(backward_kernel, heads),
         [
@@ -315,7 +325,14 @@
         [where, own, passed, in_chip(give)],
         "share",
     )
-    (mixed,) = call(mixed_kernel, [shape((rows, span), BF)], [summed], "mixed")
+    mine, yours = call(
+        row_sum_kernel,
+        [shape((rows, span), F32), shape((rows, span), BF)],
+        [where, summed],
+        "rowsum",
+    )
+    both = lax.all_gather(yours, "head", axis=0, axis_index_groups=across_rows)
+    (mixed,) = call(mixed_kernel, [shape((rows, span), BF)], [where, mine, both], "mixed")
     arrived, mixed = lax.optimization_barrier((to_neighbours(send), mixed))
     dk, dv = call(
         finish_kernel,

time: 60.9 us -> 62.5 us (1.026)
  the two profiles are of different devices: /device:TPU:259 before, /device:TPU:17 now
where the time goes in v6:
time: 62.5 us; the launch traced here: 62.2 us
  starting transfers between devices  16.5 us (26%)
  blocking collectives  16.1 us (26%)
  waiting for transfers between devices  14.5 us (23%)
  Pallas kernels  11.9 us (19%)
  local copies, waits for them, and re-layouts  2.25 us (4%)
  between operations  0.83 us (1%)
    pallas_call x9, Pallas kernels, call(): pl.pallas_call(body, out_shape=[pltpu.HBM(x.shape, x.dtype) if i in hbm_o...  11.9 us
    all_gather x4, blocking collectives, in_chip(): return lax.all_gather(x, 'ctx', axis=0, axis_index_groups=pairs)  11.6 us
    ppermute x2, starting transfers between devices, to_neighbours(): return lax.ppermute(x, 'ctx', ahead + back)  9.25 us
    all_to_all x1, waiting for transfers between devices, per_device(): gathered = lax.all_to_all(spread, 'head', 0, 0, tiled=True)  7.53 us
    all_to_all x1, waiting for transfers between devices, per_device(): lax.all_to_all(part, 'head', 0, 0, tiled=True, axis_index_groups=along_row)  6.95 us
    all_gather x1, blocking collectives, per_device(): both = lax.all_gather(yours, 'head', axis=0, axis_index_groups=across_rows)  4.5 us
    all_to_all x1, starting transfers between devices, per_device(): lax.all_to_all(part, 'head', 0, 0, tiled=True, axis_index_groups=along_row)  3.66 us
    all_to_all x1, starting transfers between devices, per_device(): gathered = lax.all_to_all(spread, 'head', 0, 0, tiled=True)  3.57 us
  transfers between devices with their start and end apart: 4, of which 2 were waited for; matrix products, arithmetic and copies ran while one was open for 0% of the time, Pallas kernels for 14%

profile of v6, /device:TPU:17, one launch (start us, length us, event | category | flops | bytes accessed | tf_op | source)
XLA Modules:
  0.0 62.2 jit_solution(10596438920291255314)
XLA Ops:
  0.6 1.0 %pack.1 = (bf16[128,512]{1,0:T(8,128)(2,1)S(1)}, bf16[128,512]{1,0:T(8,128)(2,1)S(1)}) custom-call(bf16[128,256]{1,0:T(8,128)(2,1)} %k_ref.1, bf16[128,256]{1,0:T(8,128)(2,1)} %v_ref.1, bf16[128,512]{1,0:T(8,128)(2,1)} %mg_ref.1), custom_call_target="tpu_custom_call" | custom-call | bytes 524288 | tf_op jit(solution)/shard_map/pack/pallas_call | solution.py:28
  1.6 2.3 %all-gather = bf16[256,512]{1,0:T(8,128)(2,1)S(1)} all-gather(bf16[128,512]{1,0:T(8,128)(2,1)S(1)} %get-tuple-element.24), channel_id=2, replica_groups={{0,8},{16,24},{32,40},{48,56},{64,72},{80,88},{96,104},{112,120},{128,1..., dimensions={0}, use_global_device_ids=true | all-gather | bytes 393216 | tf_op jit(solution)/shard_map/all_gather | solution.py:243
  3.9 7.3 %collective-permute-start = (bf16[2,128,512]{2,1,0:T(8,128)(2,1)S(1)}, bf16[2,128,512]{2,1,0:T(8,128)(2,1)}, u32[]{:S(2)}, u32[]{:S(2)}) collective-permute-start(bf16[2,128,512]{2,1,0:T(8,128)(2,1)S(1)} %bitcast.11), channel_id=1, source_target_pairs={{0,16},{16,32},{32,48},{48,64},{64,80},{80,96},{96,112},{112,128},... | collective-permute-start | bytes 786440 | tf_op jit(solution)/shard_map/ppermute | solution.py:238
  11.2 0.0 copy-start
  11.3 0.0 copy-start.5
  11.3 0.0 copy-start.8
  11.3 0.0 copy-start.9
  11.3 1.0 %spread.1 = bf16[8,128,512]{2,1,0:T(8,128)(2,1)} custom-call(bf16[128,512]{1,0:T(8,128)(2,1)S(1)} %get-tuple-element.28.mg_ref, bf16[2,128,512]{2,1,0:T(8,128)(2,1)S(1)} %bitcast.12), custom_call_target="tpu_custom_call" | custom-call | bytes 1441792 | tf_op jit(solution)/shard_map/spread/pallas_call | solution.py:28
  12.3 3.6 %all-to-all-start = ((bf16[8,128,512]{2,1,0:T(8,128)(2,1)}), bf16[8,128,512]{2,1,0:T(8,128)(2,1)S(1)}, u32[]{:S(2)}, u32[]{:S(2)}) async-start(bf16[8,128,512]{2,1,0:T(8,128)(2,1)} %spread.1), calls=%async_computation | async-start | bytes 2097152 | tf_op jit(solution)/shard_map/all_to_all | solution.py:276
  15.9 0.1 pad_add_fusion.where_ref
  16.0 0.0 collective-permute-done
  16.0 2.4 %all-gather.1 = bf16[4,128,512]{2,1,0:T(8,128)(2,1)S(1)} all-gather(bf16[2,128,512]{2,1,0:T(8,128)(2,1)} %collective-permute-done), channel_id=3, replica_groups={{0,8},{16,24},{32,40},{48,56},{64,72},{80,88},{96,104},{112,120},{128,1..., dimensions={0}, use_global_device_ids=true | all-gather | bytes 786432 | tf_op jit(solution)/shard_map/all_gather | solution.py:243
  18.5 0.0 copy-done
  18.5 0.0 copy-done.5
  18.5 0.0 copy-done.8
  18.5 0.0 copy-done.9
  18.5 2.8 %forward.1 = (bf16[4,2,128,512]{3,2,1,0:T(8,128)(2,1)}, bf16[2,128,640]{2,1,0:T(8,128)(2,1)S(1)}, bf16[128,256]{1,0:T(8,128)(2,1)S(1)}, bf16[640,512]{1,0:T(8,128)(2,1)S(1)}) custom-call(s32[2]{0:T(128)S(1)} %pad_add_fusion.where_ref, s32[2]{0:T(128)S(1)} %copy-done.8, s32[1,64]{1,0:T(1,128)S(1)} %bitcast.15, bf16[128,256]{1,0:T(8,128)(2,1)S(1)} %copy-done.5, ...), custom_call_target="tpu_custom_call" | custom-call | flops 28185722880 | bytes 5046544 | tf_op jit(solution)/shard_map/forward/pallas_call | solution.py:28
  21.3 0.0 copy-start.1
  21.3 0.8 %copy-done.1 = bf16[640,512]{1,0:T(8,128)(2,1)} copy-done((bf16[640,512]{1,0:T(8,128)(2,1)}, bf16[640,512]{1,0:T(8,128)(2,1)S(1)}, u32[]{:S(2)}) %copy-start.1) | copy-done | bytes 655384
  22.2 0.0 copy-start.3
  22.2 0.7 %copy-done.3 = bf16[2,128,640]{2,1,0:T(8,128)(2,1)} copy-done((bf16[2,128,640]{2,1,0:T(8,128)(2,1)}, bf16[2,128,640]{2,1,0:T(8,128)(2,1)S(1)}, u32[]{:S(2)}) %copy-start.3) | copy-done | bytes 327704
  22.9 0.0 copy-start.6
  22.9 0.6 %copy-done.6 = bf16[128,256]{1,0:T(8,128)(2,1)} copy-done((bf16[128,256]{1,0:T(8,128)(2,1)}, bf16[128,256]{1,0:T(8,128)(2,1)S(1)}, u32[]{:S(2)}) %copy-start.6) | copy-done | bytes 65560
  23.5 7.5 %all-to-all-done.mg_ref = bf16[8,128,512]{2,1,0:T(8,128)(2,1)S(1)} async-done(((bf16[8,128,512]{2,1,0:T(8,128)(2,1)}), bf16[8,128,512]{2,1,0:T(8,128)(2,1)S(1)}, u32[]{:S(2)}, u32[]{:S(2)}) %all-to-all-start) | async-done | bytes 1048608 | tf_op jit(solution)/shard_map/all_to_all | solution.py:276
  31.1 0.0 copy-start.4
  31.1 0.8 %cotangent.1.ga_ref = bf16[128,256]{1,0:T(8,128)(2,1)S(1)} custom-call(bf16[8,128,512]{2,1,0:T(8,128)(2,1)S(1)} %all-to-all-done.mg_ref, bf16[256,4096]{1,0:T(8,128)(2,1)S(1)} %copy-done), custom_call_target="tpu_custom_call" | custom-call | flops 268435456 | bytes 3211264 | tf_op jit(solution)/shard_map/cotangent/pallas_call | solution.py:28
  31.9 0.0 copy-start.2
  31.9 0.0 copy-start.7
  31.9 3.7 %all-to-all-start.1 = ((bf16[4,2,128,512]{3,2,1,0:T(8,128)(2,1)}), bf16[4,2,128,512]{3,2,1,0:T(8,128)(2,1)S(1)}, u32[]{:S(2)}, u32[]{:S(2)}) async-start(bf16[4,2,128,512]{3,2,1,0:T(8,128)(2,1)} %get-tuple-element.35), calls=%async_computation.1 | async-start | bytes 2097152 | tf_op jit(solution)/shard_map/all_to_all | solution.py:303
  35.6 0.0 copy-done.4
  35.6 0.0 copy-done.2
  35.6 0.0 copy-done.7
  35.6 2.6 %backward.1 = (bf16[128,256]{1,0:T(8,128)(2,1)}, f32[128,512]{1,0:T(8,128)S(1)}, bf16[128,512]{1,0:T(8,128)(2,1)S(1)}, bf16[3,128,512]{2,1,0:T(8,128)(2,1)S(1)}) custom-call(s32[2]{0:T(128)S(1)} %pad_add_fusion.where_ref, bf16[128,256]{1,0:T(8,128)(2,1)} %q_hbm.1, bf16[640,512]{1,0:T(8,128)(2,1)S(1)} %copy-done.2, bf16[2,128,640]{2,1,0:T(8,128)(2,1)S(1)} %copy-done.4, ...), custom_call_target="tpu_custom_call" | custom-call | flops 167772160 | bytes 2031624 | tf_op jit(solution)/shard_map/backward/pallas_call | solution.py:28
  38.2 2.5 %all-gather.2 = bf16[6,128,512]{2,1,0:T(8,128)(2,1)S(1)} all-gather(bf16[3,128,512]{2,1,0:T(8,128)(2,1)S(1)} %get-tuple-element.33), channel_id=4, replica_groups={{0,8},{16,24},{32,40},{48,56},{64,72},{80,88},{96,104},{112,120},{128,1..., dimensions={0}, use_global_device_ids=true | all-gather | bytes 1179648 | tf_op jit(solution)/shard_map/all_gather | solution.py:243
  40.7 0.6 share.1
  41.3 1.9 %collective-permute-start.1 = (bf16[2,128,512]{2,1,0:T(8,128)(2,1)S(1)}, bf16[2,128,512]{2,1,0:T(8,128)(2,1)S(1)}, u32[]{:S(2)}, u32[]{:S(2)}) collective-permute-start(bf16[2,128,512]{2,1,0:T(8,128)(2,1)S(1)} %get-tuple-element.34), channel_id=1, source_target_pairs={{0,16},{16,32},{32,48},{48,64},{64,80},{80,96},{96,112},{112,128},... | collective-permute-start | bytes 786440 | tf_op jit(solution)/shard_map/ppermute | solution.py:238
  43.3 7.0 %all-to-all-done.1.x_ref = bf16[4,2,128,512]{3,2,1,0:T(8,128)(2,1)S(1)} async-done(((bf16[4,2,128,512]{3,2,1,0:T(8,128)(2,1)}), bf16[4,2,128,512]{3,2,1,0:T(8,128)(2,1)S(1)}, u32[]{:S(2)}, u32[]{:S(2)}) %all-to-all-start.1) | async-done | bytes 1048608 | tf_op jit(solution)/shard_map/all_to_all | solution.py:303
  50.2 0.7 %rowsum.1 = (f32[128,512]{1,0:T(8,128)S(1)}, bf16[128,512]{1,0:T(8,128)(2,1)S(1)}) custom-call(s32[2]{0:T(128)S(1)} %pad_add_fusion.where_ref, bf16[4,2,128,512]{3,2,1,0:T(8,128)(2,1)S(1)} %all-to-all-done.1.x_ref), custom_call_target="tpu_custom_call" | custom-call | bytes 1441800 | tf_op jit(solution)/shard_map/rowsum/pallas_call | solution.py:28
  50.9 4.5 %all-gather.3 = bf16[256,512]{1,0:T(8,128)(2,1)S(1)} all-gather(bf16[128,512]{1,0:T(8,128)(2,1)S(1)} %get-tuple-element.37), channel_id=5, replica_groups={{0,4},{1,5},{2,6},{3,7},{8,12},{9,13},{10,14},{11,15},{16,20},{17,21},{..., dimensions={0}, use_global_device_ids=true | all-gather | bytes 393216 | tf_op jit(solution)/shard_map/all_gather | solution.py:334
  55.4 1.2 %mixed.1 = bf16[128,512]{1,0:T(8,128)(2,1)} custom-call(s32[2]{0:T(128)S(1)} %pad_add_fusion.where_ref, f32[128,512]{1,0:T(8,128)S(1)} %get-tuple-element.36.keep_ref, bf16[2,128,512]{2,1,0:T(8,128)(2,1)S(1)} %bitcast.10), custom_call_target="tpu_custom_call" | custom-call | bytes 655368 | tf_op jit(solution)/shard_map/mixed/pallas_call | solution.py:28
  56.6 0.0 collective-permute-done.1
  56.6 4.3 %all-gather.4 = bf16[4,128,512]{2,1,0:T(8,128)(2,1)S(1)} all-gather(bf16[2,128,512]{2,1,0:T(8,128)(2,1)S(1)} %collective-permute-done.1), channel_id=6, replica_groups={{0,8},{16,24},{32,40},{48,56},{64,72},{80,88},{96,104},{112,120},{128,1..., dimensions={0}, use_global_device_ids=true | all-gather | bytes 786432 | tf_op jit(solution)/shard_map/all_gather | solution.py:243
  60.9 1.2 %finish.1 = (bf16[128,256]{1,0:T(8,128)(2,1)}, bf16[128,256]{1,0:T(8,128)(2,1)}) custom-call(s32[2]{0:T(128)S(1)} %pad_add_fusion.where_ref, f32[128,512]{1,0:T(8,128)S(1)} %get-tuple-element.40.own_ref, bf16[2,2,128,512]{3,2,1,0:T(8,128)(2,1)S(1)} %bitcast.9), custom_call_target="tpu_custom_call" | custom-call | bytes 917512 | tf_op jit(solution)/shard_map/finish/pallas_call | solution.py:28
Async XLA Ops:
  3.9 12.1 %collective-permute-start = (bf16[2,128,512]{2,1,0:T(8,128)(2,1)S(1)}, bf16[2,128,512]{2,1,0:T(8,128)(2,1)}, u32[]{:S(2)}, u32[]{:S(2)}) collective-permute-start(bf16[2,128,512]{2,1,0:T(8,128)(2,1)S(1)} %bitcast.11), channel_id=1, source_target_pairs={{0,16},{16,32},{32,48},{48,64},{64,80},{80,96},{96,112},{112,128},... | collective-permute-start | bytes 786440 | tf_op jit(solution)/shard_map/ppermute | solution.py:238
  11.2 7.2 %copy-start = (bf16[256,4096]{1,0:T(8,128)(2,1)S(1)}, bf16[256,4096]{1,0:T(8,128)(2,1)}, u32[]{:S(2)}) copy-start(bf16[256,4096]{1,0:T(8,128)(2,1)} %w_ref.3) | copy-start | bytes 6291460
  11.3 7.2 %copy-start.5 = (bf16[128,256]{1,0:T(8,128)(2,1)S(1)}, bf16[128,256]{1,0:T(8,128)(2,1)}, u32[]{:S(2)}) copy-start(bf16[128,256]{1,0:T(8,128)(2,1)} %q_hbm.1) | copy-start | bytes 196612
  11.3 7.2 %copy-start.8 = (s32[2]{0:T(128)S(1)}, s32[2]{0:T(128)}, u32[]{:S(2)}) copy-start(s32[2]{0:T(128)} %dil_ref.1) | copy-start | bytes 28
  11.3 7.2 %copy-start.9 = (s32[64]{0:T(128)S(1)}, s32[64]{0:T(128)}, u32[]{:S(2)}) copy-start(s32[64]{0:T(128)} %param.12) | copy-start | bytes 772
  12.3 18.7 %all-to-all-start = ((bf16[8,128,512]{2,1,0:T(8,128)(2,1)}), bf16[8,128,512]{2,1,0:T(8,128)(2,1)S(1)}, u32[]{:S(2)}, u32[]{:S(2)}) async-start(bf16[8,128,512]{2,1,0:T(8,128)(2,1)} %spread.1), calls=%async_computation | async-start | bytes 2097152 | tf_op jit(solution)/shard_map/all_to_all | solution.py:276
  21.3 0.8 %copy-start.1 = (bf16[640,512]{1,0:T(8,128)(2,1)}, bf16[640,512]{1,0:T(8,128)(2,1)S(1)}, u32[]{:S(2)}) copy-start(bf16[640,512]{1,0:T(8,128)(2,1)S(1)} %get-tuple-element.25.win_ref) | copy-start | bytes 1966084
  22.2 0.7 %copy-start.3 = (bf16[2,128,640]{2,1,0:T(8,128)(2,1)}, bf16[2,128,640]{2,1,0:T(8,128)(2,1)S(1)}, u32[]{:S(2)}) copy-start(bf16[2,128,640]{2,1,0:T(8,128)(2,1)S(1)} %get-tuple-element.26.probs_ref) | copy-start | bytes 983044
  22.9 0.6 %copy-start.6 = (bf16[128,256]{1,0:T(8,128)(2,1)}, bf16[128,256]{1,0:T(8,128)(2,1)S(1)}, u32[]{:S(2)}) copy-start(bf16[128,256]{1,0:T(8,128)(2,1)S(1)} %get-tuple-element.27.attn_ref) | copy-start | bytes 196612
  31.1 4.5 %copy-start.4 = (bf16[2,128,640]{2,1,0:T(8,128)(2,1)S(1)}, bf16[2,128,640]{2,1,0:T(8,128)(2,1)}, u32[]{:S(2)}) copy-start(bf16[2,128,640]{2,1,0:T(8,128)(2,1)} %copy-done.3) | copy-start | bytes 983044
  31.9 3.7 %copy-start.2 = (bf16[640,512]{1,0:T(8,128)(2,1)S(1)}, bf16[640,512]{1,0:T(8,128)(2,1)}, u32[]{:S(2)}) copy-start(bf16[640,512]{1,0:T(8,128)(2,1)} %copy-done.1) | copy-start | bytes 1966084
  31.9 3.7 %copy-start.7 = (bf16[128,256]{1,0:T(8,128)(2,1)S(1)}, bf16[128,256]{1,0:T(8,128)(2,1)}, u32[]{:S(2)}) copy-start(bf16[128,256]{1,0:T(8,128)(2,1)} %copy-done.6) | copy-start | bytes 196612
  31.9 18.3 %all-to-all-start.1 = ((bf16[4,2,128,512]{3,2,1,0:T(8,128)(2,1)}), bf16[4,2,128,512]{3,2,1,0:T(8,128)(2,1)S(1)}, u32[]{:S(2)}, u32[]{:S(2)}) async-start(bf16[4,2,128,512]{3,2,1,0:T(8,128)(2,1)} %get-tuple-element.35), calls=%async_computation.1 | async-start | bytes 2097152 | tf_op jit(solution)/shard_map/all_to_all | solution.py:303
  41.3 15.3 %collective-permute-start.1 = (bf16[2,128,512]{2,1,0:T(8,128)(2,1)S(1)}, bf16[2,128,512]{2,1,0:T(8,128)(2,1)S(1)}, u32[]{:S(2)}, u32[]{:S(2)}) collective-permute-start(bf16[2,128,512]{2,1,0:T(8,128)(2,1)S(1)} %get-tuple-element.34), channel_id=1, source_target_pairs={{0,16},{16,32},{32,48},{48,64},{64,80},{80,96},{96,112},{112,128},... | collective-permute-start | bytes 786440 | tf_op jit(solution)/shard_map/ppermute | solution.py:238

commit v7 on v6

--- a/solution.py
+++ b/solution.py
@@ -54,10 +54,12 @@
         c.wait()
 
 
-def spread_kernel(mg_ref, after_ref, all_ref, sems):
-    copies = [
-        pltpu.make_async_copy(mg_ref, all_ref.at[b], sems.at[b]) for b in range(all_ref.shape[0])
-    ]
+def spread_kernel(row_ref, mine_ref, yours_ref, after_ref, all_ref, sems):
+    row = row_ref[0]
+    copies = []
+    for c in range(all_ref.shape[0]):
+        copies.append(pltpu.make_async_copy(mine_ref, all_ref.at[c, row], sems.at[2 * c]))
+        copies.append(pltpu.make_async_copy(yours_ref, all_ref.at[c, 1 - row], sems.at[2 * c + 1]))
     for c in copies:
         c.start()
     for c in copies:
@@ -140,10 +142,11 @@
 
 
 def cotangent_kernel(mg_ref, w_ref, ga_ref):
-    span = mg_ref.shape[2]
+    cols, span = mg_ref.shape[0], mg_ref.shape[3]
     total = jnp.zeros(ga_ref.shape, F32)
-    for b in range(mg_ref.shape[0]):
-        total = total + dot(mg_ref[b], w_ref[:, b * span : (b + 1) * span], ((1,), (1,)))
+    for b in range(2 * cols):
+        block = mg_ref[b % cols, b // cols]
+        total = total + dot(block, w_ref[:, b * span : (b + 1) * span], ((1,), (1,)))
     ga_ref[...] = total.astype(BF)
 
 
@@ -213,8 +216,8 @@
     dv_ref[...] = total[:, w:].astype(BF)
 
 
-def row_sum_kernel(where_ref, x_ref, keep_ref, give_ref):
-    row = where_ref[1]
+def row_sum_kernel(row_ref, x_ref, keep_ref, give_ref):
+    row = row_ref[0]
     cols = x_ref.shape[0]
 
     def total(r):
@@ -227,8 +230,8 @@
     give_ref[...] = total(1 - row).astype(BF)
 
 
-def mixed_kernel(where_ref, keep_ref, got_ref, o_ref):
-    o_ref[...] = (keep_ref[...] + got_ref[1 - where_ref[1]].astype(F32)).astype(BF)
+def mixed_kernel(keep_ref, got_ref, o_ref):
+    o_ref[...] = (keep_ref[...] + got_ref[...].astype(F32)).astype(BF)
 
 
 def to_neighbours(x):
@@ -251,8 +254,9 @@
     total = rows * lax.axis_size("ctx")
     cols = groups // 2
     along_row = [[r * cols + c for c in range(cols)] for r in range(2)]
-    across_rows = [[c, cols + c] for c in range(cols)]
-    where = jnp.stack([lax.axis_index("ctx"), lax.axis_index("head") // cols]).astype(jnp.int32)
+    where = lax.axis_index("ctx").astype(jnp.int32).reshape(1)
+    row = (lax.axis_index("head").astype(jnp.int32) // cols).reshape(1)
+    other_row = [(i, (i + cols) % groups) for i in range(groups)]
     lens = lengths.reshape(1, -1)
 
     kv, mgv = call(
@@ -263,17 +267,18 @@
         scratch=[pltpu.SemaphoreType.DMA((3,))],
         hbm_in=(0, 1, 2),
     )
-    own2 = in_chip(kv)
+    mg_other = lax.ppermute(mixed_grad, "head", other_row)
+    own2, mg_other = lax.optimization_barrier((in_chip(kv), mg_other))
     near = to_neighbours(own2)
     (spread,) = call(
         spread_kernel,
-        [shape((groups, rows, span), BF)],
-        [mgv, own2],
+        [shape((cols, 2, rows, span), BF)],
+        [row, mgv, mg_other, own2],
         "spread",
         scratch=[pltpu.SemaphoreType.DMA((groups,))],
         hbm_out=(0,),
     )
-    gathered = lax.all_to_all(spread, "head", 0, 0, tiled=True)
+    gathered = lax.all_to_all(spread, "head", 0, 0, tiled=True, axis_index_groups=along_row)
     far = in_chip(near)
     part, probs, attn, window = call(
         functools.partial(forward_kernel, heads, total),
@@ -328,16 +333,15 @@
     mine, yours = call(
         row_sum_kernel,
         [shape((rows, span), F32), shape((rows, span), BF)],
-        [where, summed],
+        [row, summed],
         "rowsum",
     )
-    both = lax.all_gather(yours, "head", axis=0, axis_index_groups=across_rows)
-    (mixed,) = call(mixed_kernel, [shape((rows, span), BF)], [where, mine, both], "mixed")
-    arrived, mixed = lax.optimization_barrier((to_neighbours(send), mixed))
+    yours = lax.ppermute(yours, "head", other_row)
+    (mixed,) = call(mixed_kernel, [shape((rows, span), BF)], [mine, yours], "mixed")
     dk, dv = call(
         finish_kernel,
         [shape((rows, width), BF), shape((rows, width), BF)],
-        [where, own, in_chip(arrived)],
+        [where, own, in_chip(to_neighbours(send))],
         "finish",
     )
     return mixed, dq, dk, dv

time: 62.5 us -> 62 us (level)
  the two profiles are of different devices: /device:TPU:17 before, /device:TPU:389 now
where the time goes in v7:
time: 62 us; the launch traced here: 61.5 us
  starting transfers between devices  24.9 us (40%)
  blocking collectives  15.7 us (25%)
  Pallas kernels  9.28 us (15%)
  waiting for transfers between devices  8.55 us (14%)
  local copies, waits for them, and re-layouts  2.24 us (4%)
  between operations  0.81 us (1%)
    all_gather x4, blocking collectives, in_chip(): return lax.all_gather(x, 'ctx', axis=0, axis_index_groups=pairs)  15.7 us
    ppermute x2, starting transfers between devices, to_neighbours(): return lax.ppermute(x, 'ctx', ahead + back)  9.32 us
    pallas_call x9, Pallas kernels, call(): pl.pallas_call(body, out_shape=[pltpu.HBM(x.shape, x.dtype) if i in hbm_o...  9.28 us
    all_to_all x1, starting transfers between devices, per_device(): lax.all_to_all(part, 'head', 0, 0, tiled=True, axis_index_groups=along_row)  6.23 us
    ppermute x2, waiting for transfers between devices, to_neighbours(): return lax.ppermute(x, 'ctx', ahead + back)  4.36 us
    all_to_all x1, starting transfers between devices, per_device(): lax.all_to_all(spread, 'head', 0, 0, tiled=True, axis_index_groups=along_...  4.25 us
    ppermute x1, starting transfers between devices, per_device(): mg_other = lax.ppermute(mixed_grad, 'head', other_row)  3.2 us
    all_to_all x1, waiting for transfers between devices, per_device(): lax.all_to_all(spread, 'head', 0, 0, tiled=True, axis_index_groups=along_...  2.51 us
  transfers between devices with their start and end apart: 6, of which 4 were waited for; matrix products, arithmetic and copies ran while one was open for 0% of the time, Pallas kernels for 13%

profile of v7, /device:TPU:389, one launch (start us, length us, event | category | flops | bytes accessed | tf_op | source)
XLA Modules:
  0.0 61.5 jit_solution(8767786740985054130)
XLA Ops:
  0.6 3.2 %collective-permute-start = (bf16[128,512]{1,0:T(8,128)(2,1)}, bf16[128,512]{1,0:T(8,128)(2,1)S(1)}, u32[]{:S(2)}, u32[]{:S(2)}) collective-permute-start(bf16[128,512]{1,0:T(8,128)(2,1)} %mg_ref.1), channel_id=1, source_target_pairs={{0,4},{1,5},{2,6},{3,7},{4,0},{5,1},{6,2},{7,3},{8,12},{9,13},{10,... | collective-permute-start | bytes 393224 | tf_op jit(solution)/shard_map/ppermute | solution.py:270
  3.8 1.0 %pack.1 = (bf16[128,512]{1,0:T(8,128)(2,1)S(1)}, bf16[128,512]{1,0:T(8,128)(2,1)S(1)}) custom-call(bf16[128,256]{1,0:T(8,128)(2,1)} %k_ref.1, bf16[128,256]{1,0:T(8,128)(2,1)} %v_ref.1, bf16[128,512]{1,0:T(8,128)(2,1)} %mg_ref.1), custom_call_target="tpu_custom_call" | custom-call | bytes 524288 | tf_op jit(solution)/shard_map/pack/pallas_call | solution.py:28
  4.8 2.6 %all-gather = bf16[256,512]{1,0:T(8,128)(2,1)S(1)} all-gather(bf16[128,512]{1,0:T(8,128)(2,1)S(1)} %get-tuple-element.25), channel_id=2, replica_groups={{0,8},{16,24},{32,40},{48,56},{64,72},{80,88},{96,104},{112,120},{128,1..., dimensions={0}, use_global_device_ids=true | all-gather | bytes 393216 | tf_op jit(solution)/shard_map/all_gather | solution.py:246
  7.4 0.0 collective-permute-done.yours_ref
  7.4 5.6 %collective-permute-start.1 = (bf16[2,128,512]{2,1,0:T(8,128)(2,1)S(1)}, bf16[2,128,512]{2,1,0:T(8,128)(2,1)}, u32[]{:S(2)}, u32[]{:S(2)}) collective-permute-start(bf16[2,128,512]{2,1,0:T(8,128)(2,1)S(1)} %bitcast.9), channel_id=1, source_target_pairs={{0,16},{16,32},{32,48},{48,64},{64,80},{80,96},{96,112},{112,128},... | collective-permute-start | bytes 786440 | tf_op jit(solution)/shard_map/ppermute | solution.py:241
  13.0 0.0 copy-start
  13.0 0.0 copy-start.5
  13.0 0.0 copy-start.8
  13.0 0.0 copy-start.9
  13.0 1.0 %spread.1 = bf16[4,2,128,512]{3,2,1,0:T(8,128)(2,1)} custom-call(s32[1]{0:T(128)} %bitcast.row_ref, bf16[128,512]{1,0:T(8,128)(2,1)S(1)} %get-tuple-element.24.mine_ref, bf16[128,512]{1,0:T(8,128)(2,1)S(1)} %collective-permute-done.yours_ref, bf16[2,128,512]{2,1,0:T(8,128)(2,1)S(1)} %bitcast.10), custom_call_target="tpu_custom_call" | custom-call | bytes 1572868 | tf_op jit(solution)/shard_map/spread/pallas_call | solution.py:28
  14.1 4.2 %all-to-all-start = ((bf16[4,2,128,512]{3,2,1,0:T(8,128)(2,1)}), bf16[4,2,128,512]{3,2,1,0:T(8,128)(2,1)S(1)}, u32[]{:S(2)}, u32[]{:S(2)}) async-start(bf16[4,2,128,512]{3,2,1,0:T(8,128)(2,1)} %spread.1), calls=%async_computation | async-start | bytes 2097152 | tf_op jit(solution)/shard_map/all_to_all | solution.py:281
  18.3 0.7 %collective-permute-done.1 = bf16[2,128,512]{2,1,0:T(8,128)(2,1)} collective-permute-done((bf16[2,128,512]{2,1,0:T(8,128)(2,1)S(1)}, bf16[2,128,512]{2,1,0:T(8,128)(2,1)}, u32[]{:S(2)}, u32[]{:S(2)}) %collective-permute-start.1) | collective-permute-done | bytes 262176 | tf_op jit(solution)/shard_map/ppermute | solution.py:241
  19.1 3.8 %all-gather.1 = bf16[4,128,512]{2,1,0:T(8,128)(2,1)S(1)} all-gather(bf16[2,128,512]{2,1,0:T(8,128)(2,1)} %collective-permute-done.1), channel_id=3, replica_groups={{0,8},{16,24},{32,40},{48,56},{64,72},{80,88},{96,104},{112,120},{128,1..., dimensions={0}, use_global_device_ids=true | all-gather | bytes 786432 | tf_op jit(solution)/shard_map/all_gather | solution.py:246
  22.9 0.0 copy-done
  22.9 0.0 copy-done.5
  22.9 0.0 copy-done.8
  22.9 0.0 copy-done.9
  22.9 2.8 %forward.1 = (bf16[4,2,128,512]{3,2,1,0:T(8,128)(2,1)}, bf16[2,128,640]{2,1,0:T(8,128)(2,1)S(1)}, bf16[128,256]{1,0:T(8,128)(2,1)S(1)}, bf16[640,512]{1,0:T(8,128)(2,1)S(1)}) custom-call(s32[1]{0:T(128)} %bitcast.2.where_ref, s32[2]{0:T(128)S(1)} %copy-done.8, s32[1,64]{1,0:T(1,128)S(1)} %bitcast.13, bf16[128,256]{1,0:T(8,128)(2,1)S(1)} %copy-done.5, ...), custom_call_target="tpu_custom_call" | custom-call | flops 28185722880 | bytes 5046540 | tf_op jit(solution)/shard_map/forward/pallas_call | solution.py:28
  25.8 0.0 copy-start.1
  25.8 0.8 %copy-done.1 = bf16[640,512]{1,0:T(8,128)(2,1)} copy-done((bf16[640,512]{1,0:T(8,128)(2,1)}, bf16[640,512]{1,0:T(8,128)(2,1)S(1)}, u32[]{:S(2)}) %copy-start.1) | copy-done | bytes 655384
  26.6 0.0 copy-start.3
  26.6 0.7 %copy-done.3 = bf16[2,128,640]{2,1,0:T(8,128)(2,1)} copy-done((bf16[2,128,640]{2,1,0:T(8,128)(2,1)}, bf16[2,128,640]{2,1,0:T(8,128)(2,1)S(1)}, u32[]{:S(2)}) %copy-start.3) | copy-done | bytes 327704
  27.3 0.0 copy-start.6
  27.3 0.6 %copy-done.6 = bf16[128,256]{1,0:T(8,128)(2,1)} copy-done((bf16[128,256]{1,0:T(8,128)(2,1)}, bf16[128,256]{1,0:T(8,128)(2,1)S(1)}, u32[]{:S(2)}) %copy-start.6) | copy-done | bytes 65560
  28.0 2.5 %all-to-all-done.mg_ref = bf16[4,2,128,512]{3,2,1,0:T(8,128)(2,1)S(1)} async-done(((bf16[4,2,128,512]{3,2,1,0:T(8,128)(2,1)}), bf16[4,2,128,512]{3,2,1,0:T(8,128)(2,1)S(1)}, u32[]{:S(2)}, u32[]{:S(2)}) %all-to-all-start) | async-done | bytes 1048608 | tf_op jit(solution)/shard_map/all_to_all | solution.py:281
  30.5 0.0 copy-start.4
  30.5 0.8 %cotangent.1.ga_ref = bf16[128,256]{1,0:T(8,128)(2,1)S(1)} custom-call(bf16[4,2,128,512]{3,2,1,0:T(8,128)(2,1)S(1)} %all-to-all-done.mg_ref, bf16[256,4096]{1,0:T(8,128)(2,1)S(1)} %copy-done), custom_call_target="tpu_custom_call" | custom-call | flops 268435456 | bytes 3211264 | tf_op jit(solution)/shard_map/cotangent/pallas_call | solution.py:28
  31.3 0.0 copy-start.2
  31.3 0.0 copy-start.7
  31.3 6.2 %all-to-all-start.1 = ((bf16[4,2,128,512]{3,2,1,0:T(8,128)(2,1)}), bf16[4,2,128,512]{3,2,1,0:T(8,128)(2,1)S(1)}, u32[]{:S(2)}, u32[]{:S(2)}) async-start(bf16[4,2,128,512]{3,2,1,0:T(8,128)(2,1)} %get-tuple-element.29), calls=%async_computation.1 | async-start | bytes 2097152 | tf_op jit(solution)/shard_map/all_to_all | solution.py:308
  37.6 0.0 copy-done.4
  37.6 0.0 copy-done.2
  37.6 0.0 copy-done.7
  37.6 2.1 %backward.1 = (bf16[128,256]{1,0:T(8,128)(2,1)}, f32[128,512]{1,0:T(8,128)S(1)}, bf16[128,512]{1,0:T(8,128)(2,1)S(1)}, bf16[3,128,512]{2,1,0:T(8,128)(2,1)S(1)}) custom-call(s32[1]{0:T(128)} %bitcast.2.where_ref, bf16[128,256]{1,0:T(8,128)(2,1)} %q_hbm.1, bf16[640,512]{1,0:T(8,128)(2,1)S(1)} %copy-done.2, bf16[2,128,640]{2,1,0:T(8,128)(2,1)S(1)} %copy-done.4, ...), custom_call_target="tpu_custom_call" | custom-call | flops 167772160 | bytes 2031620 | tf_op jit(solution)/shard_map/backward/pallas_call | solution.py:28
  39.7 3.6 %all-gather.2 = bf16[6,128,512]{2,1,0:T(8,128)(2,1)S(1)} all-gather(bf16[3,128,512]{2,1,0:T(8,128)(2,1)S(1)} %get-tuple-element.39), channel_id=4, replica_groups={{0,8},{16,24},{32,40},{48,56},{64,72},{80,88},{96,104},{112,120},{128,1..., dimensions={0}, use_global_device_ids=true | all-gather | bytes 1179648 | tf_op jit(solution)/shard_map/all_gather | solution.py:246
  43.3 0.1 share.1
  43.3 3.8 %collective-permute-start.3 = (bf16[2,128,512]{2,1,0:T(8,128)(2,1)S(1)}, bf16[2,128,512]{2,1,0:T(8,128)(2,1)S(1)}, u32[]{:S(2)}, u32[]{:S(2)}) collective-permute-start(bf16[2,128,512]{2,1,0:T(8,128)(2,1)S(1)} %get-tuple-element.41), channel_id=1, source_target_pairs={{0,16},{16,32},{32,48},{48,64},{64,80},{80,96},{96,112},{112,128},... | collective-permute-start | bytes 786440 | tf_op jit(solution)/shard_map/ppermute | solution.py:241
  47.1 1.7 %all-to-all-done.1.x_ref = bf16[4,2,128,512]{3,2,1,0:T(8,128)(2,1)S(1)} async-done(((bf16[4,2,128,512]{3,2,1,0:T(8,128)(2,1)}), bf16[4,2,128,512]{3,2,1,0:T(8,128)(2,1)S(1)}, u32[]{:S(2)}, u32[]{:S(2)}) %all-to-all-start.1) | async-done | bytes 1048608 | tf_op jit(solution)/shard_map/all_to_all | solution.py:308
  48.8 0.1 rowsum.1
  48.9 1.9 %collective-permute-start.2 = (bf16[128,512]{1,0:T(8,128)(2,1)S(1)}, bf16[128,512]{1,0:T(8,128)(2,1)S(1)}, u32[]{:S(2)}, u32[]{:S(2)}) collective-permute-start(bf16[128,512]{1,0:T(8,128)(2,1)S(1)} %get-tuple-element.31), channel_id=1, source_target_pairs={{0,4},{1,5},{2,6},{3,7},{4,0},{5,1},{6,2},{7,3},{8,12},{9,13},{10,... | collective-permute-start | bytes 393224 | tf_op jit(solution)/shard_map/ppermute | solution.py:339
  50.8 3.6 %collective-permute-done.3 = bf16[2,128,512]{2,1,0:T(8,128)(2,1)S(1)} collective-permute-done((bf16[2,128,512]{2,1,0:T(8,128)(2,1)S(1)}, bf16[2,128,512]{2,1,0:T(8,128)(2,1)S(1)}, u32[]{:S(2)}, u32[]{:S(2)}) %collective-permute-start.3) | collective-permute-done | bytes 262176 | tf_op jit(solution)/shard_map/ppermute | solution.py:241
  54.4 5.7 %all-gather.3 = bf16[4,128,512]{2,1,0:T(8,128)(2,1)S(1)} all-gather(bf16[2,128,512]{2,1,0:T(8,128)(2,1)S(1)} %collective-permute-done.3), channel_id=5, replica_groups={{0,8},{16,24},{32,40},{48,56},{64,72},{80,88},{96,104},{112,120},{128,1..., dimensions={0}, use_global_device_ids=true | all-gather | bytes 786432 | tf_op jit(solution)/shard_map/all_gather | solution.py:246
  60.2 0.7 %finish.1 = (bf16[128,256]{1,0:T(8,128)(2,1)}, bf16[128,256]{1,0:T(8,128)(2,1)}) custom-call(s32[1]{0:T(128)} %bitcast.2.where_ref, f32[128,512]{1,0:T(8,128)S(1)} %get-tuple-element.40.own_ref, bf16[2,2,128,512]{3,2,1,0:T(8,128)(2,1)S(1)} %bitcast.8), custom_call_target="tpu_custom_call" | custom-call | bytes 917508 | tf_op jit(solution)/shard_map/finish/pallas_call | solution.py:28
  60.9 0.0 collective-permute-done.2.got_ref
  60.9 0.7 %mixed.1 = bf16[128,512]{1,0:T(8,128)(2,1)} custom-call(f32[128,512]{1,0:T(8,128)S(1)} %get-tuple-element.30.keep_ref, bf16[128,512]{1,0:T(8,128)(2,1)S(1)} %collective-permute-done.2.got_ref), custom_call_target="tpu_custom_call" | custom-call | bytes 524288 | tf_op jit(solution)/shard_map/mixed/pallas_call | solution.py:28
Async XLA Ops:
  0.6 6.8 %collective-permute-start = (bf16[128,512]{1,0:T(8,128)(2,1)}, bf16[128,512]{1,0:T(8,128)(2,1)S(1)}, u32[]{:S(2)}, u32[]{:S(2)}) collective-permute-start(bf16[128,512]{1,0:T(8,128)(2,1)} %mg_ref.1), channel_id=1, source_target_pairs={{0,4},{1,5},{2,6},{3,7},{4,0},{5,1},{6,2},{7,3},{8,12},{9,13},{10,... | collective-permute-start | bytes 393224 | tf_op jit(solution)/shard_map/ppermute | solution.py:270
  7.4 11.7 %collective-permute-start.1 = (bf16[2,128,512]{2,1,0:T(8,128)(2,1)S(1)}, bf16[2,128,512]{2,1,0:T(8,128)(2,1)}, u32[]{:S(2)}, u32[]{:S(2)}) collective-permute-start(bf16[2,128,512]{2,1,0:T(8,128)(2,1)S(1)} %bitcast.9), channel_id=1, source_target_pairs={{0,16},{16,32},{32,48},{48,64},{64,80},{80,96},{96,112},{112,128},... | collective-permute-start | bytes 786440 | tf_op jit(solution)/shard_map/ppermute | solution.py:241
  13.0 9.9 %copy-start = (bf16[256,4096]{1,0:T(8,128)(2,1)S(1)}, bf16[256,4096]{1,0:T(8,128)(2,1)}, u32[]{:S(2)}) copy-start(bf16[256,4096]{1,0:T(8,128)(2,1)} %w_ref.3) | copy-start | bytes 6291460
  13.0 9.9 %copy-start.5 = (bf16[128,256]{1,0:T(8,128)(2,1)S(1)}, bf16[128,256]{1,0:T(8,128)(2,1)}, u32[]{:S(2)}) copy-start(bf16[128,256]{1,0:T(8,128)(2,1)} %q_hbm.1) | copy-start | bytes 196612
  13.0 9.9 %copy-start.8 = (s32[2]{0:T(128)S(1)}, s32[2]{0:T(128)}, u32[]{:S(2)}) copy-start(s32[2]{0:T(128)} %dil_ref.1) | copy-start | bytes 28
  13.0 9.9 %copy-start.9 = (s32[64]{0:T(128)S(1)}, s32[64]{0:T(128)}, u32[]{:S(2)}) copy-start(s32[64]{0:T(128)} %param.12) | copy-start | bytes 772
  14.1 16.4 %all-to-all-start = ((bf16[4,2,128,512]{3,2,1,0:T(8,128)(2,1)}), bf16[4,2,128,512]{3,2,1,0:T(8,128)(2,1)S(1)}, u32[]{:S(2)}, u32[]{:S(2)}) async-start(bf16[4,2,128,512]{3,2,1,0:T(8,128)(2,1)} %spread.1), calls=%async_computation | async-start | bytes 2097152 | tf_op jit(solution)/shard_map/all_to_all | solution.py:281
  25.8 0.9 %copy-start.1 = (bf16[640,512]{1,0:T(8,128)(2,1)}, bf16[640,512]{1,0:T(8,128)(2,1)S(1)}, u32[]{:S(2)}) copy-start(bf16[640,512]{1,0:T(8,128)(2,1)S(1)} %get-tuple-element.32.win_ref) | copy-start | bytes 1966084
  26.6 0.7 %copy-start.3 = (bf16[2,128,640]{2,1,0:T(8,128)(2,1)}, bf16[2,128,640]{2,1,0:T(8,128)(2,1)S(1)}, u32[]{:S(2)}) copy-start(bf16[2,128,640]{2,1,0:T(8,128)(2,1)S(1)} %get-tuple-element.33.probs_ref) | copy-start | bytes 983044
  27.3 0.6 %copy-start.6 = (bf16[128,256]{1,0:T(8,128)(2,1)}, bf16[128,256]{1,0:T(8,128)(2,1)S(1)}, u32[]{:S(2)}) copy-start(bf16[128,256]{1,0:T(8,128)(2,1)S(1)} %get-tuple-element.34.attn_ref) | copy-start | bytes 196612
  30.5 7.1 %copy-start.4 = (bf16[2,128,640]{2,1,0:T(8,128)(2,1)S(1)}, bf16[2,128,640]{2,1,0:T(8,128)(2,1)}, u32[]{:S(2)}) copy-start(bf16[2,128,640]{2,1,0:T(8,128)(2,1)} %copy-done.3) | copy-start | bytes 983044
  31.3 6.3 %copy-start.2 = (bf16[640,512]{1,0:T(8,128)(2,1)S(1)}, bf16[640,512]{1,0:T(8,128)(2,1)}, u32[]{:S(2)}) copy-start(bf16[640,512]{1,0:T(8,128)(2,1)} %copy-done.1) | copy-start | bytes 1966084
  31.3 6.3 %copy-start.7 = (bf16[128,256]{1,0:T(8,128)(2,1)S(1)}, bf16[128,256]{1,0:T(8,128)(2,1)}, u32[]{:S(2)}) copy-start(bf16[128,256]{1,0:T(8,128)(2,1)} %copy-done.6) | copy-start | bytes 196612
  31.3 17.4 %all-to-all-start.1 = ((bf16[4,2,128,512]{3,2,1,0:T(8,128)(2,1)}), bf16[4,2,128,512]{3,2,1,0:T(8,128)(2,1)S(1)}, u32[]{:S(2)}, u32[]{:S(2)}) async-start(bf16[4,2,128,512]{3,2,1,0:T(8,128)(2,1)} %get-tuple-element.29), calls=%async_computation.1 | async-start | bytes 2097152 | tf_op jit(solution)/shard_map/all_to_all | solution.py:308
  43.3 11.1 %collective-permute-start.3 = (bf16[2,128,512]{2,1,0:T(8,128)(2,1)S(1)}, bf16[2,128,512]{2,1,0:T(8,128)(2,1)S(1)}, u32[]{:S(2)}, u32[]{:S(2)}) collective-permute-start(bf16[2,128,512]{2,1,0:T(8,128)(2,1)S(1)} %get-tuple-element.41), channel_id=1, source_target_pairs={{0,16},{16,32},{32,48},{48,64},{64,80},{80,96},{96,112},{112,128},... | collective-permute-start | bytes 786440 | tf_op jit(solution)/shard_map/ppermute | solution.py:241
  48.9 12.0 %collective-permute-start.2 = (bf16[128,512]{1,0:T(8,128)(2,1)S(1)}, bf16[128,512]{1,0:T(8,128)(2,1)S(1)}, u32[]{:S(2)}, u32[]{:S(2)}) collective-permute-start(bf16[128,512]{1,0:T(8,128)(2,1)S(1)} %get-tuple-element.31), channel_id=1, source_target_pairs={{0,4},{1,5},{2,6},{3,7},{4,0},{5,1},{6,2},{7,3},{8,12},{9,13},{10,... | collective-permute-start | bytes 393224 | tf_op jit(solution)/shard_map/ppermute | solution.py:339

commit v8 on v5

--- a/solution.py
+++ b/solution.py
@@ -54,7 +54,7 @@
         c.wait()
 
 
-def spread_kernel(mg_ref, all_ref, sems):
+def spread_kernel(mg_ref, after_ref, all_ref, sems):
     copies = [
         pltpu.make_async_copy(mg_ref, all_ref.at[b], sems.at[b]) for b in range(all_ref.shape[0])
     ]
@@ -78,8 +78,8 @@
 
 
 def forward_kernel(
-    heads, total, where_ref, dil_ref, lens_ref, q_ref, prev_ref, own_ref, next_ref, w_ref,
-    part_ref, probs_ref, attn_ref, win_ref, hold_ref, sems,
+    heads, total, where_ref, row_ref, dil_ref, lens_ref, q_ref, own_ref, far_ref, w_ref,
+    keep_ref, give_ref, probs_ref, attn_ref, win_ref,
 ):
     rows = q_ref.shape[0]
     width = q_ref.shape[1]
@@ -87,7 +87,7 @@
     keys = win_ref.shape[0]
     slab = where_ref[0]
     core = lax.rem(slab, 2)
-    six = [x.at[i] for x in (prev_ref, own_ref, next_ref) for i in range(2)]
+    six = [x.at[i] for x in (far_ref.at[0], own_ref, far_ref.at[1]) for i in range(2)]
 
     @pl.when(core == 0)
     def _():
@@ -127,14 +127,12 @@
         probs_ref[h] = probs
         attn_ref[:, h * hd : (h + 1) * hd] = dot(probs, v, ((1,), (0,))).astype(BF)
     attn = attn_ref[...]
-    span = part_ref.shape[2]
-    copies = []
-    for b in range(part_ref.shape[0]):
-        hold_ref[b] = dot(attn, w_ref[:, b * span : (b + 1) * span], ((1,), (0,))).astype(BF)
-        copies.append(pltpu.make_async_copy(hold_ref.at[b], part_ref.at[b], sems.at[b]))
-        copies[-1].start()
-    for c in copies:
-        c.wait()
+    cols, span = keep_ref.shape[0], keep_ref.shape[2]
+    row = row_ref[0]
+    for r, half_ref in ((1 - row, give_ref), (row, keep_ref)):
+        for c in range(cols):
+            block = pl.ds(pl.multiple_of((r * cols + c) * span, span), span)
+            half_ref[c] = dot(attn, w_ref[:, block], ((1,), (0,))).astype(BF)
 
 
 def cotangent_kernel(mg_ref, w_ref, ga_ref):
@@ -211,17 +209,21 @@
     dv_ref[...] = total[:, w:].astype(BF)
 
 
+def rows_kernel(keep_ref, got_ref, after_ref, out_ref, hold_ref, sems):
+    copies = []
+    for c in range(keep_ref.shape[0]):
+        hold_ref[c] = (keep_ref[c].astype(F32) + got_ref[c].astype(F32)).astype(BF)
+        copies.append(pltpu.make_async_copy(hold_ref.at[c], out_ref.at[c], sems.at[c]))
+        copies[-1].start()
+    for c in copies:
+        c.wait()
+
+
 def mixed_kernel(x_ref, o_ref):
     total = x_ref[0].astype(F32)
-    for b in range(1, x_ref.shape[0]):
-        total = total + x_ref[b].astype(F32)
+    for c in range(1, x_ref.shape[0]):
+        total = total + x_ref[c].astype(F32)
     o_ref[...] = total.astype(BF)
-
-
-def shifted(x, steps):
-    count = lax.axis_size("ctx")
-    first, last = max(0, -steps), min(count, count - steps)
-    return lax.ppermute(x, "ctx", [(i, i + steps) for i in range(first, last)])
 
 
 def to_neighbours(x):
@@ -242,7 +244,11 @@
     groups = lax.axis_size("head")
     span = mixed_grad.shape[1]
     total = rows * lax.axis_size("ctx")
+    cols = groups // 2
+    along_row = [[r * cols + c for c in range(cols)] for r in range(2)]
     where = lax.axis_index("ctx").astype(jnp.int32).reshape(1)
+    row = (lax.axis_index("head").astype(jnp.int32) // cols).reshape(1)
+    other_row = [(i, (i + cols) % groups) for i in range(groups)]
     lens = lengths.reshape(1, -1)
 
     kv, mgv = call(
@@ -253,35 +259,32 @@
         scratch=[pltpu.SemaphoreType.DMA((3,))],
         hbm_in=(0, 1, 2),
     )
-    prev = shifted(kv, 2)
-    follow = shifted(kv, -2)
+    own2 = in_chip(kv)
+    near = to_neighbours(own2)
     (spread,) = call(
         spread_kernel,
         [shape((groups, rows, span), BF)],
-        [mgv],
+        [mgv, own2],
         "spread",
         scratch=[pltpu.SemaphoreType.DMA((groups,))],
         hbm_out=(0,),
     )
     gathered = lax.all_to_all(spread, "head", 0, 0, tiled=True)
-    own2, prev2, next2 = in_chip(kv), in_chip(prev), in_chip(follow)
-    part, probs, attn, window = call(
+    far = in_chip(near)
+    keep, give, probs, attn, window = call(
         functools.partial(forward_kernel, heads, total),
         [
-            shape((groups, rows, span), BF),
+            shape((cols, rows, span), BF),
+            shape((cols, rows, span), BF),
             shape((heads, rows, 5 * rows), BF),
             shape((rows, width), BF),
             shape((5 * rows, 2 * width), BF),
         ],
-        [where, dilation, lens, queries, prev2, own2, next2, out_weight],
+        [where, row, dilation, lens, queries, own2, far, out_weight],
         "forward",
         flops=80 * 2 * rows * width * (groups * span + 10 * rows),
-        scratch=[
-            pltpu.VMEM((groups, rows, span), BF),
-            pltpu.SemaphoreType.DMA((groups,)),
-        ],
-        hbm_out=(0,),
-    )
+    )
+    got_half = lax.ppermute(give, "head", other_row)
     (ga,) = call(
         cotangent_kernel,
         [shape((rows, width), BF)],
@@ -289,9 +292,7 @@
         "cotangent",
         flops=2 * rows * width * groups * span,
     )
-    ga, part = lax.optimization_barrier((ga, part))
-    summed = lax.all_to_all(part, "head", 0, 0, tiled=True)
-    dq, own, passed, give = call(
+    dq, own, passed, terms = call(
         functools.partial(backward_kernel, heads),
         [
             shape((rows, width), BF),
@@ -312,15 +313,23 @@
     send, own = call(
         share_kernel,
         [shape((2, rows, 2 * width), BF), shape((rows, 2 * width), F32)],
-        [where, own, passed, in_chip(give)],
+        [where, own, passed, in_chip(terms)],
         "share",
     )
+    (half,) = call(
+        rows_kernel,
+        [shape((cols, rows, span), BF)],
+        [keep, got_half, send],
+        "rows",
+        scratch=[pltpu.VMEM((cols, rows, span), BF), pltpu.SemaphoreType.DMA((cols,))],
+        hbm_out=(0,),
+    )
+    summed = lax.all_to_all(half, "head", 0, 0, tiled=True, axis_index_groups=along_row)
     (mixed,) = call(mixed_kernel, [shape((rows, span), BF)], [summed], "mixed")
-    arrived, mixed = lax.optimization_barrier((to_neighbours(send), mixed))
     dk, dv = call(
         finish_kernel,
         [shape((rows, width), BF), shape((rows, width), BF)],
-        [where, own, in_chip(arrived)],
+        [where, own, in_chip(to_neighbours(send))],
         "finish",
     )
     return mixed, dq, dk, dv

time: 60.9 us -> 62.6 us (1.028)
  the two profiles are of different devices: /device:TPU:259 before, /device:TPU:256 now
where the time goes in v8:
time: 62.6 us; the launch traced here: 62.1 us
  starting transfers between devices  20.4 us (33%)
  waiting for transfers between devices  17.8 us (28%)
  Pallas kernels  11 us (18%)
  blocking collectives  8.91 us (14%)
  local copies, waits for them, and re-layouts  3.29 us (5%)
  between operations  0.8 us (1%)
    pallas_call x9, Pallas kernels, call(): pl.pallas_call(body, out_shape=[pltpu.HBM(x.shape, x.dtype) if i in hbm_o...  11 us
    all_gather x4, blocking collectives, in_chip(): return lax.all_gather(x, 'ctx', axis=0, axis_index_groups=pairs)  8.91 us
    ppermute x1, waiting for transfers between devices, per_device(): got_half = lax.ppermute(give, 'head', other_row)  8 us
    ppermute x2, starting transfers between devices, to_neighbours(): return lax.ppermute(x, 'ctx', ahead + back)  6.65 us
    all_to_all x1, waiting for transfers between devices, per_device(): lax.all_to_all(half, 'head', 0, 0, tiled=True, axis_index_groups=along_row)  5.94 us
    all_to_all x1, starting transfers between devices, per_device(): gathered = lax.all_to_all(spread, 'head', 0, 0, tiled=True)  5.32 us
    all_to_all x1, starting transfers between devices, per_device(): lax.all_to_all(half, 'head', 0, 0, tiled=True, axis_index_groups=along_row)  4.3 us
    ppermute x1, starting transfers between devices, per_device(): got_half = lax.ppermute(give, 'head', other_row)  4.12 us
  transfers between devices with their start and end apart: 5, of which 3 were waited for; matrix products, arithmetic and copies ran while one was open for 0% of the time, Pallas kernels for 15%

profile of v8, /device:TPU:256, one launch (start us, length us, event | category | flops | bytes accessed | tf_op | source)
XLA Modules:
  0.0 62.1 jit_solution(2184125608063747896)
XLA Ops:
  0.6 1.0 %pack.1 = (bf16[128,512]{1,0:T(8,128)(2,1)S(1)}, bf16[128,512]{1,0:T(8,128)(2,1)S(1)}) custom-call(bf16[128,256]{1,0:T(8,128)(2,1)} %k_ref.1, bf16[128,256]{1,0:T(8,128)(2,1)} %v_ref.1, bf16[128,512]{1,0:T(8,128)(2,1)} %mg_ref.1), custom_call_target="tpu_custom_call" | custom-call | bytes 524288 | tf_op jit(solution)/shard_map/pack/pallas_call | solution.py:28
  1.6 2.0 %all-gather = bf16[256,512]{1,0:T(8,128)(2,1)S(1)} all-gather(bf16[128,512]{1,0:T(8,128)(2,1)S(1)} %get-tuple-element.19), channel_id=2, replica_groups={{0,8},{16,24},{32,40},{48,56},{64,72},{80,88},{96,104},{112,120},{128,1..., dimensions={0}, use_global_device_ids=true | all-gather | bytes 393216 | tf_op jit(solution)/shard_map/all_gather | solution.py:238
  3.6 4.5 %collective-permute-start = (bf16[2,128,512]{2,1,0:T(8,128)(2,1)S(1)}, bf16[2,128,512]{2,1,0:T(8,128)(2,1)}, u32[]{:S(2)}, u32[]{:S(2)}) collective-permute-start(bf16[2,128,512]{2,1,0:T(8,128)(2,1)S(1)} %bitcast.9), channel_id=1, source_target_pairs={{0,16},{16,32},{32,48},{48,64},{64,80},{80,96},{96,112},{112,128},... | collective-permute-start | bytes 786440 | tf_op jit(solution)/shard_map/ppermute | solution.py:233
  8.1 0.0 copy-start
  8.1 0.0 copy-start.7
  8.1 0.0 copy-start.10
  8.1 0.0 copy-start.11
  8.1 1.1 %spread.1 = bf16[8,128,512]{2,1,0:T(8,128)(2,1)} custom-call(bf16[128,512]{1,0:T(8,128)(2,1)S(1)} %get-tuple-element.25.mg_ref, bf16[2,128,512]{2,1,0:T(8,128)(2,1)S(1)} %bitcast.10), custom_call_target="tpu_custom_call" | custom-call | bytes 1441792 | tf_op jit(solution)/shard_map/spread/pallas_call | solution.py:28
  9.2 5.3 %all-to-all-start = ((bf16[8,128,512]{2,1,0:T(8,128)(2,1)}), bf16[8,128,512]{2,1,0:T(8,128)(2,1)S(1)}, u32[]{:S(2)}, u32[]{:S(2)}) async-start(bf16[8,128,512]{2,1,0:T(8,128)(2,1)} %spread.1), calls=%async_computation | async-start | bytes 2097152 | tf_op jit(solution)/shard_map/all_to_all | solution.py:272
  14.5 3.8 %collective-permute-done = bf16[2,128,512]{2,1,0:T(8,128)(2,1)} collective-permute-done((bf16[2,128,512]{2,1,0:T(8,128)(2,1)S(1)}, bf16[2,128,512]{2,1,0:T(8,128)(2,1)}, u32[]{:S(2)}, u32[]{:S(2)}) %collective-permute-start) | collective-permute-done | bytes 262176 | tf_op jit(solution)/shard_map/ppermute | solution.py:233
  18.4 2.4 %all-gather.1 = bf16[4,128,512]{2,1,0:T(8,128)(2,1)S(1)} all-gather(bf16[2,128,512]{2,1,0:T(8,128)(2,1)} %collective-permute-done), channel_id=3, replica_groups={{0,8},{16,24},{32,40},{48,56},{64,72},{80,88},{96,104},{112,120},{128,1..., dimensions={0}, use_global_device_ids=true | all-gather | bytes 786432 | tf_op jit(solution)/shard_map/all_gather | solution.py:238
  20.7 0.0 copy-done
  20.7 0.0 copy-done.7
  20.7 0.0 copy-done.10
  20.8 0.0 copy-done.11
  20.8 2.6 %forward.1 = (bf16[4,128,512]{2,1,0:T(8,128)(2,1)S(1)}, bf16[4,128,512]{2,1,0:T(8,128)(2,1)}, bf16[2,128,640]{2,1,0:T(8,128)(2,1)S(1)}, bf16[128,256]{1,0:T(8,128)(2,1)S(1)}, bf16[640,512]{1,0:T(8,128)(2,1)S(1)}) custom-call(s32[1]{0:T(128)} %bitcast.where_ref, s32[1]{0:T(128)} %bitcast.1.row_ref, s32[2]{0:T(128)S(1)} %copy-done.10, s32[1,64]{1,0:T(1,128)S(1)} %bitcast.13, ...), custom_call_target="tpu_custom_call" | custom-call | flops 28185722880 | bytes 5046544 | tf_op jit(solution)/shard_map/forward/pallas_call | solution.py:28
  23.4 0.0 copy-start.1
  23.4 0.9 %copy-done.1 = bf16[640,512]{1,0:T(8,128)(2,1)} copy-done((bf16[640,512]{1,0:T(8,128)(2,1)}, bf16[640,512]{1,0:T(8,128)(2,1)S(1)}, u32[]{:S(2)}) %copy-start.1) | copy-done | bytes 655384
  24.3 0.0 copy-start.3
  24.3 0.8 %copy-done.3 = bf16[4,128,512]{2,1,0:T(8,128)(2,1)} copy-done((bf16[4,128,512]{2,1,0:T(8,128)(2,1)}, bf16[4,128,512]{2,1,0:T(8,128)(2,1)S(1)}, u32[]{:S(2)}) %copy-start.3) | copy-done | bytes 524312
  25.1 0.0 copy-start.5
  25.1 0.7 %copy-done.5 = bf16[2,128,640]{2,1,0:T(8,128)(2,1)} copy-done((bf16[2,128,640]{2,1,0:T(8,128)(2,1)}, bf16[2,128,640]{2,1,0:T(8,128)(2,1)S(1)}, u32[]{:S(2)}) %copy-start.5) | copy-done | bytes 327704
  25.8 0.0 copy-start.8
  25.8 0.6 %copy-done.8 = bf16[128,256]{1,0:T(8,128)(2,1)} copy-done((bf16[128,256]{1,0:T(8,128)(2,1)}, bf16[128,256]{1,0:T(8,128)(2,1)S(1)}, u32[]{:S(2)}) %copy-start.8) | copy-done | bytes 65560
  26.4 0.0 copy-start.6
  26.4 0.0 copy-start.9
  26.4 4.1 %collective-permute-start.1 = (bf16[4,128,512]{2,1,0:T(8,128)(2,1)}, bf16[4,128,512]{2,1,0:T(8,128)(2,1)}, u32[]{:S(2)}, u32[]{:S(2)}) collective-permute-start(bf16[4,128,512]{2,1,0:T(8,128)(2,1)} %get-tuple-element.21), channel_id=1, source_target_pairs={{0,4},{1,5},{2,6},{3,7},{4,0},{5,1},{6,2},{7,3},{8,12},{9,13},{10,... | collective-permute-start | bytes 1572872 | tf_op jit(solution)/shard_map/ppermute | solution.py:287
  30.6 0.0 all-to-all-done.mg_ref
  30.6 0.0 copy-start.2
  30.6 0.8 %cotangent.1.ga_ref = bf16[128,256]{1,0:T(8,128)(2,1)S(1)} custom-call(bf16[8,128,512]{2,1,0:T(8,128)(2,1)S(1)} %all-to-all-done.mg_ref, bf16[256,4096]{1,0:T(8,128)(2,1)S(1)} %copy-done), custom_call_target="tpu_custom_call" | custom-call | flops 268435456 | bytes 3211264 | tf_op jit(solution)/shard_map/cotangent/pallas_call | solution.py:28
  31.4 0.0 copy-start.4
  31.4 0.0 copy-done.6
  31.4 0.0 copy-done.9
  31.4 0.2 copy-done.2
  31.7 2.1 %backward.1 = (bf16[128,256]{1,0:T(8,128)(2,1)}, f32[128,512]{1,0:T(8,128)S(1)}, bf16[128,512]{1,0:T(8,128)(2,1)S(1)}, bf16[3,128,512]{2,1,0:T(8,128)(2,1)S(1)}) custom-call(s32[1]{0:T(128)} %bitcast.where_ref, bf16[128,256]{1,0:T(8,128)(2,1)} %q_hbm.1, bf16[640,512]{1,0:T(8,128)(2,1)S(1)} %copy-done.2, bf16[2,128,640]{2,1,0:T(8,128)(2,1)S(1)} %copy-done.6, ...), custom_call_target="tpu_custom_call" | custom-call | flops 167772160 | bytes 2031620 | tf_op jit(solution)/shard_map/backward/pallas_call | solution.py:28
  33.8 2.4 %all-gather.2 = bf16[6,128,512]{2,1,0:T(8,128)(2,1)S(1)} all-gather(bf16[3,128,512]{2,1,0:T(8,128)(2,1)S(1)} %get-tuple-element.28), channel_id=4, replica_groups={{0,8},{16,24},{32,40},{48,56},{64,72},{80,88},{96,104},{112,120},{128,1..., dimensions={0}, use_global_device_ids=true | all-gather | bytes 1179648 | tf_op jit(solution)/shard_map/all_gather | solution.py:238
  36.1 0.1 share.1
  36.2 2.2 %collective-permute-start.2 = (bf16[2,128,512]{2,1,0:T(8,128)(2,1)S(1)}, bf16[2,128,512]{2,1,0:T(8,128)(2,1)S(1)}, u32[]{:S(2)}, u32[]{:S(2)}) collective-permute-start(bf16[2,128,512]{2,1,0:T(8,128)(2,1)S(1)} %get-tuple-element.29.after_ref), channel_id=1, source_target_pairs={{0,16},{16,32},{32,48},{48,64},{64,80},{80,96},{96,112},{112,128},... | collective-permute-start | bytes 786440 | tf_op jit(solution)/shard_map/ppermute | solution.py:233
  38.4 8.0 %collective-permute-done.1.got_ref = bf16[4,128,512]{2,1,0:T(8,128)(2,1)} collective-permute-done((bf16[4,128,512]{2,1,0:T(8,128)(2,1)}, bf16[4,128,512]{2,1,0:T(8,128)(2,1)}, u32[]{:S(2)}, u32[]{:S(2)}) %collective-permute-start.1) | collective-permute-done | bytes 524320 | tf_op jit(solution)/shard_map/ppermute | solution.py:287
  46.4 0.0 copy-done.4
  46.4 1.9 %rows.1 = bf16[4,128,512]{2,1,0:T(8,128)(2,1)} custom-call(bf16[4,128,512]{2,1,0:T(8,128)(2,1)S(1)} %copy-done.4, bf16[4,128,512]{2,1,0:T(8,128)(2,1)} %collective-permute-done.1.got_ref, bf16[2,128,512]{2,1,0:T(8,128)(2,1)S(1)} %get-tuple-element.29.after_ref), custom_call_target="tpu_custom_call" | custom-call | bytes 1835008 | tf_op jit(solution)/shard_map/rows/pallas_call | solution.py:28
  48.3 4.3 %all-to-all-start.1 = ((bf16[4,128,512]{2,1,0:T(8,128)(2,1)}), bf16[4,128,512]{2,1,0:T(8,128)(2,1)S(1)}, u32[]{:S(2)}, u32[]{:S(2)}) async-start(bf16[4,128,512]{2,1,0:T(8,128)(2,1)} %rows.1), calls=%async_computation.1 | async-start | bytes 1048576 | tf_op jit(solution)/shard_map/all_to_all | solution.py:327
  52.6 0.0 collective-permute-done.2
  52.6 2.2 %all-gather.3 = bf16[4,128,512]{2,1,0:T(8,128)(2,1)S(1)} all-gather(bf16[2,128,512]{2,1,0:T(8,128)(2,1)S(1)} %collective-permute-done.2), channel_id=5, replica_groups={{0,8},{16,24},{32,40},{48,56},{64,72},{80,88},{96,104},{112,120},{128,1..., dimensions={0}, use_global_device_ids=true | all-gather | bytes 786432 | tf_op jit(solution)/shard_map/all_gather | solution.py:238
  54.8 0.7 %finish.1 = (bf16[128,256]{1,0:T(8,128)(2,1)}, bf16[128,256]{1,0:T(8,128)(2,1)}) custom-call(s32[1]{0:T(128)} %bitcast.where_ref, f32[128,512]{1,0:T(8,128)S(1)} %get-tuple-element.31.own_ref, bf16[2,2,128,512]{3,2,1,0:T(8,128)(2,1)S(1)} %bitcast.8), custom_call_target="tpu_custom_call" | custom-call | bytes 917508 | tf_op jit(solution)/shard_map/finish/pallas_call | solution.py:28
  55.5 5.9 %all-to-all-done.1.x_ref = bf16[4,128,512]{2,1,0:T(8,128)(2,1)S(1)} async-done(((bf16[4,128,512]{2,1,0:T(8,128)(2,1)}), bf16[4,128,512]{2,1,0:T(8,128)(2,1)S(1)}, u32[]{:S(2)}, u32[]{:S(2)}) %all-to-all-start.1) | async-done | bytes 524320 | tf_op jit(solution)/shard_map/all_to_all | solution.py:327
  61.4 0.7 %mixed.1 = bf16[128,512]{1,0:T(8,128)(2,1)} custom-call(bf16[4,128,512]{2,1,0:T(8,128)(2,1)S(1)} %all-to-all-done.1.x_ref), custom_call_target="tpu_custom_call" | custom-call | bytes 655360 | tf_op jit(solution)/shard_map/mixed/pallas_call | solution.py:28
Async XLA Ops:
  3.6 14.8 %collective-permute-start = (bf16[2,128,512]{2,1,0:T(8,128)(2,1)S(1)}, bf16[2,128,512]{2,1,0:T(8,128)(2,1)}, u32[]{:S(2)}, u32[]{:S(2)}) collective-permute-start(bf16[2,128,512]{2,1,0:T(8,128)(2,1)S(1)} %bitcast.9), channel_id=1, source_target_pairs={{0,16},{16,32},{32,48},{48,64},{64,80},{80,96},{96,112},{112,128},... | collective-permute-start | bytes 786440 | tf_op jit(solution)/shard_map/ppermute | solution.py:233
  8.1 12.7 %copy-start = (bf16[256,4096]{1,0:T(8,128)(2,1)S(1)}, bf16[256,4096]{1,0:T(8,128)(2,1)}, u32[]{:S(2)}) copy-start(bf16[256,4096]{1,0:T(8,128)(2,1)} %w_ref.3) | copy-start | bytes 6291460
  8.1 12.6 %copy-start.7 = (bf16[128,256]{1,0:T(8,128)(2,1)S(1)}, bf16[128,256]{1,0:T(8,128)(2,1)}, u32[]{:S(2)}) copy-start(bf16[128,256]{1,0:T(8,128)(2,1)} %q_hbm.1) | copy-start | bytes 196612
  8.1 12.6 %copy-start.10 = (s32[2]{0:T(128)S(1)}, s32[2]{0:T(128)}, u32[]{:S(2)}) copy-start(s32[2]{0:T(128)} %dil_ref.1) | copy-start | bytes 28
  8.1 12.6 %copy-start.11 = (s32[64]{0:T(128)S(1)}, s32[64]{0:T(128)}, u32[]{:S(2)}) copy-start(s32[64]{0:T(128)} %param.12) | copy-start | bytes 772
  9.2 21.4 %all-to-all-start = ((bf16[8,128,512]{2,1,0:T(8,128)(2,1)}), bf16[8,128,512]{2,1,0:T(8,128)(2,1)S(1)}, u32[]{:S(2)}, u32[]{:S(2)}) async-start(bf16[8,128,512]{2,1,0:T(8,128)(2,1)} %spread.1), calls=%async_computation | async-start | bytes 2097152 | tf_op jit(solution)/shard_map/all_to_all | solution.py:272
  23.4 0.9 %copy-start.1 = (bf16[640,512]{1,0:T(8,128)(2,1)}, bf16[640,512]{1,0:T(8,128)(2,1)S(1)}, u32[]{:S(2)}) copy-start(bf16[640,512]{1,0:T(8,128)(2,1)S(1)} %get-tuple-element.22.win_ref) | copy-start | bytes 1966084
  24.3 0.8 %copy-start.3 = (bf16[4,128,512]{2,1,0:T(8,128)(2,1)}, bf16[4,128,512]{2,1,0:T(8,128)(2,1)S(1)}, u32[]{:S(2)}) copy-start(bf16[4,128,512]{2,1,0:T(8,128)(2,1)S(1)} %get-tuple-element.20.keep_ref) | copy-start | bytes 1572868
  25.1 0.7 %copy-start.5 = (bf16[2,128,640]{2,1,0:T(8,128)(2,1)}, bf16[2,128,640]{2,1,0:T(8,128)(2,1)S(1)}, u32[]{:S(2)}) copy-start(bf16[2,128,640]{2,1,0:T(8,128)(2,1)S(1)} %get-tuple-element.23.probs_ref) | copy-start | bytes 983044
  25.8 0.6 %copy-start.8 = (bf16[128,256]{1,0:T(8,128)(2,1)}, bf16[128,256]{1,0:T(8,128)(2,1)S(1)}, u32[]{:S(2)}) copy-start(bf16[128,256]{1,0:T(8,128)(2,1)S(1)} %get-tuple-element.24.attn_ref) | copy-start | bytes 196612
  26.4 5.0 %copy-start.6 = (bf16[2,128,640]{2,1,0:T(8,128)(2,1)S(1)}, bf16[2,128,640]{2,1,0:T(8,128)(2,1)}, u32[]{:S(2)}) copy-start(bf16[2,128,640]{2,1,0:T(8,128)(2,1)} %copy-done.5) | copy-start | bytes 983044
  26.4 5.0 %copy-start.9 = (bf16[128,256]{1,0:T(8,128)(2,1)S(1)}, bf16[128,256]{1,0:T(8,128)(2,1)}, u32[]{:S(2)}) copy-start(bf16[128,256]{1,0:T(8,128)(2,1)} %copy-done.8) | copy-start | bytes 196612
  26.4 19.9 %collective-permute-start.1 = (bf16[4,128,512]{2,1,0:T(8,128)(2,1)}, bf16[4,128,512]{2,1,0:T(8,128)(2,1)}, u32[]{:S(2)}, u32[]{:S(2)}) collective-permute-start(bf16[4,128,512]{2,1,0:T(8,128)(2,1)} %get-tuple-element.21), channel_id=1, source_target_pairs={{0,4},{1,5},{2,6},{3,7},{4,0},{5,1},{6,2},{7,3},{8,12},{9,13},{10,... | collective-permute-start | bytes 1572872 | tf_op jit(solution)/shard_map/ppermute | solution.py:287
  30.6 1.1 %copy-start.2 = (bf16[640,512]{1,0:T(8,128)(2,1)S(1)}, bf16[640,512]{1,0:T(8,128)(2,1)}, u32[]{:S(2)}) copy-start(bf16[640,512]{1,0:T(8,128)(2,1)} %copy-done.1) | copy-start | bytes 1966084
  31.4 15.0 %copy-start.4 = (bf16[4,128,512]{2,1,0:T(8,128)(2,1)S(1)}, bf16[4,128,512]{2,1,0:T(8,128)(2,1)}, u32[]{:S(2)}) copy-start(bf16[4,128,512]{2,1,0:T(8,128)(2,1)} %copy-done.3) | copy-start | bytes 1572868
  36.2 16.4 %collective-permute-start.2 = (bf16[2,128,512]{2,1,0:T(8,128)(2,1)S(1)}, bf16[2,128,512]{2,1,0:T(8,128)(2,1)S(1)}, u32[]{:S(2)}, u32[]{:S(2)}) collective-permute-start(bf16[2,128,512]{2,1,0:T(8,128)(2,1)S(1)} %get-tuple-element.29.after_ref), channel_id=1, source_target_pairs={{0,16},{16,32},{32,48},{48,64},{64,80},{80,96},{96,112},{112,128},... | collective-permute-start | bytes 786440 | tf_op jit(solution)/shard_map/ppermute | solution.py:233
  48.3 13.1 %all-to-all-start.1 = ((bf16[4,128,512]{2,1,0:T(8,128)(2,1)}), bf16[4,128,512]{2,1,0:T(8,128)(2,1)S(1)}, u32[]{:S(2)}, u32[]{:S(2)}) async-start(bf16[4,128,512]{2,1,0:T(8,128)(2,1)} %rows.1), calls=%async_computation.1 | async-start | bytes 1048576 | tf_op jit(solution)/shard_map/all_to_all | solution.py:327

commit v9 on v5

v9 whole, which is shorter than its diff:
```python
import functools

import jax
import jax.numpy as jnp
from jax import lax
from jax.experimental import pallas as pl
from jax.experimental.pallas import tpu as pltpu
from jax.sharding import PartitionSpec as P

HALF = 32
BF = jnp.bfloat16
F32 = jnp.float32
VMEM = pl.BlockSpec(memory_space=pltpu.VMEM)
SMEM = pl.BlockSpec(memory_space=pltpu.SMEM)
HBM = pl.BlockSpec(memory_space=pltpu.HBM)


def dot(a, b, dims):
    return lax.dot_general(a, b, (dims, ((), ())), preferred_element_type=F32)


def call(body, outs, ins, name, flops=0, scratch=(), hbm_in=(), hbm_out=()):
    moved = sum(x.size * x.dtype.itemsize for x in (*ins, *outs))
    held = [
        pltpu.with_memory_space_constraint(x, pltpu.HBM) if i in hbm_in else x
        for i, x in enumerate(ins)
    ]
    return pl.pallas_call(
        body,
        out_shape=[pltpu.HBM(x.shape, x.dtype) if i in hbm_out else x for i, x in enumerate(outs)],
        in_specs=[SMEM if x.ndim == 1 else HBM if i in hbm_in else VMEM for i, x in enumerate(ins)],
        out_specs=[HBM if i in hbm_out else VMEM for i in range(len(outs))],
        scratch_shapes=scratch,
        compiler_params=pltpu.CompilerParams(vmem_limit_bytes=24 << 20),
        cost_estimate=pl.CostEstimate(flops=flops, bytes_accessed=moved, transcendentals=0),
        name=name,
    )(*held)


def shape(dims, dtype):
    return jax.ShapeDtypeStruct(dims, dtype)


def pack_kernel(k_ref, v_ref, q_ref, mg_ref, kvq_ref, mgv_ref, sems):
    w = k_ref.shape[1]
    copies = [pltpu.make_async_copy(mg_ref, mgv_ref, sems.at[3])]
    for i, x_ref in enumerate((k_ref, v_ref, q_ref)):
        part = kvq_ref.at[:, i * w : (i + 1) * w]
        copies.append(pltpu.make_async_copy(x_ref, part, sems.at[i]))
    for c in copies:
        c.start()
    for c in copies:
        c.wait()


def spread_kernel(mg_ref, after_ref, all_ref, sems):
    copies = [
        pltpu.make_async_copy(mg_ref, all_ref.at[b], sems.at[b]) for b in range(all_ref.shape[0])
    ]
    for c in copies:
        c.start()
    for c in copies:
        c.wait()


def as_row(col):
    n = col.shape[0]
    down = lax.broadcasted_iota(jnp.int32, (n, n), 0)
    across = lax.broadcasted_iota(jnp.int32, (n, n), 1)
    return jnp.sum(jnp.where(down == across, col, 0.0), axis=0, keepdims=True)


def in_pieces(x):
    pieces = []
    for _ in range(3):
        piece = x.astype(BF).astype(F32)
        pieces.append(piece)
        x = x - piece
    return pieces


def document_codes(lens, row_pos, col_pos):
    n = lens.shape[1]
    down = lax.broadcasted_iota(jnp.int32, (n, n), 0)
    across = lax.broadcasted_iota(jnp.int32, (n, n), 1)
    wide = jnp.broadcast_to(lens, (n, n))
    ends_col = jnp.sum(jnp.where(across <= down, wide, 0.0), axis=1, keepdims=True)
    lens_col = jnp.sum(jnp.where(across == down, wide, 0.0), axis=1, keepdims=True)
    ends_row = jnp.sum(jnp.where(down <= across, lens_col, 0.0), axis=0, keepdims=True)
    row_doc = jnp.sum(jnp.where(row_pos >= ends_col, 1.0, 0.0), axis=0, keepdims=True)
    col_doc = jnp.sum(jnp.where(col_pos >= ends_row, 1.0, 0.0), axis=1, keepdims=True)
    return row_doc, col_doc


def take_window(core, own_ref, far_ref, rows, window_ref):
    six = [x.at[i] for x in (far_ref.at[0], own_ref, far_ref.at[1]) for i in range(2)]
    for value in range(2):

        @pl.when(core == value)
        def _(value=value):
            for i in range(5):
                window_ref[i * rows : (i + 1) * rows, :] = six[i + value][:rows, :]


def forward_kernel(
    heads, total, where_ref, dil_ref, lens_ref, own_ref, far_ref, w_hbm,
    part_ref, probs_out, attn_ref, win_out, back_out, logs_ref,
    hold_ref, win_ref, back_ref, probs_ref, w_ref, sems,
):
    groups, span = part_ref.shape[0], part_ref.shape[2]
    blocks = [slice(b * span, (b + 1) * span) for b in range(groups)]
    fetches = [
        pltpu.make_async_copy(w_hbm.at[:, x], w_ref.at[:, x], sems.at[groups + b])
        for b, x in enumerate(blocks)
    ]
    for c in fetches:
        c.start()
    rows = own_ref.shape[1]
    width = own_ref.shape[2] // 3
    hd = width // heads
    keys = win_ref.shape[0]
    slab = where_ref[0]
    take_window(lax.rem(slab, 2), own_ref, far_ref, rows, win_ref)
    copies = [pltpu.make_async_copy(win_ref, win_out, sems.at[2 * groups])]
    copies[0].start()
    mine = slice(2 * rows, 3 * rows)
    first = slab * rows
    row_idx = lax.broadcasted_iota(jnp.int32, (1, keys), 1) + (first - 2 * rows)
    col_idx = lax.broadcasted_iota(jnp.int32, (rows, 1), 0) + first
    row_pos, col_pos = row_idx.astype(F32), col_idx.astype(F32)
    row_doc, col_doc = document_codes(lens_ref[...].astype(F32), row_pos, col_pos)
    inside = (row_pos >= 0.0) & (row_pos < float(total))
    distance = jnp.abs(col_pos - row_pos)
    for h in range(heads):
        stride = dil_ref[h].astype(F32)

        def residue(pos, doc):
            steps = jnp.floor((pos + 0.5) / jnp.full(pos.shape, stride))
            return doc * 8.0 + (pos - steps * stride)

        row_code = jnp.where(inside, residue(row_pos, row_doc), -1.0)
        col_code = residue(col_pos, col_doc)
        mask = (row_code == col_code) & (distance <= stride * float(HALF))
        cols = slice(h * hd, (h + 1) * hd)
        vcols = slice(width + h * hd, width + (h + 1) * hd)
        qcols = slice(2 * width + h * hd, 2 * width + (h + 1) * hd)
        s = dot(win_ref[mine, qcols], win_ref[:, cols], ((1,), (1,))) * (hd**-0.5)
        s = jnp.where(mask, s, -jnp.inf)
        top = jnp.max(s, axis=1, keepdims=True)
        e = jnp.exp(s - top)
        norm = jnp.sum(e, axis=1, keepdims=True)
        probs = (e * (1.0 / norm)).astype(BF)
        probs_ref[h] = probs
        logs_ref[h] = as_row(top + jnp.log(norm))
        attn_ref[:, cols] = dot(probs, win_ref[:, vcols], ((1,), (0,))).astype(BF)
        back = dot(win_ref[mine, cols], win_ref[:, qcols], ((1,), (1,))) * (hd**-0.5)
        back_ref[h] = jnp.where(mask, back, -jnp.inf)
    copies.append(pltpu.make_async_copy(back_ref, back_out, sems.at[2 * groups + 1]))
    copies.append(pltpu.make_async_copy(probs_ref, probs_out, sems.at[2 * groups + 2]))
    copies[1].start()
    copies[2].start()
    attn = attn_ref[...]
    for b in range(groups):
        fetches[b].wait()
        hold_ref[b] = dot(attn, w_ref[:, blocks[b]], ((1,), (0,))).astype(BF)
        copies.append(pltpu.make_async_copy(hold_ref.at[b], part_ref.at[b], sems.at[b]))
        copies[-1].start()
    for c in copies:
        c.wait()


def cotangent_kernel(heads, mg_ref, w_ref, attn_ref, logs_ref, out_ref, delta_ref):
    span = mg_ref.shape[2]
    rows, width = attn_ref.shape
    hd = width // heads
    total = jnp.zeros((rows, width), F32)
    for b in range(mg_ref.shape[0]):
        total = total + dot(mg_ref[b], w_ref[:, b * span : (b + 1) * span], ((1,), (1,)))
    grad = total.astype(BF)
    out_ref[:rows, :] = grad
    product = grad.astype(F32) * attn_ref[...].astype(F32)
    extra = out_ref.shape[0] - rows
    place = lax.broadcasted_iota(jnp.int32, (extra, hd), 0)
    for h in range(heads):
        cols = slice(h * hd, (h + 1) * hd)
        delta = jnp.sum(product[:, cols], axis=1, keepdims=True)
        delta_ref[h] = delta
        stats = jnp.zeros((extra, hd), F32)
        for i, piece in enumerate(in_pieces(logs_ref[h]) + in_pieces(as_row(delta))):
            stats = jnp.where(place == i, piece, stats)
        out_ref[rows:, cols] = stats.astype(BF)


def query_kernel(heads, win_ref, probs_ref, ga_ref, delta_ref, dq_ref):
    rows, width = dq_ref.shape
    hd = width // heads
    for h in range(heads):
        cols = slice(h * hd, (h + 1) * hd)
        vcols = slice(width + h * hd, width + (h + 1) * hd)
        grad_prob = dot(ga_ref[:rows, cols], win_ref[:, vcols], ((1,), (1,)))
        slopes = (probs_ref[h].astype(F32) * (grad_prob - delta_ref[h])).astype(BF)
        dq_ref[:, cols] = (dot(slopes, win_ref[:, cols], ((1,), (0,))) * (hd**-0.5)).astype(BF)


def key_kernel(heads, where_ref, win_ref, back_ref, own_ref, far_ref, dk_ref, dv_ref, ga_ref):
    rows, width = dk_ref.shape
    hd = width // heads
    mine = slice(2 * rows, 3 * rows)
    core = lax.rem(where_ref[0], 2)
    take_window(core, own_ref, far_ref, rows, ga_ref)
    tails = [x[i, rows:, :].astype(F32) for x in (far_ref.at[0], own_ref, far_ref.at[1]) for i in range(2)]
    tails = [jnp.where(core == 0, tails[i], tails[i + 1]) for i in range(5)]
    stats = jnp.concatenate([jnp.stack([t[:, h * hd : (h + 1) * hd] for h in range(heads)]) for t in tails], axis=2)
    for h in range(heads):
        cols = slice(h * hd, (h + 1) * hd)
        vcols = slice(width + h * hd, width + (h + 1) * hd)
        qcols = slice(2 * width + h * hd, 2 * width + (h + 1) * hd)
        log_total = stats[h, 0:1] + stats[h, 1:2] + stats[h, 2:3]
        delta = stats[h, 3:4] + stats[h, 4:5] + stats[h, 5:6]
        weight = jnp.exp(back_ref[h] - log_total)
        grad_prob = dot(win_ref[mine, vcols], ga_ref[:, cols], ((1,), (1,)))
        slopes = (weight * (grad_prob - delta)).astype(BF)
        dk_ref[:, cols] = (dot(slopes, win_ref[:, qcols], ((1,), (0,))) * (hd**-0.5)).astype(BF)
        dv_ref[:, cols] = dot(weight.astype(BF), ga_ref[:, cols], ((1,), (0,))).astype(BF)


def mixed_kernel(x_ref, o_ref):
    total = x_ref[0].astype(F32)
    for c in range(1, x_ref.shape[0]):
        total = total + x_ref[c].astype(F32)
    o_ref[...] = total.astype(BF)


def to_neighbours(x):
    count = lax.axis_size("ctx")
    ahead = [(i, i + 2) for i in range(0, count - 2, 2)]
    back = [(i, i - 2) for i in range(3, count, 2)]
    return lax.ppermute(x, "ctx", ahead + back)


def in_chip(x):
    pairs = [[i, i + 1] for i in range(0, lax.axis_size("ctx"), 2)]
    return lax.all_gather(x, "ctx", axis=0, axis_index_groups=pairs)


def per_device(queries, keys, values, out_weight, mixed_grad, lengths, dilation):
    rows, width = queries.shape
    heads = dilation.shape[0]
    groups = lax.axis_size("head")
    span = mixed_grad.shape[1]
    total = rows * lax.axis_size("ctx")
    where = lax.axis_index("ctx").astype(jnp.int32).reshape(1)
    lens = lengths.reshape(1, -1)

    kvq, mgv = call(
        pack_kernel,
        [shape((rows, 3 * width), BF), shape((rows, span), BF)],
        [keys, values, queries, mixed_grad],
        "pack",
        scratch=[pltpu.SemaphoreType.DMA((4,))],
        hbm_in=(0, 1, 2, 3),
    )
    own2 = in_chip(kvq)
    near = to_neighbours(own2)
    (spread,) = call(
        spread_kernel,
        [shape((groups, rows, span), BF)],
        [mgv, own2],
        "spread",
        scratch=[pltpu.SemaphoreType.DMA((groups,))],
        hbm_out=(0,),
    )
    gathered = lax.all_to_all(spread, "head", 0, 0, tiled=True)
    far = in_chip(near)
    part, probs, attn, window, back, logs = call(
        functools.partial(forward_kernel, heads, total),
        [
            shape((groups, rows, span), BF),
            shape((heads, rows, 5 * rows), BF),
            shape((rows, width), BF),
            shape((5 * rows, 3 * width), BF),
            shape((heads, rows, 5 * rows), F32),
            shape((heads, 1, rows), F32),
        ],
        [where, dilation, lens, own2, far, out_weight],
        "forward",
        flops=80 * 2 * rows * width * (groups * span + 15 * rows),
        scratch=[
            pltpu.VMEM((groups, rows, span), BF),
            pltpu.VMEM((5 * rows, 3 * width), BF),
            pltpu.VMEM((heads, rows, 5 * rows), F32),
            pltpu.VMEM((heads, rows, 5 * rows), BF),
            pltpu.VMEM(out_weight.shape, BF),
            pltpu.SemaphoreType.DMA((2 * groups + 3,)),
        ],
        hbm_in=(5,),
        hbm_out=(0, 1, 3, 4),
    )
    ga, delta = call(
        functools.partial(cotangent_kernel, heads),
        [shape((rows + 16, width), BF), shape((heads, rows, 1), F32)],
        [gathered, out_weight, attn, logs],
        "cotangent",
        flops=2 * rows * width * groups * span,
    )
    ga, part = lax.optimization_barrier((ga, part))
    summed = lax.all_to_all(part, "head", 0, 0, tiled=True)
    ga2 = in_chip(ga)
    ga_near = to_neighbours(ga2)
    (dq,) = call(
        functools.partial(query_kernel, heads),
        [shape((rows, width), BF)],
        [window, probs, ga, delta],
        "query",
        flops=2 * rows * width * 10 * rows,
    )
    (mixed,) = call(mixed_kernel, [shape((rows, span), BF)], [summed], "mixed")
    dk, dv = call(
        functools.partial(key_kernel, heads),
        [shape((rows, width), BF), shape((rows, width), BF)],
        [where, window, back, ga2, in_chip(ga_near)],
        "key",
        flops=2 * rows * width * 15 * rows,
        scratch=[pltpu.VMEM((5 * rows, width), BF)],
    )
    return mixed, dq, dk, dv


def solution(mesh):
    placed = (
        P("ctx", "head"),
        P("ctx", "head"),
        P("ctx", "head"),
        P("head", None),
        P("ctx", "head"),
        P(),
        P("head"),
    )
    return jax.shard_map(
        per_device,
        mesh=mesh,
        in_specs=placed,
        out_specs=(P("ctx", "head"), P("ctx", "head"), P("ctx", "head"), P("ctx", "head")),
        check_vma=False,
    )
```

time: 60.9 us -> 61.2 us (level)
  the two profiles are of different devices: /device:TPU:259 before, /device:TPU:249 now
where the time goes in v9:
time: 61.2 us; the launch traced here: 60.8 us
  waiting for transfers between devices  19.7 us (32%)
  starting transfers between devices  17.5 us (29%)
  blocking collectives  10.9 us (18%)
  Pallas kernels  10.4 us (17%)
  local copies, waits for them, and re-layouts  1.62 us (3%)
  between operations  0.73 us (1%)
    ppermute x2, waiting for transfers between devices, to_neighbours(): return lax.ppermute(x, 'ctx', ahead + back)  15.8 us
    all_gather x4, blocking collectives, in_chip(): return lax.all_gather(x, 'ctx', axis=0, axis_index_groups=pairs)  10.9 us
    pallas_call x7, Pallas kernels, call(): pl.pallas_call(body, out_shape=[pltpu.HBM(x.shape, x.dtype) if i in hbm_o...  10.4 us
    ppermute x2, starting transfers between devices, to_neighbours(): return lax.ppermute(x, 'ctx', ahead + back)  6.74 us
    all_to_all x1, starting transfers between devices, per_device(): summed = lax.all_to_all(part, 'head', 0, 0, tiled=True)  5.6 us
    all_to_all x1, starting transfers between devices, per_device(): gathered = lax.all_to_all(spread, 'head', 0, 0, tiled=True)  5.21 us
    all_to_all x1, waiting for transfers between devices, per_device(): gathered = lax.all_to_all(spread, 'head', 0, 0, tiled=True)  3.87 us
    unnamed x12, local copies, waits for them, and re-layouts  1.62 us
  transfers between devices with their start and end apart: 4, of which 3 were waited for; matrix products, arithmetic and copies ran while one was open for 0% of the time, Pallas kernels for 13%

profile of v9, /device:TPU:249, one launch (start us, length us, event | category | flops | bytes accessed | tf_op | source)
XLA Modules:
  0.0 60.8 jit_solution(14762297491797914933)
XLA Ops:
  0.6 1.0 %pack.1 = (bf16[128,768]{1,0:T(8,128)(2,1)S(1)}, bf16[128,512]{1,0:T(8,128)(2,1)S(1)}) custom-call(bf16[128,256]{1,0:T(8,128)(2,1)} %k_ref.1, bf16[128,256]{1,0:T(8,128)(2,1)} %v_ref.1, bf16[128,256]{1,0:T(8,128)(2,1)} %q_ref.1, bf16[128,512]{1,0:T(8,128)(2,1)} %mg_ref.1), custom_call_target="tpu_custom_call" | custom-call | bytes 655360 | tf_op jit(solution)/shard_map/pack/pallas_call | solution.py:28
  1.6 2.4 %all-gather = bf16[256,768]{1,0:T(8,128)(2,1)S(1)} all-gather(bf16[128,768]{1,0:T(8,128)(2,1)S(1)} %get-tuple-element.19), channel_id=2, replica_groups={{0,8},{16,24},{32,40},{48,56},{64,72},{80,88},{96,104},{112,120},{128,1..., dimensions={0}, use_global_device_ids=true | all-gather | bytes 589824 | tf_op jit(solution)/shard_map/all_gather | solution.py:243
  4.0 3.8 %collective-permute-start = (bf16[2,128,768]{2,1,0:T(8,128)(2,1)S(1)}, bf16[2,128,768]{2,1,0:T(8,128)(2,1)S(1)}, u32[]{:S(2)}, u32[]{:S(2)}) collective-permute-start(bf16[2,128,768]{2,1,0:T(8,128)(2,1)S(1)} %bitcast.6), channel_id=1, source_target_pairs={{0,16},{16,32},{32,48},{48,64},{64,80},{80,96},{96,112},{112,128},... | collective-permute-start | bytes 1179656 | tf_op jit(solution)/shard_map/ppermute | solution.py:238
  7.8 0.0 copy-start.4
  7.8 0.0 copy-start.5
  7.8 1.1 %spread.1 = bf16[8,128,512]{2,1,0:T(8,128)(2,1)} custom-call(bf16[128,512]{1,0:T(8,128)(2,1)S(1)} %get-tuple-element.18.mg_ref, bf16[2,128,768]{2,1,0:T(8,128)(2,1)S(1)} %bitcast.7), custom_call_target="tpu_custom_call" | custom-call | bytes 1572864 | tf_op jit(solution)/shard_map/spread/pallas_call | solution.py:28
  8.9 5.2 %all-to-all-start = ((bf16[8,128,512]{2,1,0:T(8,128)(2,1)}), bf16[8,128,512]{2,1,0:T(8,128)(2,1)S(1)}, u32[]{:S(2)}, u32[]{:S(2)}) async-start(bf16[8,128,512]{2,1,0:T(8,128)(2,1)} %spread.1), calls=%async_computation | async-start | bytes 2097152 | tf_op jit(solution)/shard_map/all_to_all | solution.py:273
  14.1 4.1 %collective-permute-done = bf16[2,128,768]{2,1,0:T(8,128)(2,1)S(1)} collective-permute-done((bf16[2,128,768]{2,1,0:T(8,128)(2,1)S(1)}, bf16[2,128,768]{2,1,0:T(8,128)(2,1)S(1)}, u32[]{:S(2)}, u32[]{:S(2)}) %collective-permute-start) | collective-permute-done | bytes 393248 | tf_op jit(solution)/shard_map/ppermute | solution.py:238
  18.2 3.0 %all-gather.1 = bf16[4,128,768]{2,1,0:T(8,128)(2,1)S(1)} all-gather(bf16[2,128,768]{2,1,0:T(8,128)(2,1)S(1)} %collective-permute-done), channel_id=3, replica_groups={{0,8},{16,24},{32,40},{48,56},{64,72},{80,88},{96,104},{112,120},{128,1..., dimensions={0}, use_global_device_ids=true | all-gather | bytes 1179648 | tf_op jit(solution)/shard_map/all_gather | solution.py:243
  21.2 0.0 copy-done.4
  21.2 0.0 copy-done.5
  21.2 4.2 %forward.1 = (bf16[8,128,512]{2,1,0:T(8,128)(2,1)}, bf16[2,128,640]{2,1,0:T(8,128)(2,1)}, bf16[128,256]{1,0:T(8,128)(2,1)S(1)}, bf16[640,768]{1,0:T(8,128)(2,1)}...) custom-call(s32[1]{0:T(128)} %bitcast.1.where_ref, s32[2]{0:T(128)S(1)} %copy-done.4, s32[1,64]{1,0:T(1,128)S(1)} %bitcast.13, ...), custom_call_target="tpu_custom_call" | custom-call | flops 31541166080 | bytes 6358284 | tf_op jit(solution)/shard_map/forward/pallas_call | solution.py:28
  25.4 3.9 %all-to-all-done.mg_ref = bf16[8,128,512]{2,1,0:T(8,128)(2,1)S(1)} async-done(((bf16[8,128,512]{2,1,0:T(8,128)(2,1)}), bf16[8,128,512]{2,1,0:T(8,128)(2,1)S(1)}, u32[]{:S(2)}, u32[]{:S(2)}) %all-to-all-start) | async-done | bytes 1048608 | tf_op jit(solution)/shard_map/all_to_all | solution.py:273
  29.2 0.0 copy-start.1
  29.2 1.6 %copy-done.1 = bf16[256,4096]{1,0:T(8,128)(2,1)S(1)} copy-done((bf16[256,4096]{1,0:T(8,128)(2,1)S(1)}, bf16[256,4096]{1,0:T(8,128)(2,1)}, u32[]{:S(2)}) %copy-start.1) | copy-done | bytes 2097176
  30.8 0.0 copy-start
  30.8 0.0 copy-start.3
  30.8 0.9 %cotangent.1 = (bf16[144,256]{1,0:T(8,128)(2,1)S(1)}, f32[2,128,1]{2,1,0:T(8,128)S(1)}) custom-call(bf16[8,128,512]{2,1,0:T(8,128)(2,1)S(1)} %all-to-all-done.mg_ref, bf16[256,4096]{1,0:T(8,128)(2,1)S(1)} %copy-done.1, bf16[128,256]{1,0:T(8,128)(2,1)S(1)} %get-tuple-element.20.attn_ref, f32[2,1,128]{2,1,0:T(1,128)S(1)} %get-tuple-element.21.logs_ref), custom_call_target="tpu_custom_call" | custom-call | flops 268435456 | bytes 3287040 | tf_op jit(solution)/shard_map/cotangent/pallas_call | solution.py:28
  31.8 0.0 copy-start.2
  31.8 5.6 %all-to-all-start.1 = ((bf16[8,128,512]{2,1,0:T(8,128)(2,1)}), bf16[8,128,512]{2,1,0:T(8,128)(2,1)S(1)}, u32[]{:S(2)}, u32[]{:S(2)}) async-start(bf16[8,128,512]{2,1,0:T(8,128)(2,1)} %get-tuple-element.24), calls=%async_computation.1 | async-start | bytes 2097152 | tf_op jit(solution)/shard_map/all_to_all | solution.py:307
  37.4 3.5 %all-gather.2 = bf16[288,256]{1,0:T(8,128)(2,1)S(1)} all-gather(bf16[144,256]{1,0:T(8,128)(2,1)S(1)} %get-tuple-element.27.ga_ref), channel_id=4, replica_groups={{0,8},{16,24},{32,40},{48,56},{64,72},{80,88},{96,104},{112,120},{128,1..., dimensions={0}, use_global_device_ids=true | all-gather | bytes 221184 | tf_op jit(solution)/shard_map/all_gather | solution.py:243
  40.9 3.0 %collective-permute-start.1 = (bf16[2,144,256]{2,1,0:T(8,128)(2,1)S(1)}, bf16[2,144,256]{2,1,0:T(8,128)(2,1)S(1)}, u32[]{:S(2)}, u32[]{:S(2)}) collective-permute-start(bf16[2,144,256]{2,1,0:T(8,128)(2,1)S(1)} %bitcast.11), channel_id=1, source_target_pairs={{0,16},{16,32},{32,48},{48,64},{64,80},{80,96},{96,112},{112,128},... | collective-permute-start | bytes 442376 | tf_op jit(solution)/shard_map/ppermute | solution.py:238
  43.9 0.0 copy-done
  43.9 0.0 copy-done.3
  43.9 1.2 %query.1 = bf16[128,256]{1,0:T(8,128)(2,1)} custom-call(bf16[640,768]{1,0:T(8,128)(2,1)S(1)} %copy-done, bf16[2,128,640]{2,1,0:T(8,128)(2,1)S(1)} %copy-done.3, bf16[144,256]{1,0:T(8,128)(2,1)S(1)} %get-tuple-element.27.ga_ref, f32[2,128,1]{2,1,0:T(8,128)S(1)} %get-tuple-element.28.delta_ref), custom_call_target="tpu_custom_call" | custom-call | flops 83886080 | bytes 1451008 | tf_op jit(solution)/shard_map/query/pallas_call | solution.py:28
  45.0 11.7 %collective-permute-done.1 = bf16[2,144,256]{2,1,0:T(8,128)(2,1)S(1)} collective-permute-done((bf16[2,144,256]{2,1,0:T(8,128)(2,1)S(1)}, bf16[2,144,256]{2,1,0:T(8,128)(2,1)S(1)}, u32[]{:S(2)}, u32[]{:S(2)}) %collective-permute-start.1) | collective-permute-done | bytes 147488 | tf_op jit(solution)/shard_map/ppermute | solution.py:238
  56.8 2.0 %all-gather.3 = bf16[4,144,256]{2,1,0:T(8,128)(2,1)S(1)} all-gather(bf16[2,144,256]{2,1,0:T(8,128)(2,1)S(1)} %collective-permute-done.1), channel_id=5, replica_groups={{0,8},{16,24},{32,40},{48,56},{64,72},{80,88},{96,104},{112,120},{128,1..., dimensions={0}, use_global_device_ids=true | all-gather | bytes 442368 | tf_op jit(solution)/shard_map/all_gather | solution.py:243
  58.8 0.0 copy-done.2
  58.8 1.3 %key.1 = (bf16[128,256]{1,0:T(8,128)(2,1)}, bf16[128,256]{1,0:T(8,128)(2,1)}) custom-call(s32[1]{0:T(128)} %bitcast.1.where_ref, bf16[640,768]{1,0:T(8,128)(2,1)S(1)} %copy-done, f32[2,128,640]{2,1,0:T(8,128)S(1)} %copy-done.2, bf16[2,144,256]{2,1,0:T(8,128)(2,1)S(1)} %bitcast.12, bf16[2,2,144,256]{3,2,1,0:T(8,128)(2,1)S(1)} %bitcast.9), custom_call_target="tpu_custom_call" | custom-call | flops 125829120 | bytes 2211844 | tf_op jit(solution)/shard_map/key/pallas_call | solution.py:28
  60.0 0.0 all-to-all-done.1.x_ref
  60.1 0.8 %mixed.1 = bf16[128,512]{1,0:T(8,128)(2,1)} custom-call(bf16[8,128,512]{2,1,0:T(8,128)(2,1)S(1)} %all-to-all-done.1.x_ref), custom_call_target="tpu_custom_call" | custom-call | bytes 1179648 | tf_op jit(solution)/shard_map/mixed/pallas_call | solution.py:28
Async XLA Ops:
  4.0 14.2 %collective-permute-start = (bf16[2,128,768]{2,1,0:T(8,128)(2,1)S(1)}, bf16[2,128,768]{2,1,0:T(8,128)(2,1)S(1)}, u32[]{:S(2)}, u32[]{:S(2)}) collective-permute-start(bf16[2,128,768]{2,1,0:T(8,128)(2,1)S(1)} %bitcast.6), channel_id=1, source_target_pairs={{0,16},{16,32},{32,48},{48,64},{64,80},{80,96},{96,112},{112,128},... | collective-permute-start | bytes 1179656 | tf_op jit(solution)/shard_map/ppermute | solution.py:238
  7.8 13.4 %copy-start.4 = (s32[2]{0:T(128)S(1)}, s32[2]{0:T(128)}, u32[]{:S(2)}) copy-start(s32[2]{0:T(128)} %dil_ref.1) | copy-start | bytes 28
  7.8 13.4 %copy-start.5 = (s32[64]{0:T(128)S(1)}, s32[64]{0:T(128)}, u32[]{:S(2)}) copy-start(s32[64]{0:T(128)} %param.12) | copy-start | bytes 772
  8.9 20.4 %all-to-all-start = ((bf16[8,128,512]{2,1,0:T(8,128)(2,1)}), bf16[8,128,512]{2,1,0:T(8,128)(2,1)S(1)}, u32[]{:S(2)}, u32[]{:S(2)}) async-start(bf16[8,128,512]{2,1,0:T(8,128)(2,1)} %spread.1), calls=%async_computation | async-start | bytes 2097152 | tf_op jit(solution)/shard_map/all_to_all | solution.py:273
  29.2 1.6 %copy-start.1 = (bf16[256,4096]{1,0:T(8,128)(2,1)S(1)}, bf16[256,4096]{1,0:T(8,128)(2,1)}, u32[]{:S(2)}) copy-start(bf16[256,4096]{1,0:T(8,128)(2,1)} %w_ref.1) | copy-start | bytes 6291460
  30.8 13.0 %copy-start = (bf16[640,768]{1,0:T(8,128)(2,1)S(1)}, bf16[640,768]{1,0:T(8,128)(2,1)}, u32[]{:S(2)}) copy-start(bf16[640,768]{1,0:T(8,128)(2,1)} %get-tuple-element.25.win_ref) | copy-start | bytes 2949124
  30.8 13.0 %copy-start.3 = (bf16[2,128,640]{2,1,0:T(8,128)(2,1)S(1)}, bf16[2,128,640]{2,1,0:T(8,128)(2,1)}, u32[]{:S(2)}) copy-start(bf16[2,128,640]{2,1,0:T(8,128)(2,1)} %get-tuple-element.26.probs_ref) | copy-start | bytes 983044
  31.8 27.0 %copy-start.2 = (f32[2,128,640]{2,1,0:T(8,128)S(1)}, f32[2,128,640]{2,1,0:T(8,128)}, u32[]{:S(2)}) copy-start(f32[2,128,640]{2,1,0:T(8,128)} %get-tuple-element.29.back_ref) | copy-start | bytes 1966084
  31.8 28.3 %all-to-all-start.1 = ((bf16[8,128,512]{2,1,0:T(8,128)(2,1)}), bf16[8,128,512]{2,1,0:T(8,128)(2,1)S(1)}, u32[]{:S(2)}, u32[]{:S(2)}) async-start(bf16[8,128,512]{2,1,0:T(8,128)(2,1)} %get-tuple-element.24), calls=%async_computation.1 | async-start | bytes 2097152 | tf_op jit(solution)/shard_map/all_to_all | solution.py:307
  40.9 15.9 %collective-permute-start.1 = (bf16[2,144,256]{2,1,0:T(8,128)(2,1)S(1)}, bf16[2,144,256]{2,1,0:T(8,128)(2,1)S(1)}, u32[]{:S(2)}, u32[]{:S(2)}) collective-permute-start(bf16[2,144,256]{2,1,0:T(8,128)(2,1)S(1)} %bitcast.11), channel_id=1, source_target_pairs={{0,16},{16,32},{32,48},{48,64},{64,80},{80,96},{96,112},{112,128},... | collective-permute-start | bytes 442376 | tf_op jit(solution)/shard_map/ppermute | solution.py:238

commit v10 on v9

--- a/solution.py
+++ b/solution.py
@@ -103,25 +103,19 @@
 
 
 def forward_kernel(
-    heads, total, where_ref, dil_ref, lens_ref, own_ref, far_ref, w_hbm,
-    part_ref, probs_out, attn_ref, win_out, back_out, logs_ref,
-    hold_ref, win_ref, back_ref, probs_ref, w_ref, sems,
+    heads, total, where_ref, dil_ref, lens_ref, own_ref, far_ref, w_ref,
+    part_ref, probs_out, attn_out, win_out, back_out, logs_ref,
+    hold_ref, win_ref, back_ref, probs_ref, attn_ref, sems,
 ):
     groups, span = part_ref.shape[0], part_ref.shape[2]
     blocks = [slice(b * span, (b + 1) * span) for b in range(groups)]
-    fetches = [
-        pltpu.make_async_copy(w_hbm.at[:, x], w_ref.at[:, x], sems.at[groups + b])
-        for b, x in enumerate(blocks)
-    ]
-    for c in fetches:
-        c.start()
     rows = own_ref.shape[1]
     width = own_ref.shape[2] // 3
     hd = width // heads
     keys = win_ref.shape[0]
     slab = where_ref[0]
     take_window(lax.rem(slab, 2), own_ref, far_ref, rows, win_ref)
-    copies = [pltpu.make_async_copy(win_ref, win_out, sems.at[2 * groups])]
+    copies = [pltpu.make_async_copy(win_ref, win_out, sems.at[groups])]
     copies[0].start()
     mine = slice(2 * rows, 3 * rows)
     first = slab * rows
@@ -155,13 +149,13 @@
         attn_ref[:, cols] = dot(probs, win_ref[:, vcols], ((1,), (0,))).astype(BF)
         back = dot(win_ref[mine, cols], win_ref[:, qcols], ((1,), (1,))) * (hd**-0.5)
         back_ref[h] = jnp.where(mask, back, -jnp.inf)
-    copies.append(pltpu.make_async_copy(back_ref, back_out, sems.at[2 * groups + 1]))
-    copies.append(pltpu.make_async_copy(probs_ref, probs_out, sems.at[2 * groups + 2]))
-    copies[1].start()
-    copies[2].start()
+    copies.append(pltpu.make_async_copy(back_ref, back_out, sems.at[groups + 1]))
+    copies.append(pltpu.make_async_copy(probs_ref, probs_out, sems.at[groups + 2]))
+    copies.append(pltpu.make_async_copy(attn_ref, attn_out, sems.at[groups + 3]))
+    for c in copies[1:]:
+        c.start()
     attn = attn_ref[...]
     for b in range(groups):
-        fetches[b].wait()
         hold_ref[b] = dot(attn, w_ref[:, blocks[b]], ((1,), (0,))).astype(BF)
         copies.append(pltpu.make_async_copy(hold_ref.at[b], part_ref.at[b], sems.at[b]))
         copies[-1].start()
@@ -169,8 +163,10 @@
         c.wait()
 
 
-def cotangent_kernel(heads, mg_ref, w_ref, attn_ref, logs_ref, out_ref, delta_ref):
+def cotangent_kernel(heads, mg_ref, w_ref, attn_hbm, logs_ref, out_ref, delta_ref, attn_ref, sem):
     span = mg_ref.shape[2]
+    fetch = pltpu.make_async_copy(attn_hbm, attn_ref, sem)
+    fetch.start()
     rows, width = attn_ref.shape
     hd = width // heads
     total = jnp.zeros((rows, width), F32)
@@ -178,6 +174,7 @@
         total = total + dot(mg_ref[b], w_ref[:, b * span : (b + 1) * span], ((1,), (1,)))
     grad = total.astype(BF)
     out_ref[:rows, :] = grad
+    fetch.wait()
     product = grad.astype(F32) * attn_ref[...].astype(F32)
     extra = out_ref.shape[0] - rows
     place = lax.broadcasted_iota(jnp.int32, (extra, hd), 0)
@@ -191,8 +188,16 @@
         out_ref[rows:, cols] = stats.astype(BF)
 
 
-def query_kernel(heads, win_ref, probs_ref, ga_ref, delta_ref, dq_ref):
+def query_kernel(heads, win_hbm, probs_hbm, ga_ref, delta_ref, dq_ref, win_ref, probs_ref, sems):
     rows, width = dq_ref.shape
+    copies = [
+        pltpu.make_async_copy(win_hbm.at[:, : 2 * width], win_ref, sems.at[0]),
+        pltpu.make_async_copy(probs_hbm, probs_ref, sems.at[1]),
+    ]
+    for c in copies:
+        c.start()
+    for c in copies:
+        c.wait()
     hd = width // heads
     for h in range(heads):
         cols = slice(h * hd, (h + 1) * hd)
@@ -290,11 +295,10 @@
             pltpu.VMEM((5 * rows, 3 * width), BF),
             pltpu.VMEM((heads, rows, 5 * rows), F32),
             pltpu.VMEM((heads, rows, 5 * rows), BF),
-            pltpu.VMEM(out_weight.shape, BF),
-            pltpu.SemaphoreType.DMA((2 * groups + 3,)),
+            pltpu.VMEM((rows, width), BF),
+            pltpu.SemaphoreType.DMA((groups + 4,)),
         ],
-        hbm_in=(5,),
-        hbm_out=(0, 1, 3, 4),
+        hbm_out=(0, 1, 2, 3, 4),
     )
     ga, delta = call(
         functools.partial(cotangent_kernel, heads),
@@ -302,10 +306,10 @@
         [gathered, out_weight, attn, logs],
         "cotangent",
         flops=2 * rows * width * groups * span,
-    )
-    ga, part = lax.optimization_barrier((ga, part))
-    summed = lax.all_to_all(part, "head", 0, 0, tiled=True)
-    ga2 = in_chip(ga)
+        scratch=[pltpu.VMEM((rows, width), BF), pltpu.SemaphoreType.DMA],
+        hbm_in=(2,),
+    )
+    ga2, ga, part = lax.optimization_barrier((in_chip(ga), ga, part))
     ga_near = to_neighbours(ga2)
     (dq,) = call(
         functools.partial(query_kernel, heads),
@@ -313,14 +317,21 @@
         [window, probs, ga, delta],
         "query",
         flops=2 * rows * width * 10 * rows,
-    )
+        scratch=[
+            pltpu.VMEM((5 * rows, 2 * width), BF),
+            pltpu.VMEM((heads, rows, 5 * rows), BF),
+            pltpu.SemaphoreType.DMA((2,)),
+        ],
+        hbm_in=(0, 1),
+    )
+    summed = lax.all_to_all(part, "head", 0, 0, tiled=True)
     (mixed,) = call(mixed_kernel, [shape((rows, span), BF)], [summed], "mixed")
     dk, dv = call(
         functools.partial(key_kernel, heads),
         [shape((rows, width), BF), shape((rows, width), BF)],
         [where, window, back, ga2, in_chip(ga_near)],
         "key",
-        flops=2 * rows * width * 15 * rows,
+        flops=30 * 10**9,
         scratch=[pltpu.VMEM((5 * rows, width), BF)],
     )
     return mixed, dq, dk, dv

time: 61.2 us -> 59.1 us (0.966)
  the two profiles are of different devices: /device:TPU:249 before, /device:TPU:448 now
where the time goes in v10:
time: 59.1 us; the launch traced here: 58.7 us
  starting transfers between devices  20.5 us (35%)
  waiting for transfers between devices  18.2 us (31%)
  Pallas kernels  10.6 us (18%)
  blocking collectives  8.59 us (15%)
  between operations  0.73 us (1%)
    pallas_call x7, Pallas kernels, call(): pl.pallas_call(body, out_shape=[pltpu.HBM(x.shape, x.dtype) if i in hbm_o...  10.6 us
    ppermute x2, starting transfers between devices, to_neighbours(): return lax.ppermute(x, 'ctx', ahead + back)  9.09 us
    all_gather x4, blocking collectives, in_chip(): return lax.all_gather(x, 'ctx', axis=0, axis_index_groups=pairs)  8.59 us
    all_to_all x1, waiting for transfers between devices, per_device(): summed = lax.all_to_all(part, 'head', 0, 0, tiled=True)  8.4 us
    all_to_all x1, starting transfers between devices, per_device(): summed = lax.all_to_all(part, 'head', 0, 0, tiled=True)  6.12 us
    all_to_all x1, waiting for transfers between devices, per_device(): gathered = lax.all_to_all(spread, 'head', 0, 0, tiled=True)  6.12 us
    all_to_all x1, starting transfers between devices, per_device(): gathered = lax.all_to_all(spread, 'head', 0, 0, tiled=True)  5.32 us
    ppermute x2, waiting for transfers between devices, to_neighbours(): return lax.ppermute(x, 'ctx', ahead + back)  3.68 us
  transfers between devices with their start and end apart: 4, of which 3 were waited for; matrix products, arithmetic and copies ran while one was open for 0% of the time, Pallas kernels for 13%

profile of v10, /device:TPU:448, one launch (start us, length us, event | category | flops | bytes accessed | tf_op | source)
XLA Modules:
  0.0 58.7 jit_solution(12591157449725134381)
XLA Ops:
  0.6 1.0 %pack.1 = (bf16[128,768]{1,0:T(8,128)(2,1)S(1)}, bf16[128,512]{1,0:T(8,128)(2,1)S(1)}) custom-call(bf16[128,256]{1,0:T(8,128)(2,1)} %k_ref.1, bf16[128,256]{1,0:T(8,128)(2,1)} %v_ref.1, bf16[128,256]{1,0:T(8,128)(2,1)} %q_ref.1, bf16[128,512]{1,0:T(8,128)(2,1)} %mg_ref.1), custom_call_target="tpu_custom_call" | custom-call | bytes 655360 | tf_op jit(solution)/shard_map/pack/pallas_call | solution.py:28
  1.6 2.1 %all-gather = bf16[256,768]{1,0:T(8,128)(2,1)S(1)} all-gather(bf16[128,768]{1,0:T(8,128)(2,1)S(1)} %get-tuple-element.20), channel_id=2, replica_groups={{0,8},{16,24},{32,40},{48,56},{64,72},{80,88},{96,104},{112,120},{128,1..., dimensions={0}, use_global_device_ids=true | all-gather | bytes 589824 | tf_op jit(solution)/shard_map/all_gather | solution.py:248
  3.7 4.5 %collective-permute-start = (bf16[2,128,768]{2,1,0:T(8,128)(2,1)S(1)}, bf16[2,128,768]{2,1,0:T(8,128)(2,1)}, u32[]{:S(2)}, u32[]{:S(2)}) collective-permute-start(bf16[2,128,768]{2,1,0:T(8,128)(2,1)S(1)} %bitcast.6), channel_id=1, source_target_pairs={{0,16},{16,32},{32,48},{48,64},{64,80},{80,96},{96,112},{112,128},... | collective-permute-start | bytes 1179656 | tf_op jit(solution)/shard_map/ppermute | solution.py:243
  8.2 0.0 copy-start
  8.2 0.0 copy-start.2
  8.2 0.0 copy-start.3
  8.3 1.1 %spread.1 = bf16[8,128,512]{2,1,0:T(8,128)(2,1)} custom-call(bf16[128,512]{1,0:T(8,128)(2,1)S(1)} %get-tuple-element.19.mg_ref, bf16[2,128,768]{2,1,0:T(8,128)(2,1)S(1)} %bitcast.7), custom_call_target="tpu_custom_call" | custom-call | bytes 1572864 | tf_op jit(solution)/shard_map/spread/pallas_call | solution.py:28
  9.3 5.3 %all-to-all-start = ((bf16[8,128,512]{2,1,0:T(8,128)(2,1)}), bf16[8,128,512]{2,1,0:T(8,128)(2,1)S(1)}, u32[]{:S(2)}, u32[]{:S(2)}) async-start(bf16[8,128,512]{2,1,0:T(8,128)(2,1)} %spread.1), calls=%async_computation | async-start | bytes 2097152 | tf_op jit(solution)/shard_map/all_to_all | solution.py:278
  14.6 3.7 %collective-permute-done = bf16[2,128,768]{2,1,0:T(8,128)(2,1)} collective-permute-done((bf16[2,128,768]{2,1,0:T(8,128)(2,1)S(1)}, bf16[2,128,768]{2,1,0:T(8,128)(2,1)}, u32[]{:S(2)}, u32[]{:S(2)}) %collective-permute-start) | collective-permute-done | bytes 393248 | tf_op jit(solution)/shard_map/ppermute | solution.py:243
  18.3 2.6 %all-gather.1 = bf16[4,128,768]{2,1,0:T(8,128)(2,1)S(1)} all-gather(bf16[2,128,768]{2,1,0:T(8,128)(2,1)} %collective-permute-done), channel_id=3, replica_groups={{0,8},{16,24},{32,40},{48,56},{64,72},{80,88},{96,104},{112,120},{128,1..., dimensions={0}, use_global_device_ids=true | all-gather | bytes 1179648 | tf_op jit(solution)/shard_map/all_gather | solution.py:248
  20.9 0.0 copy-done
  20.9 0.0 copy-done.2
  20.9 0.0 copy-done.3
  20.9 3.2 %forward.1 = (bf16[8,128,512]{2,1,0:T(8,128)(2,1)}, bf16[2,128,640]{2,1,0:T(8,128)(2,1)}, bf16[128,256]{1,0:T(8,128)(2,1)}, bf16[640,768]{1,0:T(8,128)(2,1)}, f3...) custom-call(s32[1]{0:T(128)} %bitcast.1.where_ref, s32[2]{0:T(128)S(1)} %copy-done.2, s32[1,64]{1,0:T(1,128)S(1)} %bitcast.13, ...), custom_call_target="tpu_custom_call" | custom-call | flops 31541166080 | bytes 6358284 | tf_op jit(solution)/shard_map/forward/pallas_call | solution.py:28
  24.1 6.1 %all-to-all-done.mg_ref = bf16[8,128,512]{2,1,0:T(8,128)(2,1)S(1)} async-done(((bf16[8,128,512]{2,1,0:T(8,128)(2,1)}), bf16[8,128,512]{2,1,0:T(8,128)(2,1)S(1)}, u32[]{:S(2)}, u32[]{:S(2)}) %all-to-all-start) | async-done | bytes 1048608 | tf_op jit(solution)/shard_map/all_to_all | solution.py:278
  30.2 1.0 %cotangent.1 = (bf16[144,256]{1,0:T(8,128)(2,1)S(1)}, f32[2,128,1]{2,1,0:T(8,128)S(1)}) custom-call(bf16[8,128,512]{2,1,0:T(8,128)(2,1)S(1)} %all-to-all-done.mg_ref, bf16[256,4096]{1,0:T(8,128)(2,1)S(1)} %copy-done, bf16[128,256]{1,0:T(8,128)(2,1)} %get-tuple-element.21.attn_hbm, f32[2,1,128]{2,1,0:T(1,128)S(1)} %get-tuple-element.22.logs_ref), custom_call_target="tpu_custom_call" | custom-call | flops 268435456 | bytes 3287040 | tf_op jit(solution)/shard_map/cotangent/pallas_call | solution.py:28
  31.2 1.9 %all-gather.2 = bf16[288,256]{1,0:T(8,128)(2,1)S(1)} all-gather(bf16[144,256]{1,0:T(8,128)(2,1)S(1)} %get-tuple-element.28.ga_ref), channel_id=4, replica_groups={{0,8},{16,24},{32,40},{48,56},{64,72},{80,88},{96,104},{112,120},{128,1..., dimensions={0}, use_global_device_ids=true | all-gather | bytes 221184 | tf_op jit(solution)/shard_map/all_gather | solution.py:248
  33.1 0.0 copy-start.1
  33.1 0.0 copy-start.4
  33.1 4.6 %collective-permute-start.1 = (bf16[2,144,256]{2,1,0:T(8,128)(2,1)S(1)}, bf16[2,144,256]{2,1,0:T(8,128)(2,1)S(1)}, u32[]{:S(2)}, u32[]{:S(2)}) collective-permute-start(bf16[2,144,256]{2,1,0:T(8,128)(2,1)S(1)} %bitcast.11), channel_id=1, source_target_pairs={{0,16},{16,32},{32,48},{48,64},{64,80},{80,96},{96,112},{112,128},... | collective-permute-start | bytes 442376 | tf_op jit(solution)/shard_map/ppermute | solution.py:243
  37.7 6.1 %all-to-all-start.1 = ((bf16[8,128,512]{2,1,0:T(8,128)(2,1)}), bf16[8,128,512]{2,1,0:T(8,128)(2,1)S(1)}, u32[]{:S(2)}, u32[]{:S(2)}) async-start(bf16[8,128,512]{2,1,0:T(8,128)(2,1)} %get-tuple-element.25), calls=%async_computation.1 | async-start | bytes 2097152 | tf_op jit(solution)/shard_map/all_to_all | solution.py:327
  43.9 2.3 %query.1 = bf16[128,256]{1,0:T(8,128)(2,1)} custom-call(bf16[640,768]{1,0:T(8,128)(2,1)} %get-tuple-element.26.win_hbm.win_ref, bf16[2,128,640]{2,1,0:T(8,128)(2,1)} %get-tuple-element.27.probs_hbm, bf16[144,256]{1,0:T(8,128)(2,1)S(1)} %get-tuple-element.28.ga_ref, f32[2,128,1]{2,1,0:T(8,128)S(1)} %get-tuple-element.29.delta_ref), custom_call_target="tpu_custom_call" | custom-call | flops 83886080 | bytes 1451008 | tf_op jit(solution)/shard_map/query/pallas_call | solution.py:28
  46.2 0.0 collective-permute-done.1
  46.2 2.0 %all-gather.3 = bf16[4,144,256]{2,1,0:T(8,128)(2,1)S(1)} all-gather(bf16[2,144,256]{2,1,0:T(8,128)(2,1)S(1)} %collective-permute-done.1), channel_id=5, replica_groups={{0,8},{16,24},{32,40},{48,56},{64,72},{80,88},{96,104},{112,120},{128,1..., dimensions={0}, use_global_device_ids=true | all-gather | bytes 442368 | tf_op jit(solution)/shard_map/all_gather | solution.py:248
  48.2 0.0 copy-done.1
  48.2 0.0 copy-done.4
  48.2 1.3 %key.1 = (bf16[128,256]{1,0:T(8,128)(2,1)}, bf16[128,256]{1,0:T(8,128)(2,1)}) custom-call(s32[1]{0:T(128)} %bitcast.1.where_ref, bf16[640,768]{1,0:T(8,128)(2,1)S(1)} %copy-done.1, f32[2,128,640]{2,1,0:T(8,128)S(1)} %copy-done.4, bf16[2,144,256]{2,1,0:T(8,128)(2,1)S(1)} %bitcast.12, bf16[2,2,144,256]{3,2,1,0:T(8,128)(2,1)S(1)} %bitcast.10), custom_call_target="tpu_custom_call" | custom-call | flops 30000001024 | bytes 2211844 | tf_op jit(solution)/shard_map/key/pallas_call | solution.py:28
  49.5 8.4 %all-to-all-done.1.x_ref = bf16[8,128,512]{2,1,0:T(8,128)(2,1)S(1)} async-done(((bf16[8,128,512]{2,1,0:T(8,128)(2,1)}), bf16[8,128,512]{2,1,0:T(8,128)(2,1)S(1)}, u32[]{:S(2)}, u32[]{:S(2)}) %all-to-all-start.1) | async-done | bytes 1048608 | tf_op jit(solution)/shard_map/all_to_all | solution.py:327
  57.9 0.8 %mixed.1 = bf16[128,512]{1,0:T(8,128)(2,1)} custom-call(bf16[8,128,512]{2,1,0:T(8,128)(2,1)S(1)} %all-to-all-done.1.x_ref), custom_call_target="tpu_custom_call" | custom-call | bytes 1179648 | tf_op jit(solution)/shard_map/mixed/pallas_call | solution.py:28
Async XLA Ops:
  3.7 14.6 %collective-permute-start = (bf16[2,128,768]{2,1,0:T(8,128)(2,1)S(1)}, bf16[2,128,768]{2,1,0:T(8,128)(2,1)}, u32[]{:S(2)}, u32[]{:S(2)}) collective-permute-start(bf16[2,128,768]{2,1,0:T(8,128)(2,1)S(1)} %bitcast.6), channel_id=1, source_target_pairs={{0,16},{16,32},{32,48},{48,64},{64,80},{80,96},{96,112},{112,128},... | collective-permute-start | bytes 1179656 | tf_op jit(solution)/shard_map/ppermute | solution.py:243
  8.2 12.7 %copy-start = (bf16[256,4096]{1,0:T(8,128)(2,1)S(1)}, bf16[256,4096]{1,0:T(8,128)(2,1)}, u32[]{:S(2)}) copy-start(bf16[256,4096]{1,0:T(8,128)(2,1)} %w_ref.3) | copy-start | bytes 6291460
  8.2 12.7 %copy-start.2 = (s32[2]{0:T(128)S(1)}, s32[2]{0:T(128)}, u32[]{:S(2)}) copy-start(s32[2]{0:T(128)} %dil_ref.1) | copy-start | bytes 28
  8.2 12.7 %copy-start.3 = (s32[64]{0:T(128)S(1)}, s32[64]{0:T(128)}, u32[]{:S(2)}) copy-start(s32[64]{0:T(128)} %param.12) | copy-start | bytes 772
  9.3 20.9 %all-to-all-start = ((bf16[8,128,512]{2,1,0:T(8,128)(2,1)}), bf16[8,128,512]{2,1,0:T(8,128)(2,1)S(1)}, u32[]{:S(2)}, u32[]{:S(2)}) async-start(bf16[8,128,512]{2,1,0:T(8,128)(2,1)} %spread.1), calls=%async_computation | async-start | bytes 2097152 | tf_op jit(solution)/shard_map/all_to_all | solution.py:278
  33.1 15.1 %copy-start.1 = (bf16[640,768]{1,0:T(8,128)(2,1)S(1)}, bf16[640,768]{1,0:T(8,128)(2,1)}, u32[]{:S(2)}) copy-start(bf16[640,768]{1,0:T(8,128)(2,1)} %get-tuple-element.26.win_hbm.win_ref) | copy-start | bytes 2949124
  33.1 15.1 %copy-start.4 = (f32[2,128,640]{2,1,0:T(8,128)S(1)}, f32[2,128,640]{2,1,0:T(8,128)}, u32[]{:S(2)}) copy-start(f32[2,128,640]{2,1,0:T(8,128)} %get-tuple-element.30.back_ref) | copy-start | bytes 1966084
  33.1 13.1 %collective-permute-start.1 = (bf16[2,144,256]{2,1,0:T(8,128)(2,1)S(1)}, bf16[2,144,256]{2,1,0:T(8,128)(2,1)S(1)}, u32[]{:S(2)}, u32[]{:S(2)}) collective-permute-start(bf16[2,144,256]{2,1,0:T(8,128)(2,1)S(1)} %bitcast.11), channel_id=1, source_target_pairs={{0,16},{16,32},{32,48},{48,64},{64,80},{80,96},{96,112},{112,128},... | collective-permute-start | bytes 442376 | tf_op jit(solution)/shard_map/ppermute | solution.py:243
  37.7 20.2 %all-to-all-start.1 = ((bf16[8,128,512]{2,1,0:T(8,128)(2,1)}), bf16[8,128,512]{2,1,0:T(8,128)(2,1)S(1)}, u32[]{:S(2)}, u32[]{:S(2)}) async-start(bf16[8,128,512]{2,1,0:T(8,128)(2,1)} %get-tuple-element.25), calls=%async_computation.1 | async-start | bytes 2097152 | tf_op jit(solution)/shard_map/all_to_all | solution.py:327

commit v11 on v10

--- a/solution.py
+++ b/solution.py
@@ -103,19 +103,18 @@
 
 
 def forward_kernel(
-    heads, total, where_ref, dil_ref, lens_ref, own_ref, far_ref, w_ref,
-    part_ref, probs_out, attn_out, win_out, back_out, logs_ref,
+    heads, total, where_ref, row_ref, dil_ref, lens_ref, own_ref, far_ref, w_ref,
+    keep_out, give_out, probs_out, attn_out, win_out, back_out, logs_ref,
     hold_ref, win_ref, back_ref, probs_ref, attn_ref, sems,
 ):
-    groups, span = part_ref.shape[0], part_ref.shape[2]
-    blocks = [slice(b * span, (b + 1) * span) for b in range(groups)]
+    cols, span = keep_out.shape[0], keep_out.shape[2]
     rows = own_ref.shape[1]
     width = own_ref.shape[2] // 3
     hd = width // heads
     keys = win_ref.shape[0]
     slab = where_ref[0]
     take_window(lax.rem(slab, 2), own_ref, far_ref, rows, win_ref)
-    copies = [pltpu.make_async_copy(win_ref, win_out, sems.at[groups])]
+    copies = [pltpu.make_async_copy(win_ref, win_out, sems.at[2 * cols])]
     copies[0].start()
     mine = slice(2 * rows, 3 * rows)
     first = slab * rows
@@ -135,10 +134,10 @@
         row_code = jnp.where(inside, residue(row_pos, row_doc), -1.0)
         col_code = residue(col_pos, col_doc)
         mask = (row_code == col_code) & (distance <= stride * float(HALF))
-        cols = slice(h * hd, (h + 1) * hd)
+        hcols = slice(h * hd, (h + 1) * hd)
         vcols = slice(width + h * hd, width + (h + 1) * hd)
         qcols = slice(2 * width + h * hd, 2 * width + (h + 1) * hd)
-        s = dot(win_ref[mine, qcols], win_ref[:, cols], ((1,), (1,))) * (hd**-0.5)
+        s = dot(win_ref[mine, qcols], win_ref[:, hcols], ((1,), (1,))) * (hd**-0.5)
         s = jnp.where(mask, s, -jnp.inf)
         top = jnp.max(s, axis=1, keepdims=True)
         e = jnp.exp(s - top)
@@ -146,19 +145,22 @@
         probs = (e * (1.0 / norm)).astype(BF)
         probs_ref[h] = probs
         logs_ref[h] = as_row(top + jnp.log(norm))
-        attn_ref[:, cols] = dot(probs, win_ref[:, vcols], ((1,), (0,))).astype(BF)
-        back = dot(win_ref[mine, cols], win_ref[:, qcols], ((1,), (1,))) * (hd**-0.5)
+        attn_ref[:, hcols] = dot(probs, win_ref[:, vcols], ((1,), (0,))).astype(BF)
+        back = dot(win_ref[mine, hcols], win_ref[:, qcols], ((1,), (1,))) * (hd**-0.5)
         back_ref[h] = jnp.where(mask, back, -jnp.inf)
-    copies.append(pltpu.make_async_copy(back_ref, back_out, sems.at[groups + 1]))
-    copies.append(pltpu.make_async_copy(probs_ref, probs_out, sems.at[groups + 2]))
-    copies.append(pltpu.make_async_copy(attn_ref, attn_out, sems.at[groups + 3]))
+    copies.append(pltpu.make_async_copy(back_ref, back_out, sems.at[2 * cols + 1]))
+    copies.append(pltpu.make_async_copy(probs_ref, probs_out, sems.at[2 * cols + 2]))
+    copies.append(pltpu.make_async_copy(attn_ref, attn_out, sems.at[2 * cols + 3]))
     for c in copies[1:]:
         c.start()
     attn = attn_ref[...]
-    for b in range(groups):
-        hold_ref[b] = dot(attn, w_ref[:, blocks[b]], ((1,), (0,))).astype(BF)
-        copies.append(pltpu.make_async_copy(hold_ref.at[b], part_ref.at[b], sems.at[b]))
-        copies[-1].start()
+    for half, (r, out) in enumerate(((1 - row_ref[0], give_out), (row_ref[0], keep_out))):
+        for c in range(cols):
+            i = half * cols + c
+            block = pl.ds(pl.multiple_of((r * cols + c) * span, span), span)
+            hold_ref[i] = dot(attn, w_ref[:, block], ((1,), (0,))).astype(BF)
+            copies.append(pltpu.make_async_copy(hold_ref.at[i], out.at[c], sems.at[i]))
+            copies[-1].start()
     for c in copies:
         c.wait()
 
@@ -229,6 +231,16 @@
         dv_ref[:, cols] = dot(weight.astype(BF), ga_ref[:, cols], ((1,), (0,))).astype(BF)
 
 
+def rows_kernel(keep_ref, got_ref, out_ref, hold_ref, sems):
+    copies = []
+    for c in range(keep_ref.shape[0]):
+        hold_ref[c] = (keep_ref[c].astype(F32) + got_ref[c].astype(F32)).astype(BF)
+        copies.append(pltpu.make_async_copy(hold_ref.at[c], out_ref.at[c], sems.at[c]))
+        copies[-1].start()
+    for c in copies:
+        c.wait()
+
+
 def mixed_kernel(x_ref, o_ref):
     total = x_ref[0].astype(F32)
     for c in range(1, x_ref.shape[0]):
@@ -254,7 +266,11 @@
     groups = lax.axis_size("head")
     span = mixed_grad.shape[1]
     total = rows * lax.axis_size("ctx")
+    cols = groups // 2
+    along_row = [[r * cols + c for c in range(cols)] for r in range(2)]
+    other_row = [(i, (i + cols) % groups) for i in range(groups)]
     where = lax.axis_index("ctx").astype(jnp.int32).reshape(1)
+    row = (lax.axis_index("head").astype(jnp.int32) // cols).reshape(1)
     lens = lengths.reshape(1, -1)
 
     kvq, mgv = call(
@@ -277,17 +293,18 @@
     )
     gathered = lax.all_to_all(spread, "head", 0, 0, tiled=True)
     far = in_chip(near)
-    part, probs, attn, window, back, logs = call(
+    keep, give, probs, attn, window, back, logs = call(
         functools.partial(forward_kernel, heads, total),
         [
-            shape((groups, rows, span), BF),
+            shape((cols, rows, span), BF),
+            shape((cols, rows, span), BF),
             shape((heads, rows, 5 * rows), BF),
             shape((rows, width), BF),
             shape((5 * rows, 3 * width), BF),
             shape((heads, rows, 5 * rows), F32),
             shape((heads, 1, rows), F32),
         ],
-        [where, dilation, lens, own2, far, out_weight],
+        [where, row, dilation, lens, own2, far, out_weight],
         "forward",
         flops=80 * 2 * rows * width * (groups * span + 15 * rows),
         scratch=[
@@ -298,8 +315,9 @@
             pltpu.VMEM((rows, width), BF),
             pltpu.SemaphoreType.DMA((groups + 4,)),
         ],
-        hbm_out=(0, 1, 2, 3, 4),
-    )
+        hbm_out=(0, 1, 2, 3, 4, 5),
+    )
+    got_half = lax.ppermute(give, "head", other_row)
     ga, delta = call(
         functools.partial(cotangent_kernel, heads),
         [shape((rows + 16, width), BF), shape((heads, rows, 1), F32)],
@@ -309,7 +327,7 @@
         scratch=[pltpu.VMEM((rows, width), BF), pltpu.SemaphoreType.DMA],
         hbm_in=(2,),
     )
-    ga2, ga, part = lax.optimization_barrier((in_chip(ga), ga, part))
+    ga2, ga, keep = lax.optimization_barrier((in_chip(ga), ga, keep))
     ga_near = to_neighbours(ga2)
     (dq,) = call(
         functools.partial(query_kernel, heads),
@@ -324,7 +342,15 @@
         ],
         hbm_in=(0, 1),
     )
-    summed = lax.all_to_all(part, "head", 0, 0, tiled=True)
+    (half,) = call(
+        rows_kernel,
+        [shape((cols, rows, span), BF)],
+        [keep, got_half],
+        "rows",
+        scratch=[pltpu.VMEM((cols, rows, span), BF), pltpu.SemaphoreType.DMA((cols,))],
+        hbm_out=(0,),
+    )
+    summed = lax.all_to_all(half, "head", 0, 0, tiled=True, axis_index_groups=along_row)
     (mixed,) = call(mixed_kernel, [shape((rows, span), BF)], [summed], "mixed")
     dk, dv = call(
         functools.partial(key_kernel, heads),

time: 59.1 us -> 62.4 us (1.056)
  the two profiles are of different devices: /device:TPU:448 before, /device:TPU:416 now
where the time goes in v11:
time: 62.4 us; the launch traced here: 62 us
  waiting for transfers between devices  24.6 us (39%)
  starting transfers between devices  15.4 us (25%)
  Pallas kernels  12.6 us (20%)
  blocking collectives  8.59 us (14%)
  between operations  0.76 us (1%)
    pallas_call x8, Pallas kernels, call(): pl.pallas_call(body, out_shape=[pltpu.HBM(x.shape, x.dtype) if i in hbm_o...  12.6 us
    ppermute x1, waiting for transfers between devices, per_device(): got_half = lax.ppermute(give, 'head', other_row)  11.6 us
    ppermute x2, waiting for transfers between devices, to_neighbours(): return lax.ppermute(x, 'ctx', ahead + back)  10.5 us
    all_gather x4, blocking collectives, in_chip(): return lax.all_gather(x, 'ctx', axis=0, axis_index_groups=pairs)  8.59 us
    ppermute x2, starting transfers between devices, to_neighbours(): return lax.ppermute(x, 'ctx', ahead + back)  4.75 us
    all_to_all x1, starting transfers between devices, per_device(): gathered = lax.all_to_all(spread, 'head', 0, 0, tiled=True)  4.43 us
    all_to_all x1, starting transfers between devices, per_device(): lax.all_to_all(half, 'head', 0, 0, tiled=True, axis_index_groups=along_row)  4.3 us
    all_to_all x1, waiting for transfers between devices, per_device(): lax.all_to_all(half, 'head', 0, 0, tiled=True, axis_index_groups=along_row)  2.48 us
  transfers between devices with their start and end apart: 5, of which 3 were waited for; matrix products, arithmetic and copies ran while one was open for 0% of the time, Pallas kernels for 18%

profile of v11, /device:TPU:416, one launch (start us, length us, event | category | flops | bytes accessed | tf_op | source)
XLA Modules:
  0.0 62.0 jit_solution(12088472637525186530)
XLA Ops:
  0.6 1.0 %pack.1 = (bf16[128,768]{1,0:T(8,128)(2,1)S(1)}, bf16[128,512]{1,0:T(8,128)(2,1)S(1)}) custom-call(bf16[128,256]{1,0:T(8,128)(2,1)} %k_ref.1, bf16[128,256]{1,0:T(8,128)(2,1)} %v_ref.1, bf16[128,256]{1,0:T(8,128)(2,1)} %q_ref.1, bf16[128,512]{1,0:T(8,128)(2,1)} %mg_ref.1), custom_call_target="tpu_custom_call" | custom-call | bytes 655360 | tf_op jit(solution)/shard_map/pack/pallas_call | solution.py:28
  1.6 2.1 %all-gather = bf16[256,768]{1,0:T(8,128)(2,1)S(1)} all-gather(bf16[128,768]{1,0:T(8,128)(2,1)S(1)} %get-tuple-element.21), channel_id=2, replica_groups={{0,8},{16,24},{32,40},{48,56},{64,72},{80,88},{96,104},{112,120},{128,1..., dimensions={0}, use_global_device_ids=true | all-gather | bytes 589824 | tf_op jit(solution)/shard_map/all_gather | solution.py:260
  3.7 2.7 %collective-permute-start = (bf16[2,128,768]{2,1,0:T(8,128)(2,1)S(1)}, bf16[2,128,768]{2,1,0:T(8,128)(2,1)}, u32[]{:S(2)}, u32[]{:S(2)}) collective-permute-start(bf16[2,128,768]{2,1,0:T(8,128)(2,1)S(1)} %bitcast.7), channel_id=1, source_target_pairs={{0,16},{16,32},{32,48},{48,64},{64,80},{80,96},{96,112},{112,128},... | collective-permute-start | bytes 1179656 | tf_op jit(solution)/shard_map/ppermute | solution.py:255
  6.4 0.0 copy-start
  6.4 0.0 copy-start.3
  6.4 0.0 copy-start.4
  6.5 1.0 %spread.1 = bf16[8,128,512]{2,1,0:T(8,128)(2,1)} custom-call(bf16[128,512]{1,0:T(8,128)(2,1)S(1)} %get-tuple-element.20.mg_ref, bf16[2,128,768]{2,1,0:T(8,128)(2,1)S(1)} %bitcast.8), custom_call_target="tpu_custom_call" | custom-call | bytes 1572864 | tf_op jit(solution)/shard_map/spread/pallas_call | solution.py:28
  7.5 4.4 %all-to-all-start = ((bf16[8,128,512]{2,1,0:T(8,128)(2,1)}), bf16[8,128,512]{2,1,0:T(8,128)(2,1)S(1)}, u32[]{:S(2)}, u32[]{:S(2)}) async-start(bf16[8,128,512]{2,1,0:T(8,128)(2,1)} %spread.1), calls=%async_computation | async-start | bytes 2097152 | tf_op jit(solution)/shard_map/all_to_all | solution.py:294
  11.9 10.5 %collective-permute-done = bf16[2,128,768]{2,1,0:T(8,128)(2,1)} collective-permute-done((bf16[2,128,768]{2,1,0:T(8,128)(2,1)S(1)}, bf16[2,128,768]{2,1,0:T(8,128)(2,1)}, u32[]{:S(2)}, u32[]{:S(2)}) %collective-permute-start) | collective-permute-done | bytes 393248 | tf_op jit(solution)/shard_map/ppermute | solution.py:255
  22.5 2.6 %all-gather.1 = bf16[4,128,768]{2,1,0:T(8,128)(2,1)S(1)} all-gather(bf16[2,128,768]{2,1,0:T(8,128)(2,1)} %collective-permute-done), channel_id=3, replica_groups={{0,8},{16,24},{32,40},{48,56},{64,72},{80,88},{96,104},{112,120},{128,1..., dimensions={0}, use_global_device_ids=true | all-gather | bytes 1179648 | tf_op jit(solution)/shard_map/all_gather | solution.py:260
  25.0 0.0 copy-done
  25.0 0.0 copy-done.3
  25.0 0.0 copy-done.4
  25.0 3.3 %forward.1 = (bf16[4,128,512]{2,1,0:T(8,128)(2,1)}, bf16[4,128,512]{2,1,0:T(8,128)(2,1)}, bf16[2,128,640]{2,1,0:T(8,128)(2,1)}, bf16[128,256]{1,0:T(8,128)(2,1)}...) custom-call(s32[1]{0:T(128)} %bitcast.1.where_ref, s32[1]{0:T(128)} %bitcast.2.row_ref, ...), custom_call_target="tpu_custom_call" | custom-call | flops 31541166080 | bytes 6358288 | tf_op jit(solution)/shard_map/forward/pallas_call | solution.py:28
  28.4 1.9 %collective-permute-start.1 = (bf16[4,128,512]{2,1,0:T(8,128)(2,1)}, bf16[4,128,512]{2,1,0:T(8,128)(2,1)}, u32[]{:S(2)}, u32[]{:S(2)}) collective-permute-start(bf16[4,128,512]{2,1,0:T(8,128)(2,1)} %get-tuple-element.27), channel_id=1, source_target_pairs={{0,4},{1,5},{2,6},{3,7},{4,0},{5,1},{6,2},{7,3},{8,12},{9,13},{10,... | collective-permute-start | bytes 1572872 | tf_op jit(solution)/shard_map/ppermute | solution.py:320
  30.3 0.0 all-to-all-done.mg_ref
  30.3 0.0 copy-start.2
  30.3 1.0 %cotangent.1 = (bf16[144,256]{1,0:T(8,128)(2,1)S(1)}, f32[2,128,1]{2,1,0:T(8,128)S(1)}) custom-call(bf16[8,128,512]{2,1,0:T(8,128)(2,1)S(1)} %all-to-all-done.mg_ref, bf16[256,4096]{1,0:T(8,128)(2,1)S(1)} %copy-done, bf16[128,256]{1,0:T(8,128)(2,1)} %get-tuple-element.22.attn_hbm, f32[2,1,128]{2,1,0:T(1,128)S(1)} %get-tuple-element.23.logs_ref), custom_call_target="tpu_custom_call" | custom-call | flops 268435456 | bytes 3287040 | tf_op jit(solution)/shard_map/cotangent/pallas_call | solution.py:28
  31.3 1.9 %all-gather.2 = bf16[288,256]{1,0:T(8,128)(2,1)S(1)} all-gather(bf16[144,256]{1,0:T(8,128)(2,1)S(1)} %get-tuple-element.30.ga_ref), channel_id=4, replica_groups={{0,8},{16,24},{32,40},{48,56},{64,72},{80,88},{96,104},{112,120},{128,1..., dimensions={0}, use_global_device_ids=true | all-gather | bytes 221184 | tf_op jit(solution)/shard_map/all_gather | solution.py:260
  33.3 0.0 copy-start.1
  33.3 0.0 copy-start.5
  33.3 2.1 %collective-permute-start.2 = (bf16[2,144,256]{2,1,0:T(8,128)(2,1)S(1)}, bf16[2,144,256]{2,1,0:T(8,128)(2,1)S(1)}, u32[]{:S(2)}, u32[]{:S(2)}) collective-permute-start(bf16[2,144,256]{2,1,0:T(8,128)(2,1)S(1)} %bitcast.12), channel_id=1, source_target_pairs={{0,16},{16,32},{32,48},{48,64},{64,80},{80,96},{96,112},{112,128},... | collective-permute-start | bytes 442376 | tf_op jit(solution)/shard_map/ppermute | solution.py:255
  35.3 11.6 %collective-permute-done.1.got_ref = bf16[4,128,512]{2,1,0:T(8,128)(2,1)} collective-permute-done((bf16[4,128,512]{2,1,0:T(8,128)(2,1)}, bf16[4,128,512]{2,1,0:T(8,128)(2,1)}, u32[]{:S(2)}, u32[]{:S(2)}) %collective-permute-start.1) | collective-permute-done | bytes 524320 | tf_op jit(solution)/shard_map/ppermute | solution.py:320
  46.9 0.0 copy-done.2
  46.9 1.9 %rows.1 = bf16[4,128,512]{2,1,0:T(8,128)(2,1)} custom-call(bf16[4,128,512]{2,1,0:T(8,128)(2,1)S(1)} %copy-done.2, bf16[4,128,512]{2,1,0:T(8,128)(2,1)} %collective-permute-done.1.got_ref), custom_call_target="tpu_custom_call" | custom-call | bytes 1572864 | tf_op jit(solution)/shard_map/rows/pallas_call | solution.py:28
  48.8 4.3 %all-to-all-start.1 = ((bf16[4,128,512]{2,1,0:T(8,128)(2,1)}), bf16[4,128,512]{2,1,0:T(8,128)(2,1)S(1)}, u32[]{:S(2)}, u32[]{:S(2)}) async-start(bf16[4,128,512]{2,1,0:T(8,128)(2,1)} %rows.1), calls=%async_computation.1 | async-start | bytes 1048576 | tf_op jit(solution)/shard_map/all_to_all | solution.py:353
  53.1 2.3 %query.1 = bf16[128,256]{1,0:T(8,128)(2,1)} custom-call(bf16[640,768]{1,0:T(8,128)(2,1)} %get-tuple-element.28.win_hbm.win_ref, bf16[2,128,640]{2,1,0:T(8,128)(2,1)} %get-tuple-element.29.probs_hbm, bf16[144,256]{1,0:T(8,128)(2,1)S(1)} %get-tuple-element.30.ga_ref, f32[2,128,1]{2,1,0:T(8,128)S(1)} %get-tuple-element.31.delta_ref), custom_call_target="tpu_custom_call" | custom-call | flops 83886080 | bytes 1451008 | tf_op jit(solution)/shard_map/query/pallas_call | solution.py:28
  55.5 0.0 collective-permute-done.2
  55.5 2.0 %all-gather.3 = bf16[4,144,256]{2,1,0:T(8,128)(2,1)S(1)} all-gather(bf16[2,144,256]{2,1,0:T(8,128)(2,1)S(1)} %collective-permute-done.2), channel_id=5, replica_groups={{0,8},{16,24},{32,40},{48,56},{64,72},{80,88},{96,104},{112,120},{128,1..., dimensions={0}, use_global_device_ids=true | all-gather | bytes 442368 | tf_op jit(solution)/shard_map/all_gather | solution.py:260
  57.5 0.0 copy-done.1
  57.5 0.0 copy-done.5
  57.5 1.3 %key.1 = (bf16[128,256]{1,0:T(8,128)(2,1)}, bf16[128,256]{1,0:T(8,128)(2,1)}) custom-call(s32[1]{0:T(128)} %bitcast.1.where_ref, bf16[640,768]{1,0:T(8,128)(2,1)S(1)} %copy-done.1, f32[2,128,640]{2,1,0:T(8,128)S(1)} %copy-done.5, bf16[2,144,256]{2,1,0:T(8,128)(2,1)S(1)} %bitcast.13, bf16[2,2,144,256]{3,2,1,0:T(8,128)(2,1)S(1)} %bitcast.11), custom_call_target="tpu_custom_call" | custom-call | flops 30000001024 | bytes 2211844 | tf_op jit(solution)/shard_map/key/pallas_call | solution.py:28
  58.8 2.5 %all-to-all-done.1.x_ref = bf16[4,128,512]{2,1,0:T(8,128)(2,1)S(1)} async-done(((bf16[4,128,512]{2,1,0:T(8,128)(2,1)}), bf16[4,128,512]{2,1,0:T(8,128)(2,1)S(1)}, u32[]{:S(2)}, u32[]{:S(2)}) %all-to-all-start.1) | async-done | bytes 524320 | tf_op jit(solution)/shard_map/all_to_all | solution.py:353
  61.3 0.7 %mixed.1 = bf16[128,512]{1,0:T(8,128)(2,1)} custom-call(bf16[4,128,512]{2,1,0:T(8,128)(2,1)S(1)} %all-to-all-done.1.x_ref), custom_call_target="tpu_custom_call" | custom-call | bytes 655360 | tf_op jit(solution)/shard_map/mixed/pallas_call | solution.py:28
Async XLA Ops:
  3.7 18.7 %collective-permute-start = (bf16[2,128,768]{2,1,0:T(8,128)(2,1)S(1)}, bf16[2,128,768]{2,1,0:T(8,128)(2,1)}, u32[]{:S(2)}, u32[]{:S(2)}) collective-permute-start(bf16[2,128,768]{2,1,0:T(8,128)(2,1)S(1)} %bitcast.7), channel_id=1, source_target_pairs={{0,16},{16,32},{32,48},{48,64},{64,80},{80,96},{96,112},{112,128},... | collective-permute-start | bytes 1179656 | tf_op jit(solution)/shard_map/ppermute | solution.py:255
  6.4 18.6 %copy-start = (bf16[256,4096]{1,0:T(8,128)(2,1)S(1)}, bf16[256,4096]{1,0:T(8,128)(2,1)}, u32[]{:S(2)}) copy-start(bf16[256,4096]{1,0:T(8,128)(2,1)} %w_ref.3) | copy-start | bytes 6291460
  6.4 18.6 %copy-start.3 = (s32[2]{0:T(128)S(1)}, s32[2]{0:T(128)}, u32[]{:S(2)}) copy-start(s32[2]{0:T(128)} %dil_ref.1) | copy-start | bytes 28
  6.4 18.6 %copy-start.4 = (s32[64]{0:T(128)S(1)}, s32[64]{0:T(128)}, u32[]{:S(2)}) copy-start(s32[64]{0:T(128)} %param.12) | copy-start | bytes 772
  7.5 22.8 %all-to-all-start = ((bf16[8,128,512]{2,1,0:T(8,128)(2,1)}), bf16[8,128,512]{2,1,0:T(8,128)(2,1)S(1)}, u32[]{:S(2)}, u32[]{:S(2)}) async-start(bf16[8,128,512]{2,1,0:T(8,128)(2,1)} %spread.1), calls=%async_computation | async-start | bytes 2097152 | tf_op jit(solution)/shard_map/all_to_all | solution.py:294
  28.4 18.6 %collective-permute-start.1 = (bf16[4,128,512]{2,1,0:T(8,128)(2,1)}, bf16[4,128,512]{2,1,0:T(8,128)(2,1)}, u32[]{:S(2)}, u32[]{:S(2)}) collective-permute-start(bf16[4,128,512]{2,1,0:T(8,128)(2,1)} %get-tuple-element.27), channel_id=1, source_target_pairs={{0,4},{1,5},{2,6},{3,7},{4,0},{5,1},{6,2},{7,3},{8,12},{9,13},{10,... | collective-permute-start | bytes 1572872 | tf_op jit(solution)/shard_map/ppermute | solution.py:320
  30.3 16.6 %copy-start.2 = (bf16[4,128,512]{2,1,0:T(8,128)(2,1)S(1)}, bf16[4,128,512]{2,1,0:T(8,128)(2,1)}, u32[]{:S(2)}) copy-start(bf16[4,128,512]{2,1,0:T(8,128)(2,1)} %get-tuple-element.26.keep_ref) | copy-start | bytes 1572868
  33.3 24.3 %copy-start.1 = (bf16[640,768]{1,0:T(8,128)(2,1)S(1)}, bf16[640,768]{1,0:T(8,128)(2,1)}, u32[]{:S(2)}) copy-start(bf16[640,768]{1,0:T(8,128)(2,1)} %get-tuple-element.28.win_hbm.win_ref) | copy-start | bytes 2949124
  33.3 24.3 %copy-start.5 = (f32[2,128,640]{2,1,0:T(8,128)S(1)}, f32[2,128,640]{2,1,0:T(8,128)}, u32[]{:S(2)}) copy-start(f32[2,128,640]{2,1,0:T(8,128)} %get-tuple-element.32.back_ref) | copy-start | bytes 1966084
  33.3 22.2 %collective-permute-start.2 = (bf16[2,144,256]{2,1,0:T(8,128)(2,1)S(1)}, bf16[2,144,256]{2,1,0:T(8,128)(2,1)S(1)}, u32[]{:S(2)}, u32[]{:S(2)}) collective-permute-start(bf16[2,144,256]{2,1,0:T(8,128)(2,1)S(1)} %bitcast.12), channel_id=1, source_target_pairs={{0,16},{16,32},{32,48},{48,64},{64,80},{80,96},{96,112},{112,128},... | collective-permute-start | bytes 442376 | tf_op jit(solution)/shard_map/ppermute | solution.py:255
  48.8 12.5 %all-to-all-start.1 = ((bf16[4,128,512]{2,1,0:T(8,128)(2,1)}), bf16[4,128,512]{2,1,0:T(8,128)(2,1)S(1)}, u32[]{:S(2)}, u32[]{:S(2)}) async-start(bf16[4,128,512]{2,1,0:T(8,128)(2,1)} %rows.1), calls=%async_computation.1 | async-start | bytes 1048576 | tf_op jit(solution)/shard_map/all_to_all | solution.py:353

commit v12 on v10

--- a/solution.py
+++ b/solution.py
@@ -309,7 +309,8 @@
         scratch=[pltpu.VMEM((rows, width), BF), pltpu.SemaphoreType.DMA],
         hbm_in=(2,),
     )
-    ga2, ga, part = lax.optimization_barrier((in_chip(ga), ga, part))
+    ga, part = lax.optimization_barrier((ga, part))
+    ga2, ga = lax.optimization_barrier((in_chip(ga), ga))
     ga_near = to_neighbours(ga2)
     (dq,) = call(
         functools.partial(query_kernel, heads),
@@ -326,12 +327,13 @@
     )
     summed = lax.all_to_all(part, "head", 0, 0, tiled=True)
     (mixed,) = call(mixed_kernel, [shape((rows, span), BF)], [summed], "mixed")
+    arrived, mixed = lax.optimization_barrier((ga_near, mixed))
     dk, dv = call(
         functools.partial(key_kernel, heads),
         [shape((rows, width), BF), shape((rows, width), BF)],
-        [where, window, back, ga2, in_chip(ga_near)],
+        [where, window, back, ga2, in_chip(arrived)],
         "key",
-        flops=30 * 10**9,
+        flops=2 * rows * width * 15 * rows,
         scratch=[pltpu.VMEM((5 * rows, width), BF)],
     )
     return mixed, dq, dk, dv

time: 59.1 us -> 58.7 us (level)
  the two profiles are of different devices: /device:TPU:448 before, /device:TPU:249 now
where the time goes in v12:
time: 58.7 us; the launch traced here: 58.4 us
  waiting for transfers between devices  18.4 us (31%)
  starting transfers between devices  17.4 us (30%)
  blocking collectives  11.2 us (19%)
  Pallas kernels  10.6 us (18%)
  between operations  0.72 us (1%)
    all_gather x4, blocking collectives, in_chip(): return lax.all_gather(x, 'ctx', axis=0, axis_index_groups=pairs)  11.2 us
    pallas_call x7, Pallas kernels, call(): pl.pallas_call(body, out_shape=[pltpu.HBM(x.shape, x.dtype) if i in hbm_o...  10.6 us
    ppermute x2, waiting for transfers between devices, to_neighbours(): return lax.ppermute(x, 'ctx', ahead + back)  9.38 us
    ppermute x2, starting transfers between devices, to_neighbours(): return lax.ppermute(x, 'ctx', ahead + back)  6.74 us
    all_to_all x1, starting transfers between devices, per_device(): summed = lax.all_to_all(part, 'head', 0, 0, tiled=True)  5.47 us
    all_to_all x1, starting transfers between devices, per_device(): gathered = lax.all_to_all(spread, 'head', 0, 0, tiled=True)  5.21 us
    all_to_all x1, waiting for transfers between devices, per_device(): gathered = lax.all_to_all(spread, 'head', 0, 0, tiled=True)  4.52 us
    all_to_all x1, waiting for transfers between devices, per_device(): summed = lax.all_to_all(part, 'head', 0, 0, tiled=True)  4.46 us
  transfers between devices with their start and end apart: 4, of which 4 were waited for; matrix products, arithmetic and copies ran while one was open for 0% of the time, Pallas kernels for 13%

profile of v12, /device:TPU:249, one launch (start us, length us, event | category | flops | bytes accessed | tf_op | source)
XLA Modules:
  0.0 58.4 jit_solution(10780380401386868539)
XLA Ops:
  0.6 1.0 %pack.1 = (bf16[128,768]{1,0:T(8,128)(2,1)S(1)}, bf16[128,512]{1,0:T(8,128)(2,1)S(1)}) custom-call(bf16[128,256]{1,0:T(8,128)(2,1)} %k_ref.1, bf16[128,256]{1,0:T(8,128)(2,1)} %v_ref.1, bf16[128,256]{1,0:T(8,128)(2,1)} %q_ref.1, bf16[128,512]{1,0:T(8,128)(2,1)} %mg_ref.1), custom_call_target="tpu_custom_call" | custom-call | bytes 655360 | tf_op jit(solution)/shard_map/pack/pallas_call | solution.py:28
  1.6 2.4 %all-gather = bf16[256,768]{1,0:T(8,128)(2,1)S(1)} all-gather(bf16[128,768]{1,0:T(8,128)(2,1)S(1)} %get-tuple-element.23), channel_id=2, replica_groups={{0,8},{16,24},{32,40},{48,56},{64,72},{80,88},{96,104},{112,120},{128,1..., dimensions={0}, use_global_device_ids=true | all-gather | bytes 589824 | tf_op jit(solution)/shard_map/all_gather | solution.py:248
  4.0 3.8 %collective-permute-start = (bf16[2,128,768]{2,1,0:T(8,128)(2,1)S(1)}, bf16[2,128,768]{2,1,0:T(8,128)(2,1)}, u32[]{:S(2)}, u32[]{:S(2)}) collective-permute-start(bf16[2,128,768]{2,1,0:T(8,128)(2,1)S(1)} %bitcast.6), channel_id=1, source_target_pairs={{0,16},{16,32},{32,48},{48,64},{64,80},{80,96},{96,112},{112,128},... | collective-permute-start | bytes 1179656 | tf_op jit(solution)/shard_map/ppermute | solution.py:243
  7.8 0.0 copy-start.1
  7.8 0.0 copy-start.3
  7.8 0.0 copy-start.4
  7.8 1.1 %spread.1 = bf16[8,128,512]{2,1,0:T(8,128)(2,1)} custom-call(bf16[128,512]{1,0:T(8,128)(2,1)S(1)} %get-tuple-element.22.mg_ref, bf16[2,128,768]{2,1,0:T(8,128)(2,1)S(1)} %bitcast.7), custom_call_target="tpu_custom_call" | custom-call | bytes 1572864 | tf_op jit(solution)/shard_map/spread/pallas_call | solution.py:28
  8.9 5.2 %all-to-all-start = ((bf16[8,128,512]{2,1,0:T(8,128)(2,1)}), bf16[8,128,512]{2,1,0:T(8,128)(2,1)S(1)}, u32[]{:S(2)}, u32[]{:S(2)}) async-start(bf16[8,128,512]{2,1,0:T(8,128)(2,1)} %spread.1), calls=%async_computation | async-start | bytes 2097152 | tf_op jit(solution)/shard_map/all_to_all | solution.py:278
  14.1 4.2 %collective-permute-done = bf16[2,128,768]{2,1,0:T(8,128)(2,1)} collective-permute-done((bf16[2,128,768]{2,1,0:T(8,128)(2,1)S(1)}, bf16[2,128,768]{2,1,0:T(8,128)(2,1)}, u32[]{:S(2)}, u32[]{:S(2)}) %collective-permute-start) | collective-permute-done | bytes 393248 | tf_op jit(solution)/shard_map/ppermute | solution.py:243
  18.3 3.2 %all-gather.1 = bf16[4,128,768]{2,1,0:T(8,128)(2,1)S(1)} all-gather(bf16[2,128,768]{2,1,0:T(8,128)(2,1)} %collective-permute-done), channel_id=3, replica_groups={{0,8},{16,24},{32,40},{48,56},{64,72},{80,88},{96,104},{112,120},{128,1..., dimensions={0}, use_global_device_ids=true | all-gather | bytes 1179648 | tf_op jit(solution)/shard_map/all_gather | solution.py:248
  21.5 0.0 copy-done.1
  21.5 0.0 copy-done.3
  21.5 0.0 copy-done.4
  21.5 3.2 %forward.1 = (bf16[8,128,512]{2,1,0:T(8,128)(2,1)}, bf16[2,128,640]{2,1,0:T(8,128)(2,1)}, bf16[128,256]{1,0:T(8,128)(2,1)}, bf16[640,768]{1,0:T(8,128)(2,1)}, f3...) custom-call(s32[1]{0:T(128)} %bitcast.1.where_ref, s32[2]{0:T(128)S(1)} %copy-done.3, s32[1,64]{1,0:T(1,128)S(1)} %bitcast.13, ...), custom_call_target="tpu_custom_call" | custom-call | flops 31541166080 | bytes 6358284 | tf_op jit(solution)/shard_map/forward/pallas_call | solution.py:28
  24.7 4.5 %all-to-all-done.mg_ref = bf16[8,128,512]{2,1,0:T(8,128)(2,1)S(1)} async-done(((bf16[8,128,512]{2,1,0:T(8,128)(2,1)}), bf16[8,128,512]{2,1,0:T(8,128)(2,1)S(1)}, u32[]{:S(2)}, u32[]{:S(2)}) %all-to-all-start) | async-done | bytes 1048608 | tf_op jit(solution)/shard_map/all_to_all | solution.py:278
  29.2 1.0 %cotangent.1 = (bf16[144,256]{1,0:T(8,128)(2,1)S(1)}, f32[2,128,1]{2,1,0:T(8,128)S(1)}) custom-call(bf16[8,128,512]{2,1,0:T(8,128)(2,1)S(1)} %all-to-all-done.mg_ref, bf16[256,4096]{1,0:T(8,128)(2,1)S(1)} %copy-done.1, bf16[128,256]{1,0:T(8,128)(2,1)} %get-tuple-element.24.attn_hbm, f32[2,1,128]{2,1,0:T(1,128)S(1)} %get-tuple-element.25.logs_ref), custom_call_target="tpu_custom_call" | custom-call | flops 268435456 | bytes 3287040 | tf_op jit(solution)/shard_map/cotangent/pallas_call | solution.py:28
  30.2 5.5 %all-to-all-start.1 = ((bf16[8,128,512]{2,1,0:T(8,128)(2,1)}), bf16[8,128,512]{2,1,0:T(8,128)(2,1)S(1)}, u32[]{:S(2)}, u32[]{:S(2)}) async-start(bf16[8,128,512]{2,1,0:T(8,128)(2,1)} %get-tuple-element.30), calls=%async_computation.1 | async-start | bytes 2097152 | tf_op jit(solution)/shard_map/all_to_all | solution.py:328
  35.7 0.0 copy-start
  35.7 0.0 copy-start.2
  35.7 3.6 %all-gather.2 = bf16[288,256]{1,0:T(8,128)(2,1)S(1)} all-gather(bf16[144,256]{1,0:T(8,128)(2,1)S(1)} %get-tuple-element.34.ga_ref), channel_id=4, replica_groups={{0,8},{16,24},{32,40},{48,56},{64,72},{80,88},{96,104},{112,120},{128,1..., dimensions={0}, use_global_device_ids=true | all-gather | bytes 221184 | tf_op jit(solution)/shard_map/all_gather | solution.py:248
  39.3 3.0 %collective-permute-start.1 = (bf16[2,144,256]{2,1,0:T(8,128)(2,1)S(1)}, bf16[2,144,256]{2,1,0:T(8,128)(2,1)S(1)}, u32[]{:S(2)}, u32[]{:S(2)}) collective-permute-start(bf16[2,144,256]{2,1,0:T(8,128)(2,1)S(1)} %bitcast.11), channel_id=1, source_target_pairs={{0,16},{16,32},{32,48},{48,64},{64,80},{80,96},{96,112},{112,128},... | collective-permute-start | bytes 442376 | tf_op jit(solution)/shard_map/ppermute | solution.py:243
  42.3 2.4 %query.1 = bf16[128,256]{1,0:T(8,128)(2,1)} custom-call(bf16[640,768]{1,0:T(8,128)(2,1)} %get-tuple-element.32.win_hbm.win_ref, bf16[2,128,640]{2,1,0:T(8,128)(2,1)} %get-tuple-element.33.probs_hbm, bf16[144,256]{1,0:T(8,128)(2,1)S(1)} %get-tuple-element.34.ga_ref, f32[2,128,1]{2,1,0:T(8,128)S(1)} %get-tuple-element.35.delta_ref), custom_call_target="tpu_custom_call" | custom-call | flops 83886080 | bytes 1451008 | tf_op jit(solution)/shard_map/query/pallas_call | solution.py:28
  44.7 4.5 %all-to-all-done.1.x_ref = bf16[8,128,512]{2,1,0:T(8,128)(2,1)S(1)} async-done(((bf16[8,128,512]{2,1,0:T(8,128)(2,1)}), bf16[8,128,512]{2,1,0:T(8,128)(2,1)S(1)}, u32[]{:S(2)}, u32[]{:S(2)}) %all-to-all-start.1) | async-done | bytes 1048608 | tf_op jit(solution)/shard_map/all_to_all | solution.py:328
  49.1 0.8 %mixed.1 = bf16[128,512]{1,0:T(8,128)(2,1)} custom-call(bf16[8,128,512]{2,1,0:T(8,128)(2,1)S(1)} %all-to-all-done.1.x_ref), custom_call_target="tpu_custom_call" | custom-call | bytes 1179648 | tf_op jit(solution)/shard_map/mixed/pallas_call | solution.py:28
  49.9 5.2 %collective-permute-done.1 = bf16[2,144,256]{2,1,0:T(8,128)(2,1)S(1)} collective-permute-done((bf16[2,144,256]{2,1,0:T(8,128)(2,1)S(1)}, bf16[2,144,256]{2,1,0:T(8,128)(2,1)S(1)}, u32[]{:S(2)}, u32[]{:S(2)}) %collective-permute-start.1) | collective-permute-done | bytes 147488 | tf_op jit(solution)/shard_map/ppermute | solution.py:243
  55.1 2.0 %all-gather.3 = bf16[4,144,256]{2,1,0:T(8,128)(2,1)S(1)} all-gather(bf16[2,144,256]{2,1,0:T(8,128)(2,1)S(1)} %collective-permute-done.1), channel_id=5, replica_groups={{0,8},{16,24},{32,40},{48,56},{64,72},{80,88},{96,104},{112,120},{128,1..., dimensions={0}, use_global_device_ids=true | all-gather | bytes 442368 | tf_op jit(solution)/shard_map/all_gather | solution.py:248
  57.1 0.0 copy-done
  57.1 0.0 copy-done.2
  57.1 1.3 %key.1 = (bf16[128,256]{1,0:T(8,128)(2,1)}, bf16[128,256]{1,0:T(8,128)(2,1)}) custom-call(s32[1]{0:T(128)} %bitcast.1.where_ref, bf16[640,768]{1,0:T(8,128)(2,1)S(1)} %copy-done, f32[2,128,640]{2,1,0:T(8,128)S(1)} %copy-done.2, bf16[2,144,256]{2,1,0:T(8,128)(2,1)S(1)} %bitcast.12, bf16[2,2,144,256]{3,2,1,0:T(8,128)(2,1)S(1)} %bitcast.9), custom_call_target="tpu_custom_call" | custom-call | flops 125829120 | bytes 2211844 | tf_op jit(solution)/shard_map/key/pallas_call | solution.py:28
Async XLA Ops:
  4.0 14.3 %collective-permute-start = (bf16[2,128,768]{2,1,0:T(8,128)(2,1)S(1)}, bf16[2,128,768]{2,1,0:T(8,128)(2,1)}, u32[]{:S(2)}, u32[]{:S(2)}) collective-permute-start(bf16[2,128,768]{2,1,0:T(8,128)(2,1)S(1)} %bitcast.6), channel_id=1, source_target_pairs={{0,16},{16,32},{32,48},{48,64},{64,80},{80,96},{96,112},{112,128},... | collective-permute-start | bytes 1179656 | tf_op jit(solution)/shard_map/ppermute | solution.py:243
  7.8 13.7 %copy-start.1 = (bf16[256,4096]{1,0:T(8,128)(2,1)S(1)}, bf16[256,4096]{1,0:T(8,128)(2,1)}, u32[]{:S(2)}) copy-start(bf16[256,4096]{1,0:T(8,128)(2,1)} %w_ref.3) | copy-start | bytes 6291460
  7.8 13.7 %copy-start.3 = (s32[2]{0:T(128)S(1)}, s32[2]{0:T(128)}, u32[]{:S(2)}) copy-start(s32[2]{0:T(128)} %dil_ref.1) | copy-start | bytes 28
  7.8 13.7 %copy-start.4 = (s32[64]{0:T(128)S(1)}, s32[64]{0:T(128)}, u32[]{:S(2)}) copy-start(s32[64]{0:T(128)} %param.12) | copy-start | bytes 772
  8.9 20.4 %all-to-all-start = ((bf16[8,128,512]{2,1,0:T(8,128)(2,1)}), bf16[8,128,512]{2,1,0:T(8,128)(2,1)S(1)}, u32[]{:S(2)}, u32[]{:S(2)}) async-start(bf16[8,128,512]{2,1,0:T(8,128)(2,1)} %spread.1), calls=%async_computation | async-start | bytes 2097152 | tf_op jit(solution)/shard_map/all_to_all | solution.py:278
  30.2 18.9 %all-to-all-start.1 = ((bf16[8,128,512]{2,1,0:T(8,128)(2,1)}), bf16[8,128,512]{2,1,0:T(8,128)(2,1)S(1)}, u32[]{:S(2)}, u32[]{:S(2)}) async-start(bf16[8,128,512]{2,1,0:T(8,128)(2,1)} %get-tuple-element.30), calls=%async_computation.1 | async-start | bytes 2097152 | tf_op jit(solution)/shard_map/all_to_all | solution.py:328
  35.7 21.4 %copy-start = (bf16[640,768]{1,0:T(8,128)(2,1)S(1)}, bf16[640,768]{1,0:T(8,128)(2,1)}, u32[]{:S(2)}) copy-start(bf16[640,768]{1,0:T(8,128)(2,1)} %get-tuple-element.32.win_hbm.win_ref) | copy-start | bytes 2949124
  35.7 21.4 %copy-start.2 = (f32[2,128,640]{2,1,0:T(8,128)S(1)}, f32[2,128,640]{2,1,0:T(8,128)}, u32[]{:S(2)}) copy-start(f32[2,128,640]{2,1,0:T(8,128)} %get-tuple-element.36.back_ref) | copy-start | bytes 1966084
  39.3 15.8 %collective-permute-start.1 = (bf16[2,144,256]{2,1,0:T(8,128)(2,1)S(1)}, bf16[2,144,256]{2,1,0:T(8,128)(2,1)S(1)}, u32[]{:S(2)}, u32[]{:S(2)}) collective-permute-start(bf16[2,144,256]{2,1,0:T(8,128)(2,1)S(1)} %bitcast.11), channel_id=1, source_target_pairs={{0,16},{16,32},{32,48},{48,64},{64,80},{80,96},{96,112},{112,128},... | collective-permute-start | bytes 442376 | tf_op jit(solution)/shard_map/ppermute | solution.py:243

commit v13 on v12

--- a/solution.py
+++ b/solution.py
@@ -207,14 +207,28 @@
         dq_ref[:, cols] = (dot(slopes, win_ref[:, cols], ((1,), (0,))) * (hd**-0.5)).astype(BF)
 
 
-def key_kernel(heads, where_ref, win_ref, back_ref, own_ref, far_ref, dk_ref, dv_ref, ga_ref):
+def key_kernel(
+    heads, where_ref, win_ref, back_ref, pair_ref, prev_ref, cross_ref, next_ref,
+    dk_ref, dv_ref, ga_ref, tail_ref,
+):
     rows, width = dk_ref.shape
     hd = width // heads
     mine = slice(2 * rows, 3 * rows)
     core = lax.rem(where_ref[0], 2)
-    take_window(core, own_ref, far_ref, rows, ga_ref)
-    tails = [x[i, rows:, :].astype(F32) for x in (far_ref.at[0], own_ref, far_ref.at[1]) for i in range(2)]
-    tails = [jnp.where(core == 0, tails[i], tails[i + 1]) for i in range(5)]
+    pair = [pair_ref.at[0], pair_ref.at[1]]
+    orders = (
+        (prev_ref, cross_ref, pair[0], pair[1], next_ref),
+        (prev_ref, pair[0], pair[1], cross_ref, next_ref),
+    )
+    for value in range(2):
+
+        @pl.when(core == value)
+        def _(value=value):
+            for i, x in enumerate(orders[value]):
+                ga_ref[i * rows : (i + 1) * rows, :] = x[:rows, :]
+                tail_ref[i] = x[rows:, :]
+
+    tails = [tail_ref[i].astype(F32) for i in range(5)]
     stats = jnp.concatenate([jnp.stack([t[:, h * hd : (h + 1) * hd] for h in range(heads)]) for t in tails], axis=2)
     for h in range(heads):
         cols = slice(h * hd, (h + 1) * hd)
@@ -311,7 +325,11 @@
     )
     ga, part = lax.optimization_barrier((ga, part))
     ga2, ga = lax.optimization_barrier((in_chip(ga), ga))
-    ga_near = to_neighbours(ga2)
+    count = lax.axis_size("ctx")
+    swaps = [(i, i + 1) for i in range(1, count - 1, 2)]
+    prev_ga = lax.ppermute(ga, "ctx", [(i, i + 2) for i in range(count - 2)])
+    next_ga = lax.ppermute(ga, "ctx", [(i + 2, i) for i in range(count - 2)])
+    cross_ga = lax.ppermute(ga, "ctx", swaps + [(b, a) for a, b in swaps])
     (dq,) = call(
         functools.partial(query_kernel, heads),
         [shape((rows, width), BF)],
@@ -327,14 +345,14 @@
     )
     summed = lax.all_to_all(part, "head", 0, 0, tiled=True)
     (mixed,) = call(mixed_kernel, [shape((rows, span), BF)], [summed], "mixed")
-    arrived, mixed = lax.optimization_barrier((ga_near, mixed))
+    next_ga, mixed = lax.optimization_barrier((next_ga, mixed))
     dk, dv = call(
         functools.partial(key_kernel, heads),
         [shape((rows, width), BF), shape((rows, width), BF)],
-        [where, window, back, ga2, in_chip(arrived)],
+        [where, window, back, ga2, prev_ga, cross_ga, next_ga],
         "key",
         flops=2 * rows * width * 15 * rows,
-        scratch=[pltpu.VMEM((5 * rows, width), BF)],
+        scratch=[pltpu.VMEM((5 * rows, width), BF), pltpu.VMEM((5, 16, width), BF)],
     )
     return mixed, dq, dk, dv
 

time: 58.7 us -> 60.4 us (1.029)
  starting transfers between devices: 17.4 us -> 27.4 us
  waiting for transfers between devices: 18.4 us -> 12.1 us
  blocking collectives: 11.2 us -> 9.07 us
    ppermute x0 -> x3, starting transfers between devices: none -> 12.9 us  [the longest x1 6.5 us: per_device(): prev_ga = lax.ppermute(ga, 'ctx', [(i, i + 2) for i in range(count - 2)])]
    ppermute x2 -> x1, waiting for transfers between devices: 9.38 us -> 4.22 us  [to_neighbours(): return lax.ppermute(x, 'ctx', ahead + back)]
    all_to_all x1, waiting for transfers between devices: 4.46 us -> 0.01 us  [per_device(): summed = lax.all_to_all(part, 'head', 0, 0, tiled=True)]
    ppermute x0 -> x3, waiting for transfers between devices: none -> 3.32 us  [the longest x1 3.32 us: per_device(): cross_ga = lax.ppermute(ga, 'ctx', swaps + [(b, a) for a, b in swaps])]
    ppermute x2 -> x1, starting transfers between devices: 6.74 us -> 3.75 us  [to_neighbours(): return lax.ppermute(x, 'ctx', ahead + back)]
    all_gather x4 -> x3, blocking collectives: 11.2 us -> 9.07 us  [in_chip(): return lax.all_gather(x, 'ctx', axis=0, axis_index_groups=pairs)]
  transfers between devices with their start and end apart: 4 -> 6, of which waited for: 4 -> 3; matrix products, arithmetic and copies ran while one was open for 0% -> 0% of each run, Pallas kernels for 13% -> 12%
where the time goes in v13:
time: 60.4 us; the launch traced here: 60 us
  starting transfers between devices  27.4 us (45%)
  waiting for transfers between devices  12.1 us (20%)
  Pallas kernels  10.6 us (18%)
  blocking collectives  9.07 us (15%)
  between operations  0.76 us (1%)
    pallas_call x7, Pallas kernels, call(): pl.pallas_call(body, out_shape=[pltpu.HBM(x.shape, x.dtype) if i in hbm_o...  10.6 us
    all_gather x3, blocking collectives, in_chip(): return lax.all_gather(x, 'ctx', axis=0, axis_index_groups=pairs)  9.07 us
    ppermute x1, starting transfers between devices, per_device(): prev_ga = lax.ppermute(ga, 'ctx', [(i, i + 2) for i in range(count - 2)])  6.5 us
    all_to_all x1, starting transfers between devices, per_device(): summed = lax.all_to_all(part, 'head', 0, 0, tiled=True)  5.59 us
    all_to_all x1, starting transfers between devices, per_device(): gathered = lax.all_to_all(spread, 'head', 0, 0, tiled=True)  5.21 us
    all_to_all x1, waiting for transfers between devices, per_device(): gathered = lax.all_to_all(spread, 'head', 0, 0, tiled=True)  4.52 us
    ppermute x1, waiting for transfers between devices, to_neighbours(): return lax.ppermute(x, 'ctx', ahead + back)  4.22 us
    ppermute x1, starting transfers between devices, to_neighbours(): return lax.ppermute(x, 'ctx', ahead + back)  3.75 us
  transfers between devices with their start and end apart: 6, of which 3 were waited for; matrix products, arithmetic and copies ran while one was open for 0% of the time, Pallas kernels for 12%

profile of v13, /device:TPU:249, one launch (start us, length us, event | category | flops | bytes accessed | tf_op | source)
XLA Modules:
  0.0 60.0 jit_solution(5252119090811037715)
XLA Ops:
  0.6 1.0 %pack.1 = (bf16[128,768]{1,0:T(8,128)(2,1)S(1)}, bf16[128,512]{1,0:T(8,128)(2,1)S(1)}) custom-call(bf16[128,256]{1,0:T(8,128)(2,1)} %k_ref.1, bf16[128,256]{1,0:T(8,128)(2,1)} %v_ref.1, bf16[128,256]{1,0:T(8,128)(2,1)} %q_ref.1, bf16[128,512]{1,0:T(8,128)(2,1)} %mg_ref.1), custom_call_target="tpu_custom_call" | custom-call | bytes 655360 | tf_op jit(solution)/shard_map/pack/pallas_call | solution.py:28
  1.6 2.4 %all-gather = bf16[256,768]{1,0:T(8,128)(2,1)S(1)} all-gather(bf16[128,768]{1,0:T(8,128)(2,1)S(1)} %get-tuple-element.23), channel_id=2, replica_groups={{0,8},{16,24},{32,40},{48,56},{64,72},{80,88},{96,104},{112,120},{128,1..., dimensions={0}, use_global_device_ids=true | all-gather | bytes 589824 | tf_op jit(solution)/shard_map/all_gather | solution.py:262
  4.0 3.8 %collective-permute-start = (bf16[2,128,768]{2,1,0:T(8,128)(2,1)S(1)}, bf16[2,128,768]{2,1,0:T(8,128)(2,1)}, u32[]{:S(2)}, u32[]{:S(2)}) collective-permute-start(bf16[2,128,768]{2,1,0:T(8,128)(2,1)S(1)} %bitcast.5), channel_id=1, source_target_pairs={{0,16},{16,32},{32,48},{48,64},{64,80},{80,96},{96,112},{112,128},... | collective-permute-start | bytes 1179656 | tf_op jit(solution)/shard_map/ppermute | solution.py:257
  7.8 0.0 copy-start.1
  7.8 0.0 copy-start.3
  7.8 0.0 copy-start.4
  7.8 1.0 %spread.1 = bf16[8,128,512]{2,1,0:T(8,128)(2,1)} custom-call(bf16[128,512]{1,0:T(8,128)(2,1)S(1)} %get-tuple-element.22.mg_ref, bf16[2,128,768]{2,1,0:T(8,128)(2,1)S(1)} %bitcast.6), custom_call_target="tpu_custom_call" | custom-call | bytes 1572864 | tf_op jit(solution)/shard_map/spread/pallas_call | solution.py:28
  8.9 5.2 %all-to-all-start = ((bf16[8,128,512]{2,1,0:T(8,128)(2,1)}), bf16[8,128,512]{2,1,0:T(8,128)(2,1)S(1)}, u32[]{:S(2)}, u32[]{:S(2)}) async-start(bf16[8,128,512]{2,1,0:T(8,128)(2,1)} %spread.1), calls=%async_computation | async-start | bytes 2097152 | tf_op jit(solution)/shard_map/all_to_all | solution.py:292
  14.1 4.2 %collective-permute-done = bf16[2,128,768]{2,1,0:T(8,128)(2,1)} collective-permute-done((bf16[2,128,768]{2,1,0:T(8,128)(2,1)S(1)}, bf16[2,128,768]{2,1,0:T(8,128)(2,1)}, u32[]{:S(2)}, u32[]{:S(2)}) %collective-permute-start) | collective-permute-done | bytes 393248 | tf_op jit(solution)/shard_map/ppermute | solution.py:257
  18.3 3.2 %all-gather.1 = bf16[4,128,768]{2,1,0:T(8,128)(2,1)S(1)} all-gather(bf16[2,128,768]{2,1,0:T(8,128)(2,1)} %collective-permute-done), channel_id=3, replica_groups={{0,8},{16,24},{32,40},{48,56},{64,72},{80,88},{96,104},{112,120},{128,1..., dimensions={0}, use_global_device_ids=true | all-gather | bytes 1179648 | tf_op jit(solution)/shard_map/all_gather | solution.py:262
  21.5 0.0 copy-done.1
  21.5 0.0 copy-done.3
  21.5 0.0 copy-done.4
  21.5 3.2 %forward.1 = (bf16[8,128,512]{2,1,0:T(8,128)(2,1)}, bf16[2,128,640]{2,1,0:T(8,128)(2,1)}, bf16[128,256]{1,0:T(8,128)(2,1)}, bf16[640,768]{1,0:T(8,128)(2,1)}, f3...) custom-call(s32[1]{0:T(128)} %bitcast.1.where_ref, s32[2]{0:T(128)S(1)} %copy-done.3, s32[1,64]{1,0:T(1,128)S(1)} %bitcast.10, ...), custom_call_target="tpu_custom_call" | custom-call | flops 31541166080 | bytes 6358284 | tf_op jit(solution)/shard_map/forward/pallas_call | solution.py:28
  24.7 4.5 %all-to-all-done.mg_ref = bf16[8,128,512]{2,1,0:T(8,128)(2,1)S(1)} async-done(((bf16[8,128,512]{2,1,0:T(8,128)(2,1)}), bf16[8,128,512]{2,1,0:T(8,128)(2,1)S(1)}, u32[]{:S(2)}, u32[]{:S(2)}) %all-to-all-start) | async-done | bytes 1048608 | tf_op jit(solution)/shard_map/all_to_all | solution.py:292
  29.2 1.0 %cotangent.1 = (bf16[144,256]{1,0:T(8,128)(2,1)S(1)}, f32[2,128,1]{2,1,0:T(8,128)S(1)}) custom-call(bf16[8,128,512]{2,1,0:T(8,128)(2,1)S(1)} %all-to-all-done.mg_ref, bf16[256,4096]{1,0:T(8,128)(2,1)S(1)} %copy-done.1, bf16[128,256]{1,0:T(8,128)(2,1)} %get-tuple-element.24.attn_hbm, f32[2,1,128]{2,1,0:T(1,128)S(1)} %get-tuple-element.25.logs_ref), custom_call_target="tpu_custom_call" | custom-call | flops 268435456 | bytes 3287040 | tf_op jit(solution)/shard_map/cotangent/pallas_call | solution.py:28
  30.2 0.0 copy-start
  30.2 0.0 copy-start.2
  30.2 5.6 %all-to-all-start.1 = ((bf16[8,128,512]{2,1,0:T(8,128)(2,1)}), bf16[8,128,512]{2,1,0:T(8,128)(2,1)S(1)}, u32[]{:S(2)}, u32[]{:S(2)}) async-start(bf16[8,128,512]{2,1,0:T(8,128)(2,1)} %get-tuple-element.30), calls=%async_computation.1 | async-start | bytes 2097152 | tf_op jit(solution)/shard_map/all_to_all | solution.py:346
  35.8 3.5 %all-gather.2 = bf16[288,256]{1,0:T(8,128)(2,1)S(1)} all-gather(bf16[144,256]{1,0:T(8,128)(2,1)S(1)} %get-tuple-element.29.ga_ref), channel_id=4, replica_groups={{0,8},{16,24},{32,40},{48,56},{64,72},{80,88},{96,104},{112,120},{128,1..., dimensions={0}, use_global_device_ids=true | all-gather | bytes 221184 | tf_op jit(solution)/shard_map/all_gather | solution.py:262
  39.3 3.0 %collective-permute-start.1 = (bf16[144,256]{1,0:T(8,128)(2,1)S(1)}, bf16[144,256]{1,0:T(8,128)(2,1)S(1)}, u32[]{:S(2)}, u32[]{:S(2)}) collective-permute-start(bf16[144,256]{1,0:T(8,128)(2,1)S(1)} %get-tuple-element.29.ga_ref), channel_id=1, source_target_pairs={{16,0},{24,8},{32,16},{40,24},{48,32},{56,40},{64,48},{72,56},{80,... | collective-permute-start | bytes 221192 | tf_op jit(solution)/shard_map/ppermute | solution.py:331
  42.3 6.5 %collective-permute-start.2 = (bf16[144,256]{1,0:T(8,128)(2,1)S(1)}, bf16[144,256]{1,0:T(8,128)(2,1)S(1)}, u32[]{:S(2)}, u32[]{:S(2)}) collective-permute-start(bf16[144,256]{1,0:T(8,128)(2,1)S(1)} %get-tuple-element.29.ga_ref), channel_id=1, source_target_pairs={{0,16},{8,24},{16,32},{24,40},{32,48},{40,56},{48,64},{56,72},{64,... | collective-permute-start | bytes 221192 | tf_op jit(solution)/shard_map/ppermute | solution.py:330
  48.8 3.4 %collective-permute-start.3 = (bf16[144,256]{1,0:T(8,128)(2,1)S(1)}, bf16[144,256]{1,0:T(8,128)(2,1)S(1)}, u32[]{:S(2)}, u32[]{:S(2)}) collective-permute-start(bf16[144,256]{1,0:T(8,128)(2,1)S(1)} %get-tuple-element.29.ga_ref), channel_id=1, source_target_pairs={{8,16},{24,32},{40,48},{56,64},{72,80},{88,96},{104,112},{120,128}... | collective-permute-start | bytes 221192 | tf_op jit(solution)/shard_map/ppermute | solution.py:332
  52.2 2.4 %query.1 = bf16[128,256]{1,0:T(8,128)(2,1)} custom-call(bf16[640,768]{1,0:T(8,128)(2,1)} %get-tuple-element.32.win_hbm.win_ref, bf16[2,128,640]{2,1,0:T(8,128)(2,1)} %get-tuple-element.33.probs_hbm, bf16[144,256]{1,0:T(8,128)(2,1)S(1)} %get-tuple-element.29.ga_ref, f32[2,128,1]{2,1,0:T(8,128)S(1)} %get-tuple-element.34.delta_ref), custom_call_target="tpu_custom_call" | custom-call | flops 83886080 | bytes 1451008 | tf_op jit(solution)/shard_map/query/pallas_call | solution.py:28
  54.6 0.0 all-to-all-done.1.x_ref
  54.6 0.8 %mixed.1 = bf16[128,512]{1,0:T(8,128)(2,1)} custom-call(bf16[8,128,512]{2,1,0:T(8,128)(2,1)S(1)} %all-to-all-done.1.x_ref), custom_call_target="tpu_custom_call" | custom-call | bytes 1179648 | tf_op jit(solution)/shard_map/mixed/pallas_call | solution.py:28
  55.4 0.0 collective-permute-done.1.next_ref
  55.4 0.0 collective-permute-done.2.prev_ref
  55.4 3.3 %collective-permute-done.3.cross_ref = bf16[144,256]{1,0:T(8,128)(2,1)S(1)} collective-permute-done((bf16[144,256]{1,0:T(8,128)(2,1)S(1)}, bf16[144,256]{1,0:T(8,128)(2,1)S(1)}, u32[]{:S(2)}, u32[]{:S(2)}) %collective-permute-start.3) | collective-permute-done | bytes 73760 | tf_op jit(solution)/shard_map/ppermute | solution.py:332
  58.7 0.0 copy-done
  58.7 0.0 copy-done.2
  58.7 1.3 %key.1 = (bf16[128,256]{1,0:T(8,128)(2,1)}, bf16[128,256]{1,0:T(8,128)(2,1)}) custom-call(s32[1]{0:T(128)} %bitcast.1.where_ref, bf16[640,768]{1,0:T(8,128)(2,1)S(1)} %copy-done, f32[2,128,640]{2,1,0:T(8,128)S(1)} %copy-done.2, bf16[2,144,256]{2,1,0:T(8,128)(2,1)S(1)} %bitcast.9, bf16[144,256]{1,0:T(8,128)(2,1)S(1)} %collective-permute-done.2.prev_ref, ...), custom_call_target="tpu_custom_call" | custom-call | flops 125829120 | bytes 2138116 | tf_op jit(solution)/shard_map/key/pallas_call | solution.py:28
Async XLA Ops:
  4.0 14.3 %collective-permute-start = (bf16[2,128,768]{2,1,0:T(8,128)(2,1)S(1)}, bf16[2,128,768]{2,1,0:T(8,128)(2,1)}, u32[]{:S(2)}, u32[]{:S(2)}) collective-permute-start(bf16[2,128,768]{2,1,0:T(8,128)(2,1)S(1)} %bitcast.5), channel_id=1, source_target_pairs={{0,16},{16,32},{32,48},{48,64},{64,80},{80,96},{96,112},{112,128},... | collective-permute-start | bytes 1179656 | tf_op jit(solution)/shard_map/ppermute | solution.py:257
  7.8 13.7 %copy-start.1 = (bf16[256,4096]{1,0:T(8,128)(2,1)S(1)}, bf16[256,4096]{1,0:T(8,128)(2,1)}, u32[]{:S(2)}) copy-start(bf16[256,4096]{1,0:T(8,128)(2,1)} %w_ref.3) | copy-start | bytes 6291460
  7.8 13.7 %copy-start.3 = (s32[2]{0:T(128)S(1)}, s32[2]{0:T(128)}, u32[]{:S(2)}) copy-start(s32[2]{0:T(128)} %dil_ref.1) | copy-start | bytes 28
  7.8 13.7 %copy-start.4 = (s32[64]{0:T(128)S(1)}, s32[64]{0:T(128)}, u32[]{:S(2)}) copy-start(s32[64]{0:T(128)} %param.12) | copy-start | bytes 772
  8.9 20.4 %all-to-all-start = ((bf16[8,128,512]{2,1,0:T(8,128)(2,1)}), bf16[8,128,512]{2,1,0:T(8,128)(2,1)S(1)}, u32[]{:S(2)}, u32[]{:S(2)}) async-start(bf16[8,128,512]{2,1,0:T(8,128)(2,1)} %spread.1), calls=%async_computation | async-start | bytes 2097152 | tf_op jit(solution)/shard_map/all_to_all | solution.py:292
  30.2 28.5 %copy-start = (bf16[640,768]{1,0:T(8,128)(2,1)S(1)}, bf16[640,768]{1,0:T(8,128)(2,1)}, u32[]{:S(2)}) copy-start(bf16[640,768]{1,0:T(8,128)(2,1)} %get-tuple-element.32.win_hbm.win_ref) | copy-start | bytes 2949124
  30.2 28.5 %copy-start.2 = (f32[2,128,640]{2,1,0:T(8,128)S(1)}, f32[2,128,640]{2,1,0:T(8,128)}, u32[]{:S(2)}) copy-start(f32[2,128,640]{2,1,0:T(8,128)} %get-tuple-element.35.back_ref) | copy-start | bytes 1966084
  30.2 24.4 %all-to-all-start.1 = ((bf16[8,128,512]{2,1,0:T(8,128)(2,1)}), bf16[8,128,512]{2,1,0:T(8,128)(2,1)S(1)}, u32[]{:S(2)}, u32[]{:S(2)}) async-start(bf16[8,128,512]{2,1,0:T(8,128)(2,1)} %get-tuple-element.30), calls=%async_computation.1 | async-start | bytes 2097152 | tf_op jit(solution)/shard_map/all_to_all | solution.py:346
  39.3 16.1 %collective-permute-start.1 = (bf16[144,256]{1,0:T(8,128)(2,1)S(1)}, bf16[144,256]{1,0:T(8,128)(2,1)S(1)}, u32[]{:S(2)}, u32[]{:S(2)}) collective-permute-start(bf16[144,256]{1,0:T(8,128)(2,1)S(1)} %get-tuple-element.29.ga_ref), channel_id=1, source_target_pairs={{16,0},{24,8},{32,16},{40,24},{48,32},{56,40},{64,48},{72,56},{80,... | collective-permute-start | bytes 221192 | tf_op jit(solution)/shard_map/ppermute | solution.py:331
  42.3 13.1 %collective-permute-start.2 = (bf16[144,256]{1,0:T(8,128)(2,1)S(1)}, bf16[144,256]{1,0:T(8,128)(2,1)S(1)}, u32[]{:S(2)}, u32[]{:S(2)}) collective-permute-start(bf16[144,256]{1,0:T(8,128)(2,1)S(1)} %get-tuple-element.29.ga_ref), channel_id=1, source_target_pairs={{0,16},{8,24},{16,32},{24,40},{32,48},{40,56},{48,64},{56,72},{64,... | collective-permute-start | bytes 221192 | tf_op jit(solution)/shard_map/ppermute | solution.py:330
  48.8 9.9 %collective-permute-start.3 = (bf16[144,256]{1,0:T(8,128)(2,1)S(1)}, bf16[144,256]{1,0:T(8,128)(2,1)S(1)}, u32[]{:S(2)}, u32[]{:S(2)}) collective-permute-start(bf16[144,256]{1,0:T(8,128)(2,1)S(1)} %get-tuple-element.29.ga_ref), channel_id=1, source_target_pairs={{8,16},{24,32},{40,48},{56,64},{72,80},{88,96},{104,112},{120,128}... | collective-permute-start | bytes 221192 | tf_op jit(solution)/shard_map/ppermute | solution.py:332

commit v14 on v12

--- a/solution.py
+++ b/solution.py
@@ -289,7 +289,7 @@
         ],
         [where, dilation, lens, own2, far, out_weight],
         "forward",
-        flops=80 * 2 * rows * width * (groups * span + 15 * rows),
+        flops=2 * rows * width * (groups * span + 15 * rows),
         scratch=[
             pltpu.VMEM((groups, rows, span), BF),
             pltpu.VMEM((5 * rows, 3 * width), BF),

time: 58.7 us -> 68.6 us (1.17)
  the two profiles are of different devices: /device:TPU:249 before, /device:TPU:261 now
where the time goes in v14:
time: 68.6 us; the launch traced here: 68.2 us
  blocking collectives  26.9 us (39%)
  starting transfers between devices  19.6 us (29%)
  Pallas kernels  10.6 us (15%)
  waiting for transfers between devices  10.4 us (15%)
  between operations  0.71 us (1%)
    all_gather x4, blocking collectives, in_chip(): return lax.all_gather(x, 'ctx', axis=0, axis_index_groups=pairs)  26.9 us
    pallas_call x7, Pallas kernels, call(): pl.pallas_call(body, out_shape=[pltpu.HBM(x.shape, x.dtype) if i in hbm_o...  10.6 us
    ppermute x2, starting transfers between devices, to_neighbours(): return lax.ppermute(x, 'ctx', ahead + back)  9.33 us
    ppermute x2, waiting for transfers between devices, to_neighbours(): return lax.ppermute(x, 'ctx', ahead + back)  5.67 us
    all_to_all x1, starting transfers between devices, per_device(): gathered = lax.all_to_all(spread, 'head', 0, 0, tiled=True)  5.27 us
    all_to_all x1, starting transfers between devices, per_device(): summed = lax.all_to_all(part, 'head', 0, 0, tiled=True)  4.96 us
    all_to_all x1, waiting for transfers between devices, per_device(): summed = lax.all_to_all(part, 'head', 0, 0, tiled=True)  4.68 us
  transfers between devices with their start and end apart: 4, of which 2 were waited for; matrix products, arithmetic and copies ran while one was open for 0% of the time, Pallas kernels for 9%

profile of v14, /device:TPU:261, one launch (start us, length us, event | category | flops | bytes accessed | tf_op | source)
XLA Modules:
  0.0 68.2 jit_solution(15532338831171370033)
XLA Ops:
  0.6 1.0 %pack.1 = (bf16[128,768]{1,0:T(8,128)(2,1)S(1)}, bf16[128,512]{1,0:T(8,128)(2,1)S(1)}) custom-call(bf16[128,256]{1,0:T(8,128)(2,1)} %k_ref.1, bf16[128,256]{1,0:T(8,128)(2,1)} %v_ref.1, bf16[128,256]{1,0:T(8,128)(2,1)} %q_ref.1, bf16[128,512]{1,0:T(8,128)(2,1)} %mg_ref.1), custom_call_target="tpu_custom_call" | custom-call | bytes 655360 | tf_op jit(solution)/shard_map/pack/pallas_call | solution.py:28
  1.6 2.4 %all-gather = bf16[256,768]{1,0:T(8,128)(2,1)S(1)} all-gather(bf16[128,768]{1,0:T(8,128)(2,1)S(1)} %get-tuple-element.23), channel_id=2, replica_groups={{0,8},{16,24},{32,40},{48,56},{64,72},{80,88},{96,104},{112,120},{128,1..., dimensions={0}, use_global_device_ids=true | all-gather | bytes 589824 | tf_op jit(solution)/shard_map/all_gather | solution.py:248
  4.0 0.0 copy-start
  4.0 0.0 copy-start.3
  4.0 0.0 copy-start.4
  4.0 1.1 %spread.1 = bf16[8,128,512]{2,1,0:T(8,128)(2,1)} custom-call(bf16[128,512]{1,0:T(8,128)(2,1)S(1)} %get-tuple-element.22.mg_ref, bf16[2,128,768]{2,1,0:T(8,128)(2,1)S(1)} %bitcast.6), custom_call_target="tpu_custom_call" | custom-call | bytes 1572864 | tf_op jit(solution)/shard_map/spread/pallas_call | solution.py:28
  5.1 5.3 %all-to-all-start = ((bf16[8,128,512]{2,1,0:T(8,128)(2,1)}), bf16[8,128,512]{2,1,0:T(8,128)(2,1)S(1)}, u32[]{:S(2)}, u32[]{:S(2)}) async-start(bf16[8,128,512]{2,1,0:T(8,128)(2,1)} %spread.1), calls=%async_computation | async-start | bytes 2097152 | tf_op jit(solution)/shard_map/all_to_all | solution.py:278
  10.4 4.1 %collective-permute-start = (bf16[2,128,768]{2,1,0:T(8,128)(2,1)S(1)}, bf16[2,128,768]{2,1,0:T(8,128)(2,1)}, u32[]{:S(2)}, u32[]{:S(2)}) collective-permute-start(bf16[2,128,768]{2,1,0:T(8,128)(2,1)S(1)} %bitcast.7), channel_id=1, source_target_pairs={{0,16},{16,32},{32,48},{48,64},{64,80},{80,96},{96,112},{112,128},... | collective-permute-start | bytes 1179656 | tf_op jit(solution)/shard_map/ppermute | solution.py:243
  14.4 5.7 %collective-permute-done = bf16[2,128,768]{2,1,0:T(8,128)(2,1)} collective-permute-done((bf16[2,128,768]{2,1,0:T(8,128)(2,1)S(1)}, bf16[2,128,768]{2,1,0:T(8,128)(2,1)}, u32[]{:S(2)}, u32[]{:S(2)}) %collective-permute-start) | collective-permute-done | bytes 393248 | tf_op jit(solution)/shard_map/ppermute | solution.py:243
  20.1 16.3 %all-gather.1 = bf16[4,128,768]{2,1,0:T(8,128)(2,1)S(1)} all-gather(bf16[2,128,768]{2,1,0:T(8,128)(2,1)} %collective-permute-done), channel_id=3, replica_groups={{0,8},{16,24},{32,40},{48,56},{64,72},{80,88},{96,104},{112,120},{128,1..., dimensions={0}, use_global_device_ids=true | all-gather | bytes 1179648 | tf_op jit(solution)/shard_map/all_gather | solution.py:248
  36.4 0.0 copy-done
  36.4 0.0 copy-done.3
  36.4 0.0 copy-done.4
  36.4 3.2 %forward.1 = (bf16[8,128,512]{2,1,0:T(8,128)(2,1)}, bf16[2,128,640]{2,1,0:T(8,128)(2,1)}, bf16[128,256]{1,0:T(8,128)(2,1)}, bf16[640,768]{1,0:T(8,128)(2,1)}, f3...) custom-call(s32[1]{0:T(128)} %bitcast.1.where_ref, s32[2]{0:T(128)S(1)} %copy-done.3, s32[1,64]{1,0:T(1,128)S(1)} %bitcast.13, ...), custom_call_target="tpu_custom_call" | custom-call | flops 394264576 | bytes 6358284 | tf_op jit(solution)/shard_map/forward/pallas_call | solution.py:28
  39.6 0.0 all-to-all-done.mg_ref
  39.6 1.0 %cotangent.1 = (bf16[144,256]{1,0:T(8,128)(2,1)S(1)}, f32[2,128,1]{2,1,0:T(8,128)S(1)}) custom-call(bf16[8,128,512]{2,1,0:T(8,128)(2,1)S(1)} %all-to-all-done.mg_ref, bf16[256,4096]{1,0:T(8,128)(2,1)S(1)} %copy-done, bf16[128,256]{1,0:T(8,128)(2,1)} %get-tuple-element.24.attn_hbm, f32[2,1,128]{2,1,0:T(1,128)S(1)} %get-tuple-element.25.logs_ref), custom_call_target="tpu_custom_call" | custom-call | flops 268435456 | bytes 3287040 | tf_op jit(solution)/shard_map/cotangent/pallas_call | solution.py:28
  40.6 5.0 %all-to-all-start.1 = ((bf16[8,128,512]{2,1,0:T(8,128)(2,1)}), bf16[8,128,512]{2,1,0:T(8,128)(2,1)S(1)}, u32[]{:S(2)}, u32[]{:S(2)}) async-start(bf16[8,128,512]{2,1,0:T(8,128)(2,1)} %get-tuple-element.30), calls=%async_computation.1 | async-start | bytes 2097152 | tf_op jit(solution)/shard_map/all_to_all | solution.py:328
  45.6 0.0 copy-start.1
  45.6 0.0 copy-start.2
  45.6 2.4 %all-gather.2 = bf16[288,256]{1,0:T(8,128)(2,1)S(1)} all-gather(bf16[144,256]{1,0:T(8,128)(2,1)S(1)} %get-tuple-element.34.ga_ref), channel_id=4, replica_groups={{0,8},{16,24},{32,40},{48,56},{64,72},{80,88},{96,104},{112,120},{128,1..., dimensions={0}, use_global_device_ids=true | all-gather | bytes 221184 | tf_op jit(solution)/shard_map/all_gather | solution.py:248
  48.0 5.3 %collective-permute-start.1 = (bf16[2,144,256]{2,1,0:T(8,128)(2,1)S(1)}, bf16[2,144,256]{2,1,0:T(8,128)(2,1)S(1)}, u32[]{:S(2)}, u32[]{:S(2)}) collective-permute-start(bf16[2,144,256]{2,1,0:T(8,128)(2,1)S(1)} %bitcast.11), channel_id=1, source_target_pairs={{0,16},{16,32},{32,48},{48,64},{64,80},{80,96},{96,112},{112,128},... | collective-permute-start | bytes 442376 | tf_op jit(solution)/shard_map/ppermute | solution.py:243
  53.2 2.3 %query.1 = bf16[128,256]{1,0:T(8,128)(2,1)} custom-call(bf16[640,768]{1,0:T(8,128)(2,1)} %get-tuple-element.32.win_hbm.win_ref, bf16[2,128,640]{2,1,0:T(8,128)(2,1)} %get-tuple-element.33.probs_hbm, bf16[144,256]{1,0:T(8,128)(2,1)S(1)} %get-tuple-element.34.ga_ref, f32[2,128,1]{2,1,0:T(8,128)S(1)} %get-tuple-element.35.delta_ref), custom_call_target="tpu_custom_call" | custom-call | flops 83886080 | bytes 1451008 | tf_op jit(solution)/shard_map/query/pallas_call | solution.py:28
  55.6 4.7 %all-to-all-done.1.x_ref = bf16[8,128,512]{2,1,0:T(8,128)(2,1)S(1)} async-done(((bf16[8,128,512]{2,1,0:T(8,128)(2,1)}), bf16[8,128,512]{2,1,0:T(8,128)(2,1)S(1)}, u32[]{:S(2)}, u32[]{:S(2)}) %all-to-all-start.1) | async-done | bytes 1048608 | tf_op jit(solution)/shard_map/all_to_all | solution.py:328
  60.3 0.8 %mixed.1 = bf16[128,512]{1,0:T(8,128)(2,1)} custom-call(bf16[8,128,512]{2,1,0:T(8,128)(2,1)S(1)} %all-to-all-done.1.x_ref), custom_call_target="tpu_custom_call" | custom-call | bytes 1179648 | tf_op jit(solution)/shard_map/mixed/pallas_call | solution.py:28
  61.1 0.0 collective-permute-done.1
  61.1 5.8 %all-gather.3 = bf16[4,144,256]{2,1,0:T(8,128)(2,1)S(1)} all-gather(bf16[2,144,256]{2,1,0:T(8,128)(2,1)S(1)} %collective-permute-done.1), channel_id=5, replica_groups={{0,8},{16,24},{32,40},{48,56},{64,72},{80,88},{96,104},{112,120},{128,1..., dimensions={0}, use_global_device_ids=true | all-gather | bytes 442368 | tf_op jit(solution)/shard_map/all_gather | solution.py:248
  66.9 0.0 copy-done.1
  66.9 0.0 copy-done.2
  66.9 1.3 %key.1 = (bf16[128,256]{1,0:T(8,128)(2,1)}, bf16[128,256]{1,0:T(8,128)(2,1)}) custom-call(s32[1]{0:T(128)} %bitcast.1.where_ref, bf16[640,768]{1,0:T(8,128)(2,1)S(1)} %copy-done.1, f32[2,128,640]{2,1,0:T(8,128)S(1)} %copy-done.2, bf16[2,144,256]{2,1,0:T(8,128)(2,1)S(1)} %bitcast.12, bf16[2,2,144,256]{3,2,1,0:T(8,128)(2,1)S(1)} %bitcast.10), custom_call_target="tpu_custom_call" | custom-call | flops 125829120 | bytes 2211844 | tf_op jit(solution)/shard_map/key/pallas_call | solution.py:28
Async XLA Ops:
  4.0 32.4 %copy-start = (bf16[256,4096]{1,0:T(8,128)(2,1)S(1)}, bf16[256,4096]{1,0:T(8,128)(2,1)}, u32[]{:S(2)}) copy-start(bf16[256,4096]{1,0:T(8,128)(2,1)} %w_ref.3) | copy-start | bytes 6291460
  4.0 32.4 %copy-start.3 = (s32[2]{0:T(128)S(1)}, s32[2]{0:T(128)}, u32[]{:S(2)}) copy-start(s32[2]{0:T(128)} %dil_ref.1) | copy-start | bytes 28
  4.0 32.4 %copy-start.4 = (s32[64]{0:T(128)S(1)}, s32[64]{0:T(128)}, u32[]{:S(2)}) copy-start(s32[64]{0:T(128)} %param.12) | copy-start | bytes 772
  5.1 34.5 %all-to-all-start = ((bf16[8,128,512]{2,1,0:T(8,128)(2,1)}), bf16[8,128,512]{2,1,0:T(8,128)(2,1)S(1)}, u32[]{:S(2)}, u32[]{:S(2)}) async-start(bf16[8,128,512]{2,1,0:T(8,128)(2,1)} %spread.1), calls=%async_computation | async-start | bytes 2097152 | tf_op jit(solution)/shard_map/all_to_all | solution.py:278
  10.4 9.7 %collective-permute-start = (bf16[2,128,768]{2,1,0:T(8,128)(2,1)S(1)}, bf16[2,128,768]{2,1,0:T(8,128)(2,1)}, u32[]{:S(2)}, u32[]{:S(2)}) collective-permute-start(bf16[2,128,768]{2,1,0:T(8,128)(2,1)S(1)} %bitcast.7), channel_id=1, source_target_pairs={{0,16},{16,32},{32,48},{48,64},{64,80},{80,96},{96,112},{112,128},... | collective-permute-start | bytes 1179656 | tf_op jit(solution)/shard_map/ppermute | solution.py:243
  40.6 19.7 %all-to-all-start.1 = ((bf16[8,128,512]{2,1,0:T(8,128)(2,1)}), bf16[8,128,512]{2,1,0:T(8,128)(2,1)S(1)}, u32[]{:S(2)}, u32[]{:S(2)}) async-start(bf16[8,128,512]{2,1,0:T(8,128)(2,1)} %get-tuple-element.30), calls=%async_computation.1 | async-start | bytes 2097152 | tf_op jit(solution)/shard_map/all_to_all | solution.py:328
  45.6 21.3 %copy-start.1 = (bf16[640,768]{1,0:T(8,128)(2,1)S(1)}, bf16[640,768]{1,0:T(8,128)(2,1)}, u32[]{:S(2)}) copy-start(bf16[640,768]{1,0:T(8,128)(2,1)} %get-tuple-element.32.win_hbm.win_ref) | copy-start | bytes 2949124
  45.6 21.3 %copy-start.2 = (f32[2,128,640]{2,1,0:T(8,128)S(1)}, f32[2,128,640]{2,1,0:T(8,128)}, u32[]{:S(2)}) copy-start(f32[2,128,640]{2,1,0:T(8,128)} %get-tuple-element.36.back_ref) | copy-start | bytes 1966084
  48.0 13.1 %collective-permute-start.1 = (bf16[2,144,256]{2,1,0:T(8,128)(2,1)S(1)}, bf16[2,144,256]{2,1,0:T(8,128)(2,1)S(1)}, u32[]{:S(2)}, u32[]{:S(2)}) collective-permute-start(bf16[2,144,256]{2,1,0:T(8,128)(2,1)S(1)} %bitcast.11), channel_id=1, source_target_pairs={{0,16},{16,32},{32,48},{48,64},{64,80},{80,96},{96,112},{112,128},... | collective-permute-start | bytes 442376 | tf_op jit(solution)/shard_map/ppermute | solution.py:243
